TPU v7x, 32 devices: a whole 2x2x4 slice. The times are simulated.
32 devices in a mesh: bricks: 32 (over z, y, x, core).
Axes of the slice: x: 2, y: 2, z: 4, core: 2. Of those that a mesh axis runs over, the one named last changes fastest.
Arguments:
- voxels: bfloat16 [192, 64, 512], P('bricks'), may hold values from -6 to 6
- kernel: bfloat16 [64, 8, 3, 3, 3], replicated, may hold values from -0.4375 to 0.4375
- bias: float32 [64], replicated, may hold values from -3 to 3
- cortex: int32 [192, 512], P('bricks'), may hold values 0 or 1
- slot_to_brick: int32 [192], P('bricks'), may hold values from -1 to 95, as said below
- neighbors: int32 [192, 6], P('bricks'), may hold values from -1 to 191, as said below
- cotangent: bfloat16 [192, 64, 512], P('bricks'), may hold values from -6 to 6
Outputs:
- activated: bfloat16 [192, 64, 512], P('bricks')
- input_grad: bfloat16 [192, 64, 512], P('bricks')
- kernel_grad: float32 [64, 8, 3, 3, 3], replicated
- bias_grad: float32 [64], replicated
Inputs may be any that keep to these rules, and one draw needn't show every extreme that they name: `slot_to_brick`: the bricks 0 to 95 form a tube of 2 x 2 bricks in cross-section along the first dimension, brick (p, q, r) numbered (p 2 + q) 2 + r. Each device holds a run of consecutive bricks in its first slots, in order, the runs following device order; a device holds 2 to 6 bricks, some device exactly 6; its other slots hold -1. `neighbors`: the slot index of the brick across each face of the slot's brick in that tube, -1 outside the tube and for empty slots; the relation is symmetric. A brick across a face of the first dimension lies on a device at most 2 away, across the other faces at most 1 away, and both distances occur.
All inputs are finite; a program needn't handle non-finite values. No bound on the sum of `cortex` on one device may be relied on, other than what follows from the above.
Results may differ from a plain program's by a relative error of at most 0.0075.
Values may be sent and summed in bfloat16 or wider, within the bound.
No kernel may reach another device: no remote copies, remote signals or barrier semaphores. Data moves between devices by JAX's collectives and lax.ppermute only.
A program may use at most 128 MiB of HBM per device.

v0:
```python
import functools

import jax
import jax.numpy as jnp
import numpy as np
from jax import lax
from jax.experimental import pallas as pl
from jax.experimental.pallas import tpu as pltpu
from jax.sharding import PartitionSpec as P

CH = 64
GC = 8
TILE = 128
NEAR = 7
EDGE = 3
HEAD = 16
SUM_ROWS = 160
BF = jnp.bfloat16
F32 = jnp.float32


@functools.cache
def tables():
    strips = np.zeros((4, 512, TILE), np.float32)
    spread = np.zeros((384, 4 * TILE), np.float32)
    ends = np.zeros((4, 384, TILE), np.float32)
    shifts = np.zeros((4, 256, 9 * TILE), np.float32)
    for half in range(2):
        for xx in range(4):
            for w in range(8):
                i, xp = 2 * half + xx // 2, xx % 2
                spread[half * 64 + xx * 8 + w, i * TILE + xp * 8 + w] = 1
                spread[128 + half * 64 + 32 + xx * 8 + w, i * TILE + 32 + xp * 8 + w] = 1
                spread[256 + half * 64 + xx * 8 + w, i * TILE + 64 + xp * 8 + w] = 1
    for t in range(4):
        q, r = t // 2, t % 2
        own_y, own_z = (0 if q else 7), (0 if r else 7)
        far_y, far_z = 7 - own_y, 7 - own_z
        for half in range(2):
            for xx in range(4):
                for w in range(8):
                    plane = (4 * half + xx) * 64
                    strips[t, plane + own_y * 8 + w, half * 64 + xx * 8 + w] = 1
                    strips[t, plane + w * 8 + own_z, half * 64 + 32 + xx * 8 + w] = 1
        for xp in range(2):
            for w in range(8):
                ends[t, xp * 64 + far_y * 8 + w, xp * 8 + w] = 1
                ends[t, 128 + xp * 64 + w * 8 + far_z, 32 + xp * 8 + w] = 1
                ends[t, 256 + xp * 64 + far_y * 8 + w, 64 + xp * 8 + w] = 1
        out_y, out_z = (-1 if q else 8), (-1 if r else 8)
        for b in range(3):
            for c in range(3):
                for xp in range(2):
                    for y in range(8):
                        for z in range(8):
                            yy, zz = y + b - 1, z + c - 1
                            in_y, in_z = 0 <= yy < 8, 0 <= zz < 8
                            if in_y and in_z:
                                k = xp * 64 + yy * 8 + zz
                            elif in_z and yy == out_y:
                                k = 128 + xp * 8 + zz
                            elif in_y and zz == out_z:
                                k = 160 + xp * 8 + yy
                            elif yy == out_y and zz == out_z:
                                k = 192 + xp * 8 + far_z
                            else:
                                continue
                            shifts[t, k, (b * 3 + c) * TILE + xp * 64 + y * 8 + z] = 1
    return strips, spread, ends, shifts


def left_half(shape):
    return lax.broadcasted_iota(jnp.int32, shape, len(shape) - 1) % TILE < 64


def join_halves(left, right):
    mixed = jnp.where(left_half(left.shape), left.astype(F32), right.astype(F32))
    return mixed.astype(left.dtype)


def dot(a, b):
    return jnp.dot(a, b, preferred_element_type=F32)


def count_own(slot_ref):
    total = jnp.int32(0)
    for s in range(slot_ref.shape[0]):
        total = total + (slot_ref[s] >= 0).astype(jnp.int32)
    return total


def count_sent(head):
    return jnp.max(head.astype(F32)).astype(jnp.int32)


def kind_of(brick):
    return jnp.maximum(brick, 0) & 3


def pack_bricks(slot_ref, field_ref, strips_ref, msg_ref):
    slots = field_ref.shape[0]
    for s in range(slots):
        table = strips_ref[kind_of(slot_ref[s])]
        row = s * 2 * CH
        msg_ref[row : row + CH, :] = dot(field_ref[s], table).astype(BF)
        msg_ref[row + CH : row + 2 * CH, :] = join_halves(
            field_ref[s, :, 0:TILE], field_ref[s, :, 3 * TILE : 4 * TILE]
        )
    row = slots * 2 * CH
    count = count_own(slot_ref).astype(F32)
    msg_ref[row : row + HEAD, :] = jnp.full((HEAD, TILE), count, F32).astype(BF)


def bring(pairs, sems):
    copies = [pltpu.make_async_copy(a, b, sems.at[i]) for i, (a, b) in enumerate(pairs)]
    for copy in copies:
        copy.start()
    return copies


def pack_kernel(slot_hbm, field_hbm, strips_hbm, msg_ref, field_ref, strips_ref, slot_ref, sems):
    pairs = ((slot_hbm, slot_ref), (field_hbm, field_ref), (strips_hbm, strips_ref))
    for copy in bring(pairs, sems):
        copy.wait()
    pack_bricks(slot_ref, field_ref, strips_ref, msg_ref)


def route_body(slots, own_ref, mate_ref, near_ref, far_ref, box):
    odd = (lax.axis_index("bricks") & 1) == 1
    head = slots * 2 * CH
    mine = count_sent(own_ref[head : head + HEAD, :])
    other = count_sent(mate_ref[head : head + HEAD, :])
    for s in range(2 * slots):
        box[s] = own_ref[s * CH : (s + 1) * CH, :]
        box[2 * slots + s] = mate_ref[s * CH : (s + 1) * CH, :]
    for j in range(NEAR):
        up = jnp.where(j < mine, mine - 1 - j, slots + other - 1 - (j - mine))
        down = jnp.where(j < mine, j, slots + j - mine)
        at = jnp.clip(jnp.where(odd, up, down), 0, 2 * slots - 1)
        near_ref[j * CH : (j + 1) * CH, :] = box[2 * at + 1]
        if j < EDGE:
            near_ref[(NEAR + j) * CH : (NEAR + j + 1) * CH, :] = box[2 * at]
            far_ref[j * CH : (j + 1) * CH, :] = box[2 * at + 1]
    row = (NEAR + EDGE) * CH
    both = (mine + other).astype(F32)
    near_ref[row : row + HEAD, :] = jnp.full((HEAD, TILE), both, F32).astype(BF)


def route_kernel(slots, own_ref, mate_ref, near_ref, far_ref, box):
    route_body(slots, own_ref, mate_ref, near_ref, far_ref, box)


def route_sum_kernel(slots, own_ref, mate_ref, near_ref, far_ref, sum_ref, box):
    route_body(slots, own_ref, mate_ref, near_ref, far_ref, box)
    high = slots * 2 * CH + HEAD
    low = high + SUM_ROWS
    parts = []
    for ref in (own_ref, mate_ref):
        parts.append(
            ref[high : high + SUM_ROWS, :].astype(F32) + ref[low : low + SUM_ROWS, :].astype(F32)
        )
    sum_ref[...] = parts[0] + parts[1]


def weight_kernel(count, *refs):
    taps_hbm, sources = refs[0], refs[1 : count + 1]
    forward_ref, backward_ref = refs[count + 1 : count + 3]
    places = refs[count + 3 : 2 * count + 3]
    taps_ref, work, sems = refs[2 * count + 3 :]
    copies = bring(((taps_hbm, taps_ref),) + tuple(zip(sources, places)), sems)
    copies[0].wait()
    values = taps_ref[...].astype(F32)
    lanes = lax.broadcasted_iota(jnp.int32, (GC, CH), 1) // GC

    def block(tap):
        tile = values[tap * GC : (tap + 1) * GC, :]
        return jnp.concatenate([jnp.where(lanes == g, tile, 0.0) for g in range(CH // GC)], axis=0)

    work[...] = jnp.zeros_like(work)
    for bc in range(9):
        rows = slice(bc * CH, (bc + 1) * CH)
        work[rows, 0:TILE] = jnp.concatenate([block(bc), block(9 + bc)], axis=1)
        work[rows, TILE : TILE + CH] = block(18 + bc)
    turned = work[...].T
    forward_ref[...] = turned[0 : 3 * CH, 0 : 9 * CH].astype(BF)
    for a in range(3):
        rows = slice(a * CH, (a + 1) * CH)
        base = (2 - a) * 9 + 8
        for bc in range(0, 8, 2):
            pair = jnp.concatenate([block(base - bc), block(base - bc - 1)], axis=1)
            backward_ref[rows, bc * CH : (bc + 2) * CH] = pair.astype(BF)
        backward_ref[rows, 8 * CH : 9 * CH] = block(base - 8).astype(BF)
    for copy in copies[1:]:
        copy.wait()


def make_finder(
    slot_hbm, link_hbm, own_ref, mate_ref, first_ref, second_ref, first_far_ref, second_far_ref,
    planes, strips, slot_ref, link_ref, sems,
):
    copies = bring(((slot_hbm, slot_ref), (link_hbm, link_ref)), sems)
    slots = slot_ref.shape[0]
    odd = (lax.axis_index("bricks") & 1) == 1
    head = slots * 2 * CH
    mine = count_sent(own_ref[head : head + HEAD, :])
    other = count_sent(mate_ref[head : head + HEAD, :])
    row = (NEAR + EDGE) * CH
    counts = [count_sent(ref[row : row + HEAD, :]) for ref in (first_ref, second_ref)]
    for k, ref in enumerate((own_ref, mate_ref)):
        for s in range(slots):
            strips[k * slots + s] = ref[s * 2 * CH : s * 2 * CH + CH, :]
            planes[k * slots + s] = ref[s * 2 * CH + CH : (s + 1) * 2 * CH, :]
    for side, (near, far) in enumerate(((first_ref, first_far_ref), (second_ref, second_far_ref))):
        for j in range(NEAR):
            planes[2 * slots + side * NEAR + j] = near[j * CH : (j + 1) * CH, :]
        for j in range(EDGE):
            strips[2 * slots + side * EDGE + j] = near[(NEAR + j) * CH : (NEAR + j + 1) * CH, :]
            planes[2 * slots + 2 * NEAR + side * EDGE + j] = far[j * CH : (j + 1) * CH, :]
    nothing = 2 * slots + 2 * NEAR + 2 * EDGE
    planes[nothing] = jnp.zeros((CH, TILE), BF)
    for copy in copies:
        copy.wait()
    base = slot_ref[0]
    low_side = odd.astype(jnp.int32)
    high_side = 1 - low_side
    low_count = jnp.where(odd, counts[1], counts[0])
    high_count = jnp.where(odd, counts[0], counts[1])
    mate_first = jnp.where(odd, base - other, base + mine)
    chip_low = jnp.where(odd, base - other, base)
    chip_high = jnp.where(odd, base + mine, base + mine + other)

    def on_chip(brick):
        own = (brick >= base) & (brick < base + mine)
        return jnp.where(own, brick - base, slots + brick - mate_first)

    def find_strip(brick):
        low = 2 * slots + low_side * EDGE + (chip_low - 1 - brick)
        high = 2 * slots + high_side * EDGE + (brick - chip_high)
        at = jnp.where(brick < chip_low, low, jnp.where(brick >= chip_high, high, on_chip(brick)))
        return jnp.clip(at, 0, 2 * slots + 2 * EDGE - 1)

    def outside(distance, count, side):
        near = 2 * slots + side * NEAR + distance
        far = 2 * slots + 2 * NEAR + side * EDGE + distance - count
        return jnp.where(distance < count, near, far)

    def find_plane(brick, exists):
        low = outside(chip_low - 1 - brick, low_count, low_side)
        high = outside(brick - chip_high, high_count, high_side)
        at = jnp.where(brick < chip_low, low, jnp.where(brick >= chip_high, high, on_chip(brick)))
        return jnp.clip(jnp.where(exists, at, nothing), 0, nothing)

    return base, mine, find_strip, find_plane


def convolve_brick(
    s, base, find_strip, find_plane, link_ref, field_ref, planes, strips,
    spread_ref, ends_ref, shifts_ref, weight_ref, mixed, taps, sums,
):
    brick = base + s
    kind = brick & 3
    step_y = 2 - 2 * (kind & 2)
    step_z = 1 - 2 * (kind & 1)
    sides = (brick + step_y, brick + step_z, brick + step_y + step_z)
    has_low = link_ref[s, 0] >= 0
    has_high = link_ref[s, 1] >= 0

    def outer(near):
        high = planes[find_plane(near + 4, has_high)]
        low = planes[find_plane(near - 4, has_low)]
        return join_halves(high, low)

    beside = jnp.concatenate([strips[find_strip(m)] for m in sides], axis=1)
    halo = dot(beside, spread_ref[...]).astype(BF)
    outer_beside = jnp.concatenate([outer(m) for m in sides], axis=1)
    for i in range(4):
        rows = slice(i * CH, (i + 1) * CH)
        mixed[rows, 0:TILE] = field_ref[s, :, i * TILE : (i + 1) * TILE]
        mixed[rows, TILE:] = halo[:, i * TILE : (i + 1) * TILE]
    mixed[4 * CH :, 0:TILE] = outer(brick)
    mixed[4 * CH :, TILE:] = dot(outer_beside, ends_ref[kind]).astype(BF)
    for bc in range(0, 9, 2):
        wide = min(2, 9 - bc)
        part = dot(mixed[...], shifts_ref[kind, :, bc * TILE : (bc + wide) * TILE]).astype(BF)
        for e in range(wide):
            for i in range(5):
                taps[(bc + e) * CH : (bc + e + 1) * CH, i * TILE : (i + 1) * TILE] = part[
                    i * CH : (i + 1) * CH, e * TILE : (e + 1) * TILE
                ]
    sums[...] = dot(weight_ref[...], taps[0 : 9 * CH, :])
    turned = []
    for a in (0, 2):
        rows = slice(a * CH, (a + 1) * CH)
        turned.append(
            [pltpu.roll(sums[rows, i * TILE : (i + 1) * TILE], 64, 1) for i in range(5)]
        )
    left = left_half((CH, TILE))
    tiles = []
    for i in range(4):
        lower = jnp.where(left, turned[0][(i - 1) % 5], turned[0][i])
        upper = jnp.where(left, turned[1][i], turned[1][i + 1])
        tiles.append(sums[CH : 2 * CH, i * TILE : (i + 1) * TILE] + lower + upper)
    return tiles


def forward_kernel(
    slot_hbm, link_hbm, field_ref, own_ref, mate_ref, first_ref, second_ref, first_far_ref,
    second_far_ref, weight_ref, bias_ref, cortex_ref, upstream_ref, strips_ref, spread_ref,
    ends_ref, shifts_ref, out_ref, dpre_ref, msg_ref,
    planes, strips, mixed, taps, sums, slot_ref, link_ref, sems, spots, grads, keeps,
):
    slots = field_ref.shape[0]
    base, mine, find_strip, find_plane = make_finder(
        slot_hbm, link_hbm, own_ref, mate_ref, first_ref, second_ref, first_far_ref, second_far_ref,
        planes, strips, slot_ref, link_ref, sems,
    )
    for s in range(slots):
        keeps[s] = jnp.broadcast_to(cortex_ref[s : s + 1, :].astype(F32), (8, 512))
    taps[9 * CH :, :] = jnp.ones((HEAD, 5 * TILE), BF)
    grads[...] = jnp.zeros_like(grads)
    for s in range(slots):

        @pl.when(s >= mine)
        def _():
            out_ref[s] = jnp.zeros((CH, 512), BF)
            dpre_ref[s] = jnp.zeros((CH, 512), BF)

    square = (CH, CH)
    diagonal = lax.broadcasted_iota(jnp.int32, square, 0) == lax.broadcasted_iota(jnp.int32, square, 1)
    bias = jnp.sum(jnp.where(diagonal, bias_ref[...], 0.0), axis=1, keepdims=True)
    left = left_half((CH, TILE))
    zero = jnp.zeros((CH, TILE), F32)

    def one_brick(s, carry):
        tiles = convolve_brick(
            s, base, find_strip, find_plane, link_ref, field_ref, planes, strips,
            spread_ref, ends_ref, shifts_ref, weight_ref, mixed, taps, sums,
        )
        turned = []
        for i in range(4):
            lanes = slice(i * TILE, (i + 1) * TILE)
            pre = tiles[i] + bias
            keep = keeps[s, 0:1, lanes]
            sigma = 1.0 / (1.0 + jnp.exp(-pre))
            out_ref[s, :, lanes] = (pre * sigma * keep).astype(BF)
            slope = sigma * (1.0 + pre * (1.0 - sigma))
            dpre = (upstream_ref[s, :, lanes].astype(F32) * keep * slope).astype(BF)
            dpre_ref[s, :, lanes] = dpre
            spots[CH : 2 * CH, lanes] = dpre
            turned.append(pltpu.roll(dpre.astype(F32), 64, 1))
        spots[CH : 2 * CH, 4 * TILE :] = jnp.zeros((CH, TILE), BF)
        turned.append(zero)
        for i in range(4):
            lanes = slice(i * TILE, (i + 1) * TILE)
            spots[0:CH, lanes] = jnp.where(left, turned[i], turned[i + 1]).astype(BF)
            before = turned[i - 1] if i else zero
            spots[2 * CH :, lanes] = jnp.where(left, before, turned[i]).astype(BF)
        spots[0:CH, 4 * TILE :] = jnp.where(left, 0.0, turned[0]).astype(BF)
        spots[2 * CH :, 4 * TILE :] = jnp.where(left, turned[3], 0.0).astype(BF)
        grads[...] += lax.dot_general(
            taps[...], spots[...], (((1,), (1,)), ((), ())), preferred_element_type=F32
        )
        return carry

    lax.fori_loop(0, mine, one_brick, 0)

    pack_bricks(slot_ref, dpre_ref, strips_ref, msg_ref)
    high = slots * 2 * CH + HEAD
    low = high + SUM_ROWS
    group = lax.broadcasted_iota(jnp.int32, (GC, TILE), 1) % CH // GC
    for half, lanes in enumerate((slice(0, TILE), slice(TILE, TILE + CH))):
        group_here = group[:, : lanes.stop - lanes.start]
        rows = []
        for bc in range(9):
            total = jnp.zeros(group_here.shape, F32)
            for g in range(CH // GC):
                at = bc * CH + g * GC
                total = total + jnp.where(group_here == g, grads[at : at + GC, lanes], 0.0)
            rows.append(total)
        rows.append(grads[9 * CH : 9 * CH + GC, lanes])
        full = jnp.concatenate(rows, axis=0)
        if full.shape[1] < TILE:
            full = jnp.concatenate([full, jnp.zeros((10 * GC, TILE - full.shape[1]), F32)], axis=1)
        rounded = full.astype(BF)
        at = half * 10 * GC
        msg_ref[high + at : high + at + 10 * GC, :] = rounded
        msg_ref[low + at : low + at + 10 * GC, :] = (full - rounded.astype(F32)).astype(BF)


def backward_kernel(part, *refs):
    if part:
        refs, last_ref = refs[:13] + refs[14:], refs[13]
        field_ref, own_ref, out_ref = refs[2], refs[3], refs[13]
        slots = field_ref.shape[0]
        head = slots * 2 * CH
        half = count_sent(own_ref[head : head + HEAD, :]) // 2
        for s in range(slots):

            @pl.when(s < half)
            def _():
                out_ref[s] = last_ref[s]

    backward_body(part, *refs)


def backward_body(
    part, slot_hbm, link_hbm, field_ref, own_ref, mate_ref, first_ref, second_ref, first_far_ref,
    second_far_ref, weight_ref, spread_ref, ends_ref, shifts_ref, out_ref,
    planes, strips, mixed, taps, sums, slot_ref, link_ref, sems,
):
    slots = field_ref.shape[0]
    base, mine, find_strip, find_plane = make_finder(
        slot_hbm, link_hbm, own_ref, mate_ref, first_ref, second_ref, first_far_ref, second_far_ref,
        planes, strips, slot_ref, link_ref, sems,
    )
    if part == 1:
        for s in range(slots):

            @pl.when(s >= mine)
            def _():
                out_ref[s] = jnp.zeros((CH, 512), BF)

    def one_brick(s, carry):
        tiles = convolve_brick(
            s, base, find_strip, find_plane, link_ref, field_ref, planes, strips,
            spread_ref, ends_ref, shifts_ref, weight_ref, mixed, taps, sums,
        )
        for i in range(4):
            out_ref[s, :, i * TILE : (i + 1) * TILE] = tiles[i].astype(BF)
        return carry

    half = mine // 2
    lax.fori_loop(half * part, mine if part else half, one_brick, 0)


def finish_kernel(a_ref, b_ref, kernel_ref, bias_ref):
    first = a_ref[0 : 10 * GC, :] + b_ref[0 : 10 * GC, :]
    second = a_ref[10 * GC :, :] + b_ref[10 * GC :, :]
    turned = pltpu.roll(first, 64, 1)
    for a, part in enumerate((first, turned, second)):
        kernel_ref[a * 9 * GC : (a + 1) * 9 * GC, :] = part[0 : 9 * GC, 0:CH]
    bias_ref[...] = turned[9 * GC : 9 * GC + 1, 0:CH]


VMEM = pl.BlockSpec(memory_space=pltpu.VMEM)
HBM = pl.BlockSpec(memory_space=pltpu.HBM)


def call(kernel, ins, outs, scratch=(), flops=0, size=400000):
    return pl.pallas_call(
        kernel,
        in_specs=ins,
        out_specs=tuple(VMEM for _ in outs),
        out_shape=tuple(outs),
        scratch_shapes=list(scratch),
        compiler_params=pltpu.CompilerParams(vmem_limit_bytes=24 * 2**20),
        cost_estimate=pl.CostEstimate(flops=flops, bytes_accessed=size, transcendentals=0),
    )


def sent(block, route):
    return lax.ppermute(block, "bricks", route)


def shards(voxels, kernel, bias, cortex, slot_to_brick, neighbors, cotangent):
    slots = voxels.shape[0]
    devices = lax.axis_size("bricks")
    strips, spread, ends, shifts = (jnp.asarray(t, BF) for t in tables())
    shape = jax.ShapeDtypeStruct
    pack_rows = slots * 2 * CH + HEAD
    near_shape = shape(((NEAR + EDGE) * CH + HEAD, TILE), BF)
    far_shape = shape((EDGE * CH, TILE), BF)

    def routed(block, chips):
        pairs = []
        for d in range(devices):
            to = d + 2 * chips - 1 if d % 2 else d - 2 * chips + 1
            if 0 <= to < devices:
                pairs.append((d, to))
        return sent(block, pairs)

    def swapped(block, mask):
        return sent(block, [(d, d ^ mask) for d in range(devices)])

    box = [pltpu.VMEM((4 * slots, CH, TILE), BF)]
    work = [
        pltpu.VMEM((2 * slots + 2 * NEAR + 2 * EDGE + 1, CH, TILE), BF),
        pltpu.VMEM((2 * slots + 2 * EDGE, CH, TILE), BF),
        pltpu.VMEM((5 * CH, 2 * TILE), BF),
        pltpu.VMEM((9 * CH + HEAD, 5 * TILE), BF),
        pltpu.VMEM((3 * CH, 5 * TILE), F32),
        pltpu.SMEM(slot_to_brick.shape, jnp.int32),
        pltpu.SMEM(neighbors.shape, jnp.int32),
        pltpu.SemaphoreType.DMA((2,)),
    ]
    field = shape(voxels.shape, BF)

    own, voxels, strips = call(
        pack_kernel,
        [HBM] * 3,
        [shape((pack_rows, TILE), BF), field, shape(strips.shape, BF)],
        [pltpu.SMEM(slot_to_brick.shape, jnp.int32), pltpu.SemaphoreType.DMA((3,))],
    )(slot_to_brick, voxels, strips)
    mate = swapped(own, 1)
    weight_shape = shape((3 * CH, 9 * CH), BF)
    taps = jnp.transpose(kernel, (2, 3, 4, 1, 0)).reshape(27 * GC, CH)
    later = (cotangent, cortex, bias.reshape(1, CH), spread, ends, shifts)
    staged = call(
        functools.partial(weight_kernel, len(later)),
        [HBM] * (1 + len(later)),
        [weight_shape] * 2 + [shape(a.shape, a.dtype) for a in later],
        [
            pltpu.VMEM(taps.shape, BF),
            pltpu.VMEM((640, 256), F32),
            pltpu.SemaphoreType.DMA((1 + len(later),)),
        ],
        size=5 * 10**6,
    )(taps, *later)
    near, far = call(
        functools.partial(route_kernel, slots), [VMEM, VMEM], [near_shape, far_shape], box
    )(own, mate)
    near, far = routed(near, 1), routed(far, 2)
    near, far, staged = lax.optimization_barrier((near, far, staged))
    forward, backward, cotangent, cortex, bias, spread, ends, shifts = staged
    received = (near, swapped(near, 1), far, swapped(far, 1))
    activated, dpre, own = call(
        forward_kernel,
        [HBM, HBM] + [VMEM] * 15,
        [field, field, shape((pack_rows + 2 * SUM_ROWS, TILE), BF)],
        work
        + [
            pltpu.VMEM((3 * CH, 5 * TILE), BF),
            pltpu.VMEM((9 * CH + HEAD, 3 * CH), F32),
            pltpu.VMEM((slots, 8, 512), F32),
        ],
        flops=4 * 10**9,
    )(
        slot_to_brick, neighbors, voxels, own, mate, *received, forward, bias,
        cortex, cotangent, strips, spread, ends, shifts,
    )
    mate = swapped(own, 1)
    near, far, total = call(
        functools.partial(route_sum_kernel, slots),
        [VMEM, VMEM],
        [near_shape, far_shape, shape((SUM_ROWS, TILE), F32)],
        box,
    )(own, mate)
    state = dict(near=near, far=far)

    def send_halos():
        state.update(near=routed(state["near"], 1), far=routed(state["far"], 2))

    def tell_mate():
        near, far = state["near"], state["far"]
        state.update(second=swapped(near, 1), second_far=swapped(far, 1))

    def half_backward(part):
        last = [state["grad"]] if part else []
        (state["grad"],) = call(
            functools.partial(backward_kernel, part),
            [HBM, HBM] + [VMEM] * (11 + part),
            [field],
            work,
            flops=10**9,
        )(
            slot_to_brick, neighbors, dpre, own, mate, state["near"], state["second"],
            state["far"], state["second_far"], backward, spread, ends, shifts, *last,
        )

    beside = [send_halos, tell_mate, lambda: half_backward(0), lambda: half_backward(1)]
    masks = [2**p for p in range(1, devices.bit_length() - 1)]
    for mask in masks:
        other = swapped(total, mask)
        if beside:
            beside.pop(0)()
        if mask != masks[-1]:
            total, other, state = lax.optimization_barrier((total, other, state))
            total = total + other
    for task in beside:
        task()
    input_grad = state["grad"]
    kernel_sum, bias_sum = call(
        finish_kernel, [VMEM, VMEM], [shape((27 * GC, CH), F32), shape((1, CH), F32)]
    )(total, other)
    kernel_grad = jnp.transpose(kernel_sum.reshape(3, 3, 3, GC, CH), (4, 3, 0, 1, 2))
    return (activated, input_grad, kernel_grad, bias_sum.reshape(CH))


def solution(mesh):
    devices = mesh.shape["bricks"]
    assert devices & (devices - 1) == 0
    return jax.shard_map(
        shards,
        mesh=mesh,
        in_specs=(
            P("bricks", None, None),
            P(),
            P(),
            P("bricks", None),
            P("bricks"),
            P("bricks", None),
            P("bricks", None, None),
        ),
        out_specs=(P("bricks", None, None), P("bricks", None, None), P(), P()),
        check_vma=False,
    )
```

profile of v0, /device:TPU:0, one launch (start us, length us, event | category | flops | bytes accessed | tf_op | source)
XLA Modules:
  0.0 62.8 jit_solution(1445926800188436862)
XLA Ops:
  0.6 1.0 %copy-done.1 = bf16[4,512,128]{2,1,0:T(8,128)(2,1)S(1)} copy-done((bf16[4,512,128]{2,1,0:T(8,128)(2,1)S(1)}, bf16[4,512,128]{2,1,0:T(8,128)(2,1)}, u32[]{:S(2)}) %copy-start.1) | copy-done | bytes 524312
  1.7 1.0 %copy-done.2 = bf16[6,64,512]{2,1,0:T(8,128)(2,1)S(1)} copy-done((bf16[6,64,512]{2,1,0:T(8,128)(2,1)S(1)}, bf16[6,64,512]{2,1,0:T(8,128)(2,1)}, u32[]{:S(2)}) %copy-start.2) | copy-done | bytes 393240
  4.7 1.1 %collective-permute-done.mate_ref = bf16[784,128]{1,0:T(8,128)(2,1)S(1)} collective-permute-done((bf16[784,128]{1,0:T(8,128)(2,1)S(1)}, bf16[784,128]{1,0:T(8,128)(2,1)S(1)}, u32[]{:S(2)}, u32[]{:S(2)}) %collective-permute-start) | collective-permute-done | bytes 200736 | tf_op jit(solution)/shard_map/ppermute | solution.py:462
  7.3 1.7 %copy-done = bf16[4,256,1152]{2,1,0:T(8,128)(2,1)S(1)} copy-done((bf16[4,256,1152]{2,1,0:T(8,128)(2,1)S(1)}, bf16[4,256,1152]{2,1,0:T(8,128)(2,1)}, u32[]{:S(2)}) %copy-start) | copy-done | bytes 2359320
  9.0 1.0 %copy-done.3 = bf16[6,64,512]{2,1,0:T(8,128)(2,1)S(1)} copy-done((bf16[6,64,512]{2,1,0:T(8,128)(2,1)S(1)}, bf16[6,64,512]{2,1,0:T(8,128)(2,1)}, u32[]{:S(2)}) %copy-start.3) | copy-done | bytes 393240
  10.0 1.0 %copy-done.4 = bf16[4,384,128]{2,1,0:T(8,128)(2,1)S(1)} copy-done((bf16[4,384,128]{2,1,0:T(8,128)(2,1)S(1)}, bf16[4,384,128]{2,1,0:T(8,128)(2,1)}, u32[]{:S(2)}) %copy-start.4) | copy-done | bytes 393240
  11.0 1.0 %copy-done.5 = bf16[384,512]{1,0:T(8,128)(2,1)S(1)} copy-done((bf16[384,512]{1,0:T(8,128)(2,1)S(1)}, bf16[384,512]{1,0:T(8,128)(2,1)}, u32[]{:S(2)}) %copy-start.5) | copy-done | bytes 393240
  14.1 1.2 %shard_map.140 = (bf16[192,576]{1,0:T(8,128)(2,1)S(1)}, bf16[192,576]{1,0:T(8,128)(2,1)S(1)}, bf16[6,64,512]{2,1,0:T(8,128)(2,1)S(1)}, s32[6,512]{1,0:T(8,128)S(...) custom-call(bf16[216,64]{1,0:T(8,128)(2,1)S(1)} %bitcast.8, ...), custom_call_target="tpu_custom_call" | custom-call | bytes 5000000 | tf_op jit(solution)/shard_map/pallas_call | solution.py:508
  15.3 6.7 %collective-permute-start.3 = (bf16[656,128]{1,0:T(8,128)(2,1)S(1)}, bf16[656,128]{1,0:T(8,128)(2,1)S(1)}, u32[]{:S(2)}, u32[]{:S(2)}) collective-permute-start(bf16[656,128]{1,0:T(8,128)(2,1)S(1)} %collective-permute-done.1.first_ref), channel_id=1, source_target_pairs={{0,1},{1,0},{2,3},{3,2},{4,5},{5,4},{6,7},{7,6},{8,9},{9,8},{10,11... | collective-permute-start | bytes 503816 | tf_op jit(solution)/shard_map/ppermute | solution.py:462
  22.1 1.2 %collective-permute-done.4.second_far_ref = bf16[192,128]{1,0:T(8,128)(2,1)S(1)} collective-permute-done((bf16[192,128]{1,0:T(8,128)(2,1)S(1)}, bf16[192,128]{1,0:T(8,128)(2,1)S(1)}, u32[]{:S(2)}, u32[]{:S(2)}) %collective-permute-start.4) | collective-permute-done | bytes 49184 | tf_op jit(solution)/shard_map/ppermute | solution.py:462
  23.3 4.6 %shard_map.141 = (bf16[6,64,512]{2,1,0:T(8,128)(2,1)}, bf16[6,64,512]{2,1,0:T(8,128)(2,1)S(1)}, bf16[1104,128]{1,0:T(8,128)(2,1)S(1)}) custom-call(s32[6]{0:T(128)S(1)} %copy-done.10, s32[6,6]{1,0:T(8,128)S(1)} %copy-done.8, bf16[6,64,512]{2,1,0:T(8,128)(2,1)S(1)} %get-tuple-element.52.field_ref, bf16[784,128]{1,0:T(8,128)(2,1)S(1)} %get-tuple-element.53.own_ref, ...), custom_call_target="tpu_custom_call" | custom-call | flops 4000000000 | bytes 400000 | tf_op jit(solution)/shard_map/pallas_call | solution.py:526
  27.9 6.1 %collective-permute-start.5 = (bf16[1104,128]{1,0:T(8,128)(2,1)S(1)}, bf16[1104,128]{1,0:T(8,128)(2,1)S(1)}, u32[]{:S(2)}, u32[]{:S(2)}) collective-permute-start(bf16[1104,128]{1,0:T(8,128)(2,1)S(1)} %get-tuple-element.76.own_ref.refs_3_), channel_id=1, source_target_pairs={{0,1},{1,0},{2,3},{3,2},{4,5},{5,4},{6,7},{7,6},{8,9},{9,8},{10,11... | collective-permute-start | bytes 847880 | tf_op jit(solution)/shard_map/ppermute | solution.py:462
  34.1 1.2 %collective-permute-done.5.mate_ref.refs_4_ = bf16[1104,128]{1,0:T(8,128)(2,1)S(1)} collective-permute-done((bf16[1104,128]{1,0:T(8,128)(2,1)S(1)}, bf16[1104,128]{1,0:T(8,128)(2,1)S(1)}, u32[]{:S(2)}, u32[]{:S(2)}) %collective-permute-start.5) | collective-permute-done | bytes 282656 | tf_op jit(solution)/shard_map/ppermute | solution.py:462
  36.1 3.3 %collective-permute-start.6 = (f32[160,128]{1,0:T(8,128)S(1)}, f32[160,128]{1,0:T(8,128)S(1)}, u32[]{:S(2)}, u32[]{:S(2)}) collective-permute-start(f32[160,128]{1,0:T(8,128)S(1)} %get-tuple-element.80), channel_id=1, source_target_pairs={{0,2},{1,3},{2,0},{3,1},{4,6},{5,7},{6,4},{7,5},{8,10},{9,11},{10,... | collective-permute-start | bytes 245768 | tf_op jit(solution)/shard_map/ppermute | solution.py:462
  40.1 3.9 %collective-permute-done.6 = f32[160,128]{1,0:T(8,128)S(1)} collective-permute-done((f32[160,128]{1,0:T(8,128)S(1)}, f32[160,128]{1,0:T(8,128)S(1)}, u32[]{:S(2)}, u32[]{:S(2)}) %collective-permute-start.6) | collective-permute-done | bytes 81952 | tf_op jit(solution)/shard_map/ppermute | solution.py:462
  44.0 4.2 %collective-permute-start.9 = (f32[160,128]{1,0:T(8,128)S(1)}, f32[160,128]{1,0:T(8,128)S(1)}, u32[]{:S(2)}, u32[]{:S(2)}) collective-permute-start(f32[160,128]{1,0:T(8,128)S(1)} %add.9), channel_id=1, source_target_pairs={{0,4},{1,5},{2,6},{3,7},{4,0},{5,1},{6,2},{7,3},{8,12},{9,13},{10,... | collective-permute-start | bytes 245768 | tf_op jit(solution)/shard_map/ppermute | solution.py:462
  48.2 1.2 %collective-permute-done.11.refs_8_ = bf16[192,128]{1,0:T(8,128)(2,1)S(1)} collective-permute-done((bf16[192,128]{1,0:T(8,128)(2,1)S(1)}, bf16[192,128]{1,0:T(8,128)(2,1)S(1)}, u32[]{:S(2)}, u32[]{:S(2)}) %collective-permute-start.11) | collective-permute-done | bytes 49184 | tf_op jit(solution)/shard_map/ppermute | solution.py:462
  49.4 1.4 %collective-permute-done.9 = f32[160,128]{1,0:T(8,128)S(1)} collective-permute-done((f32[160,128]{1,0:T(8,128)S(1)}, f32[160,128]{1,0:T(8,128)S(1)}, u32[]{:S(2)}, u32[]{:S(2)}) %collective-permute-start.9) | collective-permute-done | bytes 81952 | tf_op jit(solution)/shard_map/ppermute | solution.py:462
  50.8 1.5 %collective-permute-start.12 = (f32[160,128]{1,0:T(8,128)S(1)}, f32[160,128]{1,0:T(8,128)S(1)}, u32[]{:S(2)}, u32[]{:S(2)}) collective-permute-start(f32[160,128]{1,0:T(8,128)S(1)} %add.10), channel_id=1, source_target_pairs={{0,8},{1,9},{2,10},{3,11},{4,12},{5,13},{6,14},{7,15},{8,0},{9,1},... | collective-permute-start | bytes 245768 | tf_op jit(solution)/shard_map/ppermute | solution.py:462
  52.4 1.6 %shard_map.143.refs_13_ = bf16[6,64,512]{2,1,0:T(8,128)(2,1)S(1)} custom-call(s32[6]{0:T(128)S(1)} %copy-done.10, s32[6,6]{1,0:T(8,128)S(1)} %copy-done.8, bf16[6,64,512]{2,1,0:T(8,128)(2,1)S(1)} %get-tuple-element.75.refs_2_, bf16[1104,128]{1,0:T(8,128)(2,1)S(1)} %get-tuple-element.76.own_ref.refs_3_, ...), custom_call_target="tpu_custom_call" | custom-call | flops 1000000000 | bytes 400000 | tf_op jit(solution)/shard_map/pallas_call | solution.py:559
  54.0 1.4 %collective-permute-done.12 = f32[160,128]{1,0:T(8,128)S(1)} collective-permute-done((f32[160,128]{1,0:T(8,128)S(1)}, f32[160,128]{1,0:T(8,128)S(1)}, u32[]{:S(2)}, u32[]{:S(2)}) %collective-permute-start.12) | collective-permute-done | bytes 81952 | tf_op jit(solution)/shard_map/ppermute | solution.py:462
  55.4 0.9 %collective-permute-start.13 = (f32[160,128]{1,0:T(8,128)S(1)}, f32[160,128]{1,0:T(8,128)S(1)}, u32[]{:S(2)}, u32[]{:S(2)}) collective-permute-start(f32[160,128]{1,0:T(8,128)S(1)} %add.11.a_ref), channel_id=1, source_target_pairs={{0,16},{1,17},{2,18},{3,19},{4,20},{5,21},{6,22},{7,23},{8,24},{9,... | collective-permute-start | bytes 245768 | tf_op jit(solution)/shard_map/ppermute | solution.py:462
  56.3 2.5 %shard_map.144 = bf16[6,64,512]{2,1,0:T(8,128)(2,1)} custom-call(s32[6]{0:T(128)S(1)} %copy-done.10, s32[6,6]{1,0:T(8,128)S(1)} %copy-done.8, bf16[6,64,512]{2,1,0:T(8,128)(2,1)S(1)} %get-tuple-element.75.refs_2_, bf16[1104,128]{1,0:T(8,128)(2,1)S(1)} %get-tuple-element.76.own_ref.refs_3_, bf16[1104,128]{1,0:T(8,128)(2,1)S(1)} %collective-permute-done.5.mate_ref.refs_4_, ...), custom_call_target="tpu_custom_call" | custom-call | flops 1000000000 | bytes 400000 | tf_op jit(solution)/shard_map/pallas_call | solution.py:559
  58.8 3.3 %collective-permute-done.13.b_ref = f32[160,128]{1,0:T(8,128)S(1)} collective-permute-done((f32[160,128]{1,0:T(8,128)S(1)}, f32[160,128]{1,0:T(8,128)S(1)}, u32[]{:S(2)}, u32[]{:S(2)}) %collective-permute-start.13) | collective-permute-done | bytes 81952 | tf_op jit(solution)/shard_map/ppermute | solution.py:462
  (39 shorter events, 8.1 us)
Async XLA Ops:
  0.6 1.0 %copy-start.1 = (bf16[4,512,128]{2,1,0:T(8,128)(2,1)S(1)}, bf16[4,512,128]{2,1,0:T(8,128)(2,1)}, u32[]{:S(2)}) copy-start(bf16[4,512,128]{2,1,0:T(8,128)(2,1)} %constant.8.clone.strips_hbm) | copy-start | bytes 1572868
  1.7 1.0 %copy-start.2 = (bf16[6,64,512]{2,1,0:T(8,128)(2,1)S(1)}, bf16[6,64,512]{2,1,0:T(8,128)(2,1)}, u32[]{:S(2)}) copy-start(bf16[6,64,512]{2,1,0:T(8,128)(2,1)} %field_hbm.1) | copy-start | bytes 1179652
  3.3 20.0 %copy-start.8 = (s32[6,6]{1,0:T(8,128)S(1)}, s32[6,6]{1,0:T(8,128)}, u32[]{:S(2)}) copy-start(s32[6,6]{1,0:T(8,128)} %refs_1_.5) | copy-start | bytes 436
  3.3 20.0 %copy-start.10 = (s32[6]{0:T(128)S(1)}, s32[6]{0:T(128)}, u32[]{:S(2)}) copy-start(s32[6]{0:T(128)} %refs_0_.3) | copy-start | bytes 76
  4.2 1.6 %collective-permute-start = (bf16[784,128]{1,0:T(8,128)(2,1)S(1)}, bf16[784,128]{1,0:T(8,128)(2,1)S(1)}, u32[]{:S(2)}, u32[]{:S(2)}) collective-permute-start(bf16[784,128]{1,0:T(8,128)(2,1)S(1)} %get-tuple-element.53.own_ref), channel_id=1, source_target_pairs={{0,1},{1,0},{2,3},{3,2},{4,5},{5,4},{6,7},{7,6},{8,9},{9,8},{10,11... | collective-permute-start | bytes 602120 | tf_op jit(solution)/shard_map/ppermute | solution.py:462
  5.9 9.4 %collective-permute-start.1 = (bf16[656,128]{1,0:T(8,128)(2,1)S(1)}, bf16[656,128]{1,0:T(8,128)(2,1)S(1)}, u32[]{:S(2)}, u32[]{:S(2)}) collective-permute-start(bf16[656,128]{1,0:T(8,128)(2,1)S(1)} %get-tuple-element.54), channel_id=1, source_target_pairs={{1,2},{2,1},{3,4},{4,3},{5,6},{6,5},{7,8},{8,7},{9,10},{10,9},{11,... | collective-permute-start | bytes 503816 | tf_op jit(solution)/shard_map/ppermute | solution.py:462
  6.6 8.7 %collective-permute-start.2 = (bf16[192,128]{1,0:T(8,128)(2,1)S(1)}, bf16[192,128]{1,0:T(8,128)(2,1)S(1)}, u32[]{:S(2)}, u32[]{:S(2)}) collective-permute-start(bf16[192,128]{1,0:T(8,128)(2,1)S(1)} %get-tuple-element.55), channel_id=1, source_target_pairs={{1,4},{3,6},{4,1},{5,8},{6,3},{7,10},{8,5},{9,12},{10,7},{11,14},{... | collective-permute-start | bytes 147464 | tf_op jit(solution)/shard_map/ppermute | solution.py:462
  7.3 1.7 %copy-start = (bf16[4,256,1152]{2,1,0:T(8,128)(2,1)S(1)}, bf16[4,256,1152]{2,1,0:T(8,128)(2,1)}, u32[]{:S(2)}) copy-start(bf16[4,256,1152]{2,1,0:T(8,128)(2,1)} %constant.11.clone.refs_6_) | copy-start | bytes 7077892
  9.0 1.0 %copy-start.3 = (bf16[6,64,512]{2,1,0:T(8,128)(2,1)S(1)}, bf16[6,64,512]{2,1,0:T(8,128)(2,1)}, u32[]{:S(2)}) copy-start(bf16[6,64,512]{2,1,0:T(8,128)(2,1)} %refs_1_.3) | copy-start | bytes 1179652
  10.0 1.0 %copy-start.4 = (bf16[4,384,128]{2,1,0:T(8,128)(2,1)S(1)}, bf16[4,384,128]{2,1,0:T(8,128)(2,1)}, u32[]{:S(2)}) copy-start(bf16[4,384,128]{2,1,0:T(8,128)(2,1)} %constant.10.clone.refs_5_) | copy-start | bytes 1179652
  11.0 1.0 %copy-start.5 = (bf16[384,512]{1,0:T(8,128)(2,1)S(1)}, bf16[384,512]{1,0:T(8,128)(2,1)}, u32[]{:S(2)}) copy-start(bf16[384,512]{1,0:T(8,128)(2,1)} %constant.9.clone.refs_4_) | copy-start | bytes 1179652
  12.0 0.8 %copy-start.6 = (bf16[64,8,3,3,3]{0,1,4,3,2:T(8,128)(2,1)S(1)}, bf16[64,8,3,3,3]{0,1,4,3,2:T(8,128)(2,1)}, u32[]{:S(2)}) copy-start(bf16[64,8,3,3,3]{0,1,4,3,2:T(8,128)(2,1)} %param.12) | copy-start | bytes 82948
  12.8 0.7 %copy-start.7 = (s32[6,512]{1,0:T(8,128)S(1)}, s32[6,512]{1,0:T(8,128)}, u32[]{:S(2)}) copy-start(s32[6,512]{1,0:T(8,128)} %refs_2_.1) | copy-start | bytes 36868
  15.3 8.0 %collective-permute-start.3 = (bf16[656,128]{1,0:T(8,128)(2,1)S(1)}, bf16[656,128]{1,0:T(8,128)(2,1)S(1)}, u32[]{:S(2)}, u32[]{:S(2)}) collective-permute-start(bf16[656,128]{1,0:T(8,128)(2,1)S(1)} %collective-permute-done.1.first_ref), channel_id=1, source_target_pairs={{0,1},{1,0},{2,3},{3,2},{4,5},{5,4},{6,7},{7,6},{8,9},{9,8},{10,11... | collective-permute-start | bytes 503816 | tf_op jit(solution)/shard_map/ppermute | solution.py:462
  22.1 1.2 %collective-permute-start.4 = (bf16[192,128]{1,0:T(8,128)(2,1)S(1)}, bf16[192,128]{1,0:T(8,128)(2,1)S(1)}, u32[]{:S(2)}, u32[]{:S(2)}) collective-permute-start(bf16[192,128]{1,0:T(8,128)(2,1)S(1)} %collective-permute-done.2.first_far_ref), channel_id=1, source_target_pairs={{0,1},{1,0},{2,3},{3,2},{4,5},{5,4},{6,7},{7,6},{8,9},{9,8},{10,11... | collective-permute-start | bytes 147464 | tf_op jit(solution)/shard_map/ppermute | solution.py:462
  27.9 7.3 %collective-permute-start.5 = (bf16[1104,128]{1,0:T(8,128)(2,1)S(1)}, bf16[1104,128]{1,0:T(8,128)(2,1)S(1)}, u32[]{:S(2)}, u32[]{:S(2)}) collective-permute-start(bf16[1104,128]{1,0:T(8,128)(2,1)S(1)} %get-tuple-element.76.own_ref.refs_3_), channel_id=1, source_target_pairs={{0,1},{1,0},{2,3},{3,2},{4,5},{5,4},{6,7},{7,6},{8,9},{9,8},{10,11... | collective-permute-start | bytes 847880 | tf_op jit(solution)/shard_map/ppermute | solution.py:462
  35.4 8.5 %collective-permute-start.8 = (bf16[656,128]{1,0:T(8,128)(2,1)S(1)}, bf16[656,128]{1,0:T(8,128)(2,1)S(1)}, u32[]{:S(2)}, u32[]{:S(2)}) collective-permute-start(bf16[656,128]{1,0:T(8,128)(2,1)S(1)} %get-tuple-element.79), channel_id=1, source_target_pairs={{1,2},{2,1},{3,4},{4,3},{5,6},{6,5},{7,8},{8,7},{9,10},{10,9},{11,... | collective-permute-start | bytes 503816 | tf_op jit(solution)/shard_map/ppermute | solution.py:462
  36.1 7.8 %collective-permute-start.6 = (f32[160,128]{1,0:T(8,128)S(1)}, f32[160,128]{1,0:T(8,128)S(1)}, u32[]{:S(2)}, u32[]{:S(2)}) collective-permute-start(f32[160,128]{1,0:T(8,128)S(1)} %get-tuple-element.80), channel_id=1, source_target_pairs={{0,2},{1,3},{2,0},{3,1},{4,6},{5,7},{6,4},{7,5},{8,10},{9,11},{10,... | collective-permute-start | bytes 245768 | tf_op jit(solution)/shard_map/ppermute | solution.py:462
  39.4 0.7 %collective-permute-start.7 = (bf16[192,128]{1,0:T(8,128)(2,1)S(1)}, bf16[192,128]{1,0:T(8,128)(2,1)S(1)}, u32[]{:S(2)}, u32[]{:S(2)}) collective-permute-start(bf16[192,128]{1,0:T(8,128)(2,1)S(1)} %get-tuple-element.78), channel_id=1, source_target_pairs={{1,4},{3,6},{4,1},{5,8},{6,3},{7,10},{8,5},{9,12},{10,7},{11,14},{... | collective-permute-start | bytes 147464 | tf_op jit(solution)/shard_map/ppermute | solution.py:462
  43.9 6.9 %collective-permute-start.10 = (bf16[656,128]{1,0:T(8,128)(2,1)S(1)}, bf16[656,128]{1,0:T(8,128)(2,1)S(1)}, u32[]{:S(2)}, u32[]{:S(2)}) collective-permute-start(bf16[656,128]{1,0:T(8,128)(2,1)S(1)} %collective-permute-done.8.refs_5_), channel_id=1, source_target_pairs={{0,1},{1,0},{2,3},{3,2},{4,5},{5,4},{6,7},{7,6},{8,9},{9,8},{10,11... | collective-permute-start | bytes 503816 | tf_op jit(solution)/shard_map/ppermute | solution.py:462
  44.0 6.9 %collective-permute-start.9 = (f32[160,128]{1,0:T(8,128)S(1)}, f32[160,128]{1,0:T(8,128)S(1)}, u32[]{:S(2)}, u32[]{:S(2)}) collective-permute-start(f32[160,128]{1,0:T(8,128)S(1)} %add.9), channel_id=1, source_target_pairs={{0,4},{1,5},{2,6},{3,7},{4,0},{5,1},{6,2},{7,3},{8,12},{9,13},{10,... | collective-permute-start | bytes 245768 | tf_op jit(solution)/shard_map/ppermute | solution.py:462
  48.2 1.2 %collective-permute-start.11 = (bf16[192,128]{1,0:T(8,128)(2,1)S(1)}, bf16[192,128]{1,0:T(8,128)(2,1)S(1)}, u32[]{:S(2)}, u32[]{:S(2)}) collective-permute-start(bf16[192,128]{1,0:T(8,128)(2,1)S(1)} %collective-permute-done.7.refs_7_), channel_id=1, source_target_pairs={{0,1},{1,0},{2,3},{3,2},{4,5},{5,4},{6,7},{7,6},{8,9},{9,8},{10,11... | collective-permute-start | bytes 147464 | tf_op jit(solution)/shard_map/ppermute | solution.py:462
  50.8 4.5 %collective-permute-start.12 = (f32[160,128]{1,0:T(8,128)S(1)}, f32[160,128]{1,0:T(8,128)S(1)}, u32[]{:S(2)}, u32[]{:S(2)}) collective-permute-start(f32[160,128]{1,0:T(8,128)S(1)} %add.10), channel_id=1, source_target_pairs={{0,8},{1,9},{2,10},{3,11},{4,12},{5,13},{6,14},{7,15},{8,0},{9,1},... | collective-permute-start | bytes 245768 | tf_op jit(solution)/shard_map/ppermute | solution.py:462
  55.4 6.7 %collective-permute-start.13 = (f32[160,128]{1,0:T(8,128)S(1)}, f32[160,128]{1,0:T(8,128)S(1)}, u32[]{:S(2)}, u32[]{:S(2)}) collective-permute-start(f32[160,128]{1,0:T(8,128)S(1)} %add.11.a_ref), channel_id=1, source_target_pairs={{0,16},{1,17},{2,18},{3,19},{4,20},{5,21},{6,22},{7,23},{8,24},{9,... | collective-permute-start | bytes 245768 | tf_op jit(solution)/shard_map/ppermute | solution.py:462
  (2 other events, 1.3 us)
where the time goes:
time: 62.6 us; the launch traced here: 62.8 us
  starting transfers between devices  26.1 us (42%)
  waiting for transfers between devices  14.6 us (23%)
  Pallas kernels  11.7 us (19%)
  local copies, waits for them, and re-layouts  9.53 us (15%)
  between operations  0.79 us (1%)
    ppermute x14, starting transfers between devices, sent(): return lax.ppermute(block, 'bricks', route)  26.1 us
    ppermute x14, waiting for transfers between devices, sent(): return lax.ppermute(block, 'bricks', route)  14.6 us
    unnamed x24, local copies, waits for them, and re-layouts  9.53 us
    pallas_call x1, Pallas kernels, shards(): call(forward_kernel, [HBM, HBM] + [VMEM] * 15, [field, field, shape((pack...  4.61 us
    pallas_call x2, Pallas kernels, half_backward(): call(functools.partial(backward_kernel, part), [HBM, HBM] + [VMEM] * (11...  4.05 us
  transfers between devices with their start and end apart: 14, of which 8 were waited for; matrix products, arithmetic and copies ran while one was open for 0% of the time, Pallas kernels for 8%

commit v1 on v0

--- a/solution.py
+++ b/solution.py
@@ -13,6 +13,7 @@
 TILE = 128
 NEAR = 7
 EDGE = 3
+BUSY = 10**10
 HEAD = 16
 SUM_ROWS = 160
 BF = jnp.bfloat16
@@ -162,13 +163,7 @@
     sum_ref[...] = parts[0] + parts[1]
 
 
-def weight_kernel(count, *refs):
-    taps_hbm, sources = refs[0], refs[1 : count + 1]
-    forward_ref, backward_ref = refs[count + 1 : count + 3]
-    places = refs[count + 3 : 2 * count + 3]
-    taps_ref, work, sems = refs[2 * count + 3 :]
-    copies = bring(((taps_hbm, taps_ref),) + tuple(zip(sources, places)), sems)
-    copies[0].wait()
+def weight_kernel(taps_ref, forward_ref, backward_ref, work):
     values = taps_ref[...].astype(F32)
     lanes = lax.broadcasted_iota(jnp.int32, (GC, CH), 1) // GC
 
@@ -190,8 +185,6 @@
             pair = jnp.concatenate([block(base - bc), block(base - bc - 1)], axis=1)
             backward_ref[rows, bc * CH : (bc + 2) * CH] = pair.astype(BF)
         backward_ref[rows, 8 * CH : 9 * CH] = block(base - 8).astype(BF)
-    for copy in copies[1:]:
-        copy.wait()
 
 
 def make_finder(
@@ -446,14 +439,14 @@
 HBM = pl.BlockSpec(memory_space=pltpu.HBM)
 
 
-def call(kernel, ins, outs, scratch=(), flops=0, size=400000):
+def call(kernel, ins, outs, scratch=(), flops=0, size=400000, limit=24):
     return pl.pallas_call(
         kernel,
         in_specs=ins,
         out_specs=tuple(VMEM for _ in outs),
         out_shape=tuple(outs),
         scratch_shapes=list(scratch),
-        compiler_params=pltpu.CompilerParams(vmem_limit_bytes=24 * 2**20),
+        compiler_params=pltpu.CompilerParams(vmem_limit_bytes=limit * 2**20),
         cost_estimate=pl.CostEstimate(flops=flops, bytes_accessed=size, transcendentals=0),
     )
 
@@ -495,33 +488,26 @@
     ]
     field = shape(voxels.shape, BF)
 
-    own, voxels, strips = call(
+    (own,) = call(
         pack_kernel,
         [HBM] * 3,
-        [shape((pack_rows, TILE), BF), field, shape(strips.shape, BF)],
-        [pltpu.SMEM(slot_to_brick.shape, jnp.int32), pltpu.SemaphoreType.DMA((3,))],
+        [shape((pack_rows, TILE), BF)],
+        [pltpu.VMEM(voxels.shape, BF), pltpu.VMEM(strips.shape, BF), pltpu.SMEM(slot_to_brick.shape, jnp.int32), pltpu.SemaphoreType.DMA((3,))],
+        limit=60,
     )(slot_to_brick, voxels, strips)
     mate = swapped(own, 1)
     weight_shape = shape((3 * CH, 9 * CH), BF)
     taps = jnp.transpose(kernel, (2, 3, 4, 1, 0)).reshape(27 * GC, CH)
-    later = (cotangent, cortex, bias.reshape(1, CH), spread, ends, shifts)
     staged = call(
-        functools.partial(weight_kernel, len(later)),
-        [HBM] * (1 + len(later)),
-        [weight_shape] * 2 + [shape(a.shape, a.dtype) for a in later],
-        [
-            pltpu.VMEM(taps.shape, BF),
-            pltpu.VMEM((640, 256), F32),
-            pltpu.SemaphoreType.DMA((1 + len(later),)),
-        ],
-        size=5 * 10**6,
-    )(taps, *later)
+        weight_kernel, [VMEM], [weight_shape] * 2, [pltpu.VMEM((640, 256), F32)], flops=BUSY
+    )(taps)
     near, far = call(
-        functools.partial(route_kernel, slots), [VMEM, VMEM], [near_shape, far_shape], box
+        functools.partial(route_kernel, slots), [VMEM, VMEM], [near_shape, far_shape], box,
+        flops=BUSY,
     )(own, mate)
     near, far = routed(near, 1), routed(far, 2)
     near, far, staged = lax.optimization_barrier((near, far, staged))
-    forward, backward, cotangent, cortex, bias, spread, ends, shifts = staged
+    forward, backward = staged
     received = (near, swapped(near, 1), far, swapped(far, 1))
     activated, dpre, own = call(
         forward_kernel,
@@ -535,7 +521,7 @@
         ],
         flops=4 * 10**9,
     )(
-        slot_to_brick, neighbors, voxels, own, mate, *received, forward, bias,
+        slot_to_brick, neighbors, voxels, own, mate, *received, forward, bias.reshape(1, CH),
         cortex, cotangent, strips, spread, ends, shifts,
     )
     mate = swapped(own, 1)

time: 62.6 us -> 57.7 us (0.922); the launches traced: 62.8 us -> 58.7 us
  Pallas kernels: 11.7 us -> 21.7 us
  local copies, waits for them, and re-layouts: 9.53 us -> 1 us
  starting transfers between devices: 26.1 us -> 23 us
  waiting for transfers between devices: 14.6 us -> 11.9 us
    unnamed x24 -> x26, local copies, waits for them, and re-layouts: 9.53 us -> 1 us
    pallas_call x1, Pallas kernels: 4.61 us -> 10.5 us  [shards(): call(forward_kernel, [HBM, HBM] + [VMEM] * 15, [field, field, shape((pack...]
    pallas_call x2, Pallas kernels: 4.05 us -> 7.75 us  [half_backward(): call(functools.partial(backward_kernel, part), [HBM, HBM] + [VMEM] * (11...]
    ppermute x14, starting transfers between devices: 26.1 us -> 23 us  [sent(): return lax.ppermute(block, 'bricks', route)]
    ppermute x14, waiting for transfers between devices: 14.6 us -> 11.9 us  [sent(): return lax.ppermute(block, 'bricks', route)]
  transfers between devices with their start and end apart: 14 -> 14, of which waited for: 8 -> 7; matrix products, arithmetic and copies ran while one was open for 0% -> 0% of each run, Pallas kernels for 8% -> 14%
where the time goes in v1:
time: 57.7 us; the launch traced here: 58.7 us
  starting transfers between devices  23 us (40%)
  Pallas kernels  21.7 us (38%)
  waiting for transfers between devices  11.9 us (21%)
  local copies, waits for them, and re-layouts  1 us (2%)
  between operations  0.96 us (2%)
    ppermute x14, starting transfers between devices, sent(): return lax.ppermute(block, 'bricks', route)  23 us
    ppermute x14, waiting for transfers between devices, sent(): return lax.ppermute(block, 'bricks', route)  11.9 us
    pallas_call x1, Pallas kernels, shards(): call(forward_kernel, [HBM, HBM] + [VMEM] * 15, [field, field, shape((pack...  10.5 us
    pallas_call x2, Pallas kernels, half_backward(): call(functools.partial(backward_kernel, part), [HBM, HBM] + [VMEM] * (11...  7.75 us
    pallas_call x1, Pallas kernels, shards(): call(pack_kernel, [HBM] * 3, [shape((pack_rows, TILE), BF)], [pltpu.VMEM(...  2.15 us
  transfers between devices with their start and end apart: 14, of which 7 were waited for; matrix products, arithmetic and copies ran while one was open for 0% of the time, Pallas kernels for 14%

profile of v1, /device:TPU:0, one launch (start us, length us, event | category | flops | bytes accessed | tf_op | source)
XLA Modules:
  0.0 58.7 jit_solution(15390322636207556187)
XLA Ops:
  0.6 2.2 %shard_map.138.own_ref = bf16[784,128]{1,0:T(8,128)(2,1)} custom-call(s32[6]{0:T(128)} %refs_0_.3, bf16[6,64,512]{2,1,0:T(8,128)(2,1)} %field_ref.1, bf16[4,512,128]{2,1,0:T(8,128)(2,1)} %constant.8.clone.strips_hbm.strips_ref), custom_call_target="tpu_custom_call" | custom-call | bytes 400000 | tf_op jit(solution)/shard_map/pallas_call | solution.py:491
  2.8 0.5 collective-permute-start
  3.3 1.3 %collective-permute-done.mate_ref = bf16[784,128]{1,0:T(8,128)(2,1)S(1)} collective-permute-done((bf16[784,128]{1,0:T(8,128)(2,1)}, bf16[784,128]{1,0:T(8,128)(2,1)S(1)}, u32[]{:S(2)}, u32[]{:S(2)}) %collective-permute-start) | collective-permute-done | bytes 200736 | tf_op jit(solution)/shard_map/ppermute | solution.py:455
  4.6 0.9 %copy-done.5 = bf16[784,128]{1,0:T(8,128)(2,1)S(1)} copy-done((bf16[784,128]{1,0:T(8,128)(2,1)S(1)}, bf16[784,128]{1,0:T(8,128)(2,1)}, u32[]{:S(2)}) %copy-start.5) | copy-done | bytes 200728
  5.7 0.7 %collective-permute-start.1 = (bf16[656,128]{1,0:T(8,128)(2,1)S(1)}, bf16[656,128]{1,0:T(8,128)(2,1)S(1)}, u32[]{:S(2)}, u32[]{:S(2)}) collective-permute-start(bf16[656,128]{1,0:T(8,128)(2,1)S(1)} %get-tuple-element.37), channel_id=1, source_target_pairs={{1,2},{2,1},{3,4},{4,3},{5,6},{6,5},{7,8},{8,7},{9,10},{10,9},{11,... | collective-permute-start | bytes 503816 | tf_op jit(solution)/shard_map/ppermute | solution.py:455
  6.4 0.7 %collective-permute-start.2 = (bf16[192,128]{1,0:T(8,128)(2,1)S(1)}, bf16[192,128]{1,0:T(8,128)(2,1)S(1)}, u32[]{:S(2)}, u32[]{:S(2)}) collective-permute-start(bf16[192,128]{1,0:T(8,128)(2,1)S(1)} %get-tuple-element.38), channel_id=1, source_target_pairs={{1,4},{3,6},{4,1},{5,8},{6,3},{7,10},{8,5},{9,12},{10,7},{11,14},{... | collective-permute-start | bytes 147464 | tf_op jit(solution)/shard_map/ppermute | solution.py:455
  7.2 0.3 shard_map.140
  7.5 8.5 %collective-permute-start.3 = (bf16[656,128]{1,0:T(8,128)(2,1)S(1)}, bf16[656,128]{1,0:T(8,128)(2,1)S(1)}, u32[]{:S(2)}, u32[]{:S(2)}) collective-permute-start(bf16[656,128]{1,0:T(8,128)(2,1)S(1)} %collective-permute-done.1.first_ref), channel_id=1, source_target_pairs={{0,1},{1,0},{2,3},{3,2},{4,5},{5,4},{6,7},{7,6},{8,9},{9,8},{10,11... | collective-permute-start | bytes 503816 | tf_op jit(solution)/shard_map/ppermute | solution.py:455
  16.0 1.2 %collective-permute-done.4.second_far_ref = bf16[192,128]{1,0:T(8,128)(2,1)S(1)} collective-permute-done((bf16[192,128]{1,0:T(8,128)(2,1)S(1)}, bf16[192,128]{1,0:T(8,128)(2,1)S(1)}, u32[]{:S(2)}, u32[]{:S(2)}) %collective-permute-start.4) | collective-permute-done | bytes 49184 | tf_op jit(solution)/shard_map/ppermute | solution.py:455
  17.3 10.5 %shard_map.141 = (bf16[6,64,512]{2,1,0:T(8,128)(2,1)}, bf16[6,64,512]{2,1,0:T(8,128)(2,1)S(1)}, bf16[1104,128]{1,0:T(8,128)(2,1)S(1)}) custom-call(s32[6]{0:T(128)S(1)} %copy-done.8, s32[6,6]{1,0:T(8,128)S(1)} %copy-done.7, bf16[6,64,512]{2,1,0:T(8,128)(2,1)S(1)} %copy-done.4, bf16[784,128]{1,0:T(8,128)(2,1)S(1)} %copy-done.6, ...), custom_call_target="tpu_custom_call" | custom-call | flops 4000000000 | bytes 400000 | tf_op jit(solution)/shard_map/pallas_call | solution.py:512
  27.9 1.6 %collective-permute-done.5.mate_ref.refs_4_ = bf16[1104,128]{1,0:T(8,128)(2,1)S(1)} collective-permute-done((bf16[1104,128]{1,0:T(8,128)(2,1)S(1)}, bf16[1104,128]{1,0:T(8,128)(2,1)S(1)}, u32[]{:S(2)}, u32[]{:S(2)}) %collective-permute-start.5) | collective-permute-done | bytes 282656 | tf_op jit(solution)/shard_map/ppermute | solution.py:455
  29.6 0.7 %collective-permute-start.8 = (bf16[656,128]{1,0:T(8,128)(2,1)S(1)}, bf16[656,128]{1,0:T(8,128)(2,1)S(1)}, u32[]{:S(2)}, u32[]{:S(2)}) collective-permute-start(bf16[656,128]{1,0:T(8,128)(2,1)S(1)} %get-tuple-element.49), channel_id=1, source_target_pairs={{1,2},{2,1},{3,4},{4,3},{5,6},{6,5},{7,8},{8,7},{9,10},{10,9},{11,... | collective-permute-start | bytes 503816 | tf_op jit(solution)/shard_map/ppermute | solution.py:455
  30.3 3.1 %collective-permute-start.6 = (f32[160,128]{1,0:T(8,128)S(1)}, f32[160,128]{1,0:T(8,128)S(1)}, u32[]{:S(2)}, u32[]{:S(2)}) collective-permute-start(f32[160,128]{1,0:T(8,128)S(1)} %get-tuple-element.50), channel_id=1, source_target_pairs={{0,2},{1,3},{2,0},{3,1},{4,6},{5,7},{6,4},{7,5},{8,10},{9,11},{10,... | collective-permute-start | bytes 245768 | tf_op jit(solution)/shard_map/ppermute | solution.py:455
  33.4 0.7 %collective-permute-start.7 = (bf16[192,128]{1,0:T(8,128)(2,1)S(1)}, bf16[192,128]{1,0:T(8,128)(2,1)S(1)}, u32[]{:S(2)}, u32[]{:S(2)}) collective-permute-start(bf16[192,128]{1,0:T(8,128)(2,1)S(1)} %get-tuple-element.48), channel_id=1, source_target_pairs={{1,4},{3,6},{4,1},{5,8},{6,3},{7,10},{8,5},{9,12},{10,7},{11,14},{... | collective-permute-start | bytes 147464 | tf_op jit(solution)/shard_map/ppermute | solution.py:455
  34.0 4.7 %collective-permute-done.6 = f32[160,128]{1,0:T(8,128)S(1)} collective-permute-done((f32[160,128]{1,0:T(8,128)S(1)}, f32[160,128]{1,0:T(8,128)S(1)}, u32[]{:S(2)}, u32[]{:S(2)}) %collective-permute-start.6) | collective-permute-done | bytes 81952 | tf_op jit(solution)/shard_map/ppermute | solution.py:455
  38.7 1.9 %collective-permute-start.10 = (bf16[656,128]{1,0:T(8,128)(2,1)S(1)}, bf16[656,128]{1,0:T(8,128)(2,1)S(1)}, u32[]{:S(2)}, u32[]{:S(2)}) collective-permute-start(bf16[656,128]{1,0:T(8,128)(2,1)S(1)} %collective-permute-done.8.refs_5_), channel_id=1, source_target_pairs={{0,1},{1,0},{2,3},{3,2},{4,5},{5,4},{6,7},{7,6},{8,9},{9,8},{10,11... | collective-permute-start | bytes 503816 | tf_op jit(solution)/shard_map/ppermute | solution.py:455
  40.6 1.3 %collective-permute-start.9 = (f32[160,128]{1,0:T(8,128)S(1)}, f32[160,128]{1,0:T(8,128)S(1)}, u32[]{:S(2)}, u32[]{:S(2)}) collective-permute-start(f32[160,128]{1,0:T(8,128)S(1)} %add.9), channel_id=1, source_target_pairs={{0,4},{1,5},{2,6},{3,7},{4,0},{5,1},{6,2},{7,3},{8,12},{9,13},{10,... | collective-permute-start | bytes 245768 | tf_op jit(solution)/shard_map/ppermute | solution.py:455
  42.1 1.0 %collective-permute-done.11.refs_8_ = bf16[192,128]{1,0:T(8,128)(2,1)S(1)} collective-permute-done((bf16[192,128]{1,0:T(8,128)(2,1)S(1)}, bf16[192,128]{1,0:T(8,128)(2,1)S(1)}, u32[]{:S(2)}, u32[]{:S(2)}) %collective-permute-start.11) | collective-permute-done | bytes 49184 | tf_op jit(solution)/shard_map/ppermute | solution.py:455
  43.1 2.0 %collective-permute-done.9 = f32[160,128]{1,0:T(8,128)S(1)} collective-permute-done((f32[160,128]{1,0:T(8,128)S(1)}, f32[160,128]{1,0:T(8,128)S(1)}, u32[]{:S(2)}, u32[]{:S(2)}) %collective-permute-start.9) | collective-permute-done | bytes 81952 | tf_op jit(solution)/shard_map/ppermute | solution.py:455
  45.1 3.1 %collective-permute-start.12 = (f32[160,128]{1,0:T(8,128)S(1)}, f32[160,128]{1,0:T(8,128)S(1)}, u32[]{:S(2)}, u32[]{:S(2)}) collective-permute-start(f32[160,128]{1,0:T(8,128)S(1)} %add.10), channel_id=1, source_target_pairs={{0,8},{1,9},{2,10},{3,11},{4,12},{5,13},{6,14},{7,15},{8,0},{9,1},... | collective-permute-start | bytes 245768 | tf_op jit(solution)/shard_map/ppermute | solution.py:455
  48.2 3.4 %shard_map.143.refs_13_ = bf16[6,64,512]{2,1,0:T(8,128)(2,1)S(1)} custom-call(s32[6]{0:T(128)S(1)} %copy-done.8, s32[6,6]{1,0:T(8,128)S(1)} %copy-done.7, bf16[6,64,512]{2,1,0:T(8,128)(2,1)S(1)} %get-tuple-element.45.refs_2_, bf16[1104,128]{1,0:T(8,128)(2,1)S(1)} %get-tuple-element.46.own_ref.refs_3_, ...), custom_call_target="tpu_custom_call" | custom-call | flops 1000000000 | bytes 400000 | tf_op jit(solution)/shard_map/pallas_call | solution.py:545
  51.7 1.7 %collective-permute-start.13 = (f32[160,128]{1,0:T(8,128)S(1)}, f32[160,128]{1,0:T(8,128)S(1)}, u32[]{:S(2)}, u32[]{:S(2)}) collective-permute-start(f32[160,128]{1,0:T(8,128)S(1)} %add.11.a_ref), channel_id=1, source_target_pairs={{0,16},{1,17},{2,18},{3,19},{4,20},{5,21},{6,22},{7,23},{8,24},{9,... | collective-permute-start | bytes 245768 | tf_op jit(solution)/shard_map/ppermute | solution.py:455
  53.4 4.3 %shard_map.144 = bf16[6,64,512]{2,1,0:T(8,128)(2,1)} custom-call(s32[6]{0:T(128)S(1)} %copy-done.8, s32[6,6]{1,0:T(8,128)S(1)} %copy-done.7, bf16[6,64,512]{2,1,0:T(8,128)(2,1)S(1)} %get-tuple-element.45.refs_2_, bf16[1104,128]{1,0:T(8,128)(2,1)S(1)} %get-tuple-element.46.own_ref.refs_3_, bf16[1104,128]{1,0:T(8,128)(2,1)S(1)} %collective-permute-done.5.mate_ref.refs_4_, ...), custom_call_target="tpu_custom_call" | custom-call | flops 1000000000 | bytes 400000 | tf_op jit(solution)/shard_map/pallas_call | solution.py:545
  58.0 0.7 %shard_map.145 = (f32[216,64]{1,0:T(8,128)}, f32[1,64]{1,0:T(1,128)}) custom-call(f32[160,128]{1,0:T(8,128)S(1)} %add.11.a_ref, f32[160,128]{1,0:T(8,128)S(1)} %collective-permute-done.13.b_ref), custom_call_target="tpu_custom_call" | custom-call | bytes 400000 | tf_op jit(solution)/shard_map/pallas_call | solution.py:568
  (41 shorter events, 0.9 us)
Async XLA Ops:
  2.8 1.8 %collective-permute-start = (bf16[784,128]{1,0:T(8,128)(2,1)}, bf16[784,128]{1,0:T(8,128)(2,1)S(1)}, u32[]{:S(2)}, u32[]{:S(2)}) collective-permute-start(bf16[784,128]{1,0:T(8,128)(2,1)} %shard_map.138.own_ref), channel_id=1, source_target_pairs={{0,1},{1,0},{2,3},{3,2},{4,5},{5,4},{6,7},{7,6},{8,9},{9,8},{10,11... | collective-permute-start | bytes 602120 | tf_op jit(solution)/shard_map/ppermute | solution.py:455
  5.7 1.8 %collective-permute-start.1 = (bf16[656,128]{1,0:T(8,128)(2,1)S(1)}, bf16[656,128]{1,0:T(8,128)(2,1)S(1)}, u32[]{:S(2)}, u32[]{:S(2)}) collective-permute-start(bf16[656,128]{1,0:T(8,128)(2,1)S(1)} %get-tuple-element.37), channel_id=1, source_target_pairs={{1,2},{2,1},{3,4},{4,3},{5,6},{6,5},{7,8},{8,7},{9,10},{10,9},{11,... | collective-permute-start | bytes 503816 | tf_op jit(solution)/shard_map/ppermute | solution.py:455
  6.4 1.1 %collective-permute-start.2 = (bf16[192,128]{1,0:T(8,128)(2,1)S(1)}, bf16[192,128]{1,0:T(8,128)(2,1)S(1)}, u32[]{:S(2)}, u32[]{:S(2)}) collective-permute-start(bf16[192,128]{1,0:T(8,128)(2,1)S(1)} %get-tuple-element.38), channel_id=1, source_target_pairs={{1,4},{3,6},{4,1},{5,8},{6,3},{7,10},{8,5},{9,12},{10,7},{11,14},{... | collective-permute-start | bytes 147464 | tf_op jit(solution)/shard_map/ppermute | solution.py:455
  7.1 10.2 %copy-start = (bf16[4,256,1152]{2,1,0:T(8,128)(2,1)S(1)}, bf16[4,256,1152]{2,1,0:T(8,128)(2,1)}, u32[]{:S(2)}) copy-start(bf16[4,256,1152]{2,1,0:T(8,128)(2,1)} %constant.11.clone.shifts_ref.refs_12_) | copy-start | bytes 7077892
  7.1 10.2 %copy-start.1 = (bf16[4,384,128]{2,1,0:T(8,128)(2,1)S(1)}, bf16[4,384,128]{2,1,0:T(8,128)(2,1)}, u32[]{:S(2)}) copy-start(bf16[4,384,128]{2,1,0:T(8,128)(2,1)} %constant.10.clone.ends_ref.refs_11_) | copy-start | bytes 1179652
  7.1 10.2 %copy-start.2 = (bf16[384,512]{1,0:T(8,128)(2,1)S(1)}, bf16[384,512]{1,0:T(8,128)(2,1)}, u32[]{:S(2)}) copy-start(bf16[384,512]{1,0:T(8,128)(2,1)} %constant.9.clone.spread_ref.refs_10_) | copy-start | bytes 1179652
  7.1 10.2 %copy-start.3 = (bf16[4,512,128]{2,1,0:T(8,128)(2,1)S(1)}, bf16[4,512,128]{2,1,0:T(8,128)(2,1)}, u32[]{:S(2)}) copy-start(bf16[4,512,128]{2,1,0:T(8,128)(2,1)} %constant.8.clone.strips_hbm.strips_ref) | copy-start | bytes 1572868
  7.1 10.2 %copy-start.4 = (bf16[6,64,512]{2,1,0:T(8,128)(2,1)S(1)}, bf16[6,64,512]{2,1,0:T(8,128)(2,1)}, u32[]{:S(2)}) copy-start(bf16[6,64,512]{2,1,0:T(8,128)(2,1)} %field_ref.1) | copy-start | bytes 1179652
  7.1 10.2 %copy-start.6 = (bf16[784,128]{1,0:T(8,128)(2,1)S(1)}, bf16[784,128]{1,0:T(8,128)(2,1)}, u32[]{:S(2)}) copy-start(bf16[784,128]{1,0:T(8,128)(2,1)} %shard_map.138.own_ref) | copy-start | bytes 602116
  7.1 10.2 %copy-start.7 = (s32[6,6]{1,0:T(8,128)S(1)}, s32[6,6]{1,0:T(8,128)}, u32[]{:S(2)}) copy-start(s32[6,6]{1,0:T(8,128)} %refs_1_.3) | copy-start | bytes 436
  7.1 10.2 %copy-start.8 = (s32[6]{0:T(128)S(1)}, s32[6]{0:T(128)}, u32[]{:S(2)}) copy-start(s32[6]{0:T(128)} %refs_0_.3) | copy-start | bytes 76
  7.2 10.2 %copy-start.9 = (bf16[6,64,512]{2,1,0:T(8,128)(2,1)S(1)}, bf16[6,64,512]{2,1,0:T(8,128)(2,1)}, u32[]{:S(2)}) copy-start(bf16[6,64,512]{2,1,0:T(8,128)(2,1)} %upstream_ref.1) | copy-start | bytes 1179652
  7.2 10.1 %copy-start.11 = (s32[6,512]{1,0:T(8,128)S(1)}, s32[6,512]{1,0:T(8,128)}, u32[]{:S(2)}) copy-start(s32[6,512]{1,0:T(8,128)} %cortex_ref.1) | copy-start | bytes 36868
  7.5 9.7 %collective-permute-start.3 = (bf16[656,128]{1,0:T(8,128)(2,1)S(1)}, bf16[656,128]{1,0:T(8,128)(2,1)S(1)}, u32[]{:S(2)}, u32[]{:S(2)}) collective-permute-start(bf16[656,128]{1,0:T(8,128)(2,1)S(1)} %collective-permute-done.1.first_ref), channel_id=1, source_target_pairs={{0,1},{1,0},{2,3},{3,2},{4,5},{5,4},{6,7},{7,6},{8,9},{9,8},{10,11... | collective-permute-start | bytes 503816 | tf_op jit(solution)/shard_map/ppermute | solution.py:455
  16.0 1.2 %collective-permute-start.4 = (bf16[192,128]{1,0:T(8,128)(2,1)S(1)}, bf16[192,128]{1,0:T(8,128)(2,1)S(1)}, u32[]{:S(2)}, u32[]{:S(2)}) collective-permute-start(bf16[192,128]{1,0:T(8,128)(2,1)S(1)} %collective-permute-done.2.first_far_ref), channel_id=1, source_target_pairs={{0,1},{1,0},{2,3},{3,2},{4,5},{5,4},{6,7},{7,6},{8,9},{9,8},{10,11... | collective-permute-start | bytes 147464 | tf_op jit(solution)/shard_map/ppermute | solution.py:455
  27.8 1.6 %collective-permute-start.5 = (bf16[1104,128]{1,0:T(8,128)(2,1)S(1)}, bf16[1104,128]{1,0:T(8,128)(2,1)S(1)}, u32[]{:S(2)}, u32[]{:S(2)}) collective-permute-start(bf16[1104,128]{1,0:T(8,128)(2,1)S(1)} %get-tuple-element.46.own_ref.refs_3_), channel_id=1, source_target_pairs={{0,1},{1,0},{2,3},{3,2},{4,5},{5,4},{6,7},{7,6},{8,9},{9,8},{10,11... | collective-permute-start | bytes 847880 | tf_op jit(solution)/shard_map/ppermute | solution.py:455
  29.6 9.1 %collective-permute-start.8 = (bf16[656,128]{1,0:T(8,128)(2,1)S(1)}, bf16[656,128]{1,0:T(8,128)(2,1)S(1)}, u32[]{:S(2)}, u32[]{:S(2)}) collective-permute-start(bf16[656,128]{1,0:T(8,128)(2,1)S(1)} %get-tuple-element.49), channel_id=1, source_target_pairs={{1,2},{2,1},{3,4},{4,3},{5,6},{6,5},{7,8},{8,7},{9,10},{10,9},{11,... | collective-permute-start | bytes 503816 | tf_op jit(solution)/shard_map/ppermute | solution.py:455
  30.3 8.4 %collective-permute-start.6 = (f32[160,128]{1,0:T(8,128)S(1)}, f32[160,128]{1,0:T(8,128)S(1)}, u32[]{:S(2)}, u32[]{:S(2)}) collective-permute-start(f32[160,128]{1,0:T(8,128)S(1)} %get-tuple-element.50), channel_id=1, source_target_pairs={{0,2},{1,3},{2,0},{3,1},{4,6},{5,7},{6,4},{7,5},{8,10},{9,11},{10,... | collective-permute-start | bytes 245768 | tf_op jit(solution)/shard_map/ppermute | solution.py:455
  33.4 0.7 %collective-permute-start.7 = (bf16[192,128]{1,0:T(8,128)(2,1)S(1)}, bf16[192,128]{1,0:T(8,128)(2,1)S(1)}, u32[]{:S(2)}, u32[]{:S(2)}) collective-permute-start(bf16[192,128]{1,0:T(8,128)(2,1)S(1)} %get-tuple-element.48), channel_id=1, source_target_pairs={{1,4},{3,6},{4,1},{5,8},{6,3},{7,10},{8,5},{9,12},{10,7},{11,14},{... | collective-permute-start | bytes 147464 | tf_op jit(solution)/shard_map/ppermute | solution.py:455
  38.7 6.4 %collective-permute-start.10 = (bf16[656,128]{1,0:T(8,128)(2,1)S(1)}, bf16[656,128]{1,0:T(8,128)(2,1)S(1)}, u32[]{:S(2)}, u32[]{:S(2)}) collective-permute-start(bf16[656,128]{1,0:T(8,128)(2,1)S(1)} %collective-permute-done.8.refs_5_), channel_id=1, source_target_pairs={{0,1},{1,0},{2,3},{3,2},{4,5},{5,4},{6,7},{7,6},{8,9},{9,8},{10,11... | collective-permute-start | bytes 503816 | tf_op jit(solution)/shard_map/ppermute | solution.py:455
  40.6 4.5 %collective-permute-start.9 = (f32[160,128]{1,0:T(8,128)S(1)}, f32[160,128]{1,0:T(8,128)S(1)}, u32[]{:S(2)}, u32[]{:S(2)}) collective-permute-start(f32[160,128]{1,0:T(8,128)S(1)} %add.9), channel_id=1, source_target_pairs={{0,4},{1,5},{2,6},{3,7},{4,0},{5,1},{6,2},{7,3},{8,12},{9,13},{10,... | collective-permute-start | bytes 245768 | tf_op jit(solution)/shard_map/ppermute | solution.py:455
  41.9 1.2 %collective-permute-start.11 = (bf16[192,128]{1,0:T(8,128)(2,1)S(1)}, bf16[192,128]{1,0:T(8,128)(2,1)S(1)}, u32[]{:S(2)}, u32[]{:S(2)}) collective-permute-start(bf16[192,128]{1,0:T(8,128)(2,1)S(1)} %collective-permute-done.7.refs_7_), channel_id=1, source_target_pairs={{0,1},{1,0},{2,3},{3,2},{4,5},{5,4},{6,7},{7,6},{8,9},{9,8},{10,11... | collective-permute-start | bytes 147464 | tf_op jit(solution)/shard_map/ppermute | solution.py:455
  45.1 6.5 %collective-permute-start.12 = (f32[160,128]{1,0:T(8,128)S(1)}, f32[160,128]{1,0:T(8,128)S(1)}, u32[]{:S(2)}, u32[]{:S(2)}) collective-permute-start(f32[160,128]{1,0:T(8,128)S(1)} %add.10), channel_id=1, source_target_pairs={{0,8},{1,9},{2,10},{3,11},{4,12},{5,13},{6,14},{7,15},{8,0},{9,1},... | collective-permute-start | bytes 245768 | tf_op jit(solution)/shard_map/ppermute | solution.py:455
  51.7 6.3 %collective-permute-start.13 = (f32[160,128]{1,0:T(8,128)S(1)}, f32[160,128]{1,0:T(8,128)S(1)}, u32[]{:S(2)}, u32[]{:S(2)}) collective-permute-start(f32[160,128]{1,0:T(8,128)S(1)} %add.11.a_ref), channel_id=1, source_target_pairs={{0,16},{1,17},{2,18},{3,19},{4,20},{5,21},{6,22},{7,23},{8,24},{9,... | collective-permute-start | bytes 245768 | tf_op jit(solution)/shard_map/ppermute | solution.py:455
  (3 other events, 17.5 us)

commit v2 on v1

--- a/solution.py
+++ b/solution.py
@@ -10,12 +10,15 @@
 
 CH = 64
 GC = 8
+PART = 16
+PARTS = CH // PART
+SIDES = (0, 1, 2, 3, 5, 6, 7, 8)
 TILE = 128
 NEAR = 7
 EDGE = 3
 BUSY = 10**10
 HEAD = 16
-SUM_ROWS = 160
+SUM_ROWS = 128
 BF = jnp.bfloat16
 F32 = jnp.float32
 
@@ -23,16 +26,21 @@
 @functools.cache
 def tables():
     strips = np.zeros((4, 512, TILE), np.float32)
-    spread = np.zeros((384, 4 * TILE), np.float32)
+    spread = np.zeros((256, 4 * TILE), np.float32)
     ends = np.zeros((4, 384, TILE), np.float32)
-    shifts = np.zeros((4, 256, 9 * TILE), np.float32)
+    shifts = np.zeros((4, 256, 8 * TILE), np.float32)
+    fold = np.zeros((10 * PART, 10 * GC), np.float32)
+    for bc in range(9):
+        for i in range(PART):
+            fold[bc * PART + i, bc * GC + i % GC] = 1
+    fold[9 * PART, 9 * GC] = 1
     for half in range(2):
         for xx in range(4):
             for w in range(8):
                 i, xp = 2 * half + xx // 2, xx % 2
                 spread[half * 64 + xx * 8 + w, i * TILE + xp * 8 + w] = 1
-                spread[128 + half * 64 + 32 + xx * 8 + w, i * TILE + 32 + xp * 8 + w] = 1
-                spread[256 + half * 64 + xx * 8 + w, i * TILE + 64 + xp * 8 + w] = 1
+                spread[half * 64 + 32 + xx * 8 + w, i * TILE + 32 + xp * 8 + w] = 1
+                spread[128 + half * 64 + xx * 8 + w, i * TILE + 64 + xp * 8 + w] = 1
     for t in range(4):
         q, r = t // 2, t % 2
         own_y, own_z = (0 if q else 7), (0 if r else 7)
@@ -51,6 +59,9 @@
         out_y, out_z = (-1 if q else 8), (-1 if r else 8)
         for b in range(3):
             for c in range(3):
+                if b == 1 and c == 1:
+                    continue
+                column = SIDES.index(b * 3 + c)
                 for xp in range(2):
                     for y in range(8):
                         for z in range(8):
@@ -66,8 +77,8 @@
                                 k = 192 + xp * 8 + far_z
                             else:
                                 continue
-                            shifts[t, k, (b * 3 + c) * TILE + xp * 64 + y * 8 + z] = 1
-    return strips, spread, ends, shifts
+                            shifts[t, k, column * TILE + xp * 64 + y * 8 + z] = 1
+    return strips, spread, ends, shifts, fold
 
 
 def left_half(shape):
@@ -167,24 +178,25 @@
     values = taps_ref[...].astype(F32)
     lanes = lax.broadcasted_iota(jnp.int32, (GC, CH), 1) // GC
 
-    def block(tap):
+    def block(tap, part):
         tile = values[tap * GC : (tap + 1) * GC, :]
-        return jnp.concatenate([jnp.where(lanes == g, tile, 0.0) for g in range(CH // GC)], axis=0)
+        groups = (2 * part, 2 * part + 1)
+        return jnp.concatenate([jnp.where(lanes == g, tile, 0.0) for g in groups], axis=0)
 
     work[...] = jnp.zeros_like(work)
-    for bc in range(9):
-        rows = slice(bc * CH, (bc + 1) * CH)
-        work[rows, 0:TILE] = jnp.concatenate([block(bc), block(9 + bc)], axis=1)
-        work[rows, TILE : TILE + CH] = block(18 + bc)
-    turned = work[...].T
-    forward_ref[...] = turned[0 : 3 * CH, 0 : 9 * CH].astype(BF)
-    for a in range(3):
-        rows = slice(a * CH, (a + 1) * CH)
-        base = (2 - a) * 9 + 8
-        for bc in range(0, 8, 2):
-            pair = jnp.concatenate([block(base - bc), block(base - bc - 1)], axis=1)
-            backward_ref[rows, bc * CH : (bc + 2) * CH] = pair.astype(BF)
-        backward_ref[rows, 8 * CH : 9 * CH] = block(base - 8).astype(BF)
+    for part in range(PARTS):
+        out = slice(part * PART, (part + 1) * PART)
+        for bc in range(9):
+            for a in range(3):
+                work[bc * PART : (bc + 1) * PART, a * TILE : a * TILE + CH] = block(a * 9 + bc, part)
+        for a in range(3):
+            turned = work[:, a * TILE : (a + 1) * TILE].T
+            forward_ref[part, a * PART : (a + 1) * PART, :] = turned[out, 0 : 9 * PART].astype(BF)
+    for part in range(PARTS):
+        out = slice(part * PART, (part + 1) * PART)
+        for a in range(3):
+            blocks = [block((2 - a) * 9 + 8 - bc, part)[:, out] for bc in range(9)]
+            backward_ref[part, a * PART : (a + 1) * PART, :] = jnp.concatenate(blocks, axis=1).astype(BF)
 
 
 def make_finder(
@@ -246,6 +258,14 @@
     return base, mine, find_strip, find_plane
 
 
+def put_taps(taps, bc, values):
+    for i in range(5):
+        for p in range(PARTS):
+            taps[p, bc * PART : (bc + 1) * PART, i * TILE : (i + 1) * TILE] = values[
+                i * CH + p * PART : i * CH + (p + 1) * PART, :
+            ]
+
+
 def convolve_brick(
     s, base, find_strip, find_plane, link_ref, field_ref, planes, strips,
     spread_ref, ends_ref, shifts_ref, weight_ref, mixed, taps, sums,
@@ -263,7 +283,10 @@
         low = planes[find_plane(near - 4, has_low)]
         return join_halves(high, low)
 
-    beside = jnp.concatenate([strips[find_strip(m)] for m in sides], axis=1)
+    beside_y, beside_z, beside_yz = [strips[find_strip(m)] for m in sides]
+    of_y = lax.broadcasted_iota(jnp.int32, (CH, TILE), 1) % 64 < 32
+    beside = jnp.where(of_y, beside_y.astype(F32), beside_z.astype(F32)).astype(BF)
+    beside = jnp.concatenate([beside, beside_yz], axis=1)
     halo = dot(beside, spread_ref[...]).astype(BF)
     outer_beside = jnp.concatenate([outer(m) for m in sides], axis=1)
     for i in range(4):
@@ -272,15 +295,16 @@
         mixed[rows, TILE:] = halo[:, i * TILE : (i + 1) * TILE]
     mixed[4 * CH :, 0:TILE] = outer(brick)
     mixed[4 * CH :, TILE:] = dot(outer_beside, ends_ref[kind]).astype(BF)
-    for bc in range(0, 9, 2):
-        wide = min(2, 9 - bc)
-        part = dot(mixed[...], shifts_ref[kind, :, bc * TILE : (bc + wide) * TILE]).astype(BF)
-        for e in range(wide):
-            for i in range(5):
-                taps[(bc + e) * CH : (bc + e + 1) * CH, i * TILE : (i + 1) * TILE] = part[
-                    i * CH : (i + 1) * CH, e * TILE : (e + 1) * TILE
-                ]
-    sums[...] = dot(weight_ref[...], taps[0 : 9 * CH, :])
+    for k in range(0, 8, 2):
+        part = dot(mixed[...], shifts_ref[kind, :, k * TILE : (k + 2) * TILE]).astype(BF)
+        for e in range(2):
+            put_taps(taps, SIDES[k + e], part[:, e * TILE : (e + 1) * TILE])
+    put_taps(taps, 4, mixed[:, 0:TILE])
+    for p in range(PARTS):
+        part = dot(weight_ref[p], taps[p, 0 : 9 * PART, :])
+        for a in range(3):
+            at = a * CH + p * PART
+            sums[at : at + PART, :] = part[a * PART : (a + 1) * PART, :]
     turned = []
     for a in (0, 2):
         rows = slice(a * CH, (a + 1) * CH)
@@ -299,7 +323,7 @@
 def forward_kernel(
     slot_hbm, link_hbm, field_ref, own_ref, mate_ref, first_ref, second_ref, first_far_ref,
     second_far_ref, weight_ref, bias_ref, cortex_ref, upstream_ref, strips_ref, spread_ref,
-    ends_ref, shifts_ref, out_ref, dpre_ref, msg_ref,
+    ends_ref, shifts_ref, fold_ref, out_ref, dpre_ref, msg_ref,
     planes, strips, mixed, taps, sums, slot_ref, link_ref, sems, spots, grads, keeps,
 ):
     slots = field_ref.shape[0]
@@ -309,7 +333,7 @@
     )
     for s in range(slots):
         keeps[s] = jnp.broadcast_to(cortex_ref[s : s + 1, :].astype(F32), (8, 512))
-    taps[9 * CH :, :] = jnp.ones((HEAD, 5 * TILE), BF)
+    taps[:, 9 * PART :, :] = jnp.ones((PARTS, PART, 5 * TILE), BF)
     grads[...] = jnp.zeros_like(grads)
     for s in range(slots):
 
@@ -323,6 +347,12 @@
     bias = jnp.sum(jnp.where(diagonal, bias_ref[...], 0.0), axis=1, keepdims=True)
     left = left_half((CH, TILE))
     zero = jnp.zeros((CH, TILE), F32)
+
+    def put_spots(a, i, values):
+        for p in range(PARTS):
+            spots[p, a * PART : (a + 1) * PART, i * TILE : (i + 1) * TILE] = values[
+                p * PART : (p + 1) * PART, :
+            ]
 
     def one_brick(s, carry):
         tiles = convolve_brick(
@@ -339,20 +369,20 @@
             slope = sigma * (1.0 + pre * (1.0 - sigma))
             dpre = (upstream_ref[s, :, lanes].astype(F32) * keep * slope).astype(BF)
             dpre_ref[s, :, lanes] = dpre
-            spots[CH : 2 * CH, lanes] = dpre
+            put_spots(1, i, dpre)
             turned.append(pltpu.roll(dpre.astype(F32), 64, 1))
-        spots[CH : 2 * CH, 4 * TILE :] = jnp.zeros((CH, TILE), BF)
+        put_spots(1, 4, zero.astype(BF))
         turned.append(zero)
         for i in range(4):
-            lanes = slice(i * TILE, (i + 1) * TILE)
-            spots[0:CH, lanes] = jnp.where(left, turned[i], turned[i + 1]).astype(BF)
+            put_spots(0, i, jnp.where(left, turned[i], turned[i + 1]).astype(BF))
             before = turned[i - 1] if i else zero
-            spots[2 * CH :, lanes] = jnp.where(left, before, turned[i]).astype(BF)
-        spots[0:CH, 4 * TILE :] = jnp.where(left, 0.0, turned[0]).astype(BF)
-        spots[2 * CH :, 4 * TILE :] = jnp.where(left, turned[3], 0.0).astype(BF)
-        grads[...] += lax.dot_general(
-            taps[...], spots[...], (((1,), (1,)), ((), ())), preferred_element_type=F32
-        )
+            put_spots(2, i, jnp.where(left, before, turned[i]).astype(BF))
+        put_spots(0, 4, jnp.where(left, 0.0, turned[0]).astype(BF))
+        put_spots(2, 4, jnp.where(left, turned[3], 0.0).astype(BF))
+        for p in range(PARTS):
+            grads[p] += lax.dot_general(
+                spots[p], taps[p], (((1,), (1,)), ((), ())), preferred_element_type=F32
+            )
         return carry
 
     lax.fori_loop(0, mine, one_brick, 0)
@@ -360,24 +390,24 @@
     pack_bricks(slot_ref, dpre_ref, strips_ref, msg_ref)
     high = slots * 2 * CH + HEAD
     low = high + SUM_ROWS
-    group = lax.broadcasted_iota(jnp.int32, (GC, TILE), 1) % CH // GC
-    for half, lanes in enumerate((slice(0, TILE), slice(TILE, TILE + CH))):
-        group_here = group[:, : lanes.stop - lanes.start]
-        rows = []
-        for bc in range(9):
-            total = jnp.zeros(group_here.shape, F32)
-            for g in range(CH // GC):
-                at = bc * CH + g * GC
-                total = total + jnp.where(group_here == g, grads[at : at + GC, lanes], 0.0)
-            rows.append(total)
-        rows.append(grads[9 * CH : 9 * CH + GC, lanes])
-        full = jnp.concatenate(rows, axis=0)
-        if full.shape[1] < TILE:
-            full = jnp.concatenate([full, jnp.zeros((10 * GC, TILE - full.shape[1]), F32)], axis=1)
-        rounded = full.astype(BF)
-        at = half * 10 * GC
-        msg_ref[high + at : high + at + 10 * GC, :] = rounded
-        msg_ref[low + at : low + at + 10 * GC, :] = (full - rounded.astype(F32)).astype(BF)
+    rows = jnp.concatenate(
+        [grads[p, a * PART : (a + 1) * PART, :] for a in range(3) for p in range(PARTS)], axis=0
+    )
+    group = lax.broadcasted_iota(jnp.int32, rows.shape, 0) // GC % 2
+    column = lax.broadcasted_iota(jnp.int32, rows.shape, 1)
+    same = (column // GC % 2 == group) | (column >= 9 * PART)
+    full = jnp.dot(
+        jnp.where(same, rows, 0.0), fold_ref[...],
+        precision=lax.Precision.HIGHEST, preferred_element_type=F32,
+    ).T
+    last = jnp.concatenate([full[:, TILE:], jnp.zeros((2 * GC, CH), F32)], axis=0)
+    half = SUM_ROWS - 10 * GC
+    last = jnp.concatenate([last[0:half], last[half:]], axis=1)
+    for at, values in ((0, full[:, 0:TILE]), (10 * GC, last)):
+        rounded = values.astype(BF)
+        size = values.shape[0]
+        msg_ref[high + at : high + at + size, :] = rounded
+        msg_ref[low + at : low + at + size, :] = (values - rounded.astype(F32)).astype(BF)
 
 
 def backward_kernel(part, *refs):
@@ -427,10 +457,11 @@
 
 
 def finish_kernel(a_ref, b_ref, kernel_ref, bias_ref):
-    first = a_ref[0 : 10 * GC, :] + b_ref[0 : 10 * GC, :]
-    second = a_ref[10 * GC :, :] + b_ref[10 * GC :, :]
+    total = a_ref[...] + b_ref[...]
+    first, last = total[0 : 10 * GC, :], total[10 * GC :, :]
     turned = pltpu.roll(first, 64, 1)
-    for a, part in enumerate((first, turned, second)):
+    parts = (first, turned, jnp.concatenate([last, pltpu.roll(last, 64, 1)], axis=0))
+    for a, part in enumerate(parts):
         kernel_ref[a * 9 * GC : (a + 1) * 9 * GC, :] = part[0 : 9 * GC, 0:CH]
     bias_ref[...] = turned[9 * GC : 9 * GC + 1, 0:CH]
 
@@ -458,7 +489,8 @@
 def shards(voxels, kernel, bias, cortex, slot_to_brick, neighbors, cotangent):
     slots = voxels.shape[0]
     devices = lax.axis_size("bricks")
-    strips, spread, ends, shifts = (jnp.asarray(t, BF) for t in tables())
+    strips, spread, ends, shifts, fold = (jnp.asarray(t, BF) for t in tables())
+    fold = fold.astype(F32)
     shape = jax.ShapeDtypeStruct
     pack_rows = slots * 2 * CH + HEAD
     near_shape = shape(((NEAR + EDGE) * CH + HEAD, TILE), BF)
@@ -480,7 +512,7 @@
         pltpu.VMEM((2 * slots + 2 * NEAR + 2 * EDGE + 1, CH, TILE), BF),
         pltpu.VMEM((2 * slots + 2 * EDGE, CH, TILE), BF),
         pltpu.VMEM((5 * CH, 2 * TILE), BF),
-        pltpu.VMEM((9 * CH + HEAD, 5 * TILE), BF),
+        pltpu.VMEM((PARTS, 10 * PART, 5 * TILE), BF),
         pltpu.VMEM((3 * CH, 5 * TILE), F32),
         pltpu.SMEM(slot_to_brick.shape, jnp.int32),
         pltpu.SMEM(neighbors.shape, jnp.int32),
@@ -496,10 +528,10 @@
         limit=60,
     )(slot_to_brick, voxels, strips)
     mate = swapped(own, 1)
-    weight_shape = shape((3 * CH, 9 * CH), BF)
+    weight_shape = shape((PARTS, 3 * PART, 9 * PART), BF)
     taps = jnp.transpose(kernel, (2, 3, 4, 1, 0)).reshape(27 * GC, CH)
     staged = call(
-        weight_kernel, [VMEM], [weight_shape] * 2, [pltpu.VMEM((640, 256), F32)], flops=BUSY
+        weight_kernel, [VMEM], [weight_shape] * 2, [pltpu.VMEM((2 * TILE, 3 * TILE), F32)], flops=BUSY
     )(taps)
     near, far = call(
         functools.partial(route_kernel, slots), [VMEM, VMEM], [near_shape, far_shape], box,
@@ -511,18 +543,18 @@
     received = (near, swapped(near, 1), far, swapped(far, 1))
     activated, dpre, own = call(
         forward_kernel,
-        [HBM, HBM] + [VMEM] * 15,
+        [HBM, HBM] + [VMEM] * 16,
         [field, field, shape((pack_rows + 2 * SUM_ROWS, TILE), BF)],
         work
         + [
-            pltpu.VMEM((3 * CH, 5 * TILE), BF),
-            pltpu.VMEM((9 * CH + HEAD, 3 * CH), F32),
+            pltpu.VMEM((PARTS, 3 * PART, 5 * TILE), BF),
+            pltpu.VMEM((PARTS, 3 * PART, 10 * PART), F32),
             pltpu.VMEM((slots, 8, 512), F32),
         ],
         flops=4 * 10**9,
     )(
         slot_to_brick, neighbors, voxels, own, mate, *received, forward, bias.reshape(1, CH),
-        cortex, cotangent, strips, spread, ends, shifts,
+        cortex, cotangent, strips, spread, ends, shifts, fold,
     )
     mate = swapped(own, 1)
     near, far, total = call(

time: 57.7 us -> 53.5 us (0.927)
  Pallas kernels: 21.7 us -> 11.4 us
  starting transfers between devices: 23 us -> 30.2 us
  waiting for transfers between devices: 11.9 us -> 10.5 us
    ppermute x14, starting transfers between devices: 23 us -> 30.2 us  [sent(): return lax.ppermute(block, 'bricks', route)]
    pallas_call x2, Pallas kernels: 10.8 us -> 4.53 us  [the longest x1 4.05 us: shards(): call(forward_kernel, [HBM, HBM] + [VMEM] * 16, [field, field, shape((pack...]
    pallas_call x2, Pallas kernels: 7.75 us -> 3.71 us  [half_backward(): call(functools.partial(backward_kernel, part), [HBM, HBM] + [VMEM] * (11...]
    ppermute x14, waiting for transfers between devices: 11.9 us -> 10.5 us  [sent(): return lax.ppermute(block, 'bricks', route)]
  transfers between devices with their start and end apart: 14 -> 14, of which waited for: 7 -> 8; matrix products, arithmetic and copies ran while one was open for 0% -> 0% of each run, Pallas kernels for 14% -> 8%
where the time goes in v2:
time: 53.5 us; the launch traced here: 54.1 us
  starting transfers between devices  30.2 us (56%)
  Pallas kernels  11.4 us (21%)
  waiting for transfers between devices  10.5 us (20%)
  local copies, waits for them, and re-layouts  1.01 us (2%)
  between operations  0.95 us (2%)
    ppermute x14, starting transfers between devices, sent(): return lax.ppermute(block, 'bricks', route)  30.2 us
    ppermute x14, waiting for transfers between devices, sent(): return lax.ppermute(block, 'bricks', route)  10.5 us
    pallas_call x1, Pallas kernels, shards(): call(forward_kernel, [HBM, HBM] + [VMEM] * 16, [field, field, shape((pack...  4.05 us
    pallas_call x2, Pallas kernels, half_backward(): call(functools.partial(backward_kernel, part), [HBM, HBM] + [VMEM] * (11...  3.71 us
    pallas_call x1, Pallas kernels, shards(): call(pack_kernel, [HBM] * 3, [shape((pack_rows, TILE), BF)], [pltpu.VMEM(...  2.15 us
  transfers between devices with their start and end apart: 14, of which 8 were waited for; matrix products, arithmetic and copies ran while one was open for 0% of the time, Pallas kernels for 8%

profile of v2, /device:TPU:0, one launch (start us, length us, event | category | flops | bytes accessed | tf_op | source)
XLA Modules:
  0.0 54.1 jit_solution(17842327476099139221)
XLA Ops:
  0.6 2.2 %shard_map.147.own_ref = bf16[784,128]{1,0:T(8,128)(2,1)} custom-call(s32[6]{0:T(128)} %refs_0_.3, bf16[6,64,512]{2,1,0:T(8,128)(2,1)} %field_ref.1, bf16[4,512,128]{2,1,0:T(8,128)(2,1)} %constant.10.clone.strips_hbm.strips_ref), custom_call_target="tpu_custom_call" | custom-call | bytes 400000 | tf_op jit(solution)/shard_map/pallas_call | solution.py:523
  3.3 1.3 %collective-permute-done.mate_ref = bf16[784,128]{1,0:T(8,128)(2,1)S(1)} collective-permute-done((bf16[784,128]{1,0:T(8,128)(2,1)}, bf16[784,128]{1,0:T(8,128)(2,1)S(1)}, u32[]{:S(2)}, u32[]{:S(2)}) %collective-permute-start) | collective-permute-done | bytes 200736 | tf_op jit(solution)/shard_map/ppermute | solution.py:486
  4.6 0.9 %copy-done.5 = bf16[784,128]{1,0:T(8,128)(2,1)S(1)} copy-done((bf16[784,128]{1,0:T(8,128)(2,1)S(1)}, bf16[784,128]{1,0:T(8,128)(2,1)}, u32[]{:S(2)}) %copy-start.5) | copy-done | bytes 200728
  5.7 0.7 %collective-permute-start.1 = (bf16[656,128]{1,0:T(8,128)(2,1)S(1)}, bf16[656,128]{1,0:T(8,128)(2,1)S(1)}, u32[]{:S(2)}, u32[]{:S(2)}) collective-permute-start(bf16[656,128]{1,0:T(8,128)(2,1)S(1)} %get-tuple-element.37), channel_id=1, source_target_pairs={{1,2},{2,1},{3,4},{4,3},{5,6},{6,5},{7,8},{8,7},{9,10},{10,9},{11,... | collective-permute-start | bytes 503816 | tf_op jit(solution)/shard_map/ppermute | solution.py:486
  6.4 0.7 %collective-permute-start.2 = (bf16[192,128]{1,0:T(8,128)(2,1)S(1)}, bf16[192,128]{1,0:T(8,128)(2,1)S(1)}, u32[]{:S(2)}, u32[]{:S(2)}) collective-permute-start(bf16[192,128]{1,0:T(8,128)(2,1)S(1)} %get-tuple-element.38), channel_id=1, source_target_pairs={{1,4},{3,6},{4,1},{5,8},{6,3},{7,10},{8,5},{9,12},{10,7},{11,14},{... | collective-permute-start | bytes 147464 | tf_op jit(solution)/shard_map/ppermute | solution.py:486
  7.7 8.3 %collective-permute-start.3 = (bf16[656,128]{1,0:T(8,128)(2,1)S(1)}, bf16[656,128]{1,0:T(8,128)(2,1)S(1)}, u32[]{:S(2)}, u32[]{:S(2)}) collective-permute-start(bf16[656,128]{1,0:T(8,128)(2,1)S(1)} %collective-permute-done.1.first_ref), channel_id=1, source_target_pairs={{0,1},{1,0},{2,3},{3,2},{4,5},{5,4},{6,7},{7,6},{8,9},{9,8},{10,11... | collective-permute-start | bytes 503816 | tf_op jit(solution)/shard_map/ppermute | solution.py:486
  16.0 1.2 %collective-permute-done.4.second_far_ref = bf16[192,128]{1,0:T(8,128)(2,1)S(1)} collective-permute-done((bf16[192,128]{1,0:T(8,128)(2,1)S(1)}, bf16[192,128]{1,0:T(8,128)(2,1)S(1)}, u32[]{:S(2)}, u32[]{:S(2)}) %collective-permute-start.4) | collective-permute-done | bytes 49184 | tf_op jit(solution)/shard_map/ppermute | solution.py:486
  17.4 4.0 %shard_map.150 = (bf16[6,64,512]{2,1,0:T(8,128)(2,1)}, bf16[6,64,512]{2,1,0:T(8,128)(2,1)S(1)}, bf16[1040,128]{1,0:T(8,128)(2,1)S(1)}) custom-call(s32[6]{0:T(128)S(1)} %copy-done.8, s32[6,6]{1,0:T(8,128)S(1)} %copy-done.7, bf16[6,64,512]{2,1,0:T(8,128)(2,1)S(1)} %copy-done.4, bf16[784,128]{1,0:T(8,128)(2,1)S(1)} %copy-done.6, ...), custom_call_target="tpu_custom_call" | custom-call | flops 4000000000 | bytes 400000 | tf_op jit(solution)/shard_map/pallas_call | solution.py:544
  21.4 5.0 %collective-permute-start.5 = (bf16[1040,128]{1,0:T(8,128)(2,1)S(1)}, bf16[1040,128]{1,0:T(8,128)(2,1)S(1)}, u32[]{:S(2)}, u32[]{:S(2)}) collective-permute-start(bf16[1040,128]{1,0:T(8,128)(2,1)S(1)} %get-tuple-element.46.own_ref.refs_3_), channel_id=1, source_target_pairs={{0,1},{1,0},{2,3},{3,2},{4,5},{5,4},{6,7},{7,6},{8,9},{9,8},{10,11... | collective-permute-start | bytes 798728 | tf_op jit(solution)/shard_map/ppermute | solution.py:486
  26.4 1.2 %collective-permute-done.5.mate_ref.refs_4_ = bf16[1040,128]{1,0:T(8,128)(2,1)S(1)} collective-permute-done((bf16[1040,128]{1,0:T(8,128)(2,1)S(1)}, bf16[1040,128]{1,0:T(8,128)(2,1)S(1)}, u32[]{:S(2)}, u32[]{:S(2)}) %collective-permute-start.5) | collective-permute-done | bytes 266272 | tf_op jit(solution)/shard_map/ppermute | solution.py:486
  27.7 0.7 %collective-permute-start.8 = (bf16[656,128]{1,0:T(8,128)(2,1)S(1)}, bf16[656,128]{1,0:T(8,128)(2,1)S(1)}, u32[]{:S(2)}, u32[]{:S(2)}) collective-permute-start(bf16[656,128]{1,0:T(8,128)(2,1)S(1)} %get-tuple-element.49), channel_id=1, source_target_pairs={{1,2},{2,1},{3,4},{4,3},{5,6},{6,5},{7,8},{8,7},{9,10},{10,9},{11,... | collective-permute-start | bytes 503816 | tf_op jit(solution)/shard_map/ppermute | solution.py:486
  28.4 3.3 %collective-permute-start.6 = (f32[128,128]{1,0:T(8,128)S(1)}, f32[128,128]{1,0:T(8,128)S(1)}, u32[]{:S(2)}, u32[]{:S(2)}) collective-permute-start(f32[128,128]{1,0:T(8,128)S(1)} %get-tuple-element.50), channel_id=1, source_target_pairs={{0,2},{1,3},{2,0},{3,1},{4,6},{5,7},{6,4},{7,5},{8,10},{9,11},{10,... | collective-permute-start | bytes 196616 | tf_op jit(solution)/shard_map/ppermute | solution.py:486
  31.7 0.7 %collective-permute-start.7 = (bf16[192,128]{1,0:T(8,128)(2,1)S(1)}, bf16[192,128]{1,0:T(8,128)(2,1)S(1)}, u32[]{:S(2)}, u32[]{:S(2)}) collective-permute-start(bf16[192,128]{1,0:T(8,128)(2,1)S(1)} %get-tuple-element.48), channel_id=1, source_target_pairs={{1,4},{3,6},{4,1},{5,8},{6,3},{7,10},{8,5},{9,12},{10,7},{11,14},{... | collective-permute-start | bytes 147464 | tf_op jit(solution)/shard_map/ppermute | solution.py:486
  32.4 3.5 %collective-permute-done.6 = f32[128,128]{1,0:T(8,128)S(1)} collective-permute-done((f32[128,128]{1,0:T(8,128)S(1)}, f32[128,128]{1,0:T(8,128)S(1)}, u32[]{:S(2)}, u32[]{:S(2)}) %collective-permute-start.6) | collective-permute-done | bytes 65568 | tf_op jit(solution)/shard_map/ppermute | solution.py:486
  35.9 1.7 %collective-permute-start.10 = (bf16[656,128]{1,0:T(8,128)(2,1)S(1)}, bf16[656,128]{1,0:T(8,128)(2,1)S(1)}, u32[]{:S(2)}, u32[]{:S(2)}) collective-permute-start(bf16[656,128]{1,0:T(8,128)(2,1)S(1)} %collective-permute-done.8.refs_5_), channel_id=1, source_target_pairs={{0,1},{1,0},{2,3},{3,2},{4,5},{5,4},{6,7},{7,6},{8,9},{9,8},{10,11... | collective-permute-start | bytes 503816 | tf_op jit(solution)/shard_map/ppermute | solution.py:486
  37.6 2.7 %collective-permute-start.9 = (f32[128,128]{1,0:T(8,128)S(1)}, f32[128,128]{1,0:T(8,128)S(1)}, u32[]{:S(2)}, u32[]{:S(2)}) collective-permute-start(f32[128,128]{1,0:T(8,128)S(1)} %add.9), channel_id=1, source_target_pairs={{0,4},{1,5},{2,6},{3,7},{4,0},{5,1},{6,2},{7,3},{8,12},{9,13},{10,... | collective-permute-start | bytes 196616 | tf_op jit(solution)/shard_map/ppermute | solution.py:486
  40.3 1.2 %collective-permute-done.11.refs_8_ = bf16[192,128]{1,0:T(8,128)(2,1)S(1)} collective-permute-done((bf16[192,128]{1,0:T(8,128)(2,1)S(1)}, bf16[192,128]{1,0:T(8,128)(2,1)S(1)}, u32[]{:S(2)}, u32[]{:S(2)}) %collective-permute-start.11) | collective-permute-done | bytes 49184 | tf_op jit(solution)/shard_map/ppermute | solution.py:486
  41.5 1.0 %collective-permute-done.9 = f32[128,128]{1,0:T(8,128)S(1)} collective-permute-done((f32[128,128]{1,0:T(8,128)S(1)}, f32[128,128]{1,0:T(8,128)S(1)}, u32[]{:S(2)}, u32[]{:S(2)}) %collective-permute-start.9) | collective-permute-done | bytes 65568 | tf_op jit(solution)/shard_map/ppermute | solution.py:486
  42.6 2.8 %collective-permute-start.12 = (f32[128,128]{1,0:T(8,128)S(1)}, f32[128,128]{1,0:T(8,128)S(1)}, u32[]{:S(2)}, u32[]{:S(2)}) collective-permute-start(f32[128,128]{1,0:T(8,128)S(1)} %add.10), channel_id=1, source_target_pairs={{0,8},{1,9},{2,10},{3,11},{4,12},{5,13},{6,14},{7,15},{8,0},{9,1},... | collective-permute-start | bytes 196616 | tf_op jit(solution)/shard_map/ppermute | solution.py:486
  45.4 1.4 %shard_map.152.refs_13_ = bf16[6,64,512]{2,1,0:T(8,128)(2,1)S(1)} custom-call(s32[6]{0:T(128)S(1)} %copy-done.8, s32[6,6]{1,0:T(8,128)S(1)} %copy-done.7, bf16[6,64,512]{2,1,0:T(8,128)(2,1)S(1)} %get-tuple-element.45.refs_2_, bf16[1040,128]{1,0:T(8,128)(2,1)S(1)} %get-tuple-element.46.own_ref.refs_3_, ...), custom_call_target="tpu_custom_call" | custom-call | flops 1000000000 | bytes 400000 | tf_op jit(solution)/shard_map/pallas_call | solution.py:577
  46.8 0.8 %collective-permute-done.12 = f32[128,128]{1,0:T(8,128)S(1)} collective-permute-done((f32[128,128]{1,0:T(8,128)S(1)}, f32[128,128]{1,0:T(8,128)S(1)}, u32[]{:S(2)}, u32[]{:S(2)}) %collective-permute-start.12) | collective-permute-done | bytes 65568 | tf_op jit(solution)/shard_map/ppermute | solution.py:486
  47.7 3.2 %collective-permute-start.13 = (f32[128,128]{1,0:T(8,128)S(1)}, f32[128,128]{1,0:T(8,128)S(1)}, u32[]{:S(2)}, u32[]{:S(2)}) collective-permute-start(f32[128,128]{1,0:T(8,128)S(1)} %add.11.a_ref), channel_id=1, source_target_pairs={{0,16},{1,17},{2,18},{3,19},{4,20},{5,21},{6,22},{7,23},{8,24},{9,... | collective-permute-start | bytes 196616 | tf_op jit(solution)/shard_map/ppermute | solution.py:486
  50.9 2.3 %shard_map.153 = bf16[6,64,512]{2,1,0:T(8,128)(2,1)} custom-call(s32[6]{0:T(128)S(1)} %copy-done.8, s32[6,6]{1,0:T(8,128)S(1)} %copy-done.7, bf16[6,64,512]{2,1,0:T(8,128)(2,1)S(1)} %get-tuple-element.45.refs_2_, bf16[1040,128]{1,0:T(8,128)(2,1)S(1)} %get-tuple-element.46.own_ref.refs_3_, bf16[1040,128]{1,0:T(8,128)(2,1)S(1)} %collective-permute-done.5.mate_ref.refs_4_, ...), custom_call_target="tpu_custom_call" | custom-call | flops 1000000000 | bytes 400000 | tf_op jit(solution)/shard_map/pallas_call | solution.py:577
  53.3 0.7 %shard_map.154 = (f32[216,64]{1,0:T(8,128)}, f32[1,64]{1,0:T(1,128)}) custom-call(f32[128,128]{1,0:T(8,128)S(1)} %add.11.a_ref, f32[128,128]{1,0:T(8,128)S(1)} %collective-permute-done.13.b_ref), custom_call_target="tpu_custom_call" | custom-call | bytes 400000 | tf_op jit(solution)/shard_map/pallas_call | solution.py:600
  (43 shorter events, 1.6 us)
Async XLA Ops:
  2.8 1.8 %collective-permute-start = (bf16[784,128]{1,0:T(8,128)(2,1)}, bf16[784,128]{1,0:T(8,128)(2,1)S(1)}, u32[]{:S(2)}, u32[]{:S(2)}) collective-permute-start(bf16[784,128]{1,0:T(8,128)(2,1)} %shard_map.147.own_ref), channel_id=1, source_target_pairs={{0,1},{1,0},{2,3},{3,2},{4,5},{5,4},{6,7},{7,6},{8,9},{9,8},{10,11... | collective-permute-start | bytes 602120 | tf_op jit(solution)/shard_map/ppermute | solution.py:486
  5.7 2.0 %collective-permute-start.1 = (bf16[656,128]{1,0:T(8,128)(2,1)S(1)}, bf16[656,128]{1,0:T(8,128)(2,1)S(1)}, u32[]{:S(2)}, u32[]{:S(2)}) collective-permute-start(bf16[656,128]{1,0:T(8,128)(2,1)S(1)} %get-tuple-element.37), channel_id=1, source_target_pairs={{1,2},{2,1},{3,4},{4,3},{5,6},{6,5},{7,8},{8,7},{9,10},{10,9},{11,... | collective-permute-start | bytes 503816 | tf_op jit(solution)/shard_map/ppermute | solution.py:486
  6.4 1.3 %collective-permute-start.2 = (bf16[192,128]{1,0:T(8,128)(2,1)S(1)}, bf16[192,128]{1,0:T(8,128)(2,1)S(1)}, u32[]{:S(2)}, u32[]{:S(2)}) collective-permute-start(bf16[192,128]{1,0:T(8,128)(2,1)S(1)} %get-tuple-element.38), channel_id=1, source_target_pairs={{1,4},{3,6},{4,1},{5,8},{6,3},{7,10},{8,5},{9,12},{10,7},{11,14},{... | collective-permute-start | bytes 147464 | tf_op jit(solution)/shard_map/ppermute | solution.py:486
  7.1 10.2 %copy-start = (bf16[4,256,1024]{2,1,0:T(8,128)(2,1)S(1)}, bf16[4,256,1024]{2,1,0:T(8,128)(2,1)}, u32[]{:S(2)}) copy-start(bf16[4,256,1024]{2,1,0:T(8,128)(2,1)} %constant.13.clone.shifts_ref.refs_12_) | copy-start | bytes 6291460
  7.1 10.2 %copy-start.1 = (bf16[4,384,128]{2,1,0:T(8,128)(2,1)S(1)}, bf16[4,384,128]{2,1,0:T(8,128)(2,1)}, u32[]{:S(2)}) copy-start(bf16[4,384,128]{2,1,0:T(8,128)(2,1)} %constant.12.clone.ends_ref.refs_11_) | copy-start | bytes 1179652
  7.1 10.2 %copy-start.2 = (bf16[256,512]{1,0:T(8,128)(2,1)S(1)}, bf16[256,512]{1,0:T(8,128)(2,1)}, u32[]{:S(2)}) copy-start(bf16[256,512]{1,0:T(8,128)(2,1)} %constant.11.clone.spread_ref.refs_10_) | copy-start | bytes 786436
  7.1 10.2 %copy-start.3 = (bf16[4,512,128]{2,1,0:T(8,128)(2,1)S(1)}, bf16[4,512,128]{2,1,0:T(8,128)(2,1)}, u32[]{:S(2)}) copy-start(bf16[4,512,128]{2,1,0:T(8,128)(2,1)} %constant.10.clone.strips_hbm.strips_ref) | copy-start | bytes 1572868
  7.1 10.2 %copy-start.4 = (bf16[6,64,512]{2,1,0:T(8,128)(2,1)S(1)}, bf16[6,64,512]{2,1,0:T(8,128)(2,1)}, u32[]{:S(2)}) copy-start(bf16[6,64,512]{2,1,0:T(8,128)(2,1)} %field_ref.1) | copy-start | bytes 1179652
  7.1 10.2 %copy-start.6 = (bf16[784,128]{1,0:T(8,128)(2,1)S(1)}, bf16[784,128]{1,0:T(8,128)(2,1)}, u32[]{:S(2)}) copy-start(bf16[784,128]{1,0:T(8,128)(2,1)} %shard_map.147.own_ref) | copy-start | bytes 602116
  7.1 10.2 %copy-start.7 = (s32[6,6]{1,0:T(8,128)S(1)}, s32[6,6]{1,0:T(8,128)}, u32[]{:S(2)}) copy-start(s32[6,6]{1,0:T(8,128)} %refs_1_.3) | copy-start | bytes 436
  7.1 10.2 %copy-start.8 = (s32[6]{0:T(128)S(1)}, s32[6]{0:T(128)}, u32[]{:S(2)}) copy-start(s32[6]{0:T(128)} %refs_0_.3) | copy-start | bytes 76
  7.2 10.2 %copy-start.9 = (bf16[6,64,512]{2,1,0:T(8,128)(2,1)S(1)}, bf16[6,64,512]{2,1,0:T(8,128)(2,1)}, u32[]{:S(2)}) copy-start(bf16[6,64,512]{2,1,0:T(8,128)(2,1)} %upstream_ref.1) | copy-start | bytes 1179652
  7.2 10.1 %copy-start.11 = (s32[6,512]{1,0:T(8,128)S(1)}, s32[6,512]{1,0:T(8,128)}, u32[]{:S(2)}) copy-start(s32[6,512]{1,0:T(8,128)} %cortex_ref.1) | copy-start | bytes 36868
  7.7 9.5 %collective-permute-start.3 = (bf16[656,128]{1,0:T(8,128)(2,1)S(1)}, bf16[656,128]{1,0:T(8,128)(2,1)S(1)}, u32[]{:S(2)}, u32[]{:S(2)}) collective-permute-start(bf16[656,128]{1,0:T(8,128)(2,1)S(1)} %collective-permute-done.1.first_ref), channel_id=1, source_target_pairs={{0,1},{1,0},{2,3},{3,2},{4,5},{5,4},{6,7},{7,6},{8,9},{9,8},{10,11... | collective-permute-start | bytes 503816 | tf_op jit(solution)/shard_map/ppermute | solution.py:486
  16.0 1.2 %collective-permute-start.4 = (bf16[192,128]{1,0:T(8,128)(2,1)S(1)}, bf16[192,128]{1,0:T(8,128)(2,1)S(1)}, u32[]{:S(2)}, u32[]{:S(2)}) collective-permute-start(bf16[192,128]{1,0:T(8,128)(2,1)S(1)} %collective-permute-done.2.first_far_ref), channel_id=1, source_target_pairs={{0,1},{1,0},{2,3},{3,2},{4,5},{5,4},{6,7},{7,6},{8,9},{9,8},{10,11... | collective-permute-start | bytes 147464 | tf_op jit(solution)/shard_map/ppermute | solution.py:486
  21.4 6.2 %collective-permute-start.5 = (bf16[1040,128]{1,0:T(8,128)(2,1)S(1)}, bf16[1040,128]{1,0:T(8,128)(2,1)S(1)}, u32[]{:S(2)}, u32[]{:S(2)}) collective-permute-start(bf16[1040,128]{1,0:T(8,128)(2,1)S(1)} %get-tuple-element.46.own_ref.refs_3_), channel_id=1, source_target_pairs={{0,1},{1,0},{2,3},{3,2},{4,5},{5,4},{6,7},{7,6},{8,9},{9,8},{10,11... | collective-permute-start | bytes 798728 | tf_op jit(solution)/shard_map/ppermute | solution.py:486
  27.7 8.2 %collective-permute-start.8 = (bf16[656,128]{1,0:T(8,128)(2,1)S(1)}, bf16[656,128]{1,0:T(8,128)(2,1)S(1)}, u32[]{:S(2)}, u32[]{:S(2)}) collective-permute-start(bf16[656,128]{1,0:T(8,128)(2,1)S(1)} %get-tuple-element.49), channel_id=1, source_target_pairs={{1,2},{2,1},{3,4},{4,3},{5,6},{6,5},{7,8},{8,7},{9,10},{10,9},{11,... | collective-permute-start | bytes 503816 | tf_op jit(solution)/shard_map/ppermute | solution.py:486
  28.4 7.5 %collective-permute-start.6 = (f32[128,128]{1,0:T(8,128)S(1)}, f32[128,128]{1,0:T(8,128)S(1)}, u32[]{:S(2)}, u32[]{:S(2)}) collective-permute-start(f32[128,128]{1,0:T(8,128)S(1)} %get-tuple-element.50), channel_id=1, source_target_pairs={{0,2},{1,3},{2,0},{3,1},{4,6},{5,7},{6,4},{7,5},{8,10},{9,11},{10,... | collective-permute-start | bytes 196616 | tf_op jit(solution)/shard_map/ppermute | solution.py:486
  31.7 0.7 %collective-permute-start.7 = (bf16[192,128]{1,0:T(8,128)(2,1)S(1)}, bf16[192,128]{1,0:T(8,128)(2,1)S(1)}, u32[]{:S(2)}, u32[]{:S(2)}) collective-permute-start(bf16[192,128]{1,0:T(8,128)(2,1)S(1)} %get-tuple-element.48), channel_id=1, source_target_pairs={{1,4},{3,6},{4,1},{5,8},{6,3},{7,10},{8,5},{9,12},{10,7},{11,14},{... | collective-permute-start | bytes 147464 | tf_op jit(solution)/shard_map/ppermute | solution.py:486
  35.9 6.7 %collective-permute-start.10 = (bf16[656,128]{1,0:T(8,128)(2,1)S(1)}, bf16[656,128]{1,0:T(8,128)(2,1)S(1)}, u32[]{:S(2)}, u32[]{:S(2)}) collective-permute-start(bf16[656,128]{1,0:T(8,128)(2,1)S(1)} %collective-permute-done.8.refs_5_), channel_id=1, source_target_pairs={{0,1},{1,0},{2,3},{3,2},{4,5},{5,4},{6,7},{7,6},{8,9},{9,8},{10,11... | collective-permute-start | bytes 503816 | tf_op jit(solution)/shard_map/ppermute | solution.py:486
  37.6 5.0 %collective-permute-start.9 = (f32[128,128]{1,0:T(8,128)S(1)}, f32[128,128]{1,0:T(8,128)S(1)}, u32[]{:S(2)}, u32[]{:S(2)}) collective-permute-start(f32[128,128]{1,0:T(8,128)S(1)} %add.9), channel_id=1, source_target_pairs={{0,4},{1,5},{2,6},{3,7},{4,0},{5,1},{6,2},{7,3},{8,12},{9,13},{10,... | collective-permute-start | bytes 196616 | tf_op jit(solution)/shard_map/ppermute | solution.py:486
  40.3 1.2 %collective-permute-start.11 = (bf16[192,128]{1,0:T(8,128)(2,1)S(1)}, bf16[192,128]{1,0:T(8,128)(2,1)S(1)}, u32[]{:S(2)}, u32[]{:S(2)}) collective-permute-start(bf16[192,128]{1,0:T(8,128)(2,1)S(1)} %collective-permute-done.7.refs_7_), channel_id=1, source_target_pairs={{0,1},{1,0},{2,3},{3,2},{4,5},{5,4},{6,7},{7,6},{8,9},{9,8},{10,11... | collective-permute-start | bytes 147464 | tf_op jit(solution)/shard_map/ppermute | solution.py:486
  42.6 5.1 %collective-permute-start.12 = (f32[128,128]{1,0:T(8,128)S(1)}, f32[128,128]{1,0:T(8,128)S(1)}, u32[]{:S(2)}, u32[]{:S(2)}) collective-permute-start(f32[128,128]{1,0:T(8,128)S(1)} %add.10), channel_id=1, source_target_pairs={{0,8},{1,9},{2,10},{3,11},{4,12},{5,13},{6,14},{7,15},{8,0},{9,1},... | collective-permute-start | bytes 196616 | tf_op jit(solution)/shard_map/ppermute | solution.py:486
  47.7 5.7 %collective-permute-start.13 = (f32[128,128]{1,0:T(8,128)S(1)}, f32[128,128]{1,0:T(8,128)S(1)}, u32[]{:S(2)}, u32[]{:S(2)}) collective-permute-start(f32[128,128]{1,0:T(8,128)S(1)} %add.11.a_ref), channel_id=1, source_target_pairs={{0,16},{1,17},{2,18},{3,19},{4,20},{5,21},{6,22},{7,23},{8,24},{9,... | collective-permute-start | bytes 196616 | tf_op jit(solution)/shard_map/ppermute | solution.py:486
  (4 other events, 27.6 us)

commit v3 on v2

--- a/solution.py
+++ b/solution.py
@@ -258,89 +258,96 @@
     return base, mine, find_strip, find_plane
 
 
-def put_taps(taps, bc, values):
-    for i in range(5):
-        for p in range(PARTS):
-            taps[p, bc * PART : (bc + 1) * PART, i * TILE : (i + 1) * TILE] = values[
-                i * CH + p * PART : i * CH + (p + 1) * PART, :
-            ]
-
-
-def convolve_brick(
-    s, base, find_strip, find_plane, link_ref, field_ref, planes, strips,
+def convolve_pair(
+    pair, base, find_strip, find_plane, link_ref, field_ref, planes, strips,
     spread_ref, ends_ref, shifts_ref, weight_ref, mixed, taps, sums,
 ):
-    brick = base + s
-    kind = brick & 3
-    step_y = 2 - 2 * (kind & 2)
-    step_z = 1 - 2 * (kind & 1)
-    sides = (brick + step_y, brick + step_z, brick + step_y + step_z)
-    has_low = link_ref[s, 0] >= 0
-    has_high = link_ref[s, 1] >= 0
-
-    def outer(near):
-        high = planes[find_plane(near + 4, has_high)]
-        low = planes[find_plane(near - 4, has_low)]
-        return join_halves(high, low)
-
-    beside_y, beside_z, beside_yz = [strips[find_strip(m)] for m in sides]
+    slots = (2 * pair, 2 * pair + 1)
+    kinds, outers, besides = [], [], []
     of_y = lax.broadcasted_iota(jnp.int32, (CH, TILE), 1) % 64 < 32
-    beside = jnp.where(of_y, beside_y.astype(F32), beside_z.astype(F32)).astype(BF)
-    beside = jnp.concatenate([beside, beside_yz], axis=1)
-    halo = dot(beside, spread_ref[...]).astype(BF)
-    outer_beside = jnp.concatenate([outer(m) for m in sides], axis=1)
-    for i in range(4):
-        rows = slice(i * CH, (i + 1) * CH)
-        mixed[rows, 0:TILE] = field_ref[s, :, i * TILE : (i + 1) * TILE]
-        mixed[rows, TILE:] = halo[:, i * TILE : (i + 1) * TILE]
-    mixed[4 * CH :, 0:TILE] = outer(brick)
-    mixed[4 * CH :, TILE:] = dot(outer_beside, ends_ref[kind]).astype(BF)
-    for k in range(0, 8, 2):
-        part = dot(mixed[...], shifts_ref[kind, :, k * TILE : (k + 2) * TILE]).astype(BF)
-        for e in range(2):
-            put_taps(taps, SIDES[k + e], part[:, e * TILE : (e + 1) * TILE])
-    put_taps(taps, 4, mixed[:, 0:TILE])
+    for s in slots:
+        brick = base + s
+        kind = brick & 3
+        step_y = 2 - 2 * (kind & 2)
+        step_z = 1 - 2 * (kind & 1)
+        sides = (brick + step_y, brick + step_z, brick + step_y + step_z)
+        has_low = link_ref[s, 0] >= 0
+        has_high = link_ref[s, 1] >= 0
+
+        def outer(near):
+            high = planes[find_plane(near + 4, has_high)]
+            low = planes[find_plane(near - 4, has_low)]
+            return join_halves(high, low)
+
+        beside_y, beside_z, beside_yz = [strips[find_strip(m)] for m in sides]
+        beside = jnp.where(of_y, beside_y.astype(F32), beside_z.astype(F32)).astype(BF)
+        besides.append(jnp.concatenate([beside, beside_yz], axis=1))
+        kinds.append(kind)
+        outers.append((outer(brick), jnp.concatenate([outer(m) for m in sides], axis=1)))
+    halos = dot(jnp.concatenate(besides, axis=0), spread_ref[...]).astype(BF)
+    for e, s in enumerate(slots):
+        for i in range(4):
+            rows = slice(i * CH, (i + 1) * CH)
+            mixed[e, rows, 0:TILE] = field_ref[s, :, i * TILE : (i + 1) * TILE]
+            mixed[e, rows, TILE:] = halos[e * CH : (e + 1) * CH, i * TILE : (i + 1) * TILE]
+        mixed[e, 4 * CH :, 0:TILE] = outers[e][0]
+        mixed[e, 4 * CH :, TILE:] = dot(outers[e][1], ends_ref[kinds[e]]).astype(BF)
+
+    def put_taps(e, bc, values):
+        for i in range(5):
+            lanes = slice((5 * e + i) * TILE, (5 * e + i + 1) * TILE)
+            for p in range(PARTS):
+                taps[p, bc * PART : (bc + 1) * PART, lanes] = values[
+                    i * CH + p * PART : i * CH + (p + 1) * PART, :
+                ]
+
+    for e in range(2):
+        for k in range(0, 8, 2):
+            part = dot(mixed[e], shifts_ref[kinds[e], :, k * TILE : (k + 2) * TILE]).astype(BF)
+            put_taps(e, SIDES[k], part[:, 0:TILE])
+            put_taps(e, SIDES[k + 1], part[:, TILE:])
+        put_taps(e, 4, mixed[e, :, 0:TILE])
     for p in range(PARTS):
         part = dot(weight_ref[p], taps[p, 0 : 9 * PART, :])
         for a in range(3):
             at = a * CH + p * PART
             sums[at : at + PART, :] = part[a * PART : (a + 1) * PART, :]
-    turned = []
-    for a in (0, 2):
-        rows = slice(a * CH, (a + 1) * CH)
-        turned.append(
-            [pltpu.roll(sums[rows, i * TILE : (i + 1) * TILE], 64, 1) for i in range(5)]
-        )
     left = left_half((CH, TILE))
-    tiles = []
-    for i in range(4):
-        lower = jnp.where(left, turned[0][(i - 1) % 5], turned[0][i])
-        upper = jnp.where(left, turned[1][i], turned[1][i + 1])
-        tiles.append(sums[CH : 2 * CH, i * TILE : (i + 1) * TILE] + lower + upper)
-    return tiles
+    results = []
+    for e in range(2):
+        first = 5 * e
+        turned = []
+        for a in (0, 2):
+            rows = slice(a * CH, (a + 1) * CH)
+            turned.append(
+                [
+                    pltpu.roll(sums[rows, (first + i) * TILE : (first + i + 1) * TILE], 64, 1)
+                    for i in range(5)
+                ]
+            )
+        tiles = []
+        for i in range(4):
+            lower = jnp.where(left, turned[0][(i - 1) % 5], turned[0][i])
+            upper = jnp.where(left, turned[1][i], turned[1][i + 1])
+            lanes = slice((first + i) * TILE, (first + i + 1) * TILE)
+            tiles.append(sums[CH : 2 * CH, lanes] + lower + upper)
+        results.append(tiles)
+    return results
 
 
 def forward_kernel(
     slot_hbm, link_hbm, field_ref, own_ref, mate_ref, first_ref, second_ref, first_far_ref,
     second_far_ref, weight_ref, bias_ref, cortex_ref, upstream_ref, strips_ref, spread_ref,
     ends_ref, shifts_ref, fold_ref, out_ref, dpre_ref, msg_ref,
-    planes, strips, mixed, taps, sums, slot_ref, link_ref, sems, spots, grads, keeps,
+    planes, strips, mixed, taps, sums, slot_ref, link_ref, sems, spots, grads,
 ):
     slots = field_ref.shape[0]
     base, mine, find_strip, find_plane = make_finder(
         slot_hbm, link_hbm, own_ref, mate_ref, first_ref, second_ref, first_far_ref, second_far_ref,
         planes, strips, slot_ref, link_ref, sems,
     )
-    for s in range(slots):
-        keeps[s] = jnp.broadcast_to(cortex_ref[s : s + 1, :].astype(F32), (8, 512))
-    taps[:, 9 * PART :, :] = jnp.ones((PARTS, PART, 5 * TILE), BF)
-    grads[...] = jnp.zeros_like(grads)
-    for s in range(slots):
-
-        @pl.when(s >= mine)
-        def _():
-            out_ref[s] = jnp.zeros((CH, 512), BF)
-            dpre_ref[s] = jnp.zeros((CH, 512), BF)
+    for pair in range(slots // 2):
+        taps[pair, :, 9 * PART :, :] = jnp.ones((PARTS, PART, 10 * TILE), BF)
 
     square = (CH, CH)
     diagonal = lax.broadcasted_iota(jnp.int32, square, 0) == lax.broadcasted_iota(jnp.int32, square, 1)
@@ -348,44 +355,46 @@
     left = left_half((CH, TILE))
     zero = jnp.zeros((CH, TILE), F32)
 
-    def put_spots(a, i, values):
+    def put_spots(pair, a, i, values):
         for p in range(PARTS):
-            spots[p, a * PART : (a + 1) * PART, i * TILE : (i + 1) * TILE] = values[
+            spots[pair, p, a * PART : (a + 1) * PART, i * TILE : (i + 1) * TILE] = values[
                 p * PART : (p + 1) * PART, :
             ]
 
-    def one_brick(s, carry):
-        tiles = convolve_brick(
-            s, base, find_strip, find_plane, link_ref, field_ref, planes, strips,
-            spread_ref, ends_ref, shifts_ref, weight_ref, mixed, taps, sums,
+    for pair in range(slots // 2):
+        results = convolve_pair(
+            pair, base, find_strip, find_plane, link_ref, field_ref, planes, strips,
+            spread_ref, ends_ref, shifts_ref, weight_ref, mixed.at[pair], taps.at[pair], sums.at[pair],
         )
-        turned = []
-        for i in range(4):
-            lanes = slice(i * TILE, (i + 1) * TILE)
-            pre = tiles[i] + bias
-            keep = keeps[s, 0:1, lanes]
-            sigma = 1.0 / (1.0 + jnp.exp(-pre))
-            out_ref[s, :, lanes] = (pre * sigma * keep).astype(BF)
-            slope = sigma * (1.0 + pre * (1.0 - sigma))
-            dpre = (upstream_ref[s, :, lanes].astype(F32) * keep * slope).astype(BF)
-            dpre_ref[s, :, lanes] = dpre
-            put_spots(1, i, dpre)
-            turned.append(pltpu.roll(dpre.astype(F32), 64, 1))
-        put_spots(1, 4, zero.astype(BF))
-        turned.append(zero)
-        for i in range(4):
-            put_spots(0, i, jnp.where(left, turned[i], turned[i + 1]).astype(BF))
-            before = turned[i - 1] if i else zero
-            put_spots(2, i, jnp.where(left, before, turned[i]).astype(BF))
-        put_spots(0, 4, jnp.where(left, 0.0, turned[0]).astype(BF))
-        put_spots(2, 4, jnp.where(left, turned[3], 0.0).astype(BF))
+        for e, tiles in enumerate(results):
+            s = 2 * pair + e
+            present = jnp.where(s < mine, 1.0, 0.0)
+            turned = []
+            for i in range(4):
+                lanes = slice(i * TILE, (i + 1) * TILE)
+                pre = tiles[i] + bias
+                keep = cortex_ref[s : s + 1, lanes].astype(F32) * present
+                sigma = 1.0 / (1.0 + jnp.exp(-pre))
+                out_ref[s, :, lanes] = (pre * sigma * keep).astype(BF)
+                slope = sigma * (1.0 + pre * (1.0 - sigma))
+                dpre = (upstream_ref[s, :, lanes].astype(F32) * keep * slope).astype(BF)
+                dpre_ref[s, :, lanes] = dpre
+                put_spots(pair, 1, 5 * e + i, dpre)
+                turned.append(pltpu.roll(dpre.astype(F32), 64, 1))
+            put_spots(pair, 1, 5 * e + 4, zero.astype(BF))
+            turned.append(zero)
+            for i in range(4):
+                here = jnp.where(left, turned[i], turned[i + 1])
+                put_spots(pair, 0, 5 * e + i, here.astype(BF))
+                here = jnp.where(left, turned[i - 1] if i else zero, turned[i])
+                put_spots(pair, 2, 5 * e + i, here.astype(BF))
+            put_spots(pair, 0, 5 * e + 4, jnp.where(left, 0.0, turned[0]).astype(BF))
+            put_spots(pair, 2, 5 * e + 4, jnp.where(left, turned[3], 0.0).astype(BF))
         for p in range(PARTS):
-            grads[p] += lax.dot_general(
-                spots[p], taps[p], (((1,), (1,)), ((), ())), preferred_element_type=F32
+            term = lax.dot_general(
+                spots[pair, p], taps[pair, p], (((1,), (1,)), ((), ())), preferred_element_type=F32
             )
-        return carry
-
-    lax.fori_loop(0, mine, one_brick, 0)
+            grads[p] = grads[p] + term if pair else term
 
     pack_bricks(slot_ref, dpre_ref, strips_ref, msg_ref)
     high = slots * 2 * CH + HEAD
@@ -410,50 +419,35 @@
         msg_ref[low + at : low + at + size, :] = (values - rounded.astype(F32)).astype(BF)
 
 
-def backward_kernel(part, *refs):
-    if part:
-        refs, last_ref = refs[:13] + refs[14:], refs[13]
-        field_ref, own_ref, out_ref = refs[2], refs[3], refs[13]
-        slots = field_ref.shape[0]
-        head = slots * 2 * CH
-        half = count_sent(own_ref[head : head + HEAD, :]) // 2
-        for s in range(slots):
-
-            @pl.when(s < half)
-            def _():
-                out_ref[s] = last_ref[s]
-
-    backward_body(part, *refs)
+def backward_kernel(pairs, *refs):
+    if pairs[0] == 0:
+        backward_body(pairs, *refs)
+        return
+    last_ref, out_ref = refs[13], refs[14]
+    for s in range(2 * pairs[0]):
+        out_ref[s] = last_ref[s]
+    backward_body(pairs, *refs[:13], *refs[14:])
 
 
 def backward_body(
-    part, slot_hbm, link_hbm, field_ref, own_ref, mate_ref, first_ref, second_ref, first_far_ref,
+    pairs, slot_hbm, link_hbm, field_ref, own_ref, mate_ref, first_ref, second_ref, first_far_ref,
     second_far_ref, weight_ref, spread_ref, ends_ref, shifts_ref, out_ref,
     planes, strips, mixed, taps, sums, slot_ref, link_ref, sems,
 ):
-    slots = field_ref.shape[0]
     base, mine, find_strip, find_plane = make_finder(
         slot_hbm, link_hbm, own_ref, mate_ref, first_ref, second_ref, first_far_ref, second_far_ref,
         planes, strips, slot_ref, link_ref, sems,
     )
-    if part == 1:
-        for s in range(slots):
-
-            @pl.when(s >= mine)
-            def _():
-                out_ref[s] = jnp.zeros((CH, 512), BF)
-
-    def one_brick(s, carry):
-        tiles = convolve_brick(
-            s, base, find_strip, find_plane, link_ref, field_ref, planes, strips,
-            spread_ref, ends_ref, shifts_ref, weight_ref, mixed, taps, sums,
+    for pair in pairs:
+        results = convolve_pair(
+            pair, base, find_strip, find_plane, link_ref, field_ref, planes, strips,
+            spread_ref, ends_ref, shifts_ref, weight_ref, mixed.at[pair], taps.at[pair], sums.at[pair],
         )
-        for i in range(4):
-            out_ref[s, :, i * TILE : (i + 1) * TILE] = tiles[i].astype(BF)
-        return carry
-
-    half = mine // 2
-    lax.fori_loop(half * part, mine if part else half, one_brick, 0)
+        for e, tiles in enumerate(results):
+            s = 2 * pair + e
+            present = jnp.where(s < mine, 1.0, 0.0)
+            for i in range(4):
+                out_ref[s, :, i * TILE : (i + 1) * TILE] = (tiles[i] * present).astype(BF)
 
 
 def finish_kernel(a_ref, b_ref, kernel_ref, bias_ref):
@@ -511,9 +505,9 @@
     work = [
         pltpu.VMEM((2 * slots + 2 * NEAR + 2 * EDGE + 1, CH, TILE), BF),
         pltpu.VMEM((2 * slots + 2 * EDGE, CH, TILE), BF),
-        pltpu.VMEM((5 * CH, 2 * TILE), BF),
-        pltpu.VMEM((PARTS, 10 * PART, 5 * TILE), BF),
-        pltpu.VMEM((3 * CH, 5 * TILE), F32),
+        pltpu.VMEM((slots // 2, 2, 5 * CH, 2 * TILE), BF),
+        pltpu.VMEM((slots // 2, PARTS, 10 * PART, 10 * TILE), BF),
+        pltpu.VMEM((slots // 2, 3 * CH, 10 * TILE), F32),
         pltpu.SMEM(slot_to_brick.shape, jnp.int32),
         pltpu.SMEM(neighbors.shape, jnp.int32),
         pltpu.SemaphoreType.DMA((2,)),
@@ -547,9 +541,8 @@
         [field, field, shape((pack_rows + 2 * SUM_ROWS, TILE), BF)],
         work
         + [
-            pltpu.VMEM((PARTS, 3 * PART, 5 * TILE), BF),
+            pltpu.VMEM((slots // 2, PARTS, 3 * PART, 10 * TILE), BF),
             pltpu.VMEM((PARTS, 3 * PART, 10 * PART), F32),
-            pltpu.VMEM((slots, 8, 512), F32),
         ],
         flops=4 * 10**9,
     )(
@@ -572,11 +565,11 @@
         near, far = state["near"], state["far"]
         state.update(second=swapped(near, 1), second_far=swapped(far, 1))
 
-    def half_backward(part):
-        last = [state["grad"]] if part else []
+    def part_backward(pairs):
+        last = [state["grad"]] if pairs[0] else []
         (state["grad"],) = call(
-            functools.partial(backward_kernel, part),
-            [HBM, HBM] + [VMEM] * (11 + part),
+            functools.partial(backward_kernel, pairs),
+            [HBM, HBM] + [VMEM] * (11 + len(last)),
             [field],
             work,
             flops=10**9,
@@ -585,7 +578,13 @@
             state["far"], state["second_far"], backward, spread, ends, shifts, *last,
         )
 
-    beside = [send_halos, tell_mate, lambda: half_backward(0), lambda: half_backward(1)]
+    pairs = range(slots // 2)
+    beside = [
+        send_halos,
+        tell_mate,
+        lambda: part_backward(pairs[:1]),
+        lambda: part_backward(pairs[1:]),
+    ]
     masks = [2**p for p in range(1, devices.bit_length() - 1)]
     for mask in masks:
         other = swapped(total, mask)

time: 53.5 us -> 53.8 us (level); the launches traced: 54.1 us -> 53.5 us
  starting transfers between devices: 30.2 us -> 24.5 us
  Pallas kernels: 11.4 us -> 15.4 us
  waiting for transfers between devices: 10.5 us -> 11.6 us
    ppermute x14, starting transfers between devices: 30.2 us -> 24.5 us  [sent(): return lax.ppermute(block, 'bricks', route)]
    pallas_call x1, Pallas kernels: 4.05 us -> 6.83 us  [shards(): call(forward_kernel, [HBM, HBM] + [VMEM] * 16, [field, field, shape((pack...]
    pallas_call x2, Pallas kernels: 3.71 us -> 4.9 us  [part_backward(): call(functools.partial(backward_kernel, pairs), [HBM, HBM] + [VMEM] * (11...]
    ppermute x14, waiting for transfers between devices: 10.5 us -> 11.6 us  [sent(): return lax.ppermute(block, 'bricks', route)]
  transfers between devices with their start and end apart: 14 -> 14, of which waited for: 8 -> 7; matrix products, arithmetic and copies ran while one was open for 0% -> 0% of each run, Pallas kernels for 8% -> 10%
where the time goes in v3:
time: 53.8 us; the launch traced here: 53.5 us
  starting transfers between devices  24.5 us (46%)
  Pallas kernels  15.4 us (29%)
  waiting for transfers between devices  11.6 us (22%)
  local copies, waits for them, and re-layouts  1.01 us (2%)
  between operations  0.96 us (2%)
    ppermute x14, starting transfers between devices, sent(): return lax.ppermute(block, 'bricks', route)  24.5 us
    ppermute x14, waiting for transfers between devices, sent(): return lax.ppermute(block, 'bricks', route)  11.6 us
    pallas_call x1, Pallas kernels, shards(): call(forward_kernel, [HBM, HBM] + [VMEM] * 16, [field, field, shape((pack...  6.83 us
    pallas_call x2, Pallas kernels, part_backward(): call(functools.partial(backward_kernel, pairs), [HBM, HBM] + [VMEM] * (11...  4.9 us
    pallas_call x1, Pallas kernels, shards(): call(pack_kernel, [HBM] * 3, [shape((pack_rows, TILE), BF)], [pltpu.VMEM(...  2.15 us
  transfers between devices with their start and end apart: 14, of which 7 were waited for; matrix products, arithmetic and copies ran while one was open for 0% of the time, Pallas kernels for 10%

profile of v3, /device:TPU:0, one launch (start us, length us, event | category | flops | bytes accessed | tf_op | source)
XLA Modules:
  0.0 53.5 jit_solution(4283281174131785650)
XLA Ops:
  0.6 2.2 %shard_map.147.own_ref = bf16[784,128]{1,0:T(8,128)(2,1)} custom-call(s32[6]{0:T(128)} %refs_0_.3, bf16[6,64,512]{2,1,0:T(8,128)(2,1)} %field_ref.1, bf16[4,512,128]{2,1,0:T(8,128)(2,1)} %constant.10.clone.strips_hbm.strips_ref), custom_call_target="tpu_custom_call" | custom-call | bytes 400000 | tf_op jit(solution)/shard_map/pallas_call | solution.py:517
  2.8 0.5 collective-permute-start
  3.3 1.3 %collective-permute-done.mate_ref = bf16[784,128]{1,0:T(8,128)(2,1)S(1)} collective-permute-done((bf16[784,128]{1,0:T(8,128)(2,1)}, bf16[784,128]{1,0:T(8,128)(2,1)S(1)}, u32[]{:S(2)}, u32[]{:S(2)}) %collective-permute-start) | collective-permute-done | bytes 200736 | tf_op jit(solution)/shard_map/ppermute | solution.py:480
  4.6 0.9 %copy-done.5 = bf16[784,128]{1,0:T(8,128)(2,1)S(1)} copy-done((bf16[784,128]{1,0:T(8,128)(2,1)S(1)}, bf16[784,128]{1,0:T(8,128)(2,1)}, u32[]{:S(2)}) %copy-start.5) | copy-done | bytes 200728
  5.7 0.7 %collective-permute-start.1 = (bf16[656,128]{1,0:T(8,128)(2,1)S(1)}, bf16[656,128]{1,0:T(8,128)(2,1)S(1)}, u32[]{:S(2)}, u32[]{:S(2)}) collective-permute-start(bf16[656,128]{1,0:T(8,128)(2,1)S(1)} %get-tuple-element.37), channel_id=1, source_target_pairs={{1,2},{2,1},{3,4},{4,3},{5,6},{6,5},{7,8},{8,7},{9,10},{10,9},{11,... | collective-permute-start | bytes 503816 | tf_op jit(solution)/shard_map/ppermute | solution.py:480
  6.4 0.7 %collective-permute-start.2 = (bf16[192,128]{1,0:T(8,128)(2,1)S(1)}, bf16[192,128]{1,0:T(8,128)(2,1)S(1)}, u32[]{:S(2)}, u32[]{:S(2)}) collective-permute-start(bf16[192,128]{1,0:T(8,128)(2,1)S(1)} %get-tuple-element.38), channel_id=1, source_target_pairs={{1,4},{3,6},{4,1},{5,8},{6,3},{7,10},{8,5},{9,12},{10,7},{11,14},{... | collective-permute-start | bytes 147464 | tf_op jit(solution)/shard_map/ppermute | solution.py:480
  7.7 8.3 %collective-permute-start.3 = (bf16[656,128]{1,0:T(8,128)(2,1)S(1)}, bf16[656,128]{1,0:T(8,128)(2,1)S(1)}, u32[]{:S(2)}, u32[]{:S(2)}) collective-permute-start(bf16[656,128]{1,0:T(8,128)(2,1)S(1)} %collective-permute-done.1.first_ref), channel_id=1, source_target_pairs={{0,1},{1,0},{2,3},{3,2},{4,5},{5,4},{6,7},{7,6},{8,9},{9,8},{10,11... | collective-permute-start | bytes 503816 | tf_op jit(solution)/shard_map/ppermute | solution.py:480
  16.0 1.2 %collective-permute-done.4.second_far_ref = bf16[192,128]{1,0:T(8,128)(2,1)S(1)} collective-permute-done((bf16[192,128]{1,0:T(8,128)(2,1)S(1)}, bf16[192,128]{1,0:T(8,128)(2,1)S(1)}, u32[]{:S(2)}, u32[]{:S(2)}) %collective-permute-start.4) | collective-permute-done | bytes 49184 | tf_op jit(solution)/shard_map/ppermute | solution.py:480
  17.4 6.8 %shard_map.150 = (bf16[6,64,512]{2,1,0:T(8,128)(2,1)}, bf16[6,64,512]{2,1,0:T(8,128)(2,1)S(1)}, bf16[1040,128]{1,0:T(8,128)(2,1)S(1)}) custom-call(s32[6]{0:T(128)S(1)} %copy-done.8, s32[6,6]{1,0:T(8,128)S(1)} %copy-done.7, bf16[6,64,512]{2,1,0:T(8,128)(2,1)S(1)} %copy-done.4, bf16[784,128]{1,0:T(8,128)(2,1)S(1)} %copy-done.6, ...), custom_call_target="tpu_custom_call" | custom-call | flops 4000000000 | bytes 400000 | tf_op jit(solution)/shard_map/pallas_call | solution.py:538
  24.5 1.3 %collective-permute-done.5.mate_ref.refs_4_ = bf16[1040,128]{1,0:T(8,128)(2,1)S(1)} collective-permute-done((bf16[1040,128]{1,0:T(8,128)(2,1)S(1)}, bf16[1040,128]{1,0:T(8,128)(2,1)S(1)}, u32[]{:S(2)}, u32[]{:S(2)}) %collective-permute-start.5) | collective-permute-done | bytes 266272 | tf_op jit(solution)/shard_map/ppermute | solution.py:480
  26.0 0.7 %collective-permute-start.8 = (bf16[656,128]{1,0:T(8,128)(2,1)S(1)}, bf16[656,128]{1,0:T(8,128)(2,1)S(1)}, u32[]{:S(2)}, u32[]{:S(2)}) collective-permute-start(bf16[656,128]{1,0:T(8,128)(2,1)S(1)} %get-tuple-element.49), channel_id=1, source_target_pairs={{1,2},{2,1},{3,4},{4,3},{5,6},{6,5},{7,8},{8,7},{9,10},{10,9},{11,... | collective-permute-start | bytes 503816 | tf_op jit(solution)/shard_map/ppermute | solution.py:480
  26.6 3.4 %collective-permute-start.6 = (f32[128,128]{1,0:T(8,128)S(1)}, f32[128,128]{1,0:T(8,128)S(1)}, u32[]{:S(2)}, u32[]{:S(2)}) collective-permute-start(f32[128,128]{1,0:T(8,128)S(1)} %get-tuple-element.50), channel_id=1, source_target_pairs={{0,2},{1,3},{2,0},{3,1},{4,6},{5,7},{6,4},{7,5},{8,10},{9,11},{10,... | collective-permute-start | bytes 196616 | tf_op jit(solution)/shard_map/ppermute | solution.py:480
  30.0 0.7 %collective-permute-start.7 = (bf16[192,128]{1,0:T(8,128)(2,1)S(1)}, bf16[192,128]{1,0:T(8,128)(2,1)S(1)}, u32[]{:S(2)}, u32[]{:S(2)}) collective-permute-start(bf16[192,128]{1,0:T(8,128)(2,1)S(1)} %get-tuple-element.48), channel_id=1, source_target_pairs={{1,4},{3,6},{4,1},{5,8},{6,3},{7,10},{8,5},{9,12},{10,7},{11,14},{... | collective-permute-start | bytes 147464 | tf_op jit(solution)/shard_map/ppermute | solution.py:480
  30.7 4.5 %collective-permute-done.6 = f32[128,128]{1,0:T(8,128)S(1)} collective-permute-done((f32[128,128]{1,0:T(8,128)S(1)}, f32[128,128]{1,0:T(8,128)S(1)}, u32[]{:S(2)}, u32[]{:S(2)}) %collective-permute-start.6) | collective-permute-done | bytes 65568 | tf_op jit(solution)/shard_map/ppermute | solution.py:480
  35.2 1.9 %collective-permute-start.10 = (bf16[656,128]{1,0:T(8,128)(2,1)S(1)}, bf16[656,128]{1,0:T(8,128)(2,1)S(1)}, u32[]{:S(2)}, u32[]{:S(2)}) collective-permute-start(bf16[656,128]{1,0:T(8,128)(2,1)S(1)} %collective-permute-done.8.refs_5_), channel_id=1, source_target_pairs={{0,1},{1,0},{2,3},{3,2},{4,5},{5,4},{6,7},{7,6},{8,9},{9,8},{10,11... | collective-permute-start | bytes 503816 | tf_op jit(solution)/shard_map/ppermute | solution.py:480
  37.1 3.2 %collective-permute-start.9 = (f32[128,128]{1,0:T(8,128)S(1)}, f32[128,128]{1,0:T(8,128)S(1)}, u32[]{:S(2)}, u32[]{:S(2)}) collective-permute-start(f32[128,128]{1,0:T(8,128)S(1)} %add.9), channel_id=1, source_target_pairs={{0,4},{1,5},{2,6},{3,7},{4,0},{5,1},{6,2},{7,3},{8,12},{9,13},{10,... | collective-permute-start | bytes 196616 | tf_op jit(solution)/shard_map/ppermute | solution.py:480
  40.3 1.2 %collective-permute-done.11.refs_8_ = bf16[192,128]{1,0:T(8,128)(2,1)S(1)} collective-permute-done((bf16[192,128]{1,0:T(8,128)(2,1)S(1)}, bf16[192,128]{1,0:T(8,128)(2,1)S(1)}, u32[]{:S(2)}, u32[]{:S(2)}) %collective-permute-start.11) | collective-permute-done | bytes 49184 | tf_op jit(solution)/shard_map/ppermute | solution.py:480
  41.5 1.0 %collective-permute-done.9 = f32[128,128]{1,0:T(8,128)S(1)} collective-permute-done((f32[128,128]{1,0:T(8,128)S(1)}, f32[128,128]{1,0:T(8,128)S(1)}, u32[]{:S(2)}, u32[]{:S(2)}) %collective-permute-start.9) | collective-permute-done | bytes 65568 | tf_op jit(solution)/shard_map/ppermute | solution.py:480
  42.5 1.7 %collective-permute-start.12 = (f32[128,128]{1,0:T(8,128)S(1)}, f32[128,128]{1,0:T(8,128)S(1)}, u32[]{:S(2)}, u32[]{:S(2)}) collective-permute-start(f32[128,128]{1,0:T(8,128)S(1)} %add.10), channel_id=1, source_target_pairs={{0,8},{1,9},{2,10},{3,11},{4,12},{5,13},{6,14},{7,15},{8,0},{9,1},... | collective-permute-start | bytes 196616 | tf_op jit(solution)/shard_map/ppermute | solution.py:480
  44.2 1.7 %shard_map.152.refs_13_ = bf16[6,64,512]{2,1,0:T(8,128)(2,1)S(1)} custom-call(s32[6]{0:T(128)S(1)} %copy-done.8, s32[6,6]{1,0:T(8,128)S(1)} %copy-done.7, bf16[6,64,512]{2,1,0:T(8,128)(2,1)S(1)} %get-tuple-element.45.refs_2_, bf16[1040,128]{1,0:T(8,128)(2,1)S(1)} %get-tuple-element.46.own_ref.refs_3_, ...), custom_call_target="tpu_custom_call" | custom-call | flops 1000000000 | bytes 400000 | tf_op jit(solution)/shard_map/pallas_call | solution.py:570
  45.9 1.0 %collective-permute-done.12 = f32[128,128]{1,0:T(8,128)S(1)} collective-permute-done((f32[128,128]{1,0:T(8,128)S(1)}, f32[128,128]{1,0:T(8,128)S(1)}, u32[]{:S(2)}, u32[]{:S(2)}) %collective-permute-start.12) | collective-permute-done | bytes 65568 | tf_op jit(solution)/shard_map/ppermute | solution.py:480
  46.9 2.7 %collective-permute-start.13 = (f32[128,128]{1,0:T(8,128)S(1)}, f32[128,128]{1,0:T(8,128)S(1)}, u32[]{:S(2)}, u32[]{:S(2)}) collective-permute-start(f32[128,128]{1,0:T(8,128)S(1)} %add.11.a_ref), channel_id=1, source_target_pairs={{0,16},{1,17},{2,18},{3,19},{4,20},{5,21},{6,22},{7,23},{8,24},{9,... | collective-permute-start | bytes 196616 | tf_op jit(solution)/shard_map/ppermute | solution.py:480
  49.6 3.2 %shard_map.153 = bf16[6,64,512]{2,1,0:T(8,128)(2,1)} custom-call(s32[6]{0:T(128)S(1)} %copy-done.8, s32[6,6]{1,0:T(8,128)S(1)} %copy-done.7, bf16[6,64,512]{2,1,0:T(8,128)(2,1)S(1)} %get-tuple-element.45.refs_2_, bf16[1040,128]{1,0:T(8,128)(2,1)S(1)} %get-tuple-element.46.own_ref.refs_3_, bf16[1040,128]{1,0:T(8,128)(2,1)S(1)} %collective-permute-done.5.mate_ref.refs_4_, ...), custom_call_target="tpu_custom_call" | custom-call | flops 1000000000 | bytes 400000 | tf_op jit(solution)/shard_map/pallas_call | solution.py:570
  52.8 0.7 %shard_map.154 = (f32[216,64]{1,0:T(8,128)}, f32[1,64]{1,0:T(1,128)}) custom-call(f32[128,128]{1,0:T(8,128)S(1)} %add.11.a_ref, f32[128,128]{1,0:T(8,128)S(1)} %collective-permute-done.13.b_ref), custom_call_target="tpu_custom_call" | custom-call | bytes 400000 | tf_op jit(solution)/shard_map/pallas_call | solution.py:599
  (43 shorter events, 1.2 us)
Async XLA Ops:
  2.8 1.8 %collective-permute-start = (bf16[784,128]{1,0:T(8,128)(2,1)}, bf16[784,128]{1,0:T(8,128)(2,1)S(1)}, u32[]{:S(2)}, u32[]{:S(2)}) collective-permute-start(bf16[784,128]{1,0:T(8,128)(2,1)} %shard_map.147.own_ref), channel_id=1, source_target_pairs={{0,1},{1,0},{2,3},{3,2},{4,5},{5,4},{6,7},{7,6},{8,9},{9,8},{10,11... | collective-permute-start | bytes 602120 | tf_op jit(solution)/shard_map/ppermute | solution.py:480
  5.7 2.0 %collective-permute-start.1 = (bf16[656,128]{1,0:T(8,128)(2,1)S(1)}, bf16[656,128]{1,0:T(8,128)(2,1)S(1)}, u32[]{:S(2)}, u32[]{:S(2)}) collective-permute-start(bf16[656,128]{1,0:T(8,128)(2,1)S(1)} %get-tuple-element.37), channel_id=1, source_target_pairs={{1,2},{2,1},{3,4},{4,3},{5,6},{6,5},{7,8},{8,7},{9,10},{10,9},{11,... | collective-permute-start | bytes 503816 | tf_op jit(solution)/shard_map/ppermute | solution.py:480
  6.4 1.3 %collective-permute-start.2 = (bf16[192,128]{1,0:T(8,128)(2,1)S(1)}, bf16[192,128]{1,0:T(8,128)(2,1)S(1)}, u32[]{:S(2)}, u32[]{:S(2)}) collective-permute-start(bf16[192,128]{1,0:T(8,128)(2,1)S(1)} %get-tuple-element.38), channel_id=1, source_target_pairs={{1,4},{3,6},{4,1},{5,8},{6,3},{7,10},{8,5},{9,12},{10,7},{11,14},{... | collective-permute-start | bytes 147464 | tf_op jit(solution)/shard_map/ppermute | solution.py:480
  7.1 10.2 %copy-start = (bf16[4,256,1024]{2,1,0:T(8,128)(2,1)S(1)}, bf16[4,256,1024]{2,1,0:T(8,128)(2,1)}, u32[]{:S(2)}) copy-start(bf16[4,256,1024]{2,1,0:T(8,128)(2,1)} %constant.13.clone.shifts_ref.refs_12_) | copy-start | bytes 6291460
  7.1 10.2 %copy-start.1 = (bf16[4,384,128]{2,1,0:T(8,128)(2,1)S(1)}, bf16[4,384,128]{2,1,0:T(8,128)(2,1)}, u32[]{:S(2)}) copy-start(bf16[4,384,128]{2,1,0:T(8,128)(2,1)} %constant.12.clone.ends_ref.refs_11_) | copy-start | bytes 1179652
  7.1 10.2 %copy-start.2 = (bf16[256,512]{1,0:T(8,128)(2,1)S(1)}, bf16[256,512]{1,0:T(8,128)(2,1)}, u32[]{:S(2)}) copy-start(bf16[256,512]{1,0:T(8,128)(2,1)} %constant.11.clone.spread_ref.refs_10_) | copy-start | bytes 786436
  7.1 10.2 %copy-start.3 = (bf16[4,512,128]{2,1,0:T(8,128)(2,1)S(1)}, bf16[4,512,128]{2,1,0:T(8,128)(2,1)}, u32[]{:S(2)}) copy-start(bf16[4,512,128]{2,1,0:T(8,128)(2,1)} %constant.10.clone.strips_hbm.strips_ref) | copy-start | bytes 1572868
  7.1 10.2 %copy-start.4 = (bf16[6,64,512]{2,1,0:T(8,128)(2,1)S(1)}, bf16[6,64,512]{2,1,0:T(8,128)(2,1)}, u32[]{:S(2)}) copy-start(bf16[6,64,512]{2,1,0:T(8,128)(2,1)} %field_ref.1) | copy-start | bytes 1179652
  7.1 10.2 %copy-start.6 = (bf16[784,128]{1,0:T(8,128)(2,1)S(1)}, bf16[784,128]{1,0:T(8,128)(2,1)}, u32[]{:S(2)}) copy-start(bf16[784,128]{1,0:T(8,128)(2,1)} %shard_map.147.own_ref) | copy-start | bytes 602116
  7.1 10.2 %copy-start.7 = (s32[6,6]{1,0:T(8,128)S(1)}, s32[6,6]{1,0:T(8,128)}, u32[]{:S(2)}) copy-start(s32[6,6]{1,0:T(8,128)} %refs_1_.3) | copy-start | bytes 436
  7.1 10.2 %copy-start.8 = (s32[6]{0:T(128)S(1)}, s32[6]{0:T(128)}, u32[]{:S(2)}) copy-start(s32[6]{0:T(128)} %refs_0_.3) | copy-start | bytes 76
  7.2 10.2 %copy-start.9 = (bf16[6,64,512]{2,1,0:T(8,128)(2,1)S(1)}, bf16[6,64,512]{2,1,0:T(8,128)(2,1)}, u32[]{:S(2)}) copy-start(bf16[6,64,512]{2,1,0:T(8,128)(2,1)} %upstream_ref.1) | copy-start | bytes 1179652
  7.2 10.1 %copy-start.11 = (s32[6,512]{1,0:T(8,128)S(1)}, s32[6,512]{1,0:T(8,128)}, u32[]{:S(2)}) copy-start(s32[6,512]{1,0:T(8,128)} %cortex_ref.1) | copy-start | bytes 36868
  7.7 9.5 %collective-permute-start.3 = (bf16[656,128]{1,0:T(8,128)(2,1)S(1)}, bf16[656,128]{1,0:T(8,128)(2,1)S(1)}, u32[]{:S(2)}, u32[]{:S(2)}) collective-permute-start(bf16[656,128]{1,0:T(8,128)(2,1)S(1)} %collective-permute-done.1.first_ref), channel_id=1, source_target_pairs={{0,1},{1,0},{2,3},{3,2},{4,5},{5,4},{6,7},{7,6},{8,9},{9,8},{10,11... | collective-permute-start | bytes 503816 | tf_op jit(solution)/shard_map/ppermute | solution.py:480
  16.0 1.2 %collective-permute-start.4 = (bf16[192,128]{1,0:T(8,128)(2,1)S(1)}, bf16[192,128]{1,0:T(8,128)(2,1)S(1)}, u32[]{:S(2)}, u32[]{:S(2)}) collective-permute-start(bf16[192,128]{1,0:T(8,128)(2,1)S(1)} %collective-permute-done.2.first_far_ref), channel_id=1, source_target_pairs={{0,1},{1,0},{2,3},{3,2},{4,5},{5,4},{6,7},{7,6},{8,9},{9,8},{10,11... | collective-permute-start | bytes 147464 | tf_op jit(solution)/shard_map/ppermute | solution.py:480
  24.2 1.6 %collective-permute-start.5 = (bf16[1040,128]{1,0:T(8,128)(2,1)S(1)}, bf16[1040,128]{1,0:T(8,128)(2,1)S(1)}, u32[]{:S(2)}, u32[]{:S(2)}) collective-permute-start(bf16[1040,128]{1,0:T(8,128)(2,1)S(1)} %get-tuple-element.46.own_ref.refs_3_), channel_id=1, source_target_pairs={{0,1},{1,0},{2,3},{3,2},{4,5},{5,4},{6,7},{7,6},{8,9},{9,8},{10,11... | collective-permute-start | bytes 798728 | tf_op jit(solution)/shard_map/ppermute | solution.py:480
  26.0 9.2 %collective-permute-start.8 = (bf16[656,128]{1,0:T(8,128)(2,1)S(1)}, bf16[656,128]{1,0:T(8,128)(2,1)S(1)}, u32[]{:S(2)}, u32[]{:S(2)}) collective-permute-start(bf16[656,128]{1,0:T(8,128)(2,1)S(1)} %get-tuple-element.49), channel_id=1, source_target_pairs={{1,2},{2,1},{3,4},{4,3},{5,6},{6,5},{7,8},{8,7},{9,10},{10,9},{11,... | collective-permute-start | bytes 503816 | tf_op jit(solution)/shard_map/ppermute | solution.py:480
  26.6 8.5 %collective-permute-start.6 = (f32[128,128]{1,0:T(8,128)S(1)}, f32[128,128]{1,0:T(8,128)S(1)}, u32[]{:S(2)}, u32[]{:S(2)}) collective-permute-start(f32[128,128]{1,0:T(8,128)S(1)} %get-tuple-element.50), channel_id=1, source_target_pairs={{0,2},{1,3},{2,0},{3,1},{4,6},{5,7},{6,4},{7,5},{8,10},{9,11},{10,... | collective-permute-start | bytes 196616 | tf_op jit(solution)/shard_map/ppermute | solution.py:480
  30.0 0.7 %collective-permute-start.7 = (bf16[192,128]{1,0:T(8,128)(2,1)S(1)}, bf16[192,128]{1,0:T(8,128)(2,1)S(1)}, u32[]{:S(2)}, u32[]{:S(2)}) collective-permute-start(bf16[192,128]{1,0:T(8,128)(2,1)S(1)} %get-tuple-element.48), channel_id=1, source_target_pairs={{1,4},{3,6},{4,1},{5,8},{6,3},{7,10},{8,5},{9,12},{10,7},{11,14},{... | collective-permute-start | bytes 147464 | tf_op jit(solution)/shard_map/ppermute | solution.py:480
  35.2 7.4 %collective-permute-start.10 = (bf16[656,128]{1,0:T(8,128)(2,1)S(1)}, bf16[656,128]{1,0:T(8,128)(2,1)S(1)}, u32[]{:S(2)}, u32[]{:S(2)}) collective-permute-start(bf16[656,128]{1,0:T(8,128)(2,1)S(1)} %collective-permute-done.8.refs_5_), channel_id=1, source_target_pairs={{0,1},{1,0},{2,3},{3,2},{4,5},{5,4},{6,7},{7,6},{8,9},{9,8},{10,11... | collective-permute-start | bytes 503816 | tf_op jit(solution)/shard_map/ppermute | solution.py:480
  37.1 5.5 %collective-permute-start.9 = (f32[128,128]{1,0:T(8,128)S(1)}, f32[128,128]{1,0:T(8,128)S(1)}, u32[]{:S(2)}, u32[]{:S(2)}) collective-permute-start(f32[128,128]{1,0:T(8,128)S(1)} %add.9), channel_id=1, source_target_pairs={{0,4},{1,5},{2,6},{3,7},{4,0},{5,1},{6,2},{7,3},{8,12},{9,13},{10,... | collective-permute-start | bytes 196616 | tf_op jit(solution)/shard_map/ppermute | solution.py:480
  40.3 1.2 %collective-permute-start.11 = (bf16[192,128]{1,0:T(8,128)(2,1)S(1)}, bf16[192,128]{1,0:T(8,128)(2,1)S(1)}, u32[]{:S(2)}, u32[]{:S(2)}) collective-permute-start(bf16[192,128]{1,0:T(8,128)(2,1)S(1)} %collective-permute-done.7.refs_7_), channel_id=1, source_target_pairs={{0,1},{1,0},{2,3},{3,2},{4,5},{5,4},{6,7},{7,6},{8,9},{9,8},{10,11... | collective-permute-start | bytes 147464 | tf_op jit(solution)/shard_map/ppermute | solution.py:480
  42.5 4.3 %collective-permute-start.12 = (f32[128,128]{1,0:T(8,128)S(1)}, f32[128,128]{1,0:T(8,128)S(1)}, u32[]{:S(2)}, u32[]{:S(2)}) collective-permute-start(f32[128,128]{1,0:T(8,128)S(1)} %add.10), channel_id=1, source_target_pairs={{0,8},{1,9},{2,10},{3,11},{4,12},{5,13},{6,14},{7,15},{8,0},{9,1},... | collective-permute-start | bytes 196616 | tf_op jit(solution)/shard_map/ppermute | solution.py:480
  46.9 5.9 %collective-permute-start.13 = (f32[128,128]{1,0:T(8,128)S(1)}, f32[128,128]{1,0:T(8,128)S(1)}, u32[]{:S(2)}, u32[]{:S(2)}) collective-permute-start(f32[128,128]{1,0:T(8,128)S(1)} %add.11.a_ref), channel_id=1, source_target_pairs={{0,16},{1,17},{2,18},{3,19},{4,20},{5,21},{6,22},{7,23},{8,24},{9,... | collective-permute-start | bytes 196616 | tf_op jit(solution)/shard_map/ppermute | solution.py:480
  (4 other events, 27.6 us)

commit v4 on v3

--- a/solution.py
+++ b/solution.py
@@ -14,10 +14,12 @@
 PARTS = CH // PART
 SIDES = (0, 1, 2, 3, 5, 6, 7, 8)
 TILE = 128
-NEAR = 7
+NEAR = 8
+FAR = 4
 EDGE = 3
 BUSY = 10**10
 HEAD = 16
+NEAR_ROWS = (NEAR // 2 + EDGE) * CH + HEAD
 SUM_ROWS = 128
 BF = jnp.bfloat16
 F32 = jnp.float32
@@ -145,15 +147,24 @@
     for s in range(2 * slots):
         box[s] = own_ref[s * CH : (s + 1) * CH, :]
         box[2 * slots + s] = mate_ref[s * CH : (s + 1) * CH, :]
-    for j in range(NEAR):
+
+    def place(j):
         up = jnp.where(j < mine, mine - 1 - j, slots + other - 1 - (j - mine))
         down = jnp.where(j < mine, j, slots + j - mine)
-        at = jnp.clip(jnp.where(odd, up, down), 0, 2 * slots - 1)
-        near_ref[j * CH : (j + 1) * CH, :] = box[2 * at + 1]
-        if j < EDGE:
-            near_ref[(NEAR + j) * CH : (NEAR + j + 1) * CH, :] = box[2 * at]
-            far_ref[j * CH : (j + 1) * CH, :] = box[2 * at + 1]
-    row = (NEAR + EDGE) * CH
+        return jnp.clip(jnp.where(odd, up, down), 0, 2 * slots - 1)
+
+    half = lax.broadcasted_iota(jnp.int32, (CH, TILE), 1) // 64
+    counts_here = half == odd.astype(jnp.int32)
+    for j in range(0, NEAR, 2):
+        first, second = [box[2 * place(j + e) + 1].astype(F32) for e in range(2)]
+        both = jnp.where(counts_here, first, pltpu.roll(second, 64, 1)).astype(BF)
+        near_ref[j // 2 * CH : (j // 2 + 1) * CH, :] = both
+        if j < FAR:
+            far_ref[j // 2 * CH : (j // 2 + 1) * CH, :] = both
+    for j in range(EDGE):
+        row = (NEAR // 2 + j) * CH
+        near_ref[row : row + CH, :] = box[2 * place(j)]
+    row = (NEAR // 2 + EDGE) * CH
     both = (mine + other).astype(F32)
     near_ref[row : row + HEAD, :] = jnp.full((HEAD, TILE), both, F32).astype(BF)
 
@@ -171,7 +182,21 @@
         parts.append(
             ref[high : high + SUM_ROWS, :].astype(F32) + ref[low : low + SUM_ROWS, :].astype(F32)
         )
-    sum_ref[...] = parts[0] + parts[1]
+    total = parts[0] + parts[1]
+    rounded = total.astype(BF)
+    rest = (total - rounded.astype(F32)).astype(BF)
+    near_ref[NEAR_ROWS : NEAR_ROWS + SUM_ROWS, :] = rounded
+    near_ref[NEAR_ROWS + SUM_ROWS :, :] = rest
+    sum_ref[...] = rounded.astype(F32) + rest.astype(F32)
+
+
+def join_kernel(sum_ref, first_ref, second_ref, out_ref):
+    device = lax.axis_index("bricks")
+    itself = (device & 1) != ((device >> 1) & 1)
+    high = slice(NEAR_ROWS, NEAR_ROWS + SUM_ROWS)
+    low = slice(NEAR_ROWS + SUM_ROWS, NEAR_ROWS + 2 * SUM_ROWS)
+    parts = [ref[high, :].astype(F32) + ref[low, :].astype(F32) for ref in (first_ref, second_ref)]
+    out_ref[...] = sum_ref[...] + jnp.where(itself, parts[0], parts[1])
 
 
 def weight_kernel(taps_ref, forward_ref, backward_ref, work):
@@ -209,19 +234,22 @@
     head = slots * 2 * CH
     mine = count_sent(own_ref[head : head + HEAD, :])
     other = count_sent(mate_ref[head : head + HEAD, :])
-    row = (NEAR + EDGE) * CH
+    row = (NEAR // 2 + EDGE) * CH
     counts = [count_sent(ref[row : row + HEAD, :]) for ref in (first_ref, second_ref)]
     for k, ref in enumerate((own_ref, mate_ref)):
         for s in range(slots):
             strips[k * slots + s] = ref[s * 2 * CH : s * 2 * CH + CH, :]
             planes[k * slots + s] = ref[s * 2 * CH + CH : (s + 1) * 2 * CH, :]
     for side, (near, far) in enumerate(((first_ref, first_far_ref), (second_ref, second_far_ref))):
-        for j in range(NEAR):
-            planes[2 * slots + side * NEAR + j] = near[j * CH : (j + 1) * CH, :]
+        for start, ref, count in ((side * NEAR, near, NEAR), (2 * NEAR + side * FAR, far, FAR)):
+            for j in range(0, count, 2):
+                tile = ref[j // 2 * CH : (j // 2 + 1) * CH, :]
+                planes[2 * slots + start + j] = tile
+                planes[2 * slots + start + j + 1] = pltpu.roll(tile.astype(F32), 64, 1).astype(BF)
         for j in range(EDGE):
-            strips[2 * slots + side * EDGE + j] = near[(NEAR + j) * CH : (NEAR + j + 1) * CH, :]
-            planes[2 * slots + 2 * NEAR + side * EDGE + j] = far[j * CH : (j + 1) * CH, :]
-    nothing = 2 * slots + 2 * NEAR + 2 * EDGE
+            row = (NEAR // 2 + j) * CH
+            strips[2 * slots + side * EDGE + j] = near[row : row + CH, :]
+    nothing = 2 * slots + 2 * NEAR + 2 * FAR
     planes[nothing] = jnp.zeros((CH, TILE), BF)
     for copy in copies:
         copy.wait()
@@ -246,7 +274,7 @@
 
     def outside(distance, count, side):
         near = 2 * slots + side * NEAR + distance
-        far = 2 * slots + 2 * NEAR + side * EDGE + distance - count
+        far = 2 * slots + 2 * NEAR + side * FAR + distance - count
         return jnp.where(distance < count, near, far)
 
     def find_plane(brick, exists):
@@ -487,8 +515,9 @@
     fold = fold.astype(F32)
     shape = jax.ShapeDtypeStruct
     pack_rows = slots * 2 * CH + HEAD
-    near_shape = shape(((NEAR + EDGE) * CH + HEAD, TILE), BF)
-    far_shape = shape((EDGE * CH, TILE), BF)
+    near_shape = shape((NEAR_ROWS, TILE), BF)
+    near_sum_shape = shape((NEAR_ROWS + 2 * SUM_ROWS, TILE), BF)
+    far_shape = shape((FAR // 2 * CH, TILE), BF)
 
     def routed(block, chips):
         pairs = []
@@ -503,7 +532,7 @@
 
     box = [pltpu.VMEM((4 * slots, CH, TILE), BF)]
     work = [
-        pltpu.VMEM((2 * slots + 2 * NEAR + 2 * EDGE + 1, CH, TILE), BF),
+        pltpu.VMEM((2 * slots + 2 * NEAR + 2 * FAR + 1, CH, TILE), BF),
         pltpu.VMEM((2 * slots + 2 * EDGE, CH, TILE), BF),
         pltpu.VMEM((slots // 2, 2, 5 * CH, 2 * TILE), BF),
         pltpu.VMEM((slots // 2, PARTS, 10 * PART, 10 * TILE), BF),
@@ -531,7 +560,7 @@
         functools.partial(route_kernel, slots), [VMEM, VMEM], [near_shape, far_shape], box,
         flops=BUSY,
     )(own, mate)
-    near, far = routed(near, 1), routed(far, 2)
+    far, near = routed(far, 2), routed(near, 1)
     near, far, staged = lax.optimization_barrier((near, far, staged))
     forward, backward = staged
     received = (near, swapped(near, 1), far, swapped(far, 1))
@@ -553,48 +582,45 @@
     near, far, total = call(
         functools.partial(route_sum_kernel, slots),
         [VMEM, VMEM],
-        [near_shape, far_shape, shape((SUM_ROWS, TILE), F32)],
+        [near_sum_shape, far_shape, shape((SUM_ROWS, TILE), F32)],
         box,
     )(own, mate)
-    state = dict(near=near, far=far)
-
-    def send_halos():
-        state.update(near=routed(state["near"], 1), far=routed(state["far"], 2))
-
-    def tell_mate():
-        near, far = state["near"], state["far"]
-        state.update(second=swapped(near, 1), second_far=swapped(far, 1))
-
-    def part_backward(pairs):
-        last = [state["grad"]] if pairs[0] else []
+    near = routed(near, 1)
+    second = swapped(near, 1)
+    (total,) = call(join_kernel, [VMEM] * 3, [shape((SUM_ROWS, TILE), F32)])(total, near, second)
+    state = {}
+
+    def part_backward(pair):
+        last = [state["grad"]] if pair else []
         (state["grad"],) = call(
-            functools.partial(backward_kernel, pairs),
+            functools.partial(backward_kernel, (pair,)),
             [HBM, HBM] + [VMEM] * (11 + len(last)),
             [field],
             work,
             flops=10**9,
         )(
-            slot_to_brick, neighbors, dpre, own, mate, state["near"], state["second"],
-            state["far"], state["second_far"], backward, spread, ends, shifts, *last,
+            slot_to_brick, neighbors, dpre, own, mate, near, second, far, second_far,
+            backward, spread, ends, shifts, *last,
         )
 
-    pairs = range(slots // 2)
-    beside = [
-        send_halos,
-        tell_mate,
-        lambda: part_backward(pairs[:1]),
-        lambda: part_backward(pairs[1:]),
-    ]
-    masks = [2**p for p in range(1, devices.bit_length() - 1)]
-    for mask in masks:
+    pairs = list(range(slots // 2))
+    masks = [2**p for p in range(2, devices.bit_length() - 1)]
+    for at, mask in enumerate(masks):
         other = swapped(total, mask)
-        if beside:
-            beside.pop(0)()
+        if at == 0:
+            far, total = lax.optimization_barrier((far, total))
+            far = routed(far, 2)
+        elif pairs:
+            if at == 1:
+                second_far = swapped(far, 1)
+            part_backward(pairs.pop(0))
         if mask != masks[-1]:
             total, other, state = lax.optimization_barrier((total, other, state))
             total = total + other
-    for task in beside:
-        task()
+            if at == 0:
+                far, total = lax.optimization_barrier((far, total))
+    for pair in pairs:
+        part_backward(pair)
     input_grad = state["grad"]
     kernel_sum, bias_sum = call(
         finish_kernel, [VMEM, VMEM], [shape((27 * GC, CH), F32), shape((1, CH), F32)]

time: 53.8 us -> 57.9 us (1.076)
  starting transfers between devices: 24.5 us -> 31.3 us
  waiting for transfers between devices: 11.6 us -> 7.72 us
  Pallas kernels: 15.4 us -> 16.6 us
    ppermute x14 -> x13, starting transfers between devices: 24.5 us -> 31.3 us  [sent(): return lax.ppermute(block, 'bricks', route)]
    ppermute x14 -> x13, waiting for transfers between devices: 11.6 us -> 7.72 us  [sent(): return lax.ppermute(block, 'bricks', route)]
    pallas_call x3 -> x5, Pallas kernels: 5.06 us -> 6.08 us  [the longest x3 5.83 us: part_backward(): call(functools.partial(backward_kernel, (pair,)), [HBM, HBM] + [VMEM] * (...]
  transfers between devices with their start and end apart: 14 -> 13, of which waited for: 7 -> 6; matrix products, arithmetic and copies ran while one was open for 0% -> 0% of each run, Pallas kernels for 10% -> 11%
where the time goes in v4:
time: 57.9 us; the launch traced here: 57.6 us
  starting transfers between devices  31.3 us (54%)
  Pallas kernels  16.6 us (29%)
  waiting for transfers between devices  7.72 us (13%)
  local copies, waits for them, and re-layouts  1.01 us (2%)
  between operations  0.97 us (2%)
    ppermute x13, starting transfers between devices, sent(): return lax.ppermute(block, 'bricks', route)  31.3 us
    ppermute x13, waiting for transfers between devices, sent(): return lax.ppermute(block, 'bricks', route)  7.72 us
    pallas_call x1, Pallas kernels, shards(): call(forward_kernel, [HBM, HBM] + [VMEM] * 16, [field, field, shape((pack...  6.92 us
    pallas_call x3, Pallas kernels, part_backward(): call(functools.partial(backward_kernel, (pair,)), [HBM, HBM] + [VMEM] * (...  5.83 us
    pallas_call x1, Pallas kernels, shards(): call(pack_kernel, [HBM] * 3, [shape((pack_rows, TILE), BF)], [pltpu.VMEM(...  2.14 us
  transfers between devices with their start and end apart: 13, of which 6 were waited for; matrix products, arithmetic and copies ran while one was open for 0% of the time, Pallas kernels for 11%

profile of v4, /device:TPU:0, one launch (start us, length us, event | category | flops | bytes accessed | tf_op | source)
XLA Modules:
  0.0 57.6 jit_solution(6890070876190054421)
XLA Ops:
  0.6 2.1 %shard_map.147.own_ref = bf16[784,128]{1,0:T(8,128)(2,1)} custom-call(s32[6]{0:T(128)} %refs_0_.5, bf16[6,64,512]{2,1,0:T(8,128)(2,1)} %field_ref.1, bf16[4,512,128]{2,1,0:T(8,128)(2,1)} %constant.10.clone.strips_hbm.strips_ref), custom_call_target="tpu_custom_call" | custom-call | bytes 400000 | tf_op jit(solution)/shard_map/pallas_call | solution.py:546
  2.8 0.5 collective-permute-start
  3.3 1.3 %collective-permute-done.mate_ref = bf16[784,128]{1,0:T(8,128)(2,1)S(1)} collective-permute-done((bf16[784,128]{1,0:T(8,128)(2,1)}, bf16[784,128]{1,0:T(8,128)(2,1)S(1)}, u32[]{:S(2)}, u32[]{:S(2)}) %collective-permute-start) | collective-permute-done | bytes 200736 | tf_op jit(solution)/shard_map/ppermute | solution.py:508
  4.6 0.9 %copy-done.5 = bf16[784,128]{1,0:T(8,128)(2,1)S(1)} copy-done((bf16[784,128]{1,0:T(8,128)(2,1)S(1)}, bf16[784,128]{1,0:T(8,128)(2,1)}, u32[]{:S(2)}) %copy-start.5) | copy-done | bytes 200728
  5.8 0.7 %collective-permute-start.1 = (bf16[464,128]{1,0:T(8,128)(2,1)S(1)}, bf16[464,128]{1,0:T(8,128)(2,1)S(1)}, u32[]{:S(2)}, u32[]{:S(2)}) collective-permute-start(bf16[464,128]{1,0:T(8,128)(2,1)S(1)} %get-tuple-element.29), channel_id=1, source_target_pairs={{1,2},{2,1},{3,4},{4,3},{5,6},{6,5},{7,8},{8,7},{9,10},{10,9},{11,... | collective-permute-start | bytes 356360 | tf_op jit(solution)/shard_map/ppermute | solution.py:508
  6.4 0.7 %collective-permute-start.2 = (bf16[128,128]{1,0:T(8,128)(2,1)S(1)}, bf16[128,128]{1,0:T(8,128)(2,1)S(1)}, u32[]{:S(2)}, u32[]{:S(2)}) collective-permute-start(bf16[128,128]{1,0:T(8,128)(2,1)S(1)} %get-tuple-element.30), channel_id=1, source_target_pairs={{1,4},{3,6},{4,1},{5,8},{6,3},{7,10},{8,5},{9,12},{10,7},{11,14},{... | collective-permute-start | bytes 98312 | tf_op jit(solution)/shard_map/ppermute | solution.py:508
  7.8 8.1 %collective-permute-start.3 = (bf16[464,128]{1,0:T(8,128)(2,1)S(1)}, bf16[464,128]{1,0:T(8,128)(2,1)S(1)}, u32[]{:S(2)}, u32[]{:S(2)}) collective-permute-start(bf16[464,128]{1,0:T(8,128)(2,1)S(1)} %collective-permute-done.1.first_ref), channel_id=1, source_target_pairs={{0,1},{1,0},{2,3},{3,2},{4,5},{5,4},{6,7},{7,6},{8,9},{9,8},{10,11... | collective-permute-start | bytes 356360 | tf_op jit(solution)/shard_map/ppermute | solution.py:508
  15.9 1.2 %collective-permute-done.4.second_far_ref = bf16[128,128]{1,0:T(8,128)(2,1)S(1)} collective-permute-done((bf16[128,128]{1,0:T(8,128)(2,1)S(1)}, bf16[128,128]{1,0:T(8,128)(2,1)S(1)}, u32[]{:S(2)}, u32[]{:S(2)}) %collective-permute-start.4) | collective-permute-done | bytes 32800 | tf_op jit(solution)/shard_map/ppermute | solution.py:508
  17.2 6.9 %shard_map.150 = (bf16[6,64,512]{2,1,0:T(8,128)(2,1)}, bf16[6,64,512]{2,1,0:T(8,128)(2,1)S(1)}, bf16[1040,128]{1,0:T(8,128)(2,1)S(1)}) custom-call(s32[6]{0:T(128)S(1)} %copy-done.8, s32[6,6]{1,0:T(8,128)S(1)} %copy-done.7, bf16[6,64,512]{2,1,0:T(8,128)(2,1)S(1)} %copy-done.4, bf16[784,128]{1,0:T(8,128)(2,1)S(1)} %copy-done.6, ...), custom_call_target="tpu_custom_call" | custom-call | flops 4000000000 | bytes 400000 | tf_op jit(solution)/shard_map/pallas_call | solution.py:567
  24.4 1.4 %collective-permute-done.5.mate_ref.refs_4_ = bf16[1040,128]{1,0:T(8,128)(2,1)S(1)} collective-permute-done((bf16[1040,128]{1,0:T(8,128)(2,1)S(1)}, bf16[1040,128]{1,0:T(8,128)(2,1)S(1)}, u32[]{:S(2)}, u32[]{:S(2)}) %collective-permute-start.5) | collective-permute-done | bytes 266272 | tf_op jit(solution)/shard_map/ppermute | solution.py:508
  26.0 0.7 %collective-permute-start.6 = (bf16[720,128]{1,0:T(8,128)(2,1)S(1)}, bf16[720,128]{1,0:T(8,128)(2,1)S(1)}, u32[]{:S(2)}, u32[]{:S(2)}) collective-permute-start(bf16[720,128]{1,0:T(8,128)(2,1)S(1)} %get-tuple-element.39), channel_id=1, source_target_pairs={{1,2},{2,1},{3,4},{4,3},{5,6},{6,5},{7,8},{8,7},{9,10},{10,9},{11,... | collective-permute-start | bytes 552968 | tf_op jit(solution)/shard_map/ppermute | solution.py:508
  26.7 6.7 %collective-permute-start.7 = (bf16[720,128]{1,0:T(8,128)(2,1)S(1)}, bf16[720,128]{1,0:T(8,128)(2,1)S(1)}, u32[]{:S(2)}, u32[]{:S(2)}) collective-permute-start(bf16[720,128]{1,0:T(8,128)(2,1)S(1)} %collective-permute-done.6.first_ref.refs_5_), channel_id=1, source_target_pairs={{0,1},{1,0},{2,3},{3,2},{4,5},{5,4},{6,7},{7,6},{8,9},{9,8},{10,11... | collective-permute-start | bytes 552968 | tf_op jit(solution)/shard_map/ppermute | solution.py:508
  33.4 1.1 %collective-permute-done.7.second_ref.refs_6_ = bf16[720,128]{1,0:T(8,128)(2,1)S(1)} collective-permute-done((bf16[720,128]{1,0:T(8,128)(2,1)S(1)}, bf16[720,128]{1,0:T(8,128)(2,1)S(1)}, u32[]{:S(2)}, u32[]{:S(2)}) %collective-permute-start.7) | collective-permute-done | bytes 184352 | tf_op jit(solution)/shard_map/ppermute | solution.py:508
  34.5 3.7 %collective-permute-start.9 = (f32[128,128]{1,0:T(8,128)S(1)}, f32[128,128]{1,0:T(8,128)S(1)}, u32[]{:S(2)}, u32[]{:S(2)}) collective-permute-start(f32[128,128]{1,0:T(8,128)S(1)} %shard_map.152), channel_id=1, source_target_pairs={{0,4},{1,5},{2,6},{3,7},{4,0},{5,1},{6,2},{7,3},{8,12},{9,13},{10,... | collective-permute-start | bytes 196616 | tf_op jit(solution)/shard_map/ppermute | solution.py:508
  38.1 0.7 %collective-permute-start.8 = (bf16[128,128]{1,0:T(8,128)(2,1)S(1)}, bf16[128,128]{1,0:T(8,128)(2,1)S(1)}, u32[]{:S(2)}, u32[]{:S(2)}) collective-permute-start(bf16[128,128]{1,0:T(8,128)(2,1)S(1)} %get-tuple-element.42), channel_id=1, source_target_pairs={{1,4},{3,6},{4,1},{5,8},{6,3},{7,10},{8,5},{9,12},{10,7},{11,14},{... | collective-permute-start | bytes 98312 | tf_op jit(solution)/shard_map/ppermute | solution.py:508
  38.8 1.7 %collective-permute-done.9 = f32[128,128]{1,0:T(8,128)S(1)} collective-permute-done((f32[128,128]{1,0:T(8,128)S(1)}, f32[128,128]{1,0:T(8,128)S(1)}, u32[]{:S(2)}, u32[]{:S(2)}) %collective-permute-start.9) | collective-permute-done | bytes 65568 | tf_op jit(solution)/shard_map/ppermute | solution.py:508
  40.6 2.7 %collective-permute-start.10 = (bf16[128,128]{1,0:T(8,128)(2,1)S(1)}, bf16[128,128]{1,0:T(8,128)(2,1)S(1)}, u32[]{:S(2)}, u32[]{:S(2)}) collective-permute-start(bf16[128,128]{1,0:T(8,128)(2,1)S(1)} %collective-permute-done.8.refs_7_), channel_id=1, source_target_pairs={{0,1},{1,0},{2,3},{3,2},{4,5},{5,4},{6,7},{7,6},{8,9},{9,8},{10,11... | collective-permute-start | bytes 98312 | tf_op jit(solution)/shard_map/ppermute | solution.py:508
  43.2 3.9 %collective-permute-start.11 = (f32[128,128]{1,0:T(8,128)S(1)}, f32[128,128]{1,0:T(8,128)S(1)}, u32[]{:S(2)}, u32[]{:S(2)}) collective-permute-start(f32[128,128]{1,0:T(8,128)S(1)} %add.6), channel_id=1, source_target_pairs={{0,8},{1,9},{2,10},{3,11},{4,12},{5,13},{6,14},{7,15},{8,0},{9,1},... | collective-permute-start | bytes 196616 | tf_op jit(solution)/shard_map/ppermute | solution.py:508
  47.1 1.7 %shard_map.153.refs_13_ = bf16[6,64,512]{2,1,0:T(8,128)(2,1)S(1)} custom-call(s32[6]{0:T(128)S(1)} %copy-done.8, s32[6,6]{1,0:T(8,128)S(1)} %copy-done.7, bf16[6,64,512]{2,1,0:T(8,128)(2,1)S(1)} %get-tuple-element.37.refs_2_, bf16[1040,128]{1,0:T(8,128)(2,1)S(1)} %get-tuple-element.38.own_ref.refs_3_, ...), custom_call_target="tpu_custom_call" | custom-call | flops 1000000000 | bytes 400000 | tf_op jit(solution)/shard_map/pallas_call | solution.py:595
  48.8 1.1 %collective-permute-done.11 = f32[128,128]{1,0:T(8,128)S(1)} collective-permute-done((f32[128,128]{1,0:T(8,128)S(1)}, f32[128,128]{1,0:T(8,128)S(1)}, u32[]{:S(2)}, u32[]{:S(2)}) %collective-permute-start.11) | collective-permute-done | bytes 65568 | tf_op jit(solution)/shard_map/ppermute | solution.py:508
  49.9 2.8 %collective-permute-start.12 = (f32[128,128]{1,0:T(8,128)S(1)}, f32[128,128]{1,0:T(8,128)S(1)}, u32[]{:S(2)}, u32[]{:S(2)}) collective-permute-start(f32[128,128]{1,0:T(8,128)S(1)} %add.7.a_ref), channel_id=1, source_target_pairs={{0,16},{1,17},{2,18},{3,19},{4,20},{5,21},{6,22},{7,23},{8,24},{9,... | collective-permute-start | bytes 196616 | tf_op jit(solution)/shard_map/ppermute | solution.py:508
  52.7 1.7 %shard_map.154.refs_13_ = bf16[6,64,512]{2,1,0:T(8,128)(2,1)S(1)} custom-call(s32[6]{0:T(128)S(1)} %copy-done.8, s32[6,6]{1,0:T(8,128)S(1)} %copy-done.7, bf16[6,64,512]{2,1,0:T(8,128)(2,1)S(1)} %get-tuple-element.37.refs_2_, bf16[1040,128]{1,0:T(8,128)(2,1)S(1)} %get-tuple-element.38.own_ref.refs_3_, ...), custom_call_target="tpu_custom_call" | custom-call | flops 1000000000 | bytes 400000 | tf_op jit(solution)/shard_map/pallas_call | solution.py:595
  54.4 2.4 %shard_map.155 = bf16[6,64,512]{2,1,0:T(8,128)(2,1)} custom-call(s32[6]{0:T(128)S(1)} %copy-done.8, s32[6,6]{1,0:T(8,128)S(1)} %copy-done.7, bf16[6,64,512]{2,1,0:T(8,128)(2,1)S(1)} %get-tuple-element.37.refs_2_, bf16[1040,128]{1,0:T(8,128)(2,1)S(1)} %get-tuple-element.38.own_ref.refs_3_, bf16[1040,128]{1,0:T(8,128)(2,1)S(1)} %collective-permute-done.5.mate_ref.refs_4_, ...), custom_call_target="tpu_custom_call" | custom-call | flops 1000000000 | bytes 400000 | tf_op jit(solution)/shard_map/pallas_call | solution.py:595
  56.9 0.7 %shard_map.156 = (f32[216,64]{1,0:T(8,128)}, f32[1,64]{1,0:T(1,128)}) custom-call(f32[128,128]{1,0:T(8,128)S(1)} %add.7.a_ref, f32[128,128]{1,0:T(8,128)S(1)} %collective-permute-done.12.b_ref), custom_call_target="tpu_custom_call" | custom-call | bytes 400000 | tf_op jit(solution)/shard_map/pallas_call | solution.py:625
  (42 shorter events, 1.3 us)
Async XLA Ops:
  2.8 1.8 %collective-permute-start = (bf16[784,128]{1,0:T(8,128)(2,1)}, bf16[784,128]{1,0:T(8,128)(2,1)S(1)}, u32[]{:S(2)}, u32[]{:S(2)}) collective-permute-start(bf16[784,128]{1,0:T(8,128)(2,1)} %shard_map.147.own_ref), channel_id=1, source_target_pairs={{0,1},{1,0},{2,3},{3,2},{4,5},{5,4},{6,7},{7,6},{8,9},{9,8},{10,11... | collective-permute-start | bytes 602120 | tf_op jit(solution)/shard_map/ppermute | solution.py:508
  5.8 2.0 %collective-permute-start.1 = (bf16[464,128]{1,0:T(8,128)(2,1)S(1)}, bf16[464,128]{1,0:T(8,128)(2,1)S(1)}, u32[]{:S(2)}, u32[]{:S(2)}) collective-permute-start(bf16[464,128]{1,0:T(8,128)(2,1)S(1)} %get-tuple-element.29), channel_id=1, source_target_pairs={{1,2},{2,1},{3,4},{4,3},{5,6},{6,5},{7,8},{8,7},{9,10},{10,9},{11,... | collective-permute-start | bytes 356360 | tf_op jit(solution)/shard_map/ppermute | solution.py:508
  6.4 1.3 %collective-permute-start.2 = (bf16[128,128]{1,0:T(8,128)(2,1)S(1)}, bf16[128,128]{1,0:T(8,128)(2,1)S(1)}, u32[]{:S(2)}, u32[]{:S(2)}) collective-permute-start(bf16[128,128]{1,0:T(8,128)(2,1)S(1)} %get-tuple-element.30), channel_id=1, source_target_pairs={{1,4},{3,6},{4,1},{5,8},{6,3},{7,10},{8,5},{9,12},{10,7},{11,14},{... | collective-permute-start | bytes 98312 | tf_op jit(solution)/shard_map/ppermute | solution.py:508
  7.1 10.0 %copy-start = (bf16[4,256,1024]{2,1,0:T(8,128)(2,1)S(1)}, bf16[4,256,1024]{2,1,0:T(8,128)(2,1)}, u32[]{:S(2)}) copy-start(bf16[4,256,1024]{2,1,0:T(8,128)(2,1)} %constant.13.clone.shifts_ref.refs_12_) | copy-start | bytes 6291460
  7.1 10.0 %copy-start.1 = (bf16[4,384,128]{2,1,0:T(8,128)(2,1)S(1)}, bf16[4,384,128]{2,1,0:T(8,128)(2,1)}, u32[]{:S(2)}) copy-start(bf16[4,384,128]{2,1,0:T(8,128)(2,1)} %constant.12.clone.ends_ref.refs_11_) | copy-start | bytes 1179652
  7.1 10.0 %copy-start.2 = (bf16[256,512]{1,0:T(8,128)(2,1)S(1)}, bf16[256,512]{1,0:T(8,128)(2,1)}, u32[]{:S(2)}) copy-start(bf16[256,512]{1,0:T(8,128)(2,1)} %constant.11.clone.spread_ref.refs_10_) | copy-start | bytes 786436
  7.2 10.0 %copy-start.3 = (bf16[4,512,128]{2,1,0:T(8,128)(2,1)S(1)}, bf16[4,512,128]{2,1,0:T(8,128)(2,1)}, u32[]{:S(2)}) copy-start(bf16[4,512,128]{2,1,0:T(8,128)(2,1)} %constant.10.clone.strips_hbm.strips_ref) | copy-start | bytes 1572868
  7.2 10.0 %copy-start.4 = (bf16[6,64,512]{2,1,0:T(8,128)(2,1)S(1)}, bf16[6,64,512]{2,1,0:T(8,128)(2,1)}, u32[]{:S(2)}) copy-start(bf16[6,64,512]{2,1,0:T(8,128)(2,1)} %field_ref.1) | copy-start | bytes 1179652
  7.2 10.0 %copy-start.6 = (bf16[784,128]{1,0:T(8,128)(2,1)S(1)}, bf16[784,128]{1,0:T(8,128)(2,1)}, u32[]{:S(2)}) copy-start(bf16[784,128]{1,0:T(8,128)(2,1)} %shard_map.147.own_ref) | copy-start | bytes 602116
  7.2 10.0 %copy-start.7 = (s32[6,6]{1,0:T(8,128)S(1)}, s32[6,6]{1,0:T(8,128)}, u32[]{:S(2)}) copy-start(s32[6,6]{1,0:T(8,128)} %refs_1_.5) | copy-start | bytes 436
  7.2 10.0 %copy-start.8 = (s32[6]{0:T(128)S(1)}, s32[6]{0:T(128)}, u32[]{:S(2)}) copy-start(s32[6]{0:T(128)} %refs_0_.5) | copy-start | bytes 76
  7.2 10.0 %copy-start.9 = (bf16[6,64,512]{2,1,0:T(8,128)(2,1)S(1)}, bf16[6,64,512]{2,1,0:T(8,128)(2,1)}, u32[]{:S(2)}) copy-start(bf16[6,64,512]{2,1,0:T(8,128)(2,1)} %upstream_ref.1) | copy-start | bytes 1179652
  7.2 10.0 %copy-start.11 = (s32[6,512]{1,0:T(8,128)S(1)}, s32[6,512]{1,0:T(8,128)}, u32[]{:S(2)}) copy-start(s32[6,512]{1,0:T(8,128)} %cortex_ref.1) | copy-start | bytes 36868
  7.2 9.9 %copy-start.12 = (f32[64]{0:T(128)S(1)}, f32[64]{0:T(128)}, u32[]{:S(2)}) copy-start(f32[64]{0:T(128)} %param.14) | copy-start | bytes 772
  7.8 9.3 %collective-permute-start.3 = (bf16[464,128]{1,0:T(8,128)(2,1)S(1)}, bf16[464,128]{1,0:T(8,128)(2,1)S(1)}, u32[]{:S(2)}, u32[]{:S(2)}) collective-permute-start(bf16[464,128]{1,0:T(8,128)(2,1)S(1)} %collective-permute-done.1.first_ref), channel_id=1, source_target_pairs={{0,1},{1,0},{2,3},{3,2},{4,5},{5,4},{6,7},{7,6},{8,9},{9,8},{10,11... | collective-permute-start | bytes 356360 | tf_op jit(solution)/shard_map/ppermute | solution.py:508
  15.9 1.2 %collective-permute-start.4 = (bf16[128,128]{1,0:T(8,128)(2,1)S(1)}, bf16[128,128]{1,0:T(8,128)(2,1)S(1)}, u32[]{:S(2)}, u32[]{:S(2)}) collective-permute-start(bf16[128,128]{1,0:T(8,128)(2,1)S(1)} %collective-permute-done.2.first_far_ref), channel_id=1, source_target_pairs={{0,1},{1,0},{2,3},{3,2},{4,5},{5,4},{6,7},{7,6},{8,9},{9,8},{10,11... | collective-permute-start | bytes 98312 | tf_op jit(solution)/shard_map/ppermute | solution.py:508
  24.1 1.6 %collective-permute-start.5 = (bf16[1040,128]{1,0:T(8,128)(2,1)S(1)}, bf16[1040,128]{1,0:T(8,128)(2,1)S(1)}, u32[]{:S(2)}, u32[]{:S(2)}) collective-permute-start(bf16[1040,128]{1,0:T(8,128)(2,1)S(1)} %get-tuple-element.38.own_ref.refs_3_), channel_id=1, source_target_pairs={{0,1},{1,0},{2,3},{3,2},{4,5},{5,4},{6,7},{7,6},{8,9},{9,8},{10,11... | collective-permute-start | bytes 798728 | tf_op jit(solution)/shard_map/ppermute | solution.py:508
  26.0 0.7 %collective-permute-start.6 = (bf16[720,128]{1,0:T(8,128)(2,1)S(1)}, bf16[720,128]{1,0:T(8,128)(2,1)S(1)}, u32[]{:S(2)}, u32[]{:S(2)}) collective-permute-start(bf16[720,128]{1,0:T(8,128)(2,1)S(1)} %get-tuple-element.39), channel_id=1, source_target_pairs={{1,2},{2,1},{3,4},{4,3},{5,6},{6,5},{7,8},{8,7},{9,10},{10,9},{11,... | collective-permute-start | bytes 552968 | tf_op jit(solution)/shard_map/ppermute | solution.py:508
  26.7 7.8 %collective-permute-start.7 = (bf16[720,128]{1,0:T(8,128)(2,1)S(1)}, bf16[720,128]{1,0:T(8,128)(2,1)S(1)}, u32[]{:S(2)}, u32[]{:S(2)}) collective-permute-start(bf16[720,128]{1,0:T(8,128)(2,1)S(1)} %collective-permute-done.6.first_ref.refs_5_), channel_id=1, source_target_pairs={{0,1},{1,0},{2,3},{3,2},{4,5},{5,4},{6,7},{7,6},{8,9},{9,8},{10,11... | collective-permute-start | bytes 552968 | tf_op jit(solution)/shard_map/ppermute | solution.py:508
  34.5 6.1 %collective-permute-start.9 = (f32[128,128]{1,0:T(8,128)S(1)}, f32[128,128]{1,0:T(8,128)S(1)}, u32[]{:S(2)}, u32[]{:S(2)}) collective-permute-start(f32[128,128]{1,0:T(8,128)S(1)} %shard_map.152), channel_id=1, source_target_pairs={{0,4},{1,5},{2,6},{3,7},{4,0},{5,1},{6,2},{7,3},{8,12},{9,13},{10,... | collective-permute-start | bytes 196616 | tf_op jit(solution)/shard_map/ppermute | solution.py:508
  38.1 2.4 %collective-permute-start.8 = (bf16[128,128]{1,0:T(8,128)(2,1)S(1)}, bf16[128,128]{1,0:T(8,128)(2,1)S(1)}, u32[]{:S(2)}, u32[]{:S(2)}) collective-permute-start(bf16[128,128]{1,0:T(8,128)(2,1)S(1)} %get-tuple-element.42), channel_id=1, source_target_pairs={{1,4},{3,6},{4,1},{5,8},{6,3},{7,10},{8,5},{9,12},{10,7},{11,14},{... | collective-permute-start | bytes 98312 | tf_op jit(solution)/shard_map/ppermute | solution.py:508
  40.6 6.6 %collective-permute-start.10 = (bf16[128,128]{1,0:T(8,128)(2,1)S(1)}, bf16[128,128]{1,0:T(8,128)(2,1)S(1)}, u32[]{:S(2)}, u32[]{:S(2)}) collective-permute-start(bf16[128,128]{1,0:T(8,128)(2,1)S(1)} %collective-permute-done.8.refs_7_), channel_id=1, source_target_pairs={{0,1},{1,0},{2,3},{3,2},{4,5},{5,4},{6,7},{7,6},{8,9},{9,8},{10,11... | collective-permute-start | bytes 98312 | tf_op jit(solution)/shard_map/ppermute | solution.py:508
  43.2 6.7 %collective-permute-start.11 = (f32[128,128]{1,0:T(8,128)S(1)}, f32[128,128]{1,0:T(8,128)S(1)}, u32[]{:S(2)}, u32[]{:S(2)}) collective-permute-start(f32[128,128]{1,0:T(8,128)S(1)} %add.6), channel_id=1, source_target_pairs={{0,8},{1,9},{2,10},{3,11},{4,12},{5,13},{6,14},{7,15},{8,0},{9,1},... | collective-permute-start | bytes 196616 | tf_op jit(solution)/shard_map/ppermute | solution.py:508
  49.9 7.0 %collective-permute-start.12 = (f32[128,128]{1,0:T(8,128)S(1)}, f32[128,128]{1,0:T(8,128)S(1)}, u32[]{:S(2)}, u32[]{:S(2)}) collective-permute-start(f32[128,128]{1,0:T(8,128)S(1)} %add.7.a_ref), channel_id=1, source_target_pairs={{0,16},{1,17},{2,18},{3,19},{4,20},{5,21},{6,22},{7,23},{8,24},{9,... | collective-permute-start | bytes 196616 | tf_op jit(solution)/shard_map/ppermute | solution.py:508
  (3 other events, 17.4 us)

commit v5 on v4

--- a/solution.py
+++ b/solution.py
@@ -19,7 +19,7 @@
 EDGE = 3
 BUSY = 10**10
 HEAD = 16
-NEAR_ROWS = (NEAR // 2 + EDGE) * CH + HEAD
+NEAR_ROWS = (NEAR // 2 + 2) * CH + HEAD
 SUM_ROWS = 128
 BF = jnp.bfloat16
 F32 = jnp.float32
@@ -161,10 +161,12 @@
         near_ref[j // 2 * CH : (j // 2 + 1) * CH, :] = both
         if j < FAR:
             far_ref[j // 2 * CH : (j // 2 + 1) * CH, :] = both
-    for j in range(EDGE):
-        row = (NEAR // 2 + j) * CH
-        near_ref[row : row + CH, :] = box[2 * place(j)]
-    row = (NEAR // 2 + EDGE) * CH
+    of_y = lax.broadcasted_iota(jnp.int32, (CH, TILE), 1) % 64 < 32
+    row = NEAR // 2 * CH
+    near_ref[row : row + CH, :] = box[2 * place(0)]
+    first, second = [box[2 * place(j)].astype(F32) for j in (1, 2)]
+    near_ref[row + CH : row + 2 * CH, :] = jnp.where(of_y, first, pltpu.roll(second, 32, 1)).astype(BF)
+    row = (NEAR // 2 + 2) * CH
     both = (mine + other).astype(F32)
     near_ref[row : row + HEAD, :] = jnp.full((HEAD, TILE), both, F32).astype(BF)
 
@@ -182,21 +184,12 @@
         parts.append(
             ref[high : high + SUM_ROWS, :].astype(F32) + ref[low : low + SUM_ROWS, :].astype(F32)
         )
-    total = parts[0] + parts[1]
-    rounded = total.astype(BF)
-    rest = (total - rounded.astype(F32)).astype(BF)
-    near_ref[NEAR_ROWS : NEAR_ROWS + SUM_ROWS, :] = rounded
-    near_ref[NEAR_ROWS + SUM_ROWS :, :] = rest
-    sum_ref[...] = rounded.astype(F32) + rest.astype(F32)
-
-
-def join_kernel(sum_ref, first_ref, second_ref, out_ref):
-    device = lax.axis_index("bricks")
-    itself = (device & 1) != ((device >> 1) & 1)
-    high = slice(NEAR_ROWS, NEAR_ROWS + SUM_ROWS)
-    low = slice(NEAR_ROWS + SUM_ROWS, NEAR_ROWS + 2 * SUM_ROWS)
-    parts = [ref[high, :].astype(F32) + ref[low, :].astype(F32) for ref in (first_ref, second_ref)]
-    out_ref[...] = sum_ref[...] + jnp.where(itself, parts[0], parts[1])
+    sum_ref[...] = parts[0] + parts[1]
+
+
+def merge_kernel(near_ref, far_ref, out_ref):
+    out_ref[0:NEAR_ROWS, :] = near_ref[...]
+    out_ref[NEAR_ROWS:, :] = far_ref[...]
 
 
 def weight_kernel(taps_ref, forward_ref, backward_ref, work):
@@ -225,7 +218,7 @@
 
 
 def make_finder(
-    slot_hbm, link_hbm, own_ref, mate_ref, first_ref, second_ref, first_far_ref, second_far_ref,
+    slot_hbm, link_hbm, own_ref, mate_ref, first_ref, second_ref,
     planes, strips, slot_ref, link_ref, sems,
 ):
     copies = bring(((slot_hbm, slot_ref), (link_hbm, link_ref)), sems)
@@ -234,21 +227,24 @@
     head = slots * 2 * CH
     mine = count_sent(own_ref[head : head + HEAD, :])
     other = count_sent(mate_ref[head : head + HEAD, :])
-    row = (NEAR // 2 + EDGE) * CH
+    row = (NEAR // 2 + 2) * CH
     counts = [count_sent(ref[row : row + HEAD, :]) for ref in (first_ref, second_ref)]
     for k, ref in enumerate((own_ref, mate_ref)):
         for s in range(slots):
             strips[k * slots + s] = ref[s * 2 * CH : s * 2 * CH + CH, :]
             planes[k * slots + s] = ref[s * 2 * CH + CH : (s + 1) * 2 * CH, :]
-    for side, (near, far) in enumerate(((first_ref, first_far_ref), (second_ref, second_far_ref))):
-        for start, ref, count in ((side * NEAR, near, NEAR), (2 * NEAR + side * FAR, far, FAR)):
+    for side, near in enumerate((first_ref, second_ref)):
+        for start, begin, count in ((side * NEAR, 0, NEAR), (2 * NEAR + side * FAR, NEAR_ROWS, FAR)):
             for j in range(0, count, 2):
-                tile = ref[j // 2 * CH : (j // 2 + 1) * CH, :]
+                row = begin + j // 2 * CH
+                tile = near[row : row + CH, :]
                 planes[2 * slots + start + j] = tile
                 planes[2 * slots + start + j + 1] = pltpu.roll(tile.astype(F32), 64, 1).astype(BF)
-        for j in range(EDGE):
-            row = (NEAR // 2 + j) * CH
-            strips[2 * slots + side * EDGE + j] = near[row : row + CH, :]
+        row, at = NEAR // 2 * CH, 2 * slots + side * EDGE
+        strips[at] = near[row : row + CH, :]
+        tile = near[row + CH : row + 2 * CH, :]
+        strips[at + 1] = tile
+        strips[at + 2] = pltpu.roll(tile.astype(F32), TILE - 32, 1).astype(BF)
     nothing = 2 * slots + 2 * NEAR + 2 * FAR
     planes[nothing] = jnp.zeros((CH, TILE), BF)
     for copy in copies:
@@ -364,14 +360,13 @@
 
 
 def forward_kernel(
-    slot_hbm, link_hbm, field_ref, own_ref, mate_ref, first_ref, second_ref, first_far_ref,
-    second_far_ref, weight_ref, bias_ref, cortex_ref, upstream_ref, strips_ref, spread_ref,
+    slot_hbm, link_hbm, field_ref, own_ref, mate_ref, first_ref, second_ref, weight_ref, bias_ref, cortex_ref, upstream_ref, strips_ref, spread_ref,
     ends_ref, shifts_ref, fold_ref, out_ref, dpre_ref, msg_ref,
     planes, strips, mixed, taps, sums, slot_ref, link_ref, sems, spots, grads,
 ):
     slots = field_ref.shape[0]
     base, mine, find_strip, find_plane = make_finder(
-        slot_hbm, link_hbm, own_ref, mate_ref, first_ref, second_ref, first_far_ref, second_far_ref,
+        slot_hbm, link_hbm, own_ref, mate_ref, first_ref, second_ref,
         planes, strips, slot_ref, link_ref, sems,
     )
     for pair in range(slots // 2):
@@ -451,19 +446,18 @@
     if pairs[0] == 0:
         backward_body(pairs, *refs)
         return
-    last_ref, out_ref = refs[13], refs[14]
+    last_ref, out_ref = refs[11], refs[12]
     for s in range(2 * pairs[0]):
         out_ref[s] = last_ref[s]
-    backward_body(pairs, *refs[:13], *refs[14:])
+    backward_body(pairs, *refs[:11], *refs[12:])
 
 
 def backward_body(
-    pairs, slot_hbm, link_hbm, field_ref, own_ref, mate_ref, first_ref, second_ref, first_far_ref,
-    second_far_ref, weight_ref, spread_ref, ends_ref, shifts_ref, out_ref,
+    pairs, slot_hbm, link_hbm, field_ref, own_ref, mate_ref, first_ref, second_ref, weight_ref, spread_ref, ends_ref, shifts_ref, out_ref,
     planes, strips, mixed, taps, sums, slot_ref, link_ref, sems,
 ):
     base, mine, find_strip, find_plane = make_finder(
-        slot_hbm, link_hbm, own_ref, mate_ref, first_ref, second_ref, first_far_ref, second_far_ref,
+        slot_hbm, link_hbm, own_ref, mate_ref, first_ref, second_ref,
         planes, strips, slot_ref, link_ref, sems,
     )
     for pair in pairs:
@@ -516,7 +510,6 @@
     shape = jax.ShapeDtypeStruct
     pack_rows = slots * 2 * CH + HEAD
     near_shape = shape((NEAR_ROWS, TILE), BF)
-    near_sum_shape = shape((NEAR_ROWS + 2 * SUM_ROWS, TILE), BF)
     far_shape = shape((FAR // 2 * CH, TILE), BF)
 
     def routed(block, chips):
@@ -529,6 +522,10 @@
 
     def swapped(block, mask):
         return sent(block, [(d, d ^ mask) for d in range(devices)])
+
+    def merged(near, far):
+        rows = near.shape[0] + far.shape[0]
+        return call(merge_kernel, [VMEM] * 2, [shape((rows, TILE), BF)])(near, far)[0]
 
     box = [pltpu.VMEM((4 * slots, CH, TILE), BF)]
     work = [
@@ -560,13 +557,14 @@
         functools.partial(route_kernel, slots), [VMEM, VMEM], [near_shape, far_shape], box,
         flops=BUSY,
     )(own, mate)
-    far, near = routed(far, 2), routed(near, 1)
+    near, far = routed(near, 1), routed(far, 2)
     near, far, staged = lax.optimization_barrier((near, far, staged))
     forward, backward = staged
-    received = (near, swapped(near, 1), far, swapped(far, 1))
+    first = merged(near, far)
+    second = swapped(first, 1)
     activated, dpre, own = call(
         forward_kernel,
-        [HBM, HBM] + [VMEM] * 16,
+        [HBM, HBM] + [VMEM] * 14,
         [field, field, shape((pack_rows + 2 * SUM_ROWS, TILE), BF)],
         work
         + [
@@ -575,50 +573,45 @@
         ],
         flops=4 * 10**9,
     )(
-        slot_to_brick, neighbors, voxels, own, mate, *received, forward, bias.reshape(1, CH),
+        slot_to_brick, neighbors, voxels, own, mate, first, second, forward, bias.reshape(1, CH),
         cortex, cotangent, strips, spread, ends, shifts, fold,
     )
     mate = swapped(own, 1)
     near, far, total = call(
         functools.partial(route_sum_kernel, slots),
         [VMEM, VMEM],
-        [near_sum_shape, far_shape, shape((SUM_ROWS, TILE), F32)],
+        [near_shape, far_shape, shape((SUM_ROWS, TILE), F32)],
         box,
     )(own, mate)
-    near = routed(near, 1)
-    second = swapped(near, 1)
-    (total,) = call(join_kernel, [VMEM] * 3, [shape((SUM_ROWS, TILE), F32)])(total, near, second)
     state = {}
 
     def part_backward(pair):
         last = [state["grad"]] if pair else []
         (state["grad"],) = call(
             functools.partial(backward_kernel, (pair,)),
-            [HBM, HBM] + [VMEM] * (11 + len(last)),
+            [HBM, HBM] + [VMEM] * (9 + len(last)),
             [field],
             work,
             flops=10**9,
         )(
-            slot_to_brick, neighbors, dpre, own, mate, near, second, far, second_far,
-            backward, spread, ends, shifts, *last,
+            slot_to_brick, neighbors, dpre, own, mate, state["first"], state["second"], backward,
+            spread, ends, shifts, *last,
         )
 
     pairs = list(range(slots // 2))
-    masks = [2**p for p in range(2, devices.bit_length() - 1)]
-    for at, mask in enumerate(masks):
+    masks = [2**p for p in range(1, devices.bit_length() - 1)]
+    for mask in masks:
         other = swapped(total, mask)
-        if at == 0:
-            far, total = lax.optimization_barrier((far, total))
-            far = routed(far, 2)
+        if mask == masks[0]:
+            state["near"], state["far"] = routed(near, 1), routed(far, 2)
         elif pairs:
-            if at == 1:
-                second_far = swapped(far, 1)
+            if mask == masks[1]:
+                state["first"] = merged(state.pop("near"), state.pop("far"))
+                state["second"] = swapped(state["first"], 1)
             part_backward(pairs.pop(0))
         if mask != masks[-1]:
             total, other, state = lax.optimization_barrier((total, other, state))
             total = total + other
-            if at == 0:
-                far, total = lax.optimization_barrier((far, total))
     for pair in pairs:
         part_backward(pair)
     input_grad = state["grad"]

time: 57.9 us -> 54 us (0.933)
  starting transfers between devices: 31.3 us -> 26 us
  waiting for transfers between devices: 7.72 us -> 9.26 us
    ppermute x13 -> x12, starting transfers between devices: 31.3 us -> 26 us  [sent(): return lax.ppermute(block, 'bricks', route)]
    ppermute x13 -> x12, waiting for transfers between devices: 7.72 us -> 9.26 us  [sent(): return lax.ppermute(block, 'bricks', route)]
    pallas_call x3 -> x4, Pallas kernels: 7.16 us -> 7.19 us  [the longest x1 6.94 us: shards(): call(forward_kernel, [HBM, HBM] + [VMEM] * 14, [field, field, shape((pack...]
  transfers between devices with their start and end apart: 13 -> 12, of which waited for: 6 -> 6; matrix products, arithmetic and copies ran while one was open for 0% -> 0% of each run, Pallas kernels for 11% -> 12%
where the time goes in v5:
time: 54 us; the launch traced here: 53.7 us
  starting transfers between devices  26 us (48%)
  Pallas kernels  16.5 us (31%)
  waiting for transfers between devices  9.26 us (17%)
  local copies, waits for them, and re-layouts  1.01 us (2%)
  between operations  0.96 us (2%)
    ppermute x12, starting transfers between devices, sent(): return lax.ppermute(block, 'bricks', route)  26 us
    ppermute x12, waiting for transfers between devices, sent(): return lax.ppermute(block, 'bricks', route)  9.26 us
    pallas_call x1, Pallas kernels, shards(): call(forward_kernel, [HBM, HBM] + [VMEM] * 14, [field, field, shape((pack...  6.94 us
    pallas_call x3, Pallas kernels, part_backward(): call(functools.partial(backward_kernel, (pair,)), [HBM, HBM] + [VMEM] * (...  5.73 us
    pallas_call x1, Pallas kernels, shards(): call(pack_kernel, [HBM] * 3, [shape((pack_rows, TILE), BF)], [pltpu.VMEM(...  2.15 us
  transfers between devices with their start and end apart: 12, of which 6 were waited for; matrix products, arithmetic and copies ran while one was open for 0% of the time, Pallas kernels for 12%

profile of v5, /device:TPU:0, one launch (start us, length us, event | category | flops | bytes accessed | tf_op | source)
XLA Modules:
  0.0 53.7 jit_solution(17008387875418865651)
XLA Ops:
  0.6 2.2 %shard_map.147.own_ref = bf16[784,128]{1,0:T(8,128)(2,1)} custom-call(s32[6]{0:T(128)} %refs_0_.5, bf16[6,64,512]{2,1,0:T(8,128)(2,1)} %field_ref.1, bf16[4,512,128]{2,1,0:T(8,128)(2,1)} %constant.10.clone.strips_hbm.strips_ref), custom_call_target="tpu_custom_call" | custom-call | bytes 400000 | tf_op jit(solution)/shard_map/pallas_call | solution.py:543
  2.8 0.5 collective-permute-start
  3.3 1.3 %collective-permute-done.mate_ref = bf16[784,128]{1,0:T(8,128)(2,1)S(1)} collective-permute-done((bf16[784,128]{1,0:T(8,128)(2,1)}, bf16[784,128]{1,0:T(8,128)(2,1)S(1)}, u32[]{:S(2)}, u32[]{:S(2)}) %collective-permute-start) | collective-permute-done | bytes 200736 | tf_op jit(solution)/shard_map/ppermute | solution.py:502
  4.6 0.9 %copy-done.5 = bf16[784,128]{1,0:T(8,128)(2,1)S(1)} copy-done((bf16[784,128]{1,0:T(8,128)(2,1)S(1)}, bf16[784,128]{1,0:T(8,128)(2,1)}, u32[]{:S(2)}) %copy-start.5) | copy-done | bytes 200728
  5.8 0.7 %collective-permute-start.2 = (bf16[128,128]{1,0:T(8,128)(2,1)S(1)}, bf16[128,128]{1,0:T(8,128)(2,1)S(1)}, u32[]{:S(2)}, u32[]{:S(2)}) collective-permute-start(bf16[128,128]{1,0:T(8,128)(2,1)S(1)} %get-tuple-element.35), channel_id=1, source_target_pairs={{1,4},{3,6},{4,1},{5,8},{6,3},{7,10},{8,5},{9,12},{10,7},{11,14},{... | collective-permute-start | bytes 98312 | tf_op jit(solution)/shard_map/ppermute | solution.py:502
  6.4 0.7 %collective-permute-start.1 = (bf16[400,128]{1,0:T(8,128)(2,1)S(1)}, bf16[400,128]{1,0:T(8,128)(2,1)S(1)}, u32[]{:S(2)}, u32[]{:S(2)}) collective-permute-start(bf16[400,128]{1,0:T(8,128)(2,1)S(1)} %get-tuple-element.34), channel_id=1, source_target_pairs={{1,2},{2,1},{3,4},{4,3},{5,6},{6,5},{7,8},{8,7},{9,10},{10,9},{11,... | collective-permute-start | bytes 307208 | tf_op jit(solution)/shard_map/ppermute | solution.py:502
  7.8 9.2 %collective-permute-start.3 = (bf16[528,128]{1,0:T(8,128)(2,1)S(1)}, bf16[528,128]{1,0:T(8,128)(2,1)S(1)}, u32[]{:S(2)}, u32[]{:S(2)}) collective-permute-start(bf16[528,128]{1,0:T(8,128)(2,1)S(1)} %shard_map.150.first_ref), channel_id=1, source_target_pairs={{0,1},{1,0},{2,3},{3,2},{4,5},{5,4},{6,7},{7,6},{8,9},{9,8},{10,11... | collective-permute-start | bytes 405512 | tf_op jit(solution)/shard_map/ppermute | solution.py:502
  17.0 1.0 %collective-permute-done.3.second_ref = bf16[528,128]{1,0:T(8,128)(2,1)S(1)} collective-permute-done((bf16[528,128]{1,0:T(8,128)(2,1)S(1)}, bf16[528,128]{1,0:T(8,128)(2,1)S(1)}, u32[]{:S(2)}, u32[]{:S(2)}) %collective-permute-start.3) | collective-permute-done | bytes 135200 | tf_op jit(solution)/shard_map/ppermute | solution.py:502
  18.1 6.9 %shard_map.151 = (bf16[6,64,512]{2,1,0:T(8,128)(2,1)}, bf16[6,64,512]{2,1,0:T(8,128)(2,1)S(1)}, bf16[1040,128]{1,0:T(8,128)(2,1)S(1)}) custom-call(s32[6]{0:T(128)S(1)} %copy-done.8, s32[6,6]{1,0:T(8,128)S(1)} %copy-done.7, bf16[6,64,512]{2,1,0:T(8,128)(2,1)S(1)} %copy-done.4, bf16[784,128]{1,0:T(8,128)(2,1)S(1)} %copy-done.6, ...), custom_call_target="tpu_custom_call" | custom-call | flops 4000000000 | bytes 400000 | tf_op jit(solution)/shard_map/pallas_call | solution.py:565
  25.5 1.2 %collective-permute-done.4.mate_ref.refs_4_ = bf16[1040,128]{1,0:T(8,128)(2,1)S(1)} collective-permute-done((bf16[1040,128]{1,0:T(8,128)(2,1)S(1)}, bf16[1040,128]{1,0:T(8,128)(2,1)S(1)}, u32[]{:S(2)}, u32[]{:S(2)}) %collective-permute-start.4) | collective-permute-done | bytes 266272 | tf_op jit(solution)/shard_map/ppermute | solution.py:502
  26.9 0.7 %collective-permute-start.7 = (bf16[400,128]{1,0:T(8,128)(2,1)S(1)}, bf16[400,128]{1,0:T(8,128)(2,1)S(1)}, u32[]{:S(2)}, u32[]{:S(2)}) collective-permute-start(bf16[400,128]{1,0:T(8,128)(2,1)S(1)} %get-tuple-element.46), channel_id=1, source_target_pairs={{1,2},{2,1},{3,4},{4,3},{5,6},{6,5},{7,8},{8,7},{9,10},{10,9},{11,... | collective-permute-start | bytes 307208 | tf_op jit(solution)/shard_map/ppermute | solution.py:502
  27.6 3.4 %collective-permute-start.5 = (f32[128,128]{1,0:T(8,128)S(1)}, f32[128,128]{1,0:T(8,128)S(1)}, u32[]{:S(2)}, u32[]{:S(2)}) collective-permute-start(f32[128,128]{1,0:T(8,128)S(1)} %get-tuple-element.47), channel_id=1, source_target_pairs={{0,2},{1,3},{2,0},{3,1},{4,6},{5,7},{6,4},{7,5},{8,10},{9,11},{10,... | collective-permute-start | bytes 196616 | tf_op jit(solution)/shard_map/ppermute | solution.py:502
  31.0 0.7 %collective-permute-start.6 = (bf16[128,128]{1,0:T(8,128)(2,1)S(1)}, bf16[128,128]{1,0:T(8,128)(2,1)S(1)}, u32[]{:S(2)}, u32[]{:S(2)}) collective-permute-start(bf16[128,128]{1,0:T(8,128)(2,1)S(1)} %get-tuple-element.45), channel_id=1, source_target_pairs={{1,4},{3,6},{4,1},{5,8},{6,3},{7,10},{8,5},{9,12},{10,7},{11,14},{... | collective-permute-start | bytes 98312 | tf_op jit(solution)/shard_map/ppermute | solution.py:502
  31.7 4.4 %collective-permute-done.5 = f32[128,128]{1,0:T(8,128)S(1)} collective-permute-done((f32[128,128]{1,0:T(8,128)S(1)}, f32[128,128]{1,0:T(8,128)S(1)}, u32[]{:S(2)}, u32[]{:S(2)}) %collective-permute-start.5) | collective-permute-done | bytes 65568 | tf_op jit(solution)/shard_map/ppermute | solution.py:502
  36.1 1.1 %collective-permute-start.9 = (bf16[528,128]{1,0:T(8,128)(2,1)S(1)}, bf16[528,128]{1,0:T(8,128)(2,1)S(1)}, u32[]{:S(2)}, u32[]{:S(2)}) collective-permute-start(bf16[528,128]{1,0:T(8,128)(2,1)S(1)} %shard_map.153.refs_5_), channel_id=1, source_target_pairs={{0,1},{1,0},{2,3},{3,2},{4,5},{5,4},{6,7},{7,6},{8,9},{9,8},{10,11... | collective-permute-start | bytes 405512 | tf_op jit(solution)/shard_map/ppermute | solution.py:502
  37.1 3.9 %collective-permute-start.8 = (f32[128,128]{1,0:T(8,128)S(1)}, f32[128,128]{1,0:T(8,128)S(1)}, u32[]{:S(2)}, u32[]{:S(2)}) collective-permute-start(f32[128,128]{1,0:T(8,128)S(1)} %add.9), channel_id=1, source_target_pairs={{0,4},{1,5},{2,6},{3,7},{4,0},{5,1},{6,2},{7,3},{8,12},{9,13},{10,... | collective-permute-start | bytes 196616 | tf_op jit(solution)/shard_map/ppermute | solution.py:502
  41.0 1.6 %shard_map.154.refs_11_ = bf16[6,64,512]{2,1,0:T(8,128)(2,1)S(1)} custom-call(s32[6]{0:T(128)S(1)} %copy-done.8, s32[6,6]{1,0:T(8,128)S(1)} %copy-done.7, bf16[6,64,512]{2,1,0:T(8,128)(2,1)S(1)} %get-tuple-element.42.refs_2_, bf16[1040,128]{1,0:T(8,128)(2,1)S(1)} %get-tuple-element.43.own_ref.refs_3_, ...), custom_call_target="tpu_custom_call" | custom-call | flops 1000000000 | bytes 400000 | tf_op jit(solution)/shard_map/pallas_call | solution.py:590
  42.7 0.6 %collective-permute-done.8 = f32[128,128]{1,0:T(8,128)S(1)} collective-permute-done((f32[128,128]{1,0:T(8,128)S(1)}, f32[128,128]{1,0:T(8,128)S(1)}, u32[]{:S(2)}, u32[]{:S(2)}) %collective-permute-start.8) | collective-permute-done | bytes 65568 | tf_op jit(solution)/shard_map/ppermute | solution.py:502
  43.3 1.9 %collective-permute-start.10 = (f32[128,128]{1,0:T(8,128)S(1)}, f32[128,128]{1,0:T(8,128)S(1)}, u32[]{:S(2)}, u32[]{:S(2)}) collective-permute-start(f32[128,128]{1,0:T(8,128)S(1)} %add.10), channel_id=1, source_target_pairs={{0,8},{1,9},{2,10},{3,11},{4,12},{5,13},{6,14},{7,15},{8,0},{9,1},... | collective-permute-start | bytes 196616 | tf_op jit(solution)/shard_map/ppermute | solution.py:502
  45.2 1.7 %shard_map.155.refs_11_ = bf16[6,64,512]{2,1,0:T(8,128)(2,1)S(1)} custom-call(s32[6]{0:T(128)S(1)} %copy-done.8, s32[6,6]{1,0:T(8,128)S(1)} %copy-done.7, bf16[6,64,512]{2,1,0:T(8,128)(2,1)S(1)} %get-tuple-element.42.refs_2_, bf16[1040,128]{1,0:T(8,128)(2,1)S(1)} %get-tuple-element.43.own_ref.refs_3_, ...), custom_call_target="tpu_custom_call" | custom-call | flops 1000000000 | bytes 400000 | tf_op jit(solution)/shard_map/pallas_call | solution.py:590
  46.8 0.8 %collective-permute-done.10 = f32[128,128]{1,0:T(8,128)S(1)} collective-permute-done((f32[128,128]{1,0:T(8,128)S(1)}, f32[128,128]{1,0:T(8,128)S(1)}, u32[]{:S(2)}, u32[]{:S(2)}) %collective-permute-start.10) | collective-permute-done | bytes 65568 | tf_op jit(solution)/shard_map/ppermute | solution.py:502
  47.6 2.9 %collective-permute-start.11 = (f32[128,128]{1,0:T(8,128)S(1)}, f32[128,128]{1,0:T(8,128)S(1)}, u32[]{:S(2)}, u32[]{:S(2)}) collective-permute-start(f32[128,128]{1,0:T(8,128)S(1)} %add.11.a_ref), channel_id=1, source_target_pairs={{0,16},{1,17},{2,18},{3,19},{4,20},{5,21},{6,22},{7,23},{8,24},{9,... | collective-permute-start | bytes 196616 | tf_op jit(solution)/shard_map/ppermute | solution.py:502
  50.5 2.4 %shard_map.156 = bf16[6,64,512]{2,1,0:T(8,128)(2,1)} custom-call(s32[6]{0:T(128)S(1)} %copy-done.8, s32[6,6]{1,0:T(8,128)S(1)} %copy-done.7, bf16[6,64,512]{2,1,0:T(8,128)(2,1)S(1)} %get-tuple-element.42.refs_2_, bf16[1040,128]{1,0:T(8,128)(2,1)S(1)} %get-tuple-element.43.own_ref.refs_3_, bf16[1040,128]{1,0:T(8,128)(2,1)S(1)} %collective-permute-done.4.mate_ref.refs_4_, ...), custom_call_target="tpu_custom_call" | custom-call | flops 1000000000 | bytes 400000 | tf_op jit(solution)/shard_map/pallas_call | solution.py:590
  53.0 0.7 %shard_map.157 = (f32[216,64]{1,0:T(8,128)}, f32[1,64]{1,0:T(1,128)}) custom-call(f32[128,128]{1,0:T(8,128)S(1)} %add.11.a_ref, f32[128,128]{1,0:T(8,128)S(1)} %collective-permute-done.11.b_ref), custom_call_target="tpu_custom_call" | custom-call | bytes 400000 | tf_op jit(solution)/shard_map/pallas_call | solution.py:618
  (42 shorter events, 1.5 us)
Async XLA Ops:
  2.8 1.8 %collective-permute-start = (bf16[784,128]{1,0:T(8,128)(2,1)}, bf16[784,128]{1,0:T(8,128)(2,1)S(1)}, u32[]{:S(2)}, u32[]{:S(2)}) collective-permute-start(bf16[784,128]{1,0:T(8,128)(2,1)} %shard_map.147.own_ref), channel_id=1, source_target_pairs={{0,1},{1,0},{2,3},{3,2},{4,5},{5,4},{6,7},{7,6},{8,9},{9,8},{10,11... | collective-permute-start | bytes 602120 | tf_op jit(solution)/shard_map/ppermute | solution.py:502
  5.8 2.0 %collective-permute-start.2 = (bf16[128,128]{1,0:T(8,128)(2,1)S(1)}, bf16[128,128]{1,0:T(8,128)(2,1)S(1)}, u32[]{:S(2)}, u32[]{:S(2)}) collective-permute-start(bf16[128,128]{1,0:T(8,128)(2,1)S(1)} %get-tuple-element.35), channel_id=1, source_target_pairs={{1,4},{3,6},{4,1},{5,8},{6,3},{7,10},{8,5},{9,12},{10,7},{11,14},{... | collective-permute-start | bytes 98312 | tf_op jit(solution)/shard_map/ppermute | solution.py:502
  6.4 1.3 %collective-permute-start.1 = (bf16[400,128]{1,0:T(8,128)(2,1)S(1)}, bf16[400,128]{1,0:T(8,128)(2,1)S(1)}, u32[]{:S(2)}, u32[]{:S(2)}) collective-permute-start(bf16[400,128]{1,0:T(8,128)(2,1)S(1)} %get-tuple-element.34), channel_id=1, source_target_pairs={{1,2},{2,1},{3,4},{4,3},{5,6},{6,5},{7,8},{8,7},{9,10},{10,9},{11,... | collective-permute-start | bytes 307208 | tf_op jit(solution)/shard_map/ppermute | solution.py:502
  7.1 10.9 %copy-start = (bf16[4,256,1024]{2,1,0:T(8,128)(2,1)S(1)}, bf16[4,256,1024]{2,1,0:T(8,128)(2,1)}, u32[]{:S(2)}) copy-start(bf16[4,256,1024]{2,1,0:T(8,128)(2,1)} %constant.13.clone.shifts_ref.refs_10_) | copy-start | bytes 6291460
  7.1 10.9 %copy-start.1 = (bf16[4,384,128]{2,1,0:T(8,128)(2,1)S(1)}, bf16[4,384,128]{2,1,0:T(8,128)(2,1)}, u32[]{:S(2)}) copy-start(bf16[4,384,128]{2,1,0:T(8,128)(2,1)} %constant.12.clone.ends_ref.refs_9_) | copy-start | bytes 1179652
  7.1 10.9 %copy-start.2 = (bf16[256,512]{1,0:T(8,128)(2,1)S(1)}, bf16[256,512]{1,0:T(8,128)(2,1)}, u32[]{:S(2)}) copy-start(bf16[256,512]{1,0:T(8,128)(2,1)} %constant.11.clone.spread_ref.refs_8_) | copy-start | bytes 786436
  7.2 10.9 %copy-start.3 = (bf16[4,512,128]{2,1,0:T(8,128)(2,1)S(1)}, bf16[4,512,128]{2,1,0:T(8,128)(2,1)}, u32[]{:S(2)}) copy-start(bf16[4,512,128]{2,1,0:T(8,128)(2,1)} %constant.10.clone.strips_hbm.strips_ref) | copy-start | bytes 1572868
  7.2 10.9 %copy-start.4 = (bf16[6,64,512]{2,1,0:T(8,128)(2,1)S(1)}, bf16[6,64,512]{2,1,0:T(8,128)(2,1)}, u32[]{:S(2)}) copy-start(bf16[6,64,512]{2,1,0:T(8,128)(2,1)} %field_ref.1) | copy-start | bytes 1179652
  7.2 10.9 %copy-start.6 = (bf16[784,128]{1,0:T(8,128)(2,1)S(1)}, bf16[784,128]{1,0:T(8,128)(2,1)}, u32[]{:S(2)}) copy-start(bf16[784,128]{1,0:T(8,128)(2,1)} %shard_map.147.own_ref) | copy-start | bytes 602116
  7.2 10.8 %copy-start.7 = (s32[6,6]{1,0:T(8,128)S(1)}, s32[6,6]{1,0:T(8,128)}, u32[]{:S(2)}) copy-start(s32[6,6]{1,0:T(8,128)} %refs_1_.5) | copy-start | bytes 436
  7.2 10.8 %copy-start.8 = (s32[6]{0:T(128)S(1)}, s32[6]{0:T(128)}, u32[]{:S(2)}) copy-start(s32[6]{0:T(128)} %refs_0_.5) | copy-start | bytes 76
  7.2 10.8 %copy-start.9 = (bf16[6,64,512]{2,1,0:T(8,128)(2,1)S(1)}, bf16[6,64,512]{2,1,0:T(8,128)(2,1)}, u32[]{:S(2)}) copy-start(bf16[6,64,512]{2,1,0:T(8,128)(2,1)} %upstream_ref.1) | copy-start | bytes 1179652
  7.2 10.8 %copy-start.11 = (s32[6,512]{1,0:T(8,128)S(1)}, s32[6,512]{1,0:T(8,128)}, u32[]{:S(2)}) copy-start(s32[6,512]{1,0:T(8,128)} %cortex_ref.1) | copy-start | bytes 36868
  7.2 10.8 %copy-start.12 = (f32[64]{0:T(128)S(1)}, f32[64]{0:T(128)}, u32[]{:S(2)}) copy-start(f32[64]{0:T(128)} %param.14) | copy-start | bytes 772
  7.3 10.8 %copy-start.13 = (f32[160,80]{1,0:T(8,128)S(1)}, f32[160,80]{1,0:T(8,128)}, u32[]{:S(2)}) copy-start(f32[160,80]{1,0:T(8,128)} %constant.20.fold_ref) | copy-start | bytes 153604
  7.8 10.2 %collective-permute-start.3 = (bf16[528,128]{1,0:T(8,128)(2,1)S(1)}, bf16[528,128]{1,0:T(8,128)(2,1)S(1)}, u32[]{:S(2)}, u32[]{:S(2)}) collective-permute-start(bf16[528,128]{1,0:T(8,128)(2,1)S(1)} %shard_map.150.first_ref), channel_id=1, source_target_pairs={{0,1},{1,0},{2,3},{3,2},{4,5},{5,4},{6,7},{7,6},{8,9},{9,8},{10,11... | collective-permute-start | bytes 405512 | tf_op jit(solution)/shard_map/ppermute | solution.py:502
  25.1 1.6 %collective-permute-start.4 = (bf16[1040,128]{1,0:T(8,128)(2,1)S(1)}, bf16[1040,128]{1,0:T(8,128)(2,1)S(1)}, u32[]{:S(2)}, u32[]{:S(2)}) collective-permute-start(bf16[1040,128]{1,0:T(8,128)(2,1)S(1)} %get-tuple-element.43.own_ref.refs_3_), channel_id=1, source_target_pairs={{0,1},{1,0},{2,3},{3,2},{4,5},{5,4},{6,7},{7,6},{8,9},{9,8},{10,11... | collective-permute-start | bytes 798728 | tf_op jit(solution)/shard_map/ppermute | solution.py:502
  26.9 9.1 %collective-permute-start.7 = (bf16[400,128]{1,0:T(8,128)(2,1)S(1)}, bf16[400,128]{1,0:T(8,128)(2,1)S(1)}, u32[]{:S(2)}, u32[]{:S(2)}) collective-permute-start(bf16[400,128]{1,0:T(8,128)(2,1)S(1)} %get-tuple-element.46), channel_id=1, source_target_pairs={{1,2},{2,1},{3,4},{4,3},{5,6},{6,5},{7,8},{8,7},{9,10},{10,9},{11,... | collective-permute-start | bytes 307208 | tf_op jit(solution)/shard_map/ppermute | solution.py:502
  27.6 8.5 %collective-permute-start.5 = (f32[128,128]{1,0:T(8,128)S(1)}, f32[128,128]{1,0:T(8,128)S(1)}, u32[]{:S(2)}, u32[]{:S(2)}) collective-permute-start(f32[128,128]{1,0:T(8,128)S(1)} %get-tuple-element.47), channel_id=1, source_target_pairs={{0,2},{1,3},{2,0},{3,1},{4,6},{5,7},{6,4},{7,5},{8,10},{9,11},{10,... | collective-permute-start | bytes 196616 | tf_op jit(solution)/shard_map/ppermute | solution.py:502
  31.0 0.7 %collective-permute-start.6 = (bf16[128,128]{1,0:T(8,128)(2,1)S(1)}, bf16[128,128]{1,0:T(8,128)(2,1)S(1)}, u32[]{:S(2)}, u32[]{:S(2)}) collective-permute-start(bf16[128,128]{1,0:T(8,128)(2,1)S(1)} %get-tuple-element.45), channel_id=1, source_target_pairs={{1,4},{3,6},{4,1},{5,8},{6,3},{7,10},{8,5},{9,12},{10,7},{11,14},{... | collective-permute-start | bytes 98312 | tf_op jit(solution)/shard_map/ppermute | solution.py:502
  36.1 5.0 %collective-permute-start.9 = (bf16[528,128]{1,0:T(8,128)(2,1)S(1)}, bf16[528,128]{1,0:T(8,128)(2,1)S(1)}, u32[]{:S(2)}, u32[]{:S(2)}) collective-permute-start(bf16[528,128]{1,0:T(8,128)(2,1)S(1)} %shard_map.153.refs_5_), channel_id=1, source_target_pairs={{0,1},{1,0},{2,3},{3,2},{4,5},{5,4},{6,7},{7,6},{8,9},{9,8},{10,11... | collective-permute-start | bytes 405512 | tf_op jit(solution)/shard_map/ppermute | solution.py:502
  37.1 6.2 %collective-permute-start.8 = (f32[128,128]{1,0:T(8,128)S(1)}, f32[128,128]{1,0:T(8,128)S(1)}, u32[]{:S(2)}, u32[]{:S(2)}) collective-permute-start(f32[128,128]{1,0:T(8,128)S(1)} %add.9), channel_id=1, source_target_pairs={{0,4},{1,5},{2,6},{3,7},{4,0},{5,1},{6,2},{7,3},{8,12},{9,13},{10,... | collective-permute-start | bytes 196616 | tf_op jit(solution)/shard_map/ppermute | solution.py:502
  43.3 4.3 %collective-permute-start.10 = (f32[128,128]{1,0:T(8,128)S(1)}, f32[128,128]{1,0:T(8,128)S(1)}, u32[]{:S(2)}, u32[]{:S(2)}) collective-permute-start(f32[128,128]{1,0:T(8,128)S(1)} %add.10), channel_id=1, source_target_pairs={{0,8},{1,9},{2,10},{3,11},{4,12},{5,13},{6,14},{7,15},{8,0},{9,1},... | collective-permute-start | bytes 196616 | tf_op jit(solution)/shard_map/ppermute | solution.py:502
  47.6 5.3 %collective-permute-start.11 = (f32[128,128]{1,0:T(8,128)S(1)}, f32[128,128]{1,0:T(8,128)S(1)}, u32[]{:S(2)}, u32[]{:S(2)}) collective-permute-start(f32[128,128]{1,0:T(8,128)S(1)} %add.11.a_ref), channel_id=1, source_target_pairs={{0,16},{1,17},{2,18},{3,19},{4,20},{5,21},{6,22},{7,23},{8,24},{9,... | collective-permute-start | bytes 196616 | tf_op jit(solution)/shard_map/ppermute | solution.py:502
  (2 other events, 7.4 us)

commit v6 on v5

--- a/solution.py
+++ b/solution.py
@@ -175,18 +175,6 @@
     route_body(slots, own_ref, mate_ref, near_ref, far_ref, box)
 
 
-def route_sum_kernel(slots, own_ref, mate_ref, near_ref, far_ref, sum_ref, box):
-    route_body(slots, own_ref, mate_ref, near_ref, far_ref, box)
-    high = slots * 2 * CH + HEAD
-    low = high + SUM_ROWS
-    parts = []
-    for ref in (own_ref, mate_ref):
-        parts.append(
-            ref[high : high + SUM_ROWS, :].astype(F32) + ref[low : low + SUM_ROWS, :].astype(F32)
-        )
-    sum_ref[...] = parts[0] + parts[1]
-
-
 def merge_kernel(near_ref, far_ref, out_ref):
     out_ref[0:NEAR_ROWS, :] = near_ref[...]
     out_ref[NEAR_ROWS:, :] = far_ref[...]
@@ -361,7 +349,7 @@
 
 def forward_kernel(
     slot_hbm, link_hbm, field_ref, own_ref, mate_ref, first_ref, second_ref, weight_ref, bias_ref, cortex_ref, upstream_ref, strips_ref, spread_ref,
-    ends_ref, shifts_ref, fold_ref, out_ref, dpre_ref, msg_ref,
+    ends_ref, shifts_ref, fold_ref, out_ref, dpre_ref, msg_ref, sum_ref,
     planes, strips, mixed, taps, sums, slot_ref, link_ref, sems, spots, grads,
 ):
     slots = field_ref.shape[0]
@@ -420,8 +408,6 @@
             grads[p] = grads[p] + term if pair else term
 
     pack_bricks(slot_ref, dpre_ref, strips_ref, msg_ref)
-    high = slots * 2 * CH + HEAD
-    low = high + SUM_ROWS
     rows = jnp.concatenate(
         [grads[p, a * PART : (a + 1) * PART, :] for a in range(3) for p in range(PARTS)], axis=0
     )
@@ -435,11 +421,8 @@
     last = jnp.concatenate([full[:, TILE:], jnp.zeros((2 * GC, CH), F32)], axis=0)
     half = SUM_ROWS - 10 * GC
     last = jnp.concatenate([last[0:half], last[half:]], axis=1)
-    for at, values in ((0, full[:, 0:TILE]), (10 * GC, last)):
-        rounded = values.astype(BF)
-        size = values.shape[0]
-        msg_ref[high + at : high + at + size, :] = rounded
-        msg_ref[low + at : low + at + size, :] = (values - rounded.astype(F32)).astype(BF)
+    sum_ref[0 : 10 * GC, :] = full[:, 0:TILE]
+    sum_ref[10 * GC :, :] = last
 
 
 def backward_kernel(pairs, *refs):
@@ -472,8 +455,8 @@
                 out_ref[s, :, i * TILE : (i + 1) * TILE] = (tiles[i] * present).astype(BF)
 
 
-def finish_kernel(a_ref, b_ref, kernel_ref, bias_ref):
-    total = a_ref[...] + b_ref[...]
+def finish_kernel(total_ref, kernel_ref, bias_ref):
+    total = total_ref[...]
     first, last = total[0 : 10 * GC, :], total[10 * GC :, :]
     turned = pltpu.roll(first, 64, 1)
     parts = (first, turned, jnp.concatenate([last, pltpu.roll(last, 64, 1)], axis=0))
@@ -562,10 +545,10 @@
     forward, backward = staged
     first = merged(near, far)
     second = swapped(first, 1)
-    activated, dpre, own = call(
+    activated, dpre, own, terms = call(
         forward_kernel,
         [HBM, HBM] + [VMEM] * 14,
-        [field, field, shape((pack_rows + 2 * SUM_ROWS, TILE), BF)],
+        [field, field, shape((pack_rows, TILE), BF), shape((SUM_ROWS, TILE), F32)],
         work
         + [
             pltpu.VMEM((slots // 2, PARTS, 3 * PART, 10 * TILE), BF),
@@ -576,48 +559,39 @@
         slot_to_brick, neighbors, voxels, own, mate, first, second, forward, bias.reshape(1, CH),
         cortex, cotangent, strips, spread, ends, shifts, fold,
     )
+    pieces = terms.reshape(devices, -1, min(TILE, SUM_ROWS * TILE // devices))
+    pieces = lax.all_to_all(pieces, "bricks", 0, 0)
     mate = swapped(own, 1)
-    near, far, total = call(
-        functools.partial(route_sum_kernel, slots),
-        [VMEM, VMEM],
-        [near_shape, far_shape, shape((SUM_ROWS, TILE), F32)],
-        box,
+    near, far = call(
+        functools.partial(route_kernel, slots), [VMEM, VMEM], [near_shape, far_shape], box,
+        flops=BUSY,
     )(own, mate)
+    near, far = routed(near, 1), routed(far, 2)
+    near, far, pieces = lax.optimization_barrier((near, far, pieces))
+    mine = jnp.sum(pieces, axis=0, keepdims=True)
+    total = lax.all_to_all(jnp.broadcast_to(mine, pieces.shape), "bricks", 0, 0)
+    first = merged(near, far)
+    second = swapped(first, 1)
     state = {}
 
     def part_backward(pair):
         last = [state["grad"]] if pair else []
         (state["grad"],) = call(
-            functools.partial(backward_kernel, (pair,)),
+            functools.partial(backward_kernel, tuple(range(slots // 2))),
             [HBM, HBM] + [VMEM] * (9 + len(last)),
             [field],
             work,
             flops=10**9,
         )(
-            slot_to_brick, neighbors, dpre, own, mate, state["first"], state["second"], backward,
+            slot_to_brick, neighbors, dpre, own, mate, first, second, backward,
             spread, ends, shifts, *last,
         )
 
-    pairs = list(range(slots // 2))
-    masks = [2**p for p in range(1, devices.bit_length() - 1)]
-    for mask in masks:
-        other = swapped(total, mask)
-        if mask == masks[0]:
-            state["near"], state["far"] = routed(near, 1), routed(far, 2)
-        elif pairs:
-            if mask == masks[1]:
-                state["first"] = merged(state.pop("near"), state.pop("far"))
-                state["second"] = swapped(state["first"], 1)
-            part_backward(pairs.pop(0))
-        if mask != masks[-1]:
-            total, other, state = lax.optimization_barrier((total, other, state))
-            total = total + other
-    for pair in pairs:
-        part_backward(pair)
+    part_backward(0)
     input_grad = state["grad"]
     kernel_sum, bias_sum = call(
-        finish_kernel, [VMEM, VMEM], [shape((27 * GC, CH), F32), shape((1, CH), F32)]
-    )(total, other)
+        finish_kernel, [VMEM], [shape((27 * GC, CH), F32), shape((1, CH), F32)]
+    )(total.reshape(SUM_ROWS, TILE))
     kernel_grad = jnp.transpose(kernel_sum.reshape(3, 3, 3, GC, CH), (4, 3, 0, 1, 2))
     return (activated, input_grad, kernel_grad, bias_sum.reshape(CH))
 

time: 54 us -> 63.4 us (1.17)
  blocking collectives: 0 us -> 12.7 us
  starting transfers between devices: 26 us -> 21.1 us
  waiting for transfers between devices: 9.26 us -> 6.53 us
  local copies, waits for them, and re-layouts: 1.01 us -> 3.46 us
  Pallas kernels: 16.5 us -> 17.4 us
  other arithmetic: 0.03 us -> 0.88 us
    all_to_all x0 -> x1, blocking collectives: none -> 12.7 us  [shards(): total = lax.all_to_all(jnp.broadcast_to(mine, pieces.shape), 'bricks', 0, 0)]
    ppermute x12 -> x8, starting transfers between devices: 26 us -> 15.2 us  [sent(): return lax.ppermute(block, 'bricks', route)]
    ppermute x12 -> x8, waiting for transfers between devices: 9.26 us -> 2.29 us  [sent(): return lax.ppermute(block, 'bricks', route)]
    all_to_all x0 -> x1, starting transfers between devices: none -> 5.86 us  [shards(): pieces = lax.all_to_all(pieces, 'bricks', 0, 0)]
    all_to_all x0 -> x1, waiting for transfers between devices: none -> 4.24 us  [shards(): pieces = lax.all_to_all(pieces, 'bricks', 0, 0)]
    unnamed x28 -> x36, local copies, waits for them, and re-layouts: 1.01 us -> 3.44 us
    pallas_call x1 -> x2, Pallas kernels: 0.23 us -> 2.03 us  [shards(): call(functools.partial(route_kernel, slots), [VMEM, VMEM], [near_shape, f...]
    reduce_sum x0 -> x1, other arithmetic: none -> 0.88 us  [shards(): mine = jnp.sum(pieces, axis=0, keepdims=True)]
  transfers between devices with their start and end apart: 12 -> 9, of which waited for: 6 -> 3; matrix products, arithmetic and copies ran while one was open for 0% -> 1% of each run, Pallas kernels for 12% -> 5%
where the time goes in v6:
time: 63.4 us; the launch traced here: 63 us
  starting transfers between devices  21.1 us (33%)
  Pallas kernels  17.4 us (27%)
  blocking collectives  12.7 us (20%)
  waiting for transfers between devices  6.53 us (10%)
  local copies, waits for them, and re-layouts  3.46 us (5%)
  between operations  0.94 us (1%)
  other arithmetic  0.88 us (1%)
    ppermute x8, starting transfers between devices, sent(): return lax.ppermute(block, 'bricks', route)  15.2 us
    all_to_all x1, blocking collectives, shards(): total = lax.all_to_all(jnp.broadcast_to(mine, pieces.shape), 'bricks', 0, 0)  12.7 us
    pallas_call x1, Pallas kernels, shards(): call(forward_kernel, [HBM, HBM] + [VMEM] * 14, [field, field, shape((pack...  6.92 us
    all_to_all x1, starting transfers between devices, shards(): pieces = lax.all_to_all(pieces, 'bricks', 0, 0)  5.86 us
    pallas_call x1, Pallas kernels, part_backward(): call(functools.partial(backward_kernel, tuple(range(slots // 2))), [HBM,...  5.1 us
    all_to_all x1, waiting for transfers between devices, shards(): pieces = lax.all_to_all(pieces, 'bricks', 0, 0)  4.24 us
    unnamed x36, local copies, waits for them, and re-layouts  3.44 us
    ppermute x8, waiting for transfers between devices, sent(): return lax.ppermute(block, 'bricks', route)  2.29 us
  transfers between devices with their start and end apart: 9, of which 3 were waited for; matrix products, arithmetic and copies ran while one was open for 1% of the time, Pallas kernels for 5%

profile of v6, /device:TPU:0, one launch (start us, length us, event | category | flops | bytes accessed | tf_op | source)
XLA Modules:
  0.0 63.0 jit_solution(4328849418346152556)
XLA Ops:
  0.6 2.1 %shard_map.147.own_ref = bf16[784,128]{1,0:T(8,128)(2,1)} custom-call(s32[6]{0:T(128)} %refs_0_.1, bf16[6,64,512]{2,1,0:T(8,128)(2,1)} %field_ref.1, bf16[4,512,128]{2,1,0:T(8,128)(2,1)} %constant.12.clone.strips_hbm.strips_ref), custom_call_target="tpu_custom_call" | custom-call | bytes 400000 | tf_op jit(solution)/shard_map/pallas_call | solution.py:526
  2.8 0.5 collective-permute-start
  3.3 1.3 %collective-permute-done.mate_ref = bf16[784,128]{1,0:T(8,128)(2,1)S(1)} collective-permute-done((bf16[784,128]{1,0:T(8,128)(2,1)}, bf16[784,128]{1,0:T(8,128)(2,1)S(1)}, u32[]{:S(2)}, u32[]{:S(2)}) %collective-permute-start) | collective-permute-done | bytes 200736 | tf_op jit(solution)/shard_map/ppermute | solution.py:485
  4.6 0.9 %copy-done.5 = bf16[784,128]{1,0:T(8,128)(2,1)S(1)} copy-done((bf16[784,128]{1,0:T(8,128)(2,1)S(1)}, bf16[784,128]{1,0:T(8,128)(2,1)}, u32[]{:S(2)}) %copy-start.5) | copy-done | bytes 200728
  5.8 0.7 %collective-permute-start.1 = (bf16[400,128]{1,0:T(8,128)(2,1)S(1)}, bf16[400,128]{1,0:T(8,128)(2,1)S(1)}, u32[]{:S(2)}, u32[]{:S(2)}) collective-permute-start(bf16[400,128]{1,0:T(8,128)(2,1)S(1)} %get-tuple-element.23), channel_id=1, source_target_pairs={{1,2},{2,1},{3,4},{4,3},{5,6},{6,5},{7,8},{8,7},{9,10},{10,9},{11,... | collective-permute-start | bytes 307208 | tf_op jit(solution)/shard_map/ppermute | solution.py:485
  6.4 0.7 %collective-permute-start.2 = (bf16[128,128]{1,0:T(8,128)(2,1)S(1)}, bf16[128,128]{1,0:T(8,128)(2,1)S(1)}, u32[]{:S(2)}, u32[]{:S(2)}) collective-permute-start(bf16[128,128]{1,0:T(8,128)(2,1)S(1)} %get-tuple-element.24), channel_id=1, source_target_pairs={{1,4},{3,6},{4,1},{5,8},{6,3},{7,10},{8,5},{9,12},{10,7},{11,14},{... | collective-permute-start | bytes 98312 | tf_op jit(solution)/shard_map/ppermute | solution.py:485
  7.3 0.5 shard_map.149
  7.8 8.2 %collective-permute-start.3 = (bf16[528,128]{1,0:T(8,128)(2,1)S(1)}, bf16[528,128]{1,0:T(8,128)(2,1)S(1)}, u32[]{:S(2)}, u32[]{:S(2)}) collective-permute-start(bf16[528,128]{1,0:T(8,128)(2,1)S(1)} %shard_map.150.first_ref), channel_id=1, source_target_pairs={{0,1},{1,0},{2,3},{3,2},{4,5},{5,4},{6,7},{7,6},{8,9},{9,8},{10,11... | collective-permute-start | bytes 405512 | tf_op jit(solution)/shard_map/ppermute | solution.py:485
  16.0 1.0 %collective-permute-done.3.second_ref = bf16[528,128]{1,0:T(8,128)(2,1)S(1)} collective-permute-done((bf16[528,128]{1,0:T(8,128)(2,1)S(1)}, bf16[528,128]{1,0:T(8,128)(2,1)S(1)}, u32[]{:S(2)}, u32[]{:S(2)}) %collective-permute-start.3) | collective-permute-done | bytes 135200 | tf_op jit(solution)/shard_map/ppermute | solution.py:485
  17.1 6.9 %shard_map.151 = (bf16[6,64,512]{2,1,0:T(8,128)(2,1)}, bf16[6,64,512]{2,1,0:T(8,128)(2,1)S(1)}, bf16[784,128]{1,0:T(8,128)(2,1)S(1)}, f32[128,128]{1,0:T(8,128)}) custom-call(s32[6]{0:T(128)S(1)} %copy-done.12, s32[6,6]{1,0:T(8,128)S(1)} %copy-done.11, bf16[6,64,512]{2,1,0:T(8,128)(2,1)S(1)} %copy-done.2, bf16[784,128]{1,0:T(8,128)(2,1)S(1)} %copy-done.6, ...), custom_call_target="tpu_custom_call" | custom-call | flops 4000000000 | bytes 400000 | tf_op jit(solution)/shard_map/pallas_call | solution.py:548
  24.0 0.4 collective-permute-start.4
  24.4 5.9 %all-to-all-start = ((f32[32,4,128]{2,1,0:T(4,128)}), f32[32,4,128]{2,1,0:T(4,128)}, u32[]{:S(2)}, u32[]{:S(2)}) async-start(f32[32,4,128]{2,1,0:T(4,128)} %bitcast.3), calls=%async_computation | async-start | bytes 131072 | tf_op jit(solution)/shard_map/all_to_all | solution.py:563
  30.3 1.8 %shard_map.152 = (bf16[400,128]{1,0:T(8,128)(2,1)}, bf16[128,128]{1,0:T(8,128)(2,1)S(1)}) custom-call(bf16[784,128]{1,0:T(8,128)(2,1)S(1)} %get-tuple-element.32.own_ref.refs_3_, bf16[784,128]{1,0:T(8,128)(2,1)} %collective-permute-done.4.mate_ref.refs_4_), custom_call_target="tpu_custom_call" | custom-call | flops 10000000000 | bytes 400000 | tf_op jit(solution)/shard_map/pallas_call | solution.py:565
  32.1 0.7 %collective-permute-start.5 = (bf16[400,128]{1,0:T(8,128)(2,1)}, bf16[400,128]{1,0:T(8,128)(2,1)S(1)}, u32[]{:S(2)}, u32[]{:S(2)}) collective-permute-start(bf16[400,128]{1,0:T(8,128)(2,1)} %get-tuple-element.33), channel_id=1, source_target_pairs={{1,2},{2,1},{3,4},{4,3},{5,6},{6,5},{7,8},{8,7},{9,10},{10,9},{11,... | collective-permute-start | bytes 307208 | tf_op jit(solution)/shard_map/ppermute | solution.py:485
  32.8 0.7 %collective-permute-start.6 = (bf16[128,128]{1,0:T(8,128)(2,1)S(1)}, bf16[128,128]{1,0:T(8,128)(2,1)S(1)}, u32[]{:S(2)}, u32[]{:S(2)}) collective-permute-start(bf16[128,128]{1,0:T(8,128)(2,1)S(1)} %get-tuple-element.34), channel_id=1, source_target_pairs={{1,4},{3,6},{4,1},{5,8},{6,3},{7,10},{8,5},{9,12},{10,7},{11,14},{... | collective-permute-start | bytes 98312 | tf_op jit(solution)/shard_map/ppermute | solution.py:485
  33.4 4.2 %all-to-all-done = f32[32,4,128]{2,1,0:T(4,128)} async-done(((f32[32,4,128]{2,1,0:T(4,128)}), f32[32,4,128]{2,1,0:T(4,128)}, u32[]{:S(2)}, u32[]{:S(2)}) %all-to-all-start) | async-done | bytes 65568 | tf_op jit(solution)/shard_map/all_to_all | solution.py:563
  37.7 0.6 %copy-done.7 = bf16[400,128]{1,0:T(8,128)(2,1)} copy-done((bf16[400,128]{1,0:T(8,128)(2,1)}, bf16[400,128]{1,0:T(8,128)(2,1)S(1)}, u32[]{:S(2)}) %copy-start.7) | copy-done | bytes 102424
  38.3 0.9 %copy-done.8 = bf16[400,128]{1,0:T(8,128)(2,1)S(1)} copy-done((bf16[400,128]{1,0:T(8,128)(2,1)S(1)}, bf16[400,128]{1,0:T(8,128)(2,1)}, u32[]{:S(2)}) %copy-start.8) | copy-done | bytes 102424
  39.2 3.4 %collective-permute-start.7 = (bf16[528,128]{1,0:T(8,128)(2,1)S(1)}, bf16[528,128]{1,0:T(8,128)(2,1)}, u32[]{:S(2)}, u32[]{:S(2)}) collective-permute-start(bf16[528,128]{1,0:T(8,128)(2,1)S(1)} %shard_map.153.refs_5_), channel_id=1, source_target_pairs={{0,1},{1,0},{2,3},{3,2},{4,5},{5,4},{6,7},{7,6},{8,9},{9,8},{10,11... | collective-permute-start | bytes 405512 | tf_op jit(solution)/shard_map/ppermute | solution.py:485
  42.7 0.9 %reduce_sum.9 = f32[4,128]{1,0:T(4,128)S(1)} reduce(f32[32,4,128]{2,1,0:T(4,128)} %all-to-all-done, f32[]{:T(128)} %constant.5.clone.1), dimensions={0}, to_apply=%region_0.0 | reduce | flops 15872 | bytes 67588 | tf_op jit(solution)/shard_map/reduce_sum | solution.py:571
  43.6 12.7 %all_to_all.10 = f32[32,4,128]{2,1,0:T(4,128)S(1)} all-to-all(f32[32,4,128]{2,1,0:T(4,128)S(1)} %broadcast_in_dim.2), channel_id=1, replica_groups=mesh['bricks'=32] {'bricks'}, dimensions={0} | all-to-all | bytes 131072 | tf_op jit(solution)/shard_map/all_to_all | solution.py:572
  56.3 0.7 %shard_map.155 = (f32[216,64]{1,0:T(8,128)}, f32[1,64]{1,0:T(1,128)}) custom-call(f32[128,128]{1,0:T(8,128)S(1)} %bitcast.10), custom_call_target="tpu_custom_call" | custom-call | bytes 400000 | tf_op jit(solution)/shard_map/pallas_call | solution.py:592
  57.0 0.9 %copy-done.10 = bf16[4,48,144]{2,1,0:T(8,128)(2,1)S(1)} copy-done((bf16[4,48,144]{2,1,0:T(8,128)(2,1)S(1)}, bf16[4,48,144]{2,1,0:T(8,128)(2,1)}, u32[]{:S(2)}) %copy-start.10) | copy-done | bytes 55320
  57.9 5.1 %shard_map.154 = bf16[6,64,512]{2,1,0:T(8,128)(2,1)} custom-call(s32[6]{0:T(128)S(1)} %copy-done.12, s32[6,6]{1,0:T(8,128)S(1)} %copy-done.11, bf16[6,64,512]{2,1,0:T(8,128)(2,1)S(1)} %get-tuple-element.31.refs_2_, bf16[784,128]{1,0:T(8,128)(2,1)S(1)} %get-tuple-element.32.own_ref.refs_3_, bf16[784,128]{1,0:T(8,128)(2,1)} %collective-permute-done.4.mate_ref.refs_4_, ...), custom_call_target="tpu_custom_call" | custom-call | flops 1000000000 | bytes 400000 | tf_op jit(solution)/shard_map/pallas_call | solution.py:579
  (42 shorter events, 0.4 us)
Async XLA Ops:
  0.6 6.5 %copy-start.14 = (bf16[64,8,3,3,3]{0,1,4,3,2:T(8,128)(2,1)S(1)}, bf16[64,8,3,3,3]{0,1,4,3,2:T(8,128)(2,1)}, u32[]{:S(2)}) copy-start(bf16[64,8,3,3,3]{0,1,4,3,2:T(8,128)(2,1)} %param.13) | copy-start | bytes 82948
  2.8 1.8 %collective-permute-start = (bf16[784,128]{1,0:T(8,128)(2,1)}, bf16[784,128]{1,0:T(8,128)(2,1)S(1)}, u32[]{:S(2)}, u32[]{:S(2)}) collective-permute-start(bf16[784,128]{1,0:T(8,128)(2,1)} %shard_map.147.own_ref), channel_id=1, source_target_pairs={{0,1},{1,0},{2,3},{3,2},{4,5},{5,4},{6,7},{7,6},{8,9},{9,8},{10,11... | collective-permute-start | bytes 602120 | tf_op jit(solution)/shard_map/ppermute | solution.py:485
  4.6 0.9 %copy-start.5 = (bf16[784,128]{1,0:T(8,128)(2,1)S(1)}, bf16[784,128]{1,0:T(8,128)(2,1)}, u32[]{:S(2)}) copy-start(bf16[784,128]{1,0:T(8,128)(2,1)} %shard_map.147.own_ref) | copy-start | bytes 602116
  5.8 2.0 %collective-permute-start.1 = (bf16[400,128]{1,0:T(8,128)(2,1)S(1)}, bf16[400,128]{1,0:T(8,128)(2,1)S(1)}, u32[]{:S(2)}, u32[]{:S(2)}) collective-permute-start(bf16[400,128]{1,0:T(8,128)(2,1)S(1)} %get-tuple-element.23), channel_id=1, source_target_pairs={{1,2},{2,1},{3,4},{4,3},{5,6},{6,5},{7,8},{8,7},{9,10},{10,9},{11,... | collective-permute-start | bytes 307208 | tf_op jit(solution)/shard_map/ppermute | solution.py:485
  6.4 1.3 %collective-permute-start.2 = (bf16[128,128]{1,0:T(8,128)(2,1)S(1)}, bf16[128,128]{1,0:T(8,128)(2,1)S(1)}, u32[]{:S(2)}, u32[]{:S(2)}) collective-permute-start(bf16[128,128]{1,0:T(8,128)(2,1)S(1)} %get-tuple-element.24), channel_id=1, source_target_pairs={{1,4},{3,6},{4,1},{5,8},{6,3},{7,10},{8,5},{9,12},{10,7},{11,14},{... | collective-permute-start | bytes 98312 | tf_op jit(solution)/shard_map/ppermute | solution.py:485
  7.1 9.8 %copy-start = (bf16[4,256,1024]{2,1,0:T(8,128)(2,1)S(1)}, bf16[4,256,1024]{2,1,0:T(8,128)(2,1)}, u32[]{:S(2)}) copy-start(bf16[4,256,1024]{2,1,0:T(8,128)(2,1)} %constant.15.clone.shifts_ref.refs_10_) | copy-start | bytes 6291460
  7.1 9.8 %copy-start.1 = (bf16[4,512,128]{2,1,0:T(8,128)(2,1)S(1)}, bf16[4,512,128]{2,1,0:T(8,128)(2,1)}, u32[]{:S(2)}) copy-start(bf16[4,512,128]{2,1,0:T(8,128)(2,1)} %constant.12.clone.strips_hbm.strips_ref) | copy-start | bytes 1572868
  7.1 9.8 %copy-start.2 = (bf16[6,64,512]{2,1,0:T(8,128)(2,1)S(1)}, bf16[6,64,512]{2,1,0:T(8,128)(2,1)}, u32[]{:S(2)}) copy-start(bf16[6,64,512]{2,1,0:T(8,128)(2,1)} %field_ref.1) | copy-start | bytes 1179652
  7.2 9.8 %copy-start.3 = (bf16[4,384,128]{2,1,0:T(8,128)(2,1)S(1)}, bf16[4,384,128]{2,1,0:T(8,128)(2,1)}, u32[]{:S(2)}) copy-start(bf16[4,384,128]{2,1,0:T(8,128)(2,1)} %constant.14.clone.ends_ref.refs_9_) | copy-start | bytes 1179652
  7.2 9.8 %copy-start.4 = (bf16[256,512]{1,0:T(8,128)(2,1)S(1)}, bf16[256,512]{1,0:T(8,128)(2,1)}, u32[]{:S(2)}) copy-start(bf16[256,512]{1,0:T(8,128)(2,1)} %constant.13.clone.spread_ref.refs_8_) | copy-start | bytes 786436
  7.2 9.8 %copy-start.6 = (bf16[784,128]{1,0:T(8,128)(2,1)S(1)}, bf16[784,128]{1,0:T(8,128)(2,1)}, u32[]{:S(2)}) copy-start(bf16[784,128]{1,0:T(8,128)(2,1)} %shard_map.147.own_ref) | copy-start | bytes 602116
  7.2 9.8 %copy-start.11 = (s32[6,6]{1,0:T(8,128)S(1)}, s32[6,6]{1,0:T(8,128)}, u32[]{:S(2)}) copy-start(s32[6,6]{1,0:T(8,128)} %refs_1_.1) | copy-start | bytes 436
  7.2 9.8 %copy-start.12 = (s32[6]{0:T(128)S(1)}, s32[6]{0:T(128)}, u32[]{:S(2)}) copy-start(s32[6]{0:T(128)} %refs_0_.1) | copy-start | bytes 76
  7.2 9.8 %copy-start.13 = (bf16[6,64,512]{2,1,0:T(8,128)(2,1)S(1)}, bf16[6,64,512]{2,1,0:T(8,128)(2,1)}, u32[]{:S(2)}) copy-start(bf16[6,64,512]{2,1,0:T(8,128)(2,1)} %upstream_ref.1) | copy-start | bytes 1179652
  7.2 9.8 %copy-start.15 = (s32[6,512]{1,0:T(8,128)S(1)}, s32[6,512]{1,0:T(8,128)}, u32[]{:S(2)}) copy-start(s32[6,512]{1,0:T(8,128)} %cortex_ref.1) | copy-start | bytes 36868
  7.2 9.8 %copy-start.16 = (f32[64]{0:T(128)S(1)}, f32[64]{0:T(128)}, u32[]{:S(2)}) copy-start(f32[64]{0:T(128)} %param.14) | copy-start | bytes 772
  7.3 9.8 %copy-start.17 = (f32[160,80]{1,0:T(8,128)S(1)}, f32[160,80]{1,0:T(8,128)}, u32[]{:S(2)}) copy-start(f32[160,80]{1,0:T(8,128)} %constant.22.fold_ref) | copy-start | bytes 153604
  7.7 9.2 %copy-start.9 = (bf16[4,48,144]{2,1,0:T(8,128)(2,1)}, bf16[4,48,144]{2,1,0:T(8,128)(2,1)S(1)}, u32[]{:S(2)}) copy-start(bf16[4,48,144]{2,1,0:T(8,128)(2,1)S(1)} %get-tuple-element.38.refs_7_) | copy-start | bytes 165892
  7.8 9.2 %collective-permute-start.3 = (bf16[528,128]{1,0:T(8,128)(2,1)S(1)}, bf16[528,128]{1,0:T(8,128)(2,1)S(1)}, u32[]{:S(2)}, u32[]{:S(2)}) collective-permute-start(bf16[528,128]{1,0:T(8,128)(2,1)S(1)} %shard_map.150.first_ref), channel_id=1, source_target_pairs={{0,1},{1,0},{2,3},{3,2},{4,5},{5,4},{6,7},{7,6},{8,9},{9,8},{10,11... | collective-permute-start | bytes 405512 | tf_op jit(solution)/shard_map/ppermute | solution.py:485
  24.0 6.3 %collective-permute-start.4 = (bf16[784,128]{1,0:T(8,128)(2,1)S(1)}, bf16[784,128]{1,0:T(8,128)(2,1)}, u32[]{:S(2)}, u32[]{:S(2)}) collective-permute-start(bf16[784,128]{1,0:T(8,128)(2,1)S(1)} %get-tuple-element.32.own_ref.refs_3_), channel_id=1, source_target_pairs={{0,1},{1,0},{2,3},{3,2},{4,5},{5,4},{6,7},{7,6},{8,9},{9,8},{10,11... | collective-permute-start | bytes 602120 | tf_op jit(solution)/shard_map/ppermute | solution.py:485
  24.4 13.3 %all-to-all-start = ((f32[32,4,128]{2,1,0:T(4,128)}), f32[32,4,128]{2,1,0:T(4,128)}, u32[]{:S(2)}, u32[]{:S(2)}) async-start(f32[32,4,128]{2,1,0:T(4,128)} %bitcast.3), calls=%async_computation | async-start | bytes 131072 | tf_op jit(solution)/shard_map/all_to_all | solution.py:563
  32.1 5.6 %collective-permute-start.5 = (bf16[400,128]{1,0:T(8,128)(2,1)}, bf16[400,128]{1,0:T(8,128)(2,1)S(1)}, u32[]{:S(2)}, u32[]{:S(2)}) collective-permute-start(bf16[400,128]{1,0:T(8,128)(2,1)} %get-tuple-element.33), channel_id=1, source_target_pairs={{1,2},{2,1},{3,4},{4,3},{5,6},{6,5},{7,8},{8,7},{9,10},{10,9},{11,... | collective-permute-start | bytes 307208 | tf_op jit(solution)/shard_map/ppermute | solution.py:485
  32.8 4.9 %collective-permute-start.6 = (bf16[128,128]{1,0:T(8,128)(2,1)S(1)}, bf16[128,128]{1,0:T(8,128)(2,1)S(1)}, u32[]{:S(2)}, u32[]{:S(2)}) collective-permute-start(bf16[128,128]{1,0:T(8,128)(2,1)S(1)} %get-tuple-element.34), channel_id=1, source_target_pairs={{1,4},{3,6},{4,1},{5,8},{6,3},{7,10},{8,5},{9,12},{10,7},{11,14},{... | collective-permute-start | bytes 98312 | tf_op jit(solution)/shard_map/ppermute | solution.py:485
  39.2 17.8 %collective-permute-start.7 = (bf16[528,128]{1,0:T(8,128)(2,1)S(1)}, bf16[528,128]{1,0:T(8,128)(2,1)}, u32[]{:S(2)}, u32[]{:S(2)}) collective-permute-start(bf16[528,128]{1,0:T(8,128)(2,1)S(1)} %shard_map.153.refs_5_), channel_id=1, source_target_pairs={{0,1},{1,0},{2,3},{3,2},{4,5},{5,4},{6,7},{7,6},{8,9},{9,8},{10,11... | collective-permute-start | bytes 405512 | tf_op jit(solution)/shard_map/ppermute | solution.py:485
  (3 other events, 2.4 us)

commit v7 on v6

--- a/solution.py
+++ b/solution.py
@@ -403,13 +403,14 @@
             put_spots(pair, 2, 5 * e + 4, jnp.where(left, turned[3], 0.0).astype(BF))
         for p in range(PARTS):
             term = lax.dot_general(
-                spots[pair, p], taps[pair, p], (((1,), (1,)), ((), ())), preferred_element_type=F32
+                taps[pair, p], spots[pair, p], (((1,), (1,)), ((), ())), preferred_element_type=F32
             )
             grads[p] = grads[p] + term if pair else term
 
     pack_bricks(slot_ref, dpre_ref, strips_ref, msg_ref)
+    turned = [grads[p].T for p in range(PARTS)]
     rows = jnp.concatenate(
-        [grads[p, a * PART : (a + 1) * PART, :] for a in range(3) for p in range(PARTS)], axis=0
+        [turned[p][a * PART : (a + 1) * PART, :] for a in range(3) for p in range(PARTS)], axis=0
     )
     group = lax.broadcasted_iota(jnp.int32, rows.shape, 0) // GC % 2
     column = lax.broadcasted_iota(jnp.int32, rows.shape, 1)
@@ -552,7 +553,7 @@
         work
         + [
             pltpu.VMEM((slots // 2, PARTS, 3 * PART, 10 * TILE), BF),
-            pltpu.VMEM((PARTS, 3 * PART, 10 * PART), F32),
+            pltpu.VMEM((PARTS, 10 * PART, 3 * PART), F32),
         ],
         flops=4 * 10**9,
     )(
@@ -589,6 +590,7 @@
 
     part_backward(0)
     input_grad = state["grad"]
+    total, input_grad = lax.optimization_barrier((total, input_grad))
     kernel_sum, bias_sum = call(
         finish_kernel, [VMEM], [shape((27 * GC, CH), F32), shape((1, CH), F32)]
     )(total.reshape(SUM_ROWS, TILE))

time: 63.4 us -> 60 us (0.946)
  blocking collectives: 12.7 us -> 0 us
  starting transfers between devices: 21.1 us -> 27.5 us
  local copies, waits for them, and re-layouts: 3.46 us -> 5.62 us
  waiting for transfers between devices: 6.53 us -> 7.98 us
  Pallas kernels: 17.4 us -> 16.6 us
    all_to_all x1 -> x0, blocking collectives: 12.7 us -> none  [shards(): total = lax.all_to_all(jnp.broadcast_to(mine, pieces.shape), 'bricks', 0, 0)]
    all_to_all x0 -> x1, starting transfers between devices: none -> 5.48 us  [shards(): total = lax.all_to_all(jnp.broadcast_to(mine, pieces.shape), 'bricks', 0, 0)]
    unnamed x36 -> x42, local copies, waits for them, and re-layouts: 3.44 us -> 4.98 us
    pallas_call x2, Pallas kernels: 2.03 us -> 1.11 us  [shards(): call(functools.partial(route_kernel, slots), [VMEM, VMEM], [near_shape, f...]
    all_to_all x1, waiting for transfers between devices: 4.24 us -> 5.14 us  [shards(): pieces = lax.all_to_all(pieces, 'bricks', 0, 0)]
  transfers between devices with their start and end apart: 9 -> 10, of which waited for: 3 -> 4; matrix products, arithmetic and copies ran while one was open for 1% -> 3% of each run, Pallas kernels for 5% -> 11%
where the time goes in v7:
time: 60 us; the launch traced here: 59.6 us
  starting transfers between devices  27.5 us (46%)
  Pallas kernels  16.6 us (28%)
  waiting for transfers between devices  7.98 us (13%)
  local copies, waits for them, and re-layouts  5.62 us (9%)
  between operations  0.99 us (2%)
  other arithmetic  0.88 us (1%)
    ppermute x8, starting transfers between devices, sent(): return lax.ppermute(block, 'bricks', route)  15.5 us
    pallas_call x1, Pallas kernels, shards(): call(forward_kernel, [HBM, HBM] + [VMEM] * 14, [field, field, shape((pack...  7.13 us
    all_to_all x1, starting transfers between devices, shards(): pieces = lax.all_to_all(pieces, 'bricks', 0, 0)  6.47 us
    all_to_all x1, starting transfers between devices, shards(): total = lax.all_to_all(jnp.broadcast_to(mine, pieces.shape), 'bricks', 0, 0)  5.48 us
    all_to_all x1, waiting for transfers between devices, shards(): pieces = lax.all_to_all(pieces, 'bricks', 0, 0)  5.14 us
    pallas_call x1, Pallas kernels, part_backward(): call(functools.partial(backward_kernel, tuple(range(slots // 2))), [HBM,...  5.02 us
    unnamed x42, local copies, waits for them, and re-layouts  4.98 us
    ppermute x8, waiting for transfers between devices, sent(): return lax.ppermute(block, 'bricks', route)  2.29 us
  transfers between devices with their start and end apart: 10, of which 4 were waited for; matrix products, arithmetic and copies ran while one was open for 3% of the time, Pallas kernels for 11%

profile of v7, /device:TPU:0, one launch (start us, length us, event | category | flops | bytes accessed | tf_op | source)
XLA Modules:
  0.0 59.6 jit_solution(9578687793228559038)
XLA Ops:
  0.6 2.1 %shard_map.147.own_ref = bf16[784,128]{1,0:T(8,128)(2,1)} custom-call(s32[6]{0:T(128)} %refs_0_.1, bf16[6,64,512]{2,1,0:T(8,128)(2,1)} %field_ref.1, bf16[4,512,128]{2,1,0:T(8,128)(2,1)} %constant.12.clone.strips_hbm.strips_ref), custom_call_target="tpu_custom_call" | custom-call | bytes 400000 | tf_op jit(solution)/shard_map/pallas_call | solution.py:527
  3.3 1.3 %collective-permute-done.mate_ref = bf16[784,128]{1,0:T(8,128)(2,1)S(1)} collective-permute-done((bf16[784,128]{1,0:T(8,128)(2,1)}, bf16[784,128]{1,0:T(8,128)(2,1)S(1)}, u32[]{:S(2)}, u32[]{:S(2)}) %collective-permute-start) | collective-permute-done | bytes 200736 | tf_op jit(solution)/shard_map/ppermute | solution.py:486
  4.6 0.9 %copy-done.5 = bf16[784,128]{1,0:T(8,128)(2,1)S(1)} copy-done((bf16[784,128]{1,0:T(8,128)(2,1)S(1)}, bf16[784,128]{1,0:T(8,128)(2,1)}, u32[]{:S(2)}) %copy-start.5) | copy-done | bytes 200728
  5.8 0.7 %collective-permute-start.2 = (bf16[128,128]{1,0:T(8,128)(2,1)S(1)}, bf16[128,128]{1,0:T(8,128)(2,1)S(1)}, u32[]{:S(2)}, u32[]{:S(2)}) collective-permute-start(bf16[128,128]{1,0:T(8,128)(2,1)S(1)} %get-tuple-element.26), channel_id=1, source_target_pairs={{1,4},{3,6},{4,1},{5,8},{6,3},{7,10},{8,5},{9,12},{10,7},{11,14},{... | collective-permute-start | bytes 98312 | tf_op jit(solution)/shard_map/ppermute | solution.py:486
  6.4 0.7 %collective-permute-start.1 = (bf16[400,128]{1,0:T(8,128)(2,1)S(1)}, bf16[400,128]{1,0:T(8,128)(2,1)S(1)}, u32[]{:S(2)}, u32[]{:S(2)}) collective-permute-start(bf16[400,128]{1,0:T(8,128)(2,1)S(1)} %get-tuple-element.25), channel_id=1, source_target_pairs={{1,2},{2,1},{3,4},{4,3},{5,6},{6,5},{7,8},{8,7},{9,10},{10,9},{11,... | collective-permute-start | bytes 307208 | tf_op jit(solution)/shard_map/ppermute | solution.py:486
  7.8 9.2 %collective-permute-start.3 = (bf16[528,128]{1,0:T(8,128)(2,1)S(1)}, bf16[528,128]{1,0:T(8,128)(2,1)S(1)}, u32[]{:S(2)}, u32[]{:S(2)}) collective-permute-start(bf16[528,128]{1,0:T(8,128)(2,1)S(1)} %shard_map.150.first_ref), channel_id=1, source_target_pairs={{0,1},{1,0},{2,3},{3,2},{4,5},{5,4},{6,7},{7,6},{8,9},{9,8},{10,11... | collective-permute-start | bytes 405512 | tf_op jit(solution)/shard_map/ppermute | solution.py:486
  17.0 1.0 %collective-permute-done.3.second_ref = bf16[528,128]{1,0:T(8,128)(2,1)S(1)} collective-permute-done((bf16[528,128]{1,0:T(8,128)(2,1)S(1)}, bf16[528,128]{1,0:T(8,128)(2,1)S(1)}, u32[]{:S(2)}, u32[]{:S(2)}) %collective-permute-start.3) | collective-permute-done | bytes 135200 | tf_op jit(solution)/shard_map/ppermute | solution.py:486
  18.1 7.1 %shard_map.151 = (bf16[6,64,512]{2,1,0:T(8,128)(2,1)}, bf16[6,64,512]{2,1,0:T(8,128)(2,1)S(1)}, bf16[784,128]{1,0:T(8,128)(2,1)S(1)}, f32[128,128]{1,0:T(8,128)S(1)}) custom-call(s32[6]{0:T(128)S(1)} %copy-done.15, s32[6,6]{1,0:T(8,128)S(1)} %copy-done.14, bf16[6,64,512]{2,1,0:T(8,128)(2,1)S(1)} %copy-done.2, bf16[784,128]{1,0:T(8,128)(2,1)S(1)} %copy-done.6, ...), custom_call_target="tpu_custom_call" | custom-call | flops 4000000000 | bytes 400000 | tf_op jit(solution)/shard_map/pallas_call | solution.py:549
  25.3 0.6 %copy-done.13 = f32[128,128]{1,0:T(8,128)} copy-done((f32[128,128]{1,0:T(8,128)}, f32[128,128]{1,0:T(8,128)S(1)}, u32[]{:S(2)}) %copy-start.13) | copy-done | bytes 65560
  26.2 6.5 %all-to-all-start = ((f32[32,4,128]{2,1,0:T(4,128)}), f32[32,4,128]{2,1,0:T(4,128)}, u32[]{:S(2)}, u32[]{:S(2)}) async-start(f32[32,4,128]{2,1,0:T(4,128)} %bitcast.11), calls=%async_computation | async-start | bytes 131072 | tf_op jit(solution)/shard_map/all_to_all | solution.py:564
  32.7 0.9 %shard_map.152 = (bf16[400,128]{1,0:T(8,128)(2,1)}, bf16[128,128]{1,0:T(8,128)(2,1)}) custom-call(bf16[784,128]{1,0:T(8,128)(2,1)S(1)} %get-tuple-element.33.own_ref.refs_3_, bf16[784,128]{1,0:T(8,128)(2,1)S(1)} %collective-permute-done.4.mate_ref.refs_4_), custom_call_target="tpu_custom_call" | custom-call | flops 10000000000 | bytes 400000 | tf_op jit(solution)/shard_map/pallas_call | solution.py:566
  33.6 0.7 %collective-permute-start.5 = (bf16[400,128]{1,0:T(8,128)(2,1)}, bf16[400,128]{1,0:T(8,128)(2,1)S(1)}, u32[]{:S(2)}, u32[]{:S(2)}) collective-permute-start(bf16[400,128]{1,0:T(8,128)(2,1)} %get-tuple-element.34), channel_id=1, source_target_pairs={{1,2},{2,1},{3,4},{4,3},{5,6},{6,5},{7,8},{8,7},{9,10},{10,9},{11,... | collective-permute-start | bytes 307208 | tf_op jit(solution)/shard_map/ppermute | solution.py:486
  34.3 0.7 %collective-permute-start.6 = (bf16[128,128]{1,0:T(8,128)(2,1)}, bf16[128,128]{1,0:T(8,128)(2,1)S(1)}, u32[]{:S(2)}, u32[]{:S(2)}) collective-permute-start(bf16[128,128]{1,0:T(8,128)(2,1)} %get-tuple-element.35), channel_id=1, source_target_pairs={{1,4},{3,6},{4,1},{5,8},{6,3},{7,10},{8,5},{9,12},{10,7},{11,14},{... | collective-permute-start | bytes 98312 | tf_op jit(solution)/shard_map/ppermute | solution.py:486
  35.0 5.1 %all-to-all-done = f32[32,4,128]{2,1,0:T(4,128)} async-done(((f32[32,4,128]{2,1,0:T(4,128)}), f32[32,4,128]{2,1,0:T(4,128)}, u32[]{:S(2)}, u32[]{:S(2)}) %all-to-all-start) | async-done | bytes 65568 | tf_op jit(solution)/shard_map/all_to_all | solution.py:564
  40.1 0.6 %copy-done.9 = bf16[400,128]{1,0:T(8,128)(2,1)} copy-done((bf16[400,128]{1,0:T(8,128)(2,1)}, bf16[400,128]{1,0:T(8,128)(2,1)S(1)}, u32[]{:S(2)}) %copy-start.9) | copy-done | bytes 102424
  40.8 0.9 %copy-done.10 = bf16[400,128]{1,0:T(8,128)(2,1)S(1)} copy-done((bf16[400,128]{1,0:T(8,128)(2,1)S(1)}, bf16[400,128]{1,0:T(8,128)(2,1)}, u32[]{:S(2)}) %copy-start.10) | copy-done | bytes 102424
  41.7 2.7 %collective-permute-start.7 = (bf16[528,128]{1,0:T(8,128)(2,1)S(1)}, bf16[528,128]{1,0:T(8,128)(2,1)}, u32[]{:S(2)}, u32[]{:S(2)}) collective-permute-start(bf16[528,128]{1,0:T(8,128)(2,1)S(1)} %shard_map.153.refs_5_), channel_id=1, source_target_pairs={{0,1},{1,0},{2,3},{3,2},{4,5},{5,4},{6,7},{7,6},{8,9},{9,8},{10,11... | collective-permute-start | bytes 405512 | tf_op jit(solution)/shard_map/ppermute | solution.py:486
  44.4 0.9 %reduce_sum.9 = f32[4,128]{1,0:T(4,128)S(1)} reduce(f32[32,4,128]{2,1,0:T(4,128)} %all-to-all-done, f32[]{:T(128)} %constant.5.clone.1), dimensions={0}, to_apply=%region_0.0 | reduce | flops 15872 | bytes 67588 | tf_op jit(solution)/shard_map/reduce_sum | solution.py:572
  45.3 0.6 %broadcast_in_dim.2 = f32[32,4,128]{2,1,0:T(4,128)} broadcast(f32[4,128]{1,0:T(4,128)S(1)} %reduce_sum.9), dimensions={1,2} | broadcast | bytes 67584 | tf_op jit(solution)/shard_map/broadcast_in_dim | solution.py:573
  45.9 5.5 %all-to-all-start.1 = ((f32[32,4,128]{2,1,0:T(4,128)}), f32[32,4,128]{2,1,0:T(4,128)S(1)}, u32[]{:S(2)}, u32[]{:S(2)}) async-start(f32[32,4,128]{2,1,0:T(4,128)} %broadcast_in_dim.2), calls=%async_computation.1 | async-start | bytes 131072 | tf_op jit(solution)/shard_map/all_to_all | solution.py:573
  51.4 0.9 %copy-done.8 = bf16[784,128]{1,0:T(8,128)(2,1)S(1)} copy-done((bf16[784,128]{1,0:T(8,128)(2,1)S(1)}, bf16[784,128]{1,0:T(8,128)(2,1)}, u32[]{:S(2)}) %copy-start.8) | copy-done | bytes 200728
  52.4 0.9 %copy-done.12 = bf16[4,48,144]{2,1,0:T(8,128)(2,1)S(1)} copy-done((bf16[4,48,144]{2,1,0:T(8,128)(2,1)S(1)}, bf16[4,48,144]{2,1,0:T(8,128)(2,1)}, u32[]{:S(2)}) %copy-start.12) | copy-done | bytes 55320
  53.3 5.0 %shard_map.154 = bf16[6,64,512]{2,1,0:T(8,128)(2,1)} custom-call(s32[6]{0:T(128)S(1)} %copy-done.15, s32[6,6]{1,0:T(8,128)S(1)} %copy-done.14, bf16[6,64,512]{2,1,0:T(8,128)(2,1)S(1)} %get-tuple-element.38.refs_2_, bf16[784,128]{1,0:T(8,128)(2,1)S(1)} %get-tuple-element.33.own_ref.refs_3_, bf16[784,128]{1,0:T(8,128)(2,1)S(1)} %copy-done.8, ...), custom_call_target="tpu_custom_call" | custom-call | flops 1000000000 | bytes 400000 | tf_op jit(solution)/shard_map/pallas_call | solution.py:580
  58.8 0.7 %shard_map.155 = (f32[216,64]{1,0:T(8,128)}, f32[1,64]{1,0:T(1,128)}) custom-call(f32[128,128]{1,0:T(8,128)S(1)} %bitcast.10), custom_call_target="tpu_custom_call" | custom-call | bytes 400000 | tf_op jit(solution)/shard_map/pallas_call | solution.py:594
  (49 shorter events, 2.3 us)
Async XLA Ops:
  0.6 6.5 %copy-start.17 = (bf16[64,8,3,3,3]{0,1,4,3,2:T(8,128)(2,1)S(1)}, bf16[64,8,3,3,3]{0,1,4,3,2:T(8,128)(2,1)}, u32[]{:S(2)}) copy-start(bf16[64,8,3,3,3]{0,1,4,3,2:T(8,128)(2,1)} %param.13) | copy-start | bytes 82948
  2.8 1.8 %collective-permute-start = (bf16[784,128]{1,0:T(8,128)(2,1)}, bf16[784,128]{1,0:T(8,128)(2,1)S(1)}, u32[]{:S(2)}, u32[]{:S(2)}) collective-permute-start(bf16[784,128]{1,0:T(8,128)(2,1)} %shard_map.147.own_ref), channel_id=1, source_target_pairs={{0,1},{1,0},{2,3},{3,2},{4,5},{5,4},{6,7},{7,6},{8,9},{9,8},{10,11... | collective-permute-start | bytes 602120 | tf_op jit(solution)/shard_map/ppermute | solution.py:486
  5.8 2.0 %collective-permute-start.2 = (bf16[128,128]{1,0:T(8,128)(2,1)S(1)}, bf16[128,128]{1,0:T(8,128)(2,1)S(1)}, u32[]{:S(2)}, u32[]{:S(2)}) collective-permute-start(bf16[128,128]{1,0:T(8,128)(2,1)S(1)} %get-tuple-element.26), channel_id=1, source_target_pairs={{1,4},{3,6},{4,1},{5,8},{6,3},{7,10},{8,5},{9,12},{10,7},{11,14},{... | collective-permute-start | bytes 98312 | tf_op jit(solution)/shard_map/ppermute | solution.py:486
  6.4 1.3 %collective-permute-start.1 = (bf16[400,128]{1,0:T(8,128)(2,1)S(1)}, bf16[400,128]{1,0:T(8,128)(2,1)S(1)}, u32[]{:S(2)}, u32[]{:S(2)}) collective-permute-start(bf16[400,128]{1,0:T(8,128)(2,1)S(1)} %get-tuple-element.25), channel_id=1, source_target_pairs={{1,2},{2,1},{3,4},{4,3},{5,6},{6,5},{7,8},{8,7},{9,10},{10,9},{11,... | collective-permute-start | bytes 307208 | tf_op jit(solution)/shard_map/ppermute | solution.py:486
  7.1 10.9 %copy-start = (bf16[4,256,1024]{2,1,0:T(8,128)(2,1)S(1)}, bf16[4,256,1024]{2,1,0:T(8,128)(2,1)}, u32[]{:S(2)}) copy-start(bf16[4,256,1024]{2,1,0:T(8,128)(2,1)} %constant.15.clone.shifts_ref.refs_10_) | copy-start | bytes 6291460
  7.1 10.9 %copy-start.1 = (bf16[4,512,128]{2,1,0:T(8,128)(2,1)S(1)}, bf16[4,512,128]{2,1,0:T(8,128)(2,1)}, u32[]{:S(2)}) copy-start(bf16[4,512,128]{2,1,0:T(8,128)(2,1)} %constant.12.clone.strips_hbm.strips_ref) | copy-start | bytes 1572868
  7.1 10.9 %copy-start.2 = (bf16[6,64,512]{2,1,0:T(8,128)(2,1)S(1)}, bf16[6,64,512]{2,1,0:T(8,128)(2,1)}, u32[]{:S(2)}) copy-start(bf16[6,64,512]{2,1,0:T(8,128)(2,1)} %field_ref.1) | copy-start | bytes 1179652
  7.2 10.9 %copy-start.3 = (bf16[4,384,128]{2,1,0:T(8,128)(2,1)S(1)}, bf16[4,384,128]{2,1,0:T(8,128)(2,1)}, u32[]{:S(2)}) copy-start(bf16[4,384,128]{2,1,0:T(8,128)(2,1)} %constant.14.clone.ends_ref.refs_9_) | copy-start | bytes 1179652
  7.2 10.9 %copy-start.4 = (bf16[256,512]{1,0:T(8,128)(2,1)S(1)}, bf16[256,512]{1,0:T(8,128)(2,1)}, u32[]{:S(2)}) copy-start(bf16[256,512]{1,0:T(8,128)(2,1)} %constant.13.clone.spread_ref.refs_8_) | copy-start | bytes 786436
  7.2 10.9 %copy-start.6 = (bf16[784,128]{1,0:T(8,128)(2,1)S(1)}, bf16[784,128]{1,0:T(8,128)(2,1)}, u32[]{:S(2)}) copy-start(bf16[784,128]{1,0:T(8,128)(2,1)} %shard_map.147.own_ref) | copy-start | bytes 602116
  7.2 10.9 %copy-start.14 = (s32[6,6]{1,0:T(8,128)S(1)}, s32[6,6]{1,0:T(8,128)}, u32[]{:S(2)}) copy-start(s32[6,6]{1,0:T(8,128)} %refs_1_.1) | copy-start | bytes 436
  7.2 10.9 %copy-start.15 = (s32[6]{0:T(128)S(1)}, s32[6]{0:T(128)}, u32[]{:S(2)}) copy-start(s32[6]{0:T(128)} %refs_0_.1) | copy-start | bytes 76
  7.2 10.9 %copy-start.16 = (bf16[6,64,512]{2,1,0:T(8,128)(2,1)S(1)}, bf16[6,64,512]{2,1,0:T(8,128)(2,1)}, u32[]{:S(2)}) copy-start(bf16[6,64,512]{2,1,0:T(8,128)(2,1)} %upstream_ref.1) | copy-start | bytes 1179652
  7.2 10.9 %copy-start.18 = (s32[6,512]{1,0:T(8,128)S(1)}, s32[6,512]{1,0:T(8,128)}, u32[]{:S(2)}) copy-start(s32[6,512]{1,0:T(8,128)} %cortex_ref.1) | copy-start | bytes 36868
  7.2 10.9 %copy-start.19 = (f32[64]{0:T(128)S(1)}, f32[64]{0:T(128)}, u32[]{:S(2)}) copy-start(f32[64]{0:T(128)} %param.14) | copy-start | bytes 772
  7.3 10.9 %copy-start.20 = (f32[160,80]{1,0:T(8,128)S(1)}, f32[160,80]{1,0:T(8,128)}, u32[]{:S(2)}) copy-start(f32[160,80]{1,0:T(8,128)} %constant.22.fold_ref) | copy-start | bytes 153604
  7.7 10.3 %copy-start.11 = (bf16[4,48,144]{2,1,0:T(8,128)(2,1)}, bf16[4,48,144]{2,1,0:T(8,128)(2,1)S(1)}, u32[]{:S(2)}) copy-start(bf16[4,48,144]{2,1,0:T(8,128)(2,1)S(1)} %get-tuple-element.41.refs_7_) | copy-start | bytes 165892
  7.8 10.2 %collective-permute-start.3 = (bf16[528,128]{1,0:T(8,128)(2,1)S(1)}, bf16[528,128]{1,0:T(8,128)(2,1)S(1)}, u32[]{:S(2)}, u32[]{:S(2)}) collective-permute-start(bf16[528,128]{1,0:T(8,128)(2,1)S(1)} %shard_map.150.first_ref), channel_id=1, source_target_pairs={{0,1},{1,0},{2,3},{3,2},{4,5},{5,4},{6,7},{7,6},{8,9},{9,8},{10,11... | collective-permute-start | bytes 405512 | tf_op jit(solution)/shard_map/ppermute | solution.py:486
  25.9 6.9 %collective-permute-start.4 = (bf16[784,128]{1,0:T(8,128)(2,1)S(1)}, bf16[784,128]{1,0:T(8,128)(2,1)S(1)}, u32[]{:S(2)}, u32[]{:S(2)}) collective-permute-start(bf16[784,128]{1,0:T(8,128)(2,1)S(1)} %get-tuple-element.33.own_ref.refs_3_), channel_id=1, source_target_pairs={{0,1},{1,0},{2,3},{3,2},{4,5},{5,4},{6,7},{7,6},{8,9},{9,8},{10,11... | collective-permute-start | bytes 602120 | tf_op jit(solution)/shard_map/ppermute | solution.py:486
  26.2 13.9 %all-to-all-start = ((f32[32,4,128]{2,1,0:T(4,128)}), f32[32,4,128]{2,1,0:T(4,128)}, u32[]{:S(2)}, u32[]{:S(2)}) async-start(f32[32,4,128]{2,1,0:T(4,128)} %bitcast.11), calls=%async_computation | async-start | bytes 131072 | tf_op jit(solution)/shard_map/all_to_all | solution.py:564
  33.6 6.5 %collective-permute-start.5 = (bf16[400,128]{1,0:T(8,128)(2,1)}, bf16[400,128]{1,0:T(8,128)(2,1)S(1)}, u32[]{:S(2)}, u32[]{:S(2)}) collective-permute-start(bf16[400,128]{1,0:T(8,128)(2,1)} %get-tuple-element.34), channel_id=1, source_target_pairs={{1,2},{2,1},{3,4},{4,3},{5,6},{6,5},{7,8},{8,7},{9,10},{10,9},{11,... | collective-permute-start | bytes 307208 | tf_op jit(solution)/shard_map/ppermute | solution.py:486
  34.3 5.8 %collective-permute-start.6 = (bf16[128,128]{1,0:T(8,128)(2,1)}, bf16[128,128]{1,0:T(8,128)(2,1)S(1)}, u32[]{:S(2)}, u32[]{:S(2)}) collective-permute-start(bf16[128,128]{1,0:T(8,128)(2,1)} %get-tuple-element.35), channel_id=1, source_target_pairs={{1,4},{3,6},{4,1},{5,8},{6,3},{7,10},{8,5},{9,12},{10,7},{11,14},{... | collective-permute-start | bytes 98312 | tf_op jit(solution)/shard_map/ppermute | solution.py:486
  41.7 9.8 %collective-permute-start.7 = (bf16[528,128]{1,0:T(8,128)(2,1)S(1)}, bf16[528,128]{1,0:T(8,128)(2,1)}, u32[]{:S(2)}, u32[]{:S(2)}) collective-permute-start(bf16[528,128]{1,0:T(8,128)(2,1)S(1)} %shard_map.153.refs_5_), channel_id=1, source_target_pairs={{0,1},{1,0},{2,3},{3,2},{4,5},{5,4},{6,7},{7,6},{8,9},{9,8},{10,11... | collective-permute-start | bytes 405512 | tf_op jit(solution)/shard_map/ppermute | solution.py:486
  45.9 12.9 %all-to-all-start.1 = ((f32[32,4,128]{2,1,0:T(4,128)}), f32[32,4,128]{2,1,0:T(4,128)S(1)}, u32[]{:S(2)}, u32[]{:S(2)}) async-start(f32[32,4,128]{2,1,0:T(4,128)} %broadcast_in_dim.2), calls=%async_computation.1 | async-start | bytes 131072 | tf_op jit(solution)/shard_map/all_to_all | solution.py:573
  (7 other events, 5.8 us)

commit v8 on v5

--- a/solution.py
+++ b/solution.py
@@ -20,6 +20,7 @@
 BUSY = 10**10
 HEAD = 16
 NEAR_ROWS = (NEAR // 2 + 2) * CH + HEAD
+MESSAGE_ROWS = NEAR_ROWS + FAR // 2 * CH
 SUM_ROWS = 128
 BF = jnp.bfloat16
 F32 = jnp.float32
@@ -139,44 +140,62 @@
     pack_bricks(slot_ref, field_ref, strips_ref, msg_ref)
 
 
-def route_body(slots, own_ref, mate_ref, near_ref, far_ref, box):
-    odd = (lax.axis_index("bricks") & 1) == 1
+def unpack(slots, own_ref, mate_ref, box):
     head = slots * 2 * CH
-    mine = count_sent(own_ref[head : head + HEAD, :])
-    other = count_sent(mate_ref[head : head + HEAD, :])
     for s in range(2 * slots):
         box[s] = own_ref[s * CH : (s + 1) * CH, :]
         box[2 * slots + s] = mate_ref[s * CH : (s + 1) * CH, :]
-
-    def place(j):
-        up = jnp.where(j < mine, mine - 1 - j, slots + other - 1 - (j - mine))
-        down = jnp.where(j < mine, j, slots + j - mine)
-        return jnp.clip(jnp.where(odd, up, down), 0, 2 * slots - 1)
+    return [count_sent(ref[head : head + HEAD, :]) for ref in (own_ref, mate_ref)]
+
+
+def write_message(place, up, count, box, near_ref, far_ref):
+    last = box.shape[0] // 2 - 1
+
+    def at(j):
+        return jnp.clip(place(j), 0, last)
 
     half = lax.broadcasted_iota(jnp.int32, (CH, TILE), 1) // 64
-    counts_here = half == odd.astype(jnp.int32)
+    counts_here = half == jnp.asarray(up).astype(jnp.int32)
     for j in range(0, NEAR, 2):
-        first, second = [box[2 * place(j + e) + 1].astype(F32) for e in range(2)]
+        first, second = [box[2 * at(j + e) + 1].astype(F32) for e in range(2)]
         both = jnp.where(counts_here, first, pltpu.roll(second, 64, 1)).astype(BF)
         near_ref[j // 2 * CH : (j // 2 + 1) * CH, :] = both
         if j < FAR:
             far_ref[j // 2 * CH : (j // 2 + 1) * CH, :] = both
     of_y = lax.broadcasted_iota(jnp.int32, (CH, TILE), 1) % 64 < 32
     row = NEAR // 2 * CH
-    near_ref[row : row + CH, :] = box[2 * place(0)]
-    first, second = [box[2 * place(j)].astype(F32) for j in (1, 2)]
+    near_ref[row : row + CH, :] = box[2 * at(0)]
+    first, second = [box[2 * at(j)].astype(F32) for j in (1, 2)]
     near_ref[row + CH : row + 2 * CH, :] = jnp.where(of_y, first, pltpu.roll(second, 32, 1)).astype(BF)
     row = (NEAR // 2 + 2) * CH
-    both = (mine + other).astype(F32)
-    near_ref[row : row + HEAD, :] = jnp.full((HEAD, TILE), both, F32).astype(BF)
+    near_ref[row : row + HEAD, :] = jnp.full((HEAD, TILE), count.astype(F32), F32).astype(BF)
 
 
 def route_kernel(slots, own_ref, mate_ref, near_ref, far_ref, box):
-    route_body(slots, own_ref, mate_ref, near_ref, far_ref, box)
-
-
-def route_sum_kernel(slots, own_ref, mate_ref, near_ref, far_ref, sum_ref, box):
-    route_body(slots, own_ref, mate_ref, near_ref, far_ref, box)
+    odd = (lax.axis_index("bricks") & 1) == 1
+    mine, other = unpack(slots, own_ref, mate_ref, box)
+
+    def place(j):
+        up = jnp.where(j < mine, mine - 1 - j, slots + other - 1 - (j - mine))
+        down = jnp.where(j < mine, j, slots + j - mine)
+        return jnp.where(odd, up, down)
+
+    write_message(place, odd, mine + other, box, near_ref, far_ref)
+
+
+def route_sum_kernel(
+    slots, own_ref, mate_ref, up_near_ref, up_far_ref, down_near_ref, down_far_ref, sum_ref, box
+):
+    mine, other = unpack(slots, own_ref, mate_ref, box)
+
+    def from_end(j):
+        return jnp.where(j < mine, mine - 1 - j, slots + other - 1 - (j - mine))
+
+    def from_start(j):
+        return jnp.where(j < other, slots + j, j - other)
+
+    write_message(from_end, True, mine + other, box, up_near_ref, up_far_ref)
+    write_message(from_start, False, mine + other, box, down_near_ref, down_far_ref)
     high = slots * 2 * CH + HEAD
     low = high + SUM_ROWS
     parts = []
@@ -187,9 +206,11 @@
     sum_ref[...] = parts[0] + parts[1]
 
 
-def merge_kernel(near_ref, far_ref, out_ref):
-    out_ref[0:NEAR_ROWS, :] = near_ref[...]
-    out_ref[NEAR_ROWS:, :] = far_ref[...]
+def merge_kernel(*refs):
+    out_ref, row = refs[-1], 0
+    for ref in refs[:-1]:
+        out_ref[row : row + ref.shape[0], :] = ref[...]
+        row += ref.shape[0]
 
 
 def weight_kernel(taps_ref, forward_ref, backward_ref, work):
@@ -219,7 +240,7 @@
 
 def make_finder(
     slot_hbm, link_hbm, own_ref, mate_ref, first_ref, second_ref,
-    planes, strips, slot_ref, link_ref, sems,
+    planes, strips, slot_ref, link_ref, sems, shared,
 ):
     copies = bring(((slot_hbm, slot_ref), (link_hbm, link_ref)), sems)
     slots = slot_ref.shape[0]
@@ -227,33 +248,54 @@
     head = slots * 2 * CH
     mine = count_sent(own_ref[head : head + HEAD, :])
     other = count_sent(mate_ref[head : head + HEAD, :])
-    row = (NEAR // 2 + 2) * CH
-    counts = [count_sent(ref[row : row + HEAD, :]) for ref in (first_ref, second_ref)]
     for k, ref in enumerate((own_ref, mate_ref)):
         for s in range(slots):
             strips[k * slots + s] = ref[s * 2 * CH : s * 2 * CH + CH, :]
             planes[k * slots + s] = ref[s * 2 * CH + CH : (s + 1) * 2 * CH, :]
-    for side, near in enumerate((first_ref, second_ref)):
+
+    def take(near, top, side):
         for start, begin, count in ((side * NEAR, 0, NEAR), (2 * NEAR + side * FAR, NEAR_ROWS, FAR)):
             for j in range(0, count, 2):
-                row = begin + j // 2 * CH
+                row = top + begin + j // 2 * CH
                 tile = near[row : row + CH, :]
                 planes[2 * slots + start + j] = tile
                 planes[2 * slots + start + j + 1] = pltpu.roll(tile.astype(F32), 64, 1).astype(BF)
-        row, at = NEAR // 2 * CH, 2 * slots + side * EDGE
+        row, at = top + NEAR // 2 * CH, 2 * slots + side * EDGE
         strips[at] = near[row : row + CH, :]
         tile = near[row + CH : row + 2 * CH, :]
         strips[at + 1] = tile
         strips[at + 2] = pltpu.roll(tile.astype(F32), TILE - 32, 1).astype(BF)
+
+    def count_of(ref, top):
+        row = top + (NEAR // 2 + 2) * CH
+        return count_sent(ref[row : row + HEAD, :])
+
+    if shared:
+        for here, ref in ((odd, first_ref), (jnp.logical_not(odd), second_ref)):
+
+            @pl.when(here)
+            def _():
+                take(ref, 0, 0)
+                take(ref, MESSAGE_ROWS, 1)
+
+        low_count, high_count = [
+            jnp.where(odd, count_of(first_ref, top), count_of(second_ref, top))
+            for top in (0, MESSAGE_ROWS)
+        ]
+        low_side, high_side = 0, 1
+    else:
+        take(first_ref, 0, 0)
+        take(second_ref, 0, 1)
+        counts = count_of(first_ref, 0), count_of(second_ref, 0)
+        low_count = jnp.where(odd, counts[1], counts[0])
+        high_count = jnp.where(odd, counts[0], counts[1])
+        low_side = odd.astype(jnp.int32)
+        high_side = 1 - low_side
     nothing = 2 * slots + 2 * NEAR + 2 * FAR
     planes[nothing] = jnp.zeros((CH, TILE), BF)
     for copy in copies:
         copy.wait()
     base = slot_ref[0]
-    low_side = odd.astype(jnp.int32)
-    high_side = 1 - low_side
-    low_count = jnp.where(odd, counts[1], counts[0])
-    high_count = jnp.where(odd, counts[0], counts[1])
     mate_first = jnp.where(odd, base - other, base + mine)
     chip_low = jnp.where(odd, base - other, base)
     chip_high = jnp.where(odd, base + mine, base + mine + other)
@@ -367,7 +409,7 @@
     slots = field_ref.shape[0]
     base, mine, find_strip, find_plane = make_finder(
         slot_hbm, link_hbm, own_ref, mate_ref, first_ref, second_ref,
-        planes, strips, slot_ref, link_ref, sems,
+        planes, strips, slot_ref, link_ref, sems, False,
     )
     for pair in range(slots // 2):
         taps[pair, :, 9 * PART :, :] = jnp.ones((PARTS, PART, 10 * TILE), BF)
@@ -458,7 +500,7 @@
 ):
     base, mine, find_strip, find_plane = make_finder(
         slot_hbm, link_hbm, own_ref, mate_ref, first_ref, second_ref,
-        planes, strips, slot_ref, link_ref, sems,
+        planes, strips, slot_ref, link_ref, sems, True,
     )
     for pair in pairs:
         results = convolve_pair(
@@ -472,8 +514,9 @@
                 out_ref[s, :, i * TILE : (i + 1) * TILE] = (tiles[i] * present).astype(BF)
 
 
-def finish_kernel(a_ref, b_ref, kernel_ref, bias_ref):
-    total = a_ref[...] + b_ref[...]
+def finish_kernel(own_ref, mate_ref, kernel_ref, bias_ref):
+    odd = (lax.axis_index("bricks") & 1) == 1
+    total = jnp.where(odd, mate_ref[...], own_ref[...])
     first, last = total[0 : 10 * GC, :], total[10 * GC :, :]
     turned = pltpu.roll(first, 64, 1)
     parts = (first, turned, jnp.concatenate([last, pltpu.roll(last, 64, 1)], axis=0))
@@ -523,9 +566,15 @@
     def swapped(block, mask):
         return sent(block, [(d, d ^ mask) for d in range(devices)])
 
-    def merged(near, far):
-        rows = near.shape[0] + far.shape[0]
-        return call(merge_kernel, [VMEM] * 2, [shape((rows, TILE), BF)])(near, far)[0]
+    def merged(*parts):
+        rows = sum(part.shape[0] for part in parts)
+        return call(merge_kernel, [VMEM] * len(parts), [shape((rows, TILE), BF)])(*parts)[0]
+
+    def among_odd(block, step):
+        return sent(block, [(d, d + step) for d in range(1, devices, 2) if 0 <= d + step < devices])
+
+    def among_even(block, mask):
+        return sent(block, [(d, d ^ mask) for d in range(0, devices, 2)])
 
     box = [pltpu.VMEM((4 * slots, CH, TILE), BF)]
     work = [
@@ -577,18 +626,18 @@
         cortex, cotangent, strips, spread, ends, shifts, fold,
     )
     mate = swapped(own, 1)
-    near, far, total = call(
+    *halos, total = call(
         functools.partial(route_sum_kernel, slots),
         [VMEM, VMEM],
-        [near_shape, far_shape, shape((SUM_ROWS, TILE), F32)],
+        [near_shape, far_shape] * 2 + [shape((SUM_ROWS, TILE), F32)],
         box,
     )(own, mate)
     state = {}
 
-    def part_backward(pair):
-        last = [state["grad"]] if pair else []
+    def part_backward(*pairs):
+        last = [state["grad"]] if pairs[0] else []
         (state["grad"],) = call(
-            functools.partial(backward_kernel, (pair,)),
+            functools.partial(backward_kernel, pairs),
             [HBM, HBM] + [VMEM] * (9 + len(last)),
             [field],
             work,
@@ -600,20 +649,21 @@
 
     pairs = list(range(slots // 2))
     masks = [2**p for p in range(1, devices.bit_length() - 1)]
-    for mask in masks:
-        other = swapped(total, mask)
-        if mask == masks[0]:
-            state["near"], state["far"] = routed(near, 1), routed(far, 2)
-        elif pairs:
-            if mask == masks[1]:
-                state["first"] = merged(state.pop("near"), state.pop("far"))
-                state["second"] = swapped(state["first"], 1)
-            part_backward(pairs.pop(0))
-        if mask != masks[-1]:
-            total, other, state = lax.optimization_barrier((total, other, state))
-            total = total + other
-    for pair in pairs:
-        part_backward(pair)
+    for at, mask in enumerate(masks):
+        other = among_even(total, mask)
+        if at == 0:
+            halos = [among_odd(block, step) for block, step in zip(halos, (2, 4, -2, -4))]
+        elif at == 1:
+            total, other, halos = lax.optimization_barrier((total, other, halos))
+        elif at == 2:
+            state["first"] = merged(*halos)
+            state["second"] = sent(state["first"], [(d, d - 1) for d in range(1, devices, 2)])
+        elif at == 3:
+            part_backward(*pairs[:-1])
+        total, other, state = lax.optimization_barrier((total, other, state))
+        total = total + other
+    other = sent(total, [(d, d + 1) for d in range(0, devices, 2)])
+    part_backward(pairs[-1])
     input_grad = state["grad"]
     kernel_sum, bias_sum = call(
         finish_kernel, [VMEM, VMEM], [shape((27 * GC, CH), F32), shape((1, CH), F32)]

time: 54 us -> 59.8 us (1.11)
  starting transfers between devices: 26 us -> 33.7 us
  waiting for transfers between devices: 9.26 us -> 7.94 us
  Pallas kernels: 16.5 us -> 15.7 us
    ppermute x12 -> x15, starting transfers between devices: 26 us -> 33.7 us  [sent(): return lax.ppermute(block, 'bricks', route)]
    ppermute x12 -> x15, waiting for transfers between devices: 9.26 us -> 7.94 us  [sent(): return lax.ppermute(block, 'bricks', route)]
    pallas_call x5 -> x4, Pallas kernels: 5.75 us -> 4.9 us  [the longest x2 4.87 us: part_backward(): call(functools.partial(backward_kernel, pairs), [HBM, HBM] + [VMEM] * (9...]
  transfers between devices with their start and end apart: 12 -> 15, of which waited for: 6 -> 6; matrix products, arithmetic and copies ran while one was open for 0% -> 0% of each run, Pallas kernels for 12% -> 9%
where the time goes in v8:
time: 59.8 us; the launch traced here: 59.4 us
  starting transfers between devices  33.7 us (56%)
  Pallas kernels  15.7 us (26%)
  waiting for transfers between devices  7.94 us (13%)
  between operations  1.05 us (2%)
  local copies, waits for them, and re-layouts  1.01 us (2%)
    ppermute x15, starting transfers between devices, sent(): return lax.ppermute(block, 'bricks', route)  33.7 us
    ppermute x15, waiting for transfers between devices, sent(): return lax.ppermute(block, 'bricks', route)  7.94 us
    pallas_call x1, Pallas kernels, shards(): call(forward_kernel, [HBM, HBM] + [VMEM] * 14, [field, field, shape((pack...  6.92 us
    pallas_call x2, Pallas kernels, part_backward(): call(functools.partial(backward_kernel, pairs), [HBM, HBM] + [VMEM] * (9...  4.87 us
    pallas_call x1, Pallas kernels, shards(): call(pack_kernel, [HBM] * 3, [shape((pack_rows, TILE), BF)], [pltpu.VMEM(...  2.14 us
  transfers between devices with their start and end apart: 15, of which 6 were waited for; matrix products, arithmetic and copies ran while one was open for 0% of the time, Pallas kernels for 9%

profile of v8, /device:TPU:0, one launch (start us, length us, event | category | flops | bytes accessed | tf_op | source)
XLA Modules:
  0.0 59.4 jit_solution(6143835960307954143)
XLA Ops:
  0.6 2.1 %shard_map.147.own_ref = bf16[784,128]{1,0:T(8,128)(2,1)} custom-call(s32[6]{0:T(128)} %refs_0_.3, bf16[6,64,512]{2,1,0:T(8,128)(2,1)} %field_ref.1, bf16[4,512,128]{2,1,0:T(8,128)(2,1)} %constant.10.clone.strips_hbm.strips_ref), custom_call_target="tpu_custom_call" | custom-call | bytes 400000 | tf_op jit(solution)/shard_map/pallas_call | solution.py:592
  3.3 1.3 %collective-permute-done.mate_ref = bf16[784,128]{1,0:T(8,128)(2,1)S(1)} collective-permute-done((bf16[784,128]{1,0:T(8,128)(2,1)}, bf16[784,128]{1,0:T(8,128)(2,1)S(1)}, u32[]{:S(2)}, u32[]{:S(2)}) %collective-permute-start) | collective-permute-done | bytes 200736 | tf_op jit(solution)/shard_map/ppermute | solution.py:545
  4.6 0.9 %copy-done.5 = bf16[784,128]{1,0:T(8,128)(2,1)S(1)} copy-done((bf16[784,128]{1,0:T(8,128)(2,1)S(1)}, bf16[784,128]{1,0:T(8,128)(2,1)}, u32[]{:S(2)}) %copy-start.5) | copy-done | bytes 200728
  5.8 0.7 %collective-permute-start.1 = (bf16[400,128]{1,0:T(8,128)(2,1)S(1)}, bf16[400,128]{1,0:T(8,128)(2,1)S(1)}, u32[]{:S(2)}, u32[]{:S(2)}) collective-permute-start(bf16[400,128]{1,0:T(8,128)(2,1)S(1)} %get-tuple-element.41), channel_id=1, source_target_pairs={{1,2},{2,1},{3,4},{4,3},{5,6},{6,5},{7,8},{8,7},{9,10},{10,9},{11,... | collective-permute-start | bytes 307208 | tf_op jit(solution)/shard_map/ppermute | solution.py:545
  6.4 0.7 %collective-permute-start.2 = (bf16[128,128]{1,0:T(8,128)(2,1)S(1)}, bf16[128,128]{1,0:T(8,128)(2,1)S(1)}, u32[]{:S(2)}, u32[]{:S(2)}) collective-permute-start(bf16[128,128]{1,0:T(8,128)(2,1)S(1)} %get-tuple-element.42), channel_id=1, source_target_pairs={{1,4},{3,6},{4,1},{5,8},{6,3},{7,10},{8,5},{9,12},{10,7},{11,14},{... | collective-permute-start | bytes 98312 | tf_op jit(solution)/shard_map/ppermute | solution.py:545
  7.8 8.2 %collective-permute-start.3 = (bf16[528,128]{1,0:T(8,128)(2,1)S(1)}, bf16[528,128]{1,0:T(8,128)(2,1)S(1)}, u32[]{:S(2)}, u32[]{:S(2)}) collective-permute-start(bf16[528,128]{1,0:T(8,128)(2,1)S(1)} %shard_map.150.first_ref), channel_id=1, source_target_pairs={{0,1},{1,0},{2,3},{3,2},{4,5},{5,4},{6,7},{7,6},{8,9},{9,8},{10,11... | collective-permute-start | bytes 405512 | tf_op jit(solution)/shard_map/ppermute | solution.py:545
  16.0 1.0 %collective-permute-done.3.second_ref = bf16[528,128]{1,0:T(8,128)(2,1)S(1)} collective-permute-done((bf16[528,128]{1,0:T(8,128)(2,1)S(1)}, bf16[528,128]{1,0:T(8,128)(2,1)S(1)}, u32[]{:S(2)}, u32[]{:S(2)}) %collective-permute-start.3) | collective-permute-done | bytes 135200 | tf_op jit(solution)/shard_map/ppermute | solution.py:545
  17.1 6.9 %shard_map.151 = (bf16[6,64,512]{2,1,0:T(8,128)(2,1)}, bf16[6,64,512]{2,1,0:T(8,128)(2,1)S(1)}, bf16[1040,128]{1,0:T(8,128)(2,1)S(1)}) custom-call(s32[6]{0:T(128)S(1)} %copy-done.8, s32[6,6]{1,0:T(8,128)S(1)} %copy-done.7, bf16[6,64,512]{2,1,0:T(8,128)(2,1)S(1)} %copy-done.4, bf16[784,128]{1,0:T(8,128)(2,1)S(1)} %copy-done.6, ...), custom_call_target="tpu_custom_call" | custom-call | flops 4000000000 | bytes 400000 | tf_op jit(solution)/shard_map/pallas_call | solution.py:614
  24.4 1.2 %collective-permute-done.4.mate_ref.refs_4_ = bf16[1040,128]{1,0:T(8,128)(2,1)S(1)} collective-permute-done((bf16[1040,128]{1,0:T(8,128)(2,1)S(1)}, bf16[1040,128]{1,0:T(8,128)(2,1)S(1)}, u32[]{:S(2)}, u32[]{:S(2)}) %collective-permute-start.4) | collective-permute-done | bytes 266272 | tf_op jit(solution)/shard_map/ppermute | solution.py:545
  25.8 3.4 %collective-permute-start.5 = (f32[128,128]{1,0:T(8,128)S(1)}, f32[128,128]{1,0:T(8,128)S(1)}, u32[]{:S(2)}, u32[]{:S(2)}) collective-permute-start(f32[128,128]{1,0:T(8,128)S(1)} %get-tuple-element.52), channel_id=1, source_target_pairs={{0,2},{2,0},{4,6},{6,4},{8,10},{10,8},{12,14},{14,12},{16,18},{18,... | collective-permute-start | bytes 196616 | tf_op jit(solution)/shard_map/ppermute | solution.py:545
  29.2 0.7 %collective-permute-start.7 = (bf16[400,128]{1,0:T(8,128)(2,1)S(1)}, bf16[400,128]{1,0:T(8,128)(2,1)S(1)}, u32[]{:S(2)}, u32[]{:S(2)}) collective-permute-start(bf16[400,128]{1,0:T(8,128)(2,1)S(1)} %get-tuple-element.54), channel_id=1, source_target_pairs={{1,3},{3,5},{5,7},{7,9},{9,11},{11,13},{13,15},{15,17},{17,19},{19... | collective-permute-start | bytes 307208 | tf_op jit(solution)/shard_map/ppermute | solution.py:545
  29.9 0.7 %collective-permute-start.9 = (bf16[400,128]{1,0:T(8,128)(2,1)S(1)}, bf16[400,128]{1,0:T(8,128)(2,1)S(1)}, u32[]{:S(2)}, u32[]{:S(2)}) collective-permute-start(bf16[400,128]{1,0:T(8,128)(2,1)S(1)} %get-tuple-element.56), channel_id=1, source_target_pairs={{3,1},{5,3},{7,5},{9,7},{11,9},{13,11},{15,13},{17,15},{19,17},{21... | collective-permute-start | bytes 307208 | tf_op jit(solution)/shard_map/ppermute | solution.py:545
  30.6 1.4 %collective-permute-done.5 = f32[128,128]{1,0:T(8,128)S(1)} collective-permute-done((f32[128,128]{1,0:T(8,128)S(1)}, f32[128,128]{1,0:T(8,128)S(1)}, u32[]{:S(2)}, u32[]{:S(2)}) %collective-permute-start.5) | collective-permute-done | bytes 65568 | tf_op jit(solution)/shard_map/ppermute | solution.py:545
  32.0 4.3 %collective-permute-start.6 = (f32[128,128]{1,0:T(8,128)S(1)}, f32[128,128]{1,0:T(8,128)S(1)}, u32[]{:S(2)}, u32[]{:S(2)}) collective-permute-start(f32[128,128]{1,0:T(8,128)S(1)} %add.12), channel_id=1, source_target_pairs={{0,4},{2,6},{4,0},{6,2},{8,12},{10,14},{12,8},{14,10},{16,20},{18,... | collective-permute-start | bytes 196616 | tf_op jit(solution)/shard_map/ppermute | solution.py:545
  36.4 0.7 %collective-permute-start.10 = (bf16[128,128]{1,0:T(8,128)(2,1)S(1)}, bf16[128,128]{1,0:T(8,128)(2,1)S(1)}, u32[]{:S(2)}, u32[]{:S(2)}) collective-permute-start(bf16[128,128]{1,0:T(8,128)(2,1)S(1)} %get-tuple-element.57), channel_id=1, source_target_pairs={{5,1},{7,3},{9,5},{11,7},{13,9},{15,11},{17,13},{19,15},{21,17},{2... | collective-permute-start | bytes 98312 | tf_op jit(solution)/shard_map/ppermute | solution.py:545
  37.7 0.8 %collective-permute-done.6 = f32[128,128]{1,0:T(8,128)S(1)} collective-permute-done((f32[128,128]{1,0:T(8,128)S(1)}, f32[128,128]{1,0:T(8,128)S(1)}, u32[]{:S(2)}, u32[]{:S(2)}) %collective-permute-start.6) | collective-permute-done | bytes 65568 | tf_op jit(solution)/shard_map/ppermute | solution.py:545
  38.6 1.3 %collective-permute-start.12 = (bf16[1056,128]{1,0:T(8,128)(2,1)S(1)}, bf16[1056,128]{1,0:T(8,128)(2,1)S(1)}, u32[]{:S(2)}, u32[]{:S(2)}) collective-permute-start(bf16[1056,128]{1,0:T(8,128)(2,1)S(1)} %shard_map.153.refs_5_), channel_id=1, source_target_pairs={{1,0},{3,2},{5,4},{7,6},{9,8},{11,10},{13,12},{15,14},{17,16},{19,... | collective-permute-start | bytes 811016 | tf_op jit(solution)/shard_map/ppermute | solution.py:545
  39.9 5.3 %collective-permute-start.11 = (f32[128,128]{1,0:T(8,128)S(1)}, f32[128,128]{1,0:T(8,128)S(1)}, u32[]{:S(2)}, u32[]{:S(2)}) collective-permute-start(f32[128,128]{1,0:T(8,128)S(1)} %add.13), channel_id=1, source_target_pairs={{0,8},{2,10},{4,12},{6,14},{8,0},{10,2},{12,4},{14,6},{16,24},{18,... | collective-permute-start | bytes 196616 | tf_op jit(solution)/shard_map/ppermute | solution.py:545
  45.3 2.2 %collective-permute-done.11 = f32[128,128]{1,0:T(8,128)S(1)} collective-permute-done((f32[128,128]{1,0:T(8,128)S(1)}, f32[128,128]{1,0:T(8,128)S(1)}, u32[]{:S(2)}, u32[]{:S(2)}) %collective-permute-start.11) | collective-permute-done | bytes 65568 | tf_op jit(solution)/shard_map/ppermute | solution.py:545
  47.5 4.9 %collective-permute-start.13 = (f32[128,128]{1,0:T(8,128)S(1)}, f32[128,128]{1,0:T(8,128)S(1)}, u32[]{:S(2)}, u32[]{:S(2)}) collective-permute-start(f32[128,128]{1,0:T(8,128)S(1)} %add.14), channel_id=1, source_target_pairs={{0,16},{2,18},{4,20},{6,22},{8,24},{10,26},{12,28},{14,30},{16,0},... | collective-permute-start | bytes 196616 | tf_op jit(solution)/shard_map/ppermute | solution.py:545
  52.4 2.5 %shard_map.154.refs_11_ = bf16[6,64,512]{2,1,0:T(8,128)(2,1)S(1)} custom-call(s32[6]{0:T(128)S(1)} %copy-done.8, s32[6,6]{1,0:T(8,128)S(1)} %copy-done.7, bf16[6,64,512]{2,1,0:T(8,128)(2,1)S(1)} %get-tuple-element.49.refs_2_, bf16[1040,128]{1,0:T(8,128)(2,1)S(1)} %get-tuple-element.50.own_ref.refs_3_, ...), custom_call_target="tpu_custom_call" | custom-call | flops 1000000000 | bytes 400000 | tf_op jit(solution)/shard_map/pallas_call | solution.py:639
  55.0 1.3 %collective-permute-start.14 = (f32[128,128]{1,0:T(8,128)S(1)}, f32[128,128]{1,0:T(8,128)S(1)}, u32[]{:S(2)}, u32[]{:S(2)}) collective-permute-start(f32[128,128]{1,0:T(8,128)S(1)} %add.15.own_ref), channel_id=1, source_target_pairs={{0,1},{2,3},{4,5},{6,7},{8,9},{10,11},{12,13},{14,15},{16,17},{18,... | collective-permute-start | bytes 196616 | tf_op jit(solution)/shard_map/ppermute | solution.py:545
  56.3 2.4 %shard_map.155 = bf16[6,64,512]{2,1,0:T(8,128)(2,1)} custom-call(s32[6]{0:T(128)S(1)} %copy-done.8, s32[6,6]{1,0:T(8,128)S(1)} %copy-done.7, bf16[6,64,512]{2,1,0:T(8,128)(2,1)S(1)} %get-tuple-element.49.refs_2_, bf16[1040,128]{1,0:T(8,128)(2,1)S(1)} %get-tuple-element.50.own_ref.refs_3_, bf16[1040,128]{1,0:T(8,128)(2,1)S(1)} %collective-permute-done.4.mate_ref.refs_4_, ...), custom_call_target="tpu_custom_call" | custom-call | flops 1000000000 | bytes 400000 | tf_op jit(solution)/shard_map/pallas_call | solution.py:639
  58.7 0.7 %shard_map.156 = (f32[216,64]{1,0:T(8,128)}, f32[1,64]{1,0:T(1,128)}) custom-call(f32[128,128]{1,0:T(8,128)S(1)} %add.15.own_ref, f32[128,128]{1,0:T(8,128)S(1)} %collective-permute-done.14.mate_ref), custom_call_target="tpu_custom_call" | custom-call | bytes 400000 | tf_op jit(solution)/shard_map/pallas_call | solution.py:668
  (48 shorter events, 2.8 us)
Async XLA Ops:
  2.8 1.8 %collective-permute-start = (bf16[784,128]{1,0:T(8,128)(2,1)}, bf16[784,128]{1,0:T(8,128)(2,1)S(1)}, u32[]{:S(2)}, u32[]{:S(2)}) collective-permute-start(bf16[784,128]{1,0:T(8,128)(2,1)} %shard_map.147.own_ref), channel_id=1, source_target_pairs={{0,1},{1,0},{2,3},{3,2},{4,5},{5,4},{6,7},{7,6},{8,9},{9,8},{10,11... | collective-permute-start | bytes 602120 | tf_op jit(solution)/shard_map/ppermute | solution.py:545
  5.8 2.0 %collective-permute-start.1 = (bf16[400,128]{1,0:T(8,128)(2,1)S(1)}, bf16[400,128]{1,0:T(8,128)(2,1)S(1)}, u32[]{:S(2)}, u32[]{:S(2)}) collective-permute-start(bf16[400,128]{1,0:T(8,128)(2,1)S(1)} %get-tuple-element.41), channel_id=1, source_target_pairs={{1,2},{2,1},{3,4},{4,3},{5,6},{6,5},{7,8},{8,7},{9,10},{10,9},{11,... | collective-permute-start | bytes 307208 | tf_op jit(solution)/shard_map/ppermute | solution.py:545
  6.4 1.3 %collective-permute-start.2 = (bf16[128,128]{1,0:T(8,128)(2,1)S(1)}, bf16[128,128]{1,0:T(8,128)(2,1)S(1)}, u32[]{:S(2)}, u32[]{:S(2)}) collective-permute-start(bf16[128,128]{1,0:T(8,128)(2,1)S(1)} %get-tuple-element.42), channel_id=1, source_target_pairs={{1,4},{3,6},{4,1},{5,8},{6,3},{7,10},{8,5},{9,12},{10,7},{11,14},{... | collective-permute-start | bytes 98312 | tf_op jit(solution)/shard_map/ppermute | solution.py:545
  7.1 9.8 %copy-start = (bf16[4,256,1024]{2,1,0:T(8,128)(2,1)S(1)}, bf16[4,256,1024]{2,1,0:T(8,128)(2,1)}, u32[]{:S(2)}) copy-start(bf16[4,256,1024]{2,1,0:T(8,128)(2,1)} %constant.13.clone.shifts_ref.refs_10_) | copy-start | bytes 6291460
  7.1 9.8 %copy-start.1 = (bf16[4,384,128]{2,1,0:T(8,128)(2,1)S(1)}, bf16[4,384,128]{2,1,0:T(8,128)(2,1)}, u32[]{:S(2)}) copy-start(bf16[4,384,128]{2,1,0:T(8,128)(2,1)} %constant.12.clone.ends_ref.refs_9_) | copy-start | bytes 1179652
  7.1 9.8 %copy-start.2 = (bf16[256,512]{1,0:T(8,128)(2,1)S(1)}, bf16[256,512]{1,0:T(8,128)(2,1)}, u32[]{:S(2)}) copy-start(bf16[256,512]{1,0:T(8,128)(2,1)} %constant.11.clone.spread_ref.refs_8_) | copy-start | bytes 786436
  7.2 9.8 %copy-start.3 = (bf16[4,512,128]{2,1,0:T(8,128)(2,1)S(1)}, bf16[4,512,128]{2,1,0:T(8,128)(2,1)}, u32[]{:S(2)}) copy-start(bf16[4,512,128]{2,1,0:T(8,128)(2,1)} %constant.10.clone.strips_hbm.strips_ref) | copy-start | bytes 1572868
  7.2 9.8 %copy-start.4 = (bf16[6,64,512]{2,1,0:T(8,128)(2,1)S(1)}, bf16[6,64,512]{2,1,0:T(8,128)(2,1)}, u32[]{:S(2)}) copy-start(bf16[6,64,512]{2,1,0:T(8,128)(2,1)} %field_ref.1) | copy-start | bytes 1179652
  7.2 9.8 %copy-start.6 = (bf16[784,128]{1,0:T(8,128)(2,1)S(1)}, bf16[784,128]{1,0:T(8,128)(2,1)}, u32[]{:S(2)}) copy-start(bf16[784,128]{1,0:T(8,128)(2,1)} %shard_map.147.own_ref) | copy-start | bytes 602116
  7.2 9.8 %copy-start.7 = (s32[6,6]{1,0:T(8,128)S(1)}, s32[6,6]{1,0:T(8,128)}, u32[]{:S(2)}) copy-start(s32[6,6]{1,0:T(8,128)} %refs_1_.3) | copy-start | bytes 436
  7.2 9.8 %copy-start.8 = (s32[6]{0:T(128)S(1)}, s32[6]{0:T(128)}, u32[]{:S(2)}) copy-start(s32[6]{0:T(128)} %refs_0_.3) | copy-start | bytes 76
  7.2 9.8 %copy-start.9 = (bf16[6,64,512]{2,1,0:T(8,128)(2,1)S(1)}, bf16[6,64,512]{2,1,0:T(8,128)(2,1)}, u32[]{:S(2)}) copy-start(bf16[6,64,512]{2,1,0:T(8,128)(2,1)} %upstream_ref.1) | copy-start | bytes 1179652
  7.8 9.2 %collective-permute-start.3 = (bf16[528,128]{1,0:T(8,128)(2,1)S(1)}, bf16[528,128]{1,0:T(8,128)(2,1)S(1)}, u32[]{:S(2)}, u32[]{:S(2)}) collective-permute-start(bf16[528,128]{1,0:T(8,128)(2,1)S(1)} %shard_map.150.first_ref), channel_id=1, source_target_pairs={{0,1},{1,0},{2,3},{3,2},{4,5},{5,4},{6,7},{7,6},{8,9},{9,8},{10,11... | collective-permute-start | bytes 405512 | tf_op jit(solution)/shard_map/ppermute | solution.py:545
  24.0 1.6 %collective-permute-start.4 = (bf16[1040,128]{1,0:T(8,128)(2,1)S(1)}, bf16[1040,128]{1,0:T(8,128)(2,1)S(1)}, u32[]{:S(2)}, u32[]{:S(2)}) collective-permute-start(bf16[1040,128]{1,0:T(8,128)(2,1)S(1)} %get-tuple-element.50.own_ref.refs_3_), channel_id=1, source_target_pairs={{0,1},{1,0},{2,3},{3,2},{4,5},{5,4},{6,7},{7,6},{8,9},{9,8},{10,11... | collective-permute-start | bytes 798728 | tf_op jit(solution)/shard_map/ppermute | solution.py:545
  25.8 6.2 %collective-permute-start.5 = (f32[128,128]{1,0:T(8,128)S(1)}, f32[128,128]{1,0:T(8,128)S(1)}, u32[]{:S(2)}, u32[]{:S(2)}) collective-permute-start(f32[128,128]{1,0:T(8,128)S(1)} %get-tuple-element.52), channel_id=1, source_target_pairs={{0,2},{2,0},{4,6},{6,4},{8,10},{10,8},{12,14},{14,12},{16,18},{18,... | collective-permute-start | bytes 196616 | tf_op jit(solution)/shard_map/ppermute | solution.py:545
  29.2 8.5 %collective-permute-start.7 = (bf16[400,128]{1,0:T(8,128)(2,1)S(1)}, bf16[400,128]{1,0:T(8,128)(2,1)S(1)}, u32[]{:S(2)}, u32[]{:S(2)}) collective-permute-start(bf16[400,128]{1,0:T(8,128)(2,1)S(1)} %get-tuple-element.54), channel_id=1, source_target_pairs={{1,3},{3,5},{5,7},{7,9},{9,11},{11,13},{13,15},{15,17},{17,19},{19... | collective-permute-start | bytes 307208 | tf_op jit(solution)/shard_map/ppermute | solution.py:545
  29.9 7.8 %collective-permute-start.9 = (bf16[400,128]{1,0:T(8,128)(2,1)S(1)}, bf16[400,128]{1,0:T(8,128)(2,1)S(1)}, u32[]{:S(2)}, u32[]{:S(2)}) collective-permute-start(bf16[400,128]{1,0:T(8,128)(2,1)S(1)} %get-tuple-element.56), channel_id=1, source_target_pairs={{3,1},{5,3},{7,5},{9,7},{11,9},{13,11},{15,13},{17,15},{19,17},{21... | collective-permute-start | bytes 307208 | tf_op jit(solution)/shard_map/ppermute | solution.py:545
  32.0 6.6 %collective-permute-start.6 = (f32[128,128]{1,0:T(8,128)S(1)}, f32[128,128]{1,0:T(8,128)S(1)}, u32[]{:S(2)}, u32[]{:S(2)}) collective-permute-start(f32[128,128]{1,0:T(8,128)S(1)} %add.12), channel_id=1, source_target_pairs={{0,4},{2,6},{4,0},{6,2},{8,12},{10,14},{12,8},{14,10},{16,20},{18,... | collective-permute-start | bytes 196616 | tf_op jit(solution)/shard_map/ppermute | solution.py:545
  36.4 1.3 %collective-permute-start.10 = (bf16[128,128]{1,0:T(8,128)(2,1)S(1)}, bf16[128,128]{1,0:T(8,128)(2,1)S(1)}, u32[]{:S(2)}, u32[]{:S(2)}) collective-permute-start(bf16[128,128]{1,0:T(8,128)(2,1)S(1)} %get-tuple-element.57), channel_id=1, source_target_pairs={{5,1},{7,3},{9,5},{11,7},{13,9},{15,11},{17,13},{19,15},{21,17},{2... | collective-permute-start | bytes 98312 | tf_op jit(solution)/shard_map/ppermute | solution.py:545
  37.0 0.7 %collective-permute-start.8 = (bf16[128,128]{1,0:T(8,128)(2,1)S(1)}, bf16[128,128]{1,0:T(8,128)(2,1)S(1)}, u32[]{:S(2)}, u32[]{:S(2)}) collective-permute-start(bf16[128,128]{1,0:T(8,128)(2,1)S(1)} %get-tuple-element.55), channel_id=1, source_target_pairs={{1,5},{3,7},{5,9},{7,11},{9,13},{11,15},{13,17},{15,19},{17,21},{1... | collective-permute-start | bytes 98312 | tf_op jit(solution)/shard_map/ppermute | solution.py:545
  38.6 8.9 %collective-permute-start.12 = (bf16[1056,128]{1,0:T(8,128)(2,1)S(1)}, bf16[1056,128]{1,0:T(8,128)(2,1)S(1)}, u32[]{:S(2)}, u32[]{:S(2)}) collective-permute-start(bf16[1056,128]{1,0:T(8,128)(2,1)S(1)} %shard_map.153.refs_5_), channel_id=1, source_target_pairs={{1,0},{3,2},{5,4},{7,6},{9,8},{11,10},{13,12},{15,14},{17,16},{19,... | collective-permute-start | bytes 811016 | tf_op jit(solution)/shard_map/ppermute | solution.py:545
  39.9 7.6 %collective-permute-start.11 = (f32[128,128]{1,0:T(8,128)S(1)}, f32[128,128]{1,0:T(8,128)S(1)}, u32[]{:S(2)}, u32[]{:S(2)}) collective-permute-start(f32[128,128]{1,0:T(8,128)S(1)} %add.13), channel_id=1, source_target_pairs={{0,8},{2,10},{4,12},{6,14},{8,0},{10,2},{12,4},{14,6},{16,24},{18,... | collective-permute-start | bytes 196616 | tf_op jit(solution)/shard_map/ppermute | solution.py:545
  47.5 7.4 %collective-permute-start.13 = (f32[128,128]{1,0:T(8,128)S(1)}, f32[128,128]{1,0:T(8,128)S(1)}, u32[]{:S(2)}, u32[]{:S(2)}) collective-permute-start(f32[128,128]{1,0:T(8,128)S(1)} %add.14), channel_id=1, source_target_pairs={{0,16},{2,18},{4,20},{6,22},{8,24},{10,26},{12,28},{14,30},{16,0},... | collective-permute-start | bytes 196616 | tf_op jit(solution)/shard_map/ppermute | solution.py:545
  55.0 3.7 %collective-permute-start.14 = (f32[128,128]{1,0:T(8,128)S(1)}, f32[128,128]{1,0:T(8,128)S(1)}, u32[]{:S(2)}, u32[]{:S(2)}) collective-permute-start(f32[128,128]{1,0:T(8,128)S(1)} %add.15.own_ref), channel_id=1, source_target_pairs={{0,1},{2,3},{4,5},{6,7},{8,9},{10,11},{12,13},{14,15},{16,17},{18,... | collective-permute-start | bytes 196616 | tf_op jit(solution)/shard_map/ppermute | solution.py:545
  (5 other events, 36.8 us)

commit v9 on v5

--- a/solution.py
+++ b/solution.py
@@ -493,7 +493,7 @@
         out_specs=tuple(VMEM for _ in outs),
         out_shape=tuple(outs),
         scratch_shapes=list(scratch),
-        compiler_params=pltpu.CompilerParams(vmem_limit_bytes=limit * 2**20),
+        compiler_params=pltpu.CompilerParams(vmem_limit_bytes=int(limit * 2**20)),
         cost_estimate=pl.CostEstimate(flops=flops, bytes_accessed=size, transcendentals=0),
     )
 
@@ -545,7 +545,7 @@
         [HBM] * 3,
         [shape((pack_rows, TILE), BF)],
         [pltpu.VMEM(voxels.shape, BF), pltpu.VMEM(strips.shape, BF), pltpu.SMEM(slot_to_brick.shape, jnp.int32), pltpu.SemaphoreType.DMA((3,))],
-        limit=60,
+        limit=53.5,
     )(slot_to_brick, voxels, strips)
     mate = swapped(own, 1)
     weight_shape = shape((PARTS, 3 * PART, 9 * PART), BF)
@@ -561,7 +561,7 @@
     near, far, staged = lax.optimization_barrier((near, far, staged))
     forward, backward = staged
     first = merged(near, far)
-    second = swapped(first, 1)
+    second = merged(swapped(near, 1), swapped(far, 1))
     activated, dpre, own = call(
         forward_kernel,
         [HBM, HBM] + [VMEM] * 14,

time: 54 us -> 52.7 us (0.976)
  Pallas kernels: 16.5 us -> 15.8 us
    pallas_call x1, Pallas kernels: 2.15 us -> 1.46 us  [shards(): call(pack_kernel, [HBM] * 3, [shape((pack_rows, TILE), BF)], [pltpu.VMEM(...]
    ppermute x12 -> x13, starting transfers between devices: 26 us -> 25.5 us  [sent(): return lax.ppermute(block, 'bricks', route)]
    ppermute x12 -> x13, waiting for transfers between devices: 9.26 us -> 9.46 us  [sent(): return lax.ppermute(block, 'bricks', route)]
  transfers between devices with their start and end apart: 12 -> 13, of which waited for: 6 -> 6; matrix products, arithmetic and copies ran while one was open for 0% -> 0% of each run, Pallas kernels for 12% -> 12%
where the time goes in v9:
time: 52.7 us; the launch traced here: 52.5 us
  starting transfers between devices  25.5 us (48%)
  Pallas kernels  15.8 us (30%)
  waiting for transfers between devices  9.46 us (18%)
  between operations  0.96 us (2%)
  local copies, waits for them, and re-layouts  0.72 us (1%)
    ppermute x13, starting transfers between devices, sent(): return lax.ppermute(block, 'bricks', route)  25.5 us
    ppermute x13, waiting for transfers between devices, sent(): return lax.ppermute(block, 'bricks', route)  9.46 us
    pallas_call x1, Pallas kernels, shards(): call(forward_kernel, [HBM, HBM] + [VMEM] * 14, [field, field, shape((pack...  6.94 us
    pallas_call x3, Pallas kernels, part_backward(): call(functools.partial(backward_kernel, (pair,)), [HBM, HBM] + [VMEM] * (...  5.73 us
    pallas_call x1, Pallas kernels, shards(): call(pack_kernel, [HBM] * 3, [shape((pack_rows, TILE), BF)], [pltpu.VMEM(...  1.46 us
  transfers between devices with their start and end apart: 13, of which 6 were waited for; matrix products, arithmetic and copies ran while one was open for 0% of the time, Pallas kernels for 12%

profile of v9, /device:TPU:0, one launch (start us, length us, event | category | flops | bytes accessed | tf_op | source)
XLA Modules:
  0.0 52.5 jit_solution(6284533357718011642)
XLA Ops:
  0.6 0.6 %copy-done.6 = s32[6]{0:T(128)S(1)} copy-done((s32[6]{0:T(128)S(1)}, s32[6]{0:T(128)}, u32[]{:S(2)}) %copy-start.6) | copy-done | bytes 48
  1.3 1.5 %shard_map.147.own_ref = bf16[784,128]{1,0:T(8,128)(2,1)S(1)} custom-call(s32[6]{0:T(128)S(1)} %copy-done.6, bf16[6,64,512]{2,1,0:T(8,128)(2,1)} %field_ref.1, bf16[4,512,128]{2,1,0:T(8,128)(2,1)} %constant.10.clone.strips_hbm.strips_ref), custom_call_target="tpu_custom_call" | custom-call | bytes 400000 | tf_op jit(solution)/shard_map/pallas_call | solution.py:543
  2.8 0.5 collective-permute-start
  3.3 1.1 %collective-permute-done.mate_ref = bf16[784,128]{1,0:T(8,128)(2,1)S(1)} collective-permute-done((bf16[784,128]{1,0:T(8,128)(2,1)S(1)}, bf16[784,128]{1,0:T(8,128)(2,1)S(1)}, u32[]{:S(2)}, u32[]{:S(2)}) %collective-permute-start) | collective-permute-done | bytes 200736 | tf_op jit(solution)/shard_map/ppermute | solution.py:502
  4.6 0.7 %collective-permute-start.2 = (bf16[128,128]{1,0:T(8,128)(2,1)S(1)}, bf16[128,128]{1,0:T(8,128)(2,1)S(1)}, u32[]{:S(2)}, u32[]{:S(2)}) collective-permute-start(bf16[128,128]{1,0:T(8,128)(2,1)S(1)} %get-tuple-element.35), channel_id=1, source_target_pairs={{1,4},{3,6},{4,1},{5,8},{6,3},{7,10},{8,5},{9,12},{10,7},{11,14},{... | collective-permute-start | bytes 98312 | tf_op jit(solution)/shard_map/ppermute | solution.py:502
  5.3 0.7 %collective-permute-start.1 = (bf16[400,128]{1,0:T(8,128)(2,1)S(1)}, bf16[400,128]{1,0:T(8,128)(2,1)S(1)}, u32[]{:S(2)}, u32[]{:S(2)}) collective-permute-start(bf16[400,128]{1,0:T(8,128)(2,1)S(1)} %get-tuple-element.34), channel_id=1, source_target_pairs={{1,2},{2,1},{3,4},{4,3},{5,6},{6,5},{7,8},{8,7},{9,10},{10,9},{11,... | collective-permute-start | bytes 307208 | tf_op jit(solution)/shard_map/ppermute | solution.py:502
  6.6 9.2 %collective-permute-start.3 = (bf16[400,128]{1,0:T(8,128)(2,1)S(1)}, bf16[400,128]{1,0:T(8,128)(2,1)S(1)}, u32[]{:S(2)}, u32[]{:S(2)}) collective-permute-start(bf16[400,128]{1,0:T(8,128)(2,1)S(1)} %collective-permute-done.1.near_ref), channel_id=1, source_target_pairs={{0,1},{1,0},{2,3},{3,2},{4,5},{5,4},{6,7},{7,6},{8,9},{9,8},{10,11... | collective-permute-start | bytes 307208 | tf_op jit(solution)/shard_map/ppermute | solution.py:502
  15.8 1.2 %collective-permute-done.4.far_ref = bf16[128,128]{1,0:T(8,128)(2,1)S(1)} collective-permute-done((bf16[128,128]{1,0:T(8,128)(2,1)S(1)}, bf16[128,128]{1,0:T(8,128)(2,1)S(1)}, u32[]{:S(2)}, u32[]{:S(2)}) %collective-permute-start.4) | collective-permute-done | bytes 32800 | tf_op jit(solution)/shard_map/ppermute | solution.py:502
  17.1 6.9 %shard_map.152 = (bf16[6,64,512]{2,1,0:T(8,128)(2,1)}, bf16[6,64,512]{2,1,0:T(8,128)(2,1)S(1)}, bf16[1040,128]{1,0:T(8,128)(2,1)S(1)}) custom-call(s32[6]{0:T(128)S(1)} %copy-done.6, s32[6,6]{1,0:T(8,128)S(1)} %copy-done.5, bf16[6,64,512]{2,1,0:T(8,128)(2,1)S(1)} %copy-done.4, bf16[784,128]{1,0:T(8,128)(2,1)S(1)} %shard_map.147.own_ref, ...), custom_call_target="tpu_custom_call" | custom-call | flops 4000000000 | bytes 400000 | tf_op jit(solution)/shard_map/pallas_call | solution.py:565
  24.3 1.4 %collective-permute-done.5.mate_ref.refs_4_ = bf16[1040,128]{1,0:T(8,128)(2,1)S(1)} collective-permute-done((bf16[1040,128]{1,0:T(8,128)(2,1)S(1)}, bf16[1040,128]{1,0:T(8,128)(2,1)S(1)}, u32[]{:S(2)}, u32[]{:S(2)}) %collective-permute-start.5) | collective-permute-done | bytes 266272 | tf_op jit(solution)/shard_map/ppermute | solution.py:502
  25.9 0.7 %collective-permute-start.8 = (bf16[400,128]{1,0:T(8,128)(2,1)S(1)}, bf16[400,128]{1,0:T(8,128)(2,1)S(1)}, u32[]{:S(2)}, u32[]{:S(2)}) collective-permute-start(bf16[400,128]{1,0:T(8,128)(2,1)S(1)} %get-tuple-element.46), channel_id=1, source_target_pairs={{1,2},{2,1},{3,4},{4,3},{5,6},{6,5},{7,8},{8,7},{9,10},{10,9},{11,... | collective-permute-start | bytes 307208 | tf_op jit(solution)/shard_map/ppermute | solution.py:502
  26.6 3.4 %collective-permute-start.6 = (f32[128,128]{1,0:T(8,128)S(1)}, f32[128,128]{1,0:T(8,128)S(1)}, u32[]{:S(2)}, u32[]{:S(2)}) collective-permute-start(f32[128,128]{1,0:T(8,128)S(1)} %get-tuple-element.47), channel_id=1, source_target_pairs={{0,2},{1,3},{2,0},{3,1},{4,6},{5,7},{6,4},{7,5},{8,10},{9,11},{10,... | collective-permute-start | bytes 196616 | tf_op jit(solution)/shard_map/ppermute | solution.py:502
  30.0 0.7 %collective-permute-start.7 = (bf16[128,128]{1,0:T(8,128)(2,1)S(1)}, bf16[128,128]{1,0:T(8,128)(2,1)S(1)}, u32[]{:S(2)}, u32[]{:S(2)}) collective-permute-start(bf16[128,128]{1,0:T(8,128)(2,1)S(1)} %get-tuple-element.45), channel_id=1, source_target_pairs={{1,4},{3,6},{4,1},{5,8},{6,3},{7,10},{8,5},{9,12},{10,7},{11,14},{... | collective-permute-start | bytes 98312 | tf_op jit(solution)/shard_map/ppermute | solution.py:502
  30.7 4.4 %collective-permute-done.6 = f32[128,128]{1,0:T(8,128)S(1)} collective-permute-done((f32[128,128]{1,0:T(8,128)S(1)}, f32[128,128]{1,0:T(8,128)S(1)}, u32[]{:S(2)}, u32[]{:S(2)}) %collective-permute-start.6) | collective-permute-done | bytes 65568 | tf_op jit(solution)/shard_map/ppermute | solution.py:502
  35.0 1.0 %collective-permute-start.10 = (bf16[528,128]{1,0:T(8,128)(2,1)S(1)}, bf16[528,128]{1,0:T(8,128)(2,1)S(1)}, u32[]{:S(2)}, u32[]{:S(2)}) collective-permute-start(bf16[528,128]{1,0:T(8,128)(2,1)S(1)} %shard_map.154.refs_5_), channel_id=1, source_target_pairs={{0,1},{1,0},{2,3},{3,2},{4,5},{5,4},{6,7},{7,6},{8,9},{9,8},{10,11... | collective-permute-start | bytes 405512 | tf_op jit(solution)/shard_map/ppermute | solution.py:502
  36.1 3.7 %collective-permute-start.9 = (f32[128,128]{1,0:T(8,128)S(1)}, f32[128,128]{1,0:T(8,128)S(1)}, u32[]{:S(2)}, u32[]{:S(2)}) collective-permute-start(f32[128,128]{1,0:T(8,128)S(1)} %add.9), channel_id=1, source_target_pairs={{0,4},{1,5},{2,6},{3,7},{4,0},{5,1},{6,2},{7,3},{8,12},{9,13},{10,... | collective-permute-start | bytes 196616 | tf_op jit(solution)/shard_map/ppermute | solution.py:502
  39.8 1.6 %shard_map.155.refs_11_ = bf16[6,64,512]{2,1,0:T(8,128)(2,1)S(1)} custom-call(s32[6]{0:T(128)S(1)} %copy-done.6, s32[6,6]{1,0:T(8,128)S(1)} %copy-done.5, bf16[6,64,512]{2,1,0:T(8,128)(2,1)S(1)} %get-tuple-element.42.refs_2_, bf16[1040,128]{1,0:T(8,128)(2,1)S(1)} %get-tuple-element.43.own_ref.refs_3_, ...), custom_call_target="tpu_custom_call" | custom-call | flops 1000000000 | bytes 400000 | tf_op jit(solution)/shard_map/pallas_call | solution.py:590
  41.4 0.6 %collective-permute-done.9 = f32[128,128]{1,0:T(8,128)S(1)} collective-permute-done((f32[128,128]{1,0:T(8,128)S(1)}, f32[128,128]{1,0:T(8,128)S(1)}, u32[]{:S(2)}, u32[]{:S(2)}) %collective-permute-start.9) | collective-permute-done | bytes 65568 | tf_op jit(solution)/shard_map/ppermute | solution.py:502
  42.1 1.9 %collective-permute-start.11 = (f32[128,128]{1,0:T(8,128)S(1)}, f32[128,128]{1,0:T(8,128)S(1)}, u32[]{:S(2)}, u32[]{:S(2)}) collective-permute-start(f32[128,128]{1,0:T(8,128)S(1)} %add.10), channel_id=1, source_target_pairs={{0,8},{1,9},{2,10},{3,11},{4,12},{5,13},{6,14},{7,15},{8,0},{9,1},... | collective-permute-start | bytes 196616 | tf_op jit(solution)/shard_map/ppermute | solution.py:502
  44.0 1.7 %shard_map.156.refs_11_ = bf16[6,64,512]{2,1,0:T(8,128)(2,1)S(1)} custom-call(s32[6]{0:T(128)S(1)} %copy-done.6, s32[6,6]{1,0:T(8,128)S(1)} %copy-done.5, bf16[6,64,512]{2,1,0:T(8,128)(2,1)S(1)} %get-tuple-element.42.refs_2_, bf16[1040,128]{1,0:T(8,128)(2,1)S(1)} %get-tuple-element.43.own_ref.refs_3_, ...), custom_call_target="tpu_custom_call" | custom-call | flops 1000000000 | bytes 400000 | tf_op jit(solution)/shard_map/pallas_call | solution.py:590
  45.6 0.8 %collective-permute-done.11 = f32[128,128]{1,0:T(8,128)S(1)} collective-permute-done((f32[128,128]{1,0:T(8,128)S(1)}, f32[128,128]{1,0:T(8,128)S(1)}, u32[]{:S(2)}, u32[]{:S(2)}) %collective-permute-start.11) | collective-permute-done | bytes 65568 | tf_op jit(solution)/shard_map/ppermute | solution.py:502
  46.4 2.9 %collective-permute-start.12 = (f32[128,128]{1,0:T(8,128)S(1)}, f32[128,128]{1,0:T(8,128)S(1)}, u32[]{:S(2)}, u32[]{:S(2)}) collective-permute-start(f32[128,128]{1,0:T(8,128)S(1)} %add.11.a_ref), channel_id=1, source_target_pairs={{0,16},{1,17},{2,18},{3,19},{4,20},{5,21},{6,22},{7,23},{8,24},{9,... | collective-permute-start | bytes 196616 | tf_op jit(solution)/shard_map/ppermute | solution.py:502
  49.3 2.4 %shard_map.157 = bf16[6,64,512]{2,1,0:T(8,128)(2,1)} custom-call(s32[6]{0:T(128)S(1)} %copy-done.6, s32[6,6]{1,0:T(8,128)S(1)} %copy-done.5, bf16[6,64,512]{2,1,0:T(8,128)(2,1)S(1)} %get-tuple-element.42.refs_2_, bf16[1040,128]{1,0:T(8,128)(2,1)S(1)} %get-tuple-element.43.own_ref.refs_3_, bf16[1040,128]{1,0:T(8,128)(2,1)S(1)} %collective-permute-done.5.mate_ref.refs_4_, ...), custom_call_target="tpu_custom_call" | custom-call | flops 1000000000 | bytes 400000 | tf_op jit(solution)/shard_map/pallas_call | solution.py:590
  51.8 0.7 %shard_map.158 = (f32[216,64]{1,0:T(8,128)}, f32[1,64]{1,0:T(1,128)}) custom-call(f32[128,128]{1,0:T(8,128)S(1)} %add.11.a_ref, f32[128,128]{1,0:T(8,128)S(1)} %collective-permute-done.12.b_ref), custom_call_target="tpu_custom_call" | custom-call | bytes 400000 | tf_op jit(solution)/shard_map/pallas_call | solution.py:618
  (41 shorter events, 1.3 us)
Async XLA Ops:
  2.8 3.2 %copy-start.8 = (bf16[64,8,3,3,3]{0,1,4,3,2:T(8,128)(2,1)S(1)}, bf16[64,8,3,3,3]{0,1,4,3,2:T(8,128)(2,1)}, u32[]{:S(2)}) copy-start(bf16[64,8,3,3,3]{0,1,4,3,2:T(8,128)(2,1)} %param.13) | copy-start | bytes 82948
  2.8 1.6 %collective-permute-start = (bf16[784,128]{1,0:T(8,128)(2,1)S(1)}, bf16[784,128]{1,0:T(8,128)(2,1)S(1)}, u32[]{:S(2)}, u32[]{:S(2)}) collective-permute-start(bf16[784,128]{1,0:T(8,128)(2,1)S(1)} %shard_map.147.own_ref), channel_id=1, source_target_pairs={{0,1},{1,0},{2,3},{3,2},{4,5},{5,4},{6,7},{7,6},{8,9},{9,8},{10,11... | collective-permute-start | bytes 602120 | tf_op jit(solution)/shard_map/ppermute | solution.py:502
  4.6 2.0 %collective-permute-start.2 = (bf16[128,128]{1,0:T(8,128)(2,1)S(1)}, bf16[128,128]{1,0:T(8,128)(2,1)S(1)}, u32[]{:S(2)}, u32[]{:S(2)}) collective-permute-start(bf16[128,128]{1,0:T(8,128)(2,1)S(1)} %get-tuple-element.35), channel_id=1, source_target_pairs={{1,4},{3,6},{4,1},{5,8},{6,3},{7,10},{8,5},{9,12},{10,7},{11,14},{... | collective-permute-start | bytes 98312 | tf_op jit(solution)/shard_map/ppermute | solution.py:502
  5.3 1.3 %collective-permute-start.1 = (bf16[400,128]{1,0:T(8,128)(2,1)S(1)}, bf16[400,128]{1,0:T(8,128)(2,1)S(1)}, u32[]{:S(2)}, u32[]{:S(2)}) collective-permute-start(bf16[400,128]{1,0:T(8,128)(2,1)S(1)} %get-tuple-element.34), channel_id=1, source_target_pairs={{1,2},{2,1},{3,4},{4,3},{5,6},{6,5},{7,8},{8,7},{9,10},{10,9},{11,... | collective-permute-start | bytes 307208 | tf_op jit(solution)/shard_map/ppermute | solution.py:502
  6.0 11.1 %copy-start = (bf16[4,256,1024]{2,1,0:T(8,128)(2,1)S(1)}, bf16[4,256,1024]{2,1,0:T(8,128)(2,1)}, u32[]{:S(2)}) copy-start(bf16[4,256,1024]{2,1,0:T(8,128)(2,1)} %constant.13.clone.shifts_ref.refs_10_) | copy-start | bytes 6291460
  6.0 11.0 %copy-start.1 = (bf16[4,384,128]{2,1,0:T(8,128)(2,1)S(1)}, bf16[4,384,128]{2,1,0:T(8,128)(2,1)}, u32[]{:S(2)}) copy-start(bf16[4,384,128]{2,1,0:T(8,128)(2,1)} %constant.12.clone.ends_ref.refs_9_) | copy-start | bytes 1179652
  6.0 11.0 %copy-start.2 = (bf16[256,512]{1,0:T(8,128)(2,1)S(1)}, bf16[256,512]{1,0:T(8,128)(2,1)}, u32[]{:S(2)}) copy-start(bf16[256,512]{1,0:T(8,128)(2,1)} %constant.11.clone.spread_ref.refs_8_) | copy-start | bytes 786436
  6.0 11.0 %copy-start.3 = (bf16[4,512,128]{2,1,0:T(8,128)(2,1)S(1)}, bf16[4,512,128]{2,1,0:T(8,128)(2,1)}, u32[]{:S(2)}) copy-start(bf16[4,512,128]{2,1,0:T(8,128)(2,1)} %constant.10.clone.strips_hbm.strips_ref) | copy-start | bytes 1572868
  6.0 11.0 %copy-start.4 = (bf16[6,64,512]{2,1,0:T(8,128)(2,1)S(1)}, bf16[6,64,512]{2,1,0:T(8,128)(2,1)}, u32[]{:S(2)}) copy-start(bf16[6,64,512]{2,1,0:T(8,128)(2,1)} %field_ref.1) | copy-start | bytes 1179652
  6.0 11.0 %copy-start.5 = (s32[6,6]{1,0:T(8,128)S(1)}, s32[6,6]{1,0:T(8,128)}, u32[]{:S(2)}) copy-start(s32[6,6]{1,0:T(8,128)} %refs_1_.5) | copy-start | bytes 436
  6.0 11.0 %copy-start.7 = (bf16[6,64,512]{2,1,0:T(8,128)(2,1)S(1)}, bf16[6,64,512]{2,1,0:T(8,128)(2,1)}, u32[]{:S(2)}) copy-start(bf16[6,64,512]{2,1,0:T(8,128)(2,1)} %upstream_ref.1) | copy-start | bytes 1179652
  6.0 11.0 %copy-start.9 = (s32[6,512]{1,0:T(8,128)S(1)}, s32[6,512]{1,0:T(8,128)}, u32[]{:S(2)}) copy-start(s32[6,512]{1,0:T(8,128)} %cortex_ref.1) | copy-start | bytes 36868
  6.0 11.0 %copy-start.10 = (f32[64]{0:T(128)S(1)}, f32[64]{0:T(128)}, u32[]{:S(2)}) copy-start(f32[64]{0:T(128)} %param.14) | copy-start | bytes 772
  6.1 11.0 %copy-start.11 = (f32[160,80]{1,0:T(8,128)S(1)}, f32[160,80]{1,0:T(8,128)}, u32[]{:S(2)}) copy-start(f32[160,80]{1,0:T(8,128)} %constant.20.fold_ref) | copy-start | bytes 153604
  6.6 10.4 %collective-permute-start.3 = (bf16[400,128]{1,0:T(8,128)(2,1)S(1)}, bf16[400,128]{1,0:T(8,128)(2,1)S(1)}, u32[]{:S(2)}, u32[]{:S(2)}) collective-permute-start(bf16[400,128]{1,0:T(8,128)(2,1)S(1)} %collective-permute-done.1.near_ref), channel_id=1, source_target_pairs={{0,1},{1,0},{2,3},{3,2},{4,5},{5,4},{6,7},{7,6},{8,9},{9,8},{10,11... | collective-permute-start | bytes 307208 | tf_op jit(solution)/shard_map/ppermute | solution.py:502
  15.8 1.2 %collective-permute-start.4 = (bf16[128,128]{1,0:T(8,128)(2,1)S(1)}, bf16[128,128]{1,0:T(8,128)(2,1)S(1)}, u32[]{:S(2)}, u32[]{:S(2)}) collective-permute-start(bf16[128,128]{1,0:T(8,128)(2,1)S(1)} %collective-permute-done.2.far_ref), channel_id=1, source_target_pairs={{0,1},{1,0},{2,3},{3,2},{4,5},{5,4},{6,7},{7,6},{8,9},{9,8},{10,11... | collective-permute-start | bytes 98312 | tf_op jit(solution)/shard_map/ppermute | solution.py:502
  24.0 1.6 %collective-permute-start.5 = (bf16[1040,128]{1,0:T(8,128)(2,1)S(1)}, bf16[1040,128]{1,0:T(8,128)(2,1)S(1)}, u32[]{:S(2)}, u32[]{:S(2)}) collective-permute-start(bf16[1040,128]{1,0:T(8,128)(2,1)S(1)} %get-tuple-element.43.own_ref.refs_3_), channel_id=1, source_target_pairs={{0,1},{1,0},{2,3},{3,2},{4,5},{5,4},{6,7},{7,6},{8,9},{9,8},{10,11... | collective-permute-start | bytes 798728 | tf_op jit(solution)/shard_map/ppermute | solution.py:502
  25.9 9.1 %collective-permute-start.8 = (bf16[400,128]{1,0:T(8,128)(2,1)S(1)}, bf16[400,128]{1,0:T(8,128)(2,1)S(1)}, u32[]{:S(2)}, u32[]{:S(2)}) collective-permute-start(bf16[400,128]{1,0:T(8,128)(2,1)S(1)} %get-tuple-element.46), channel_id=1, source_target_pairs={{1,2},{2,1},{3,4},{4,3},{5,6},{6,5},{7,8},{8,7},{9,10},{10,9},{11,... | collective-permute-start | bytes 307208 | tf_op jit(solution)/shard_map/ppermute | solution.py:502
  26.6 8.5 %collective-permute-start.6 = (f32[128,128]{1,0:T(8,128)S(1)}, f32[128,128]{1,0:T(8,128)S(1)}, u32[]{:S(2)}, u32[]{:S(2)}) collective-permute-start(f32[128,128]{1,0:T(8,128)S(1)} %get-tuple-element.47), channel_id=1, source_target_pairs={{0,2},{1,3},{2,0},{3,1},{4,6},{5,7},{6,4},{7,5},{8,10},{9,11},{10,... | collective-permute-start | bytes 196616 | tf_op jit(solution)/shard_map/ppermute | solution.py:502
  30.0 0.7 %collective-permute-start.7 = (bf16[128,128]{1,0:T(8,128)(2,1)S(1)}, bf16[128,128]{1,0:T(8,128)(2,1)S(1)}, u32[]{:S(2)}, u32[]{:S(2)}) collective-permute-start(bf16[128,128]{1,0:T(8,128)(2,1)S(1)} %get-tuple-element.45), channel_id=1, source_target_pairs={{1,4},{3,6},{4,1},{5,8},{6,3},{7,10},{8,5},{9,12},{10,7},{11,14},{... | collective-permute-start | bytes 98312 | tf_op jit(solution)/shard_map/ppermute | solution.py:502
  35.0 4.7 %collective-permute-start.10 = (bf16[528,128]{1,0:T(8,128)(2,1)S(1)}, bf16[528,128]{1,0:T(8,128)(2,1)S(1)}, u32[]{:S(2)}, u32[]{:S(2)}) collective-permute-start(bf16[528,128]{1,0:T(8,128)(2,1)S(1)} %shard_map.154.refs_5_), channel_id=1, source_target_pairs={{0,1},{1,0},{2,3},{3,2},{4,5},{5,4},{6,7},{7,6},{8,9},{9,8},{10,11... | collective-permute-start | bytes 405512 | tf_op jit(solution)/shard_map/ppermute | solution.py:502
  36.1 6.0 %collective-permute-start.9 = (f32[128,128]{1,0:T(8,128)S(1)}, f32[128,128]{1,0:T(8,128)S(1)}, u32[]{:S(2)}, u32[]{:S(2)}) collective-permute-start(f32[128,128]{1,0:T(8,128)S(1)} %add.9), channel_id=1, source_target_pairs={{0,4},{1,5},{2,6},{3,7},{4,0},{5,1},{6,2},{7,3},{8,12},{9,13},{10,... | collective-permute-start | bytes 196616 | tf_op jit(solution)/shard_map/ppermute | solution.py:502
  42.1 4.3 %collective-permute-start.11 = (f32[128,128]{1,0:T(8,128)S(1)}, f32[128,128]{1,0:T(8,128)S(1)}, u32[]{:S(2)}, u32[]{:S(2)}) collective-permute-start(f32[128,128]{1,0:T(8,128)S(1)} %add.10), channel_id=1, source_target_pairs={{0,8},{1,9},{2,10},{3,11},{4,12},{5,13},{6,14},{7,15},{8,0},{9,1},... | collective-permute-start | bytes 196616 | tf_op jit(solution)/shard_map/ppermute | solution.py:502
  46.4 5.3 %collective-permute-start.12 = (f32[128,128]{1,0:T(8,128)S(1)}, f32[128,128]{1,0:T(8,128)S(1)}, u32[]{:S(2)}, u32[]{:S(2)}) collective-permute-start(f32[128,128]{1,0:T(8,128)S(1)} %add.11.a_ref), channel_id=1, source_target_pairs={{0,16},{1,17},{2,18},{3,19},{4,20},{5,21},{6,22},{7,23},{8,24},{9,... | collective-permute-start | bytes 196616 | tf_op jit(solution)/shard_map/ppermute | solution.py:502
  (1 other events, 0.7 us)

commit v10 on v9

--- a/solution.py
+++ b/solution.py
@@ -557,7 +557,7 @@
         functools.partial(route_kernel, slots), [VMEM, VMEM], [near_shape, far_shape], box,
         flops=BUSY,
     )(own, mate)
-    near, far = routed(near, 1), routed(far, 2)
+    far, near = routed(far, 2), routed(near, 1)
     near, far, staged = lax.optimization_barrier((near, far, staged))
     forward, backward = staged
     first = merged(near, far)

time: 52.7 us -> 52.7 us (level)
  no operation moved by 1% of the time
where the time goes in v10:
time: 52.7 us; the launch traced here: 52.5 us
  starting transfers between devices  25.5 us (48%)
  Pallas kernels  15.8 us (30%)
  waiting for transfers between devices  9.46 us (18%)
  between operations  0.96 us (2%)
  local copies, waits for them, and re-layouts  0.72 us (1%)
    ppermute x13, starting transfers between devices, sent(): return lax.ppermute(block, 'bricks', route)  25.5 us
    ppermute x13, waiting for transfers between devices, sent(): return lax.ppermute(block, 'bricks', route)  9.46 us
    pallas_call x1, Pallas kernels, shards(): call(forward_kernel, [HBM, HBM] + [VMEM] * 14, [field, field, shape((pack...  6.94 us
    pallas_call x3, Pallas kernels, part_backward(): call(functools.partial(backward_kernel, (pair,)), [HBM, HBM] + [VMEM] * (...  5.73 us
    pallas_call x1, Pallas kernels, shards(): call(pack_kernel, [HBM] * 3, [shape((pack_rows, TILE), BF)], [pltpu.VMEM(...  1.46 us
  transfers between devices with their start and end apart: 13, of which 6 were waited for; matrix products, arithmetic and copies ran while one was open for 0% of the time, Pallas kernels for 12%

profile of v10, /device:TPU:0, one launch (start us, length us, event | category | flops | bytes accessed | tf_op | source)
XLA Modules:
  0.0 52.5 jit_solution(6284533357718011642)
XLA Ops:
  0.6 0.6 %copy-done.6 = s32[6]{0:T(128)S(1)} copy-done((s32[6]{0:T(128)S(1)}, s32[6]{0:T(128)}, u32[]{:S(2)}) %copy-start.6) | copy-done | bytes 48
  1.3 1.5 %shard_map.147.own_ref = bf16[784,128]{1,0:T(8,128)(2,1)S(1)} custom-call(s32[6]{0:T(128)S(1)} %copy-done.6, bf16[6,64,512]{2,1,0:T(8,128)(2,1)} %field_ref.1, bf16[4,512,128]{2,1,0:T(8,128)(2,1)} %constant.10.clone.strips_hbm.strips_ref), custom_call_target="tpu_custom_call" | custom-call | bytes 400000 | tf_op jit(solution)/shard_map/pallas_call | solution.py:543
  2.8 0.5 collective-permute-start
  3.3 1.1 %collective-permute-done.mate_ref = bf16[784,128]{1,0:T(8,128)(2,1)S(1)} collective-permute-done((bf16[784,128]{1,0:T(8,128)(2,1)S(1)}, bf16[784,128]{1,0:T(8,128)(2,1)S(1)}, u32[]{:S(2)}, u32[]{:S(2)}) %collective-permute-start) | collective-permute-done | bytes 200736 | tf_op jit(solution)/shard_map/ppermute | solution.py:502
  4.6 0.7 %collective-permute-start.2 = (bf16[128,128]{1,0:T(8,128)(2,1)S(1)}, bf16[128,128]{1,0:T(8,128)(2,1)S(1)}, u32[]{:S(2)}, u32[]{:S(2)}) collective-permute-start(bf16[128,128]{1,0:T(8,128)(2,1)S(1)} %get-tuple-element.35), channel_id=1, source_target_pairs={{1,4},{3,6},{4,1},{5,8},{6,3},{7,10},{8,5},{9,12},{10,7},{11,14},{... | collective-permute-start | bytes 98312 | tf_op jit(solution)/shard_map/ppermute | solution.py:502
  5.3 0.7 %collective-permute-start.1 = (bf16[400,128]{1,0:T(8,128)(2,1)S(1)}, bf16[400,128]{1,0:T(8,128)(2,1)S(1)}, u32[]{:S(2)}, u32[]{:S(2)}) collective-permute-start(bf16[400,128]{1,0:T(8,128)(2,1)S(1)} %get-tuple-element.34), channel_id=1, source_target_pairs={{1,2},{2,1},{3,4},{4,3},{5,6},{6,5},{7,8},{8,7},{9,10},{10,9},{11,... | collective-permute-start | bytes 307208 | tf_op jit(solution)/shard_map/ppermute | solution.py:502
  6.6 9.2 %collective-permute-start.3 = (bf16[400,128]{1,0:T(8,128)(2,1)S(1)}, bf16[400,128]{1,0:T(8,128)(2,1)S(1)}, u32[]{:S(2)}, u32[]{:S(2)}) collective-permute-start(bf16[400,128]{1,0:T(8,128)(2,1)S(1)} %collective-permute-done.1.near_ref), channel_id=1, source_target_pairs={{0,1},{1,0},{2,3},{3,2},{4,5},{5,4},{6,7},{7,6},{8,9},{9,8},{10,11... | collective-permute-start | bytes 307208 | tf_op jit(solution)/shard_map/ppermute | solution.py:502
  15.8 1.2 %collective-permute-done.4.far_ref = bf16[128,128]{1,0:T(8,128)(2,1)S(1)} collective-permute-done((bf16[128,128]{1,0:T(8,128)(2,1)S(1)}, bf16[128,128]{1,0:T(8,128)(2,1)S(1)}, u32[]{:S(2)}, u32[]{:S(2)}) %collective-permute-start.4) | collective-permute-done | bytes 32800 | tf_op jit(solution)/shard_map/ppermute | solution.py:502
  17.1 6.9 %shard_map.152 = (bf16[6,64,512]{2,1,0:T(8,128)(2,1)}, bf16[6,64,512]{2,1,0:T(8,128)(2,1)S(1)}, bf16[1040,128]{1,0:T(8,128)(2,1)S(1)}) custom-call(s32[6]{0:T(128)S(1)} %copy-done.6, s32[6,6]{1,0:T(8,128)S(1)} %copy-done.5, bf16[6,64,512]{2,1,0:T(8,128)(2,1)S(1)} %copy-done.4, bf16[784,128]{1,0:T(8,128)(2,1)S(1)} %shard_map.147.own_ref, ...), custom_call_target="tpu_custom_call" | custom-call | flops 4000000000 | bytes 400000 | tf_op jit(solution)/shard_map/pallas_call | solution.py:565
  24.3 1.4 %collective-permute-done.5.mate_ref.refs_4_ = bf16[1040,128]{1,0:T(8,128)(2,1)S(1)} collective-permute-done((bf16[1040,128]{1,0:T(8,128)(2,1)S(1)}, bf16[1040,128]{1,0:T(8,128)(2,1)S(1)}, u32[]{:S(2)}, u32[]{:S(2)}) %collective-permute-start.5) | collective-permute-done | bytes 266272 | tf_op jit(solution)/shard_map/ppermute | solution.py:502
  25.9 0.7 %collective-permute-start.8 = (bf16[400,128]{1,0:T(8,128)(2,1)S(1)}, bf16[400,128]{1,0:T(8,128)(2,1)S(1)}, u32[]{:S(2)}, u32[]{:S(2)}) collective-permute-start(bf16[400,128]{1,0:T(8,128)(2,1)S(1)} %get-tuple-element.46), channel_id=1, source_target_pairs={{1,2},{2,1},{3,4},{4,3},{5,6},{6,5},{7,8},{8,7},{9,10},{10,9},{11,... | collective-permute-start | bytes 307208 | tf_op jit(solution)/shard_map/ppermute | solution.py:502
  26.6 3.4 %collective-permute-start.6 = (f32[128,128]{1,0:T(8,128)S(1)}, f32[128,128]{1,0:T(8,128)S(1)}, u32[]{:S(2)}, u32[]{:S(2)}) collective-permute-start(f32[128,128]{1,0:T(8,128)S(1)} %get-tuple-element.47), channel_id=1, source_target_pairs={{0,2},{1,3},{2,0},{3,1},{4,6},{5,7},{6,4},{7,5},{8,10},{9,11},{10,... | collective-permute-start | bytes 196616 | tf_op jit(solution)/shard_map/ppermute | solution.py:502
  30.0 0.7 %collective-permute-start.7 = (bf16[128,128]{1,0:T(8,128)(2,1)S(1)}, bf16[128,128]{1,0:T(8,128)(2,1)S(1)}, u32[]{:S(2)}, u32[]{:S(2)}) collective-permute-start(bf16[128,128]{1,0:T(8,128)(2,1)S(1)} %get-tuple-element.45), channel_id=1, source_target_pairs={{1,4},{3,6},{4,1},{5,8},{6,3},{7,10},{8,5},{9,12},{10,7},{11,14},{... | collective-permute-start | bytes 98312 | tf_op jit(solution)/shard_map/ppermute | solution.py:502
  30.7 4.4 %collective-permute-done.6 = f32[128,128]{1,0:T(8,128)S(1)} collective-permute-done((f32[128,128]{1,0:T(8,128)S(1)}, f32[128,128]{1,0:T(8,128)S(1)}, u32[]{:S(2)}, u32[]{:S(2)}) %collective-permute-start.6) | collective-permute-done | bytes 65568 | tf_op jit(solution)/shard_map/ppermute | solution.py:502
  35.0 1.0 %collective-permute-start.10 = (bf16[528,128]{1,0:T(8,128)(2,1)S(1)}, bf16[528,128]{1,0:T(8,128)(2,1)S(1)}, u32[]{:S(2)}, u32[]{:S(2)}) collective-permute-start(bf16[528,128]{1,0:T(8,128)(2,1)S(1)} %shard_map.154.refs_5_), channel_id=1, source_target_pairs={{0,1},{1,0},{2,3},{3,2},{4,5},{5,4},{6,7},{7,6},{8,9},{9,8},{10,11... | collective-permute-start | bytes 405512 | tf_op jit(solution)/shard_map/ppermute | solution.py:502
  36.1 3.7 %collective-permute-start.9 = (f32[128,128]{1,0:T(8,128)S(1)}, f32[128,128]{1,0:T(8,128)S(1)}, u32[]{:S(2)}, u32[]{:S(2)}) collective-permute-start(f32[128,128]{1,0:T(8,128)S(1)} %add.9), channel_id=1, source_target_pairs={{0,4},{1,5},{2,6},{3,7},{4,0},{5,1},{6,2},{7,3},{8,12},{9,13},{10,... | collective-permute-start | bytes 196616 | tf_op jit(solution)/shard_map/ppermute | solution.py:502
  39.8 1.6 %shard_map.155.refs_11_ = bf16[6,64,512]{2,1,0:T(8,128)(2,1)S(1)} custom-call(s32[6]{0:T(128)S(1)} %copy-done.6, s32[6,6]{1,0:T(8,128)S(1)} %copy-done.5, bf16[6,64,512]{2,1,0:T(8,128)(2,1)S(1)} %get-tuple-element.42.refs_2_, bf16[1040,128]{1,0:T(8,128)(2,1)S(1)} %get-tuple-element.43.own_ref.refs_3_, ...), custom_call_target="tpu_custom_call" | custom-call | flops 1000000000 | bytes 400000 | tf_op jit(solution)/shard_map/pallas_call | solution.py:590
  41.4 0.6 %collective-permute-done.9 = f32[128,128]{1,0:T(8,128)S(1)} collective-permute-done((f32[128,128]{1,0:T(8,128)S(1)}, f32[128,128]{1,0:T(8,128)S(1)}, u32[]{:S(2)}, u32[]{:S(2)}) %collective-permute-start.9) | collective-permute-done | bytes 65568 | tf_op jit(solution)/shard_map/ppermute | solution.py:502
  42.1 1.9 %collective-permute-start.11 = (f32[128,128]{1,0:T(8,128)S(1)}, f32[128,128]{1,0:T(8,128)S(1)}, u32[]{:S(2)}, u32[]{:S(2)}) collective-permute-start(f32[128,128]{1,0:T(8,128)S(1)} %add.10), channel_id=1, source_target_pairs={{0,8},{1,9},{2,10},{3,11},{4,12},{5,13},{6,14},{7,15},{8,0},{9,1},... | collective-permute-start | bytes 196616 | tf_op jit(solution)/shard_map/ppermute | solution.py:502
  44.0 1.7 %shard_map.156.refs_11_ = bf16[6,64,512]{2,1,0:T(8,128)(2,1)S(1)} custom-call(s32[6]{0:T(128)S(1)} %copy-done.6, s32[6,6]{1,0:T(8,128)S(1)} %copy-done.5, bf16[6,64,512]{2,1,0:T(8,128)(2,1)S(1)} %get-tuple-element.42.refs_2_, bf16[1040,128]{1,0:T(8,128)(2,1)S(1)} %get-tuple-element.43.own_ref.refs_3_, ...), custom_call_target="tpu_custom_call" | custom-call | flops 1000000000 | bytes 400000 | tf_op jit(solution)/shard_map/pallas_call | solution.py:590
  45.6 0.8 %collective-permute-done.11 = f32[128,128]{1,0:T(8,128)S(1)} collective-permute-done((f32[128,128]{1,0:T(8,128)S(1)}, f32[128,128]{1,0:T(8,128)S(1)}, u32[]{:S(2)}, u32[]{:S(2)}) %collective-permute-start.11) | collective-permute-done | bytes 65568 | tf_op jit(solution)/shard_map/ppermute | solution.py:502
  46.4 2.9 %collective-permute-start.12 = (f32[128,128]{1,0:T(8,128)S(1)}, f32[128,128]{1,0:T(8,128)S(1)}, u32[]{:S(2)}, u32[]{:S(2)}) collective-permute-start(f32[128,128]{1,0:T(8,128)S(1)} %add.11.a_ref), channel_id=1, source_target_pairs={{0,16},{1,17},{2,18},{3,19},{4,20},{5,21},{6,22},{7,23},{8,24},{9,... | collective-permute-start | bytes 196616 | tf_op jit(solution)/shard_map/ppermute | solution.py:502
  49.3 2.4 %shard_map.157 = bf16[6,64,512]{2,1,0:T(8,128)(2,1)} custom-call(s32[6]{0:T(128)S(1)} %copy-done.6, s32[6,6]{1,0:T(8,128)S(1)} %copy-done.5, bf16[6,64,512]{2,1,0:T(8,128)(2,1)S(1)} %get-tuple-element.42.refs_2_, bf16[1040,128]{1,0:T(8,128)(2,1)S(1)} %get-tuple-element.43.own_ref.refs_3_, bf16[1040,128]{1,0:T(8,128)(2,1)S(1)} %collective-permute-done.5.mate_ref.refs_4_, ...), custom_call_target="tpu_custom_call" | custom-call | flops 1000000000 | bytes 400000 | tf_op jit(solution)/shard_map/pallas_call | solution.py:590
  51.8 0.7 %shard_map.158 = (f32[216,64]{1,0:T(8,128)}, f32[1,64]{1,0:T(1,128)}) custom-call(f32[128,128]{1,0:T(8,128)S(1)} %add.11.a_ref, f32[128,128]{1,0:T(8,128)S(1)} %collective-permute-done.12.b_ref), custom_call_target="tpu_custom_call" | custom-call | bytes 400000 | tf_op jit(solution)/shard_map/pallas_call | solution.py:618
  (41 shorter events, 1.3 us)
Async XLA Ops:
  2.8 3.2 %copy-start.8 = (bf16[64,8,3,3,3]{0,1,4,3,2:T(8,128)(2,1)S(1)}, bf16[64,8,3,3,3]{0,1,4,3,2:T(8,128)(2,1)}, u32[]{:S(2)}) copy-start(bf16[64,8,3,3,3]{0,1,4,3,2:T(8,128)(2,1)} %param.13) | copy-start | bytes 82948
  2.8 1.6 %collective-permute-start = (bf16[784,128]{1,0:T(8,128)(2,1)S(1)}, bf16[784,128]{1,0:T(8,128)(2,1)S(1)}, u32[]{:S(2)}, u32[]{:S(2)}) collective-permute-start(bf16[784,128]{1,0:T(8,128)(2,1)S(1)} %shard_map.147.own_ref), channel_id=1, source_target_pairs={{0,1},{1,0},{2,3},{3,2},{4,5},{5,4},{6,7},{7,6},{8,9},{9,8},{10,11... | collective-permute-start | bytes 602120 | tf_op jit(solution)/shard_map/ppermute | solution.py:502
  4.6 2.0 %collective-permute-start.2 = (bf16[128,128]{1,0:T(8,128)(2,1)S(1)}, bf16[128,128]{1,0:T(8,128)(2,1)S(1)}, u32[]{:S(2)}, u32[]{:S(2)}) collective-permute-start(bf16[128,128]{1,0:T(8,128)(2,1)S(1)} %get-tuple-element.35), channel_id=1, source_target_pairs={{1,4},{3,6},{4,1},{5,8},{6,3},{7,10},{8,5},{9,12},{10,7},{11,14},{... | collective-permute-start | bytes 98312 | tf_op jit(solution)/shard_map/ppermute | solution.py:502
  5.3 1.3 %collective-permute-start.1 = (bf16[400,128]{1,0:T(8,128)(2,1)S(1)}, bf16[400,128]{1,0:T(8,128)(2,1)S(1)}, u32[]{:S(2)}, u32[]{:S(2)}) collective-permute-start(bf16[400,128]{1,0:T(8,128)(2,1)S(1)} %get-tuple-element.34), channel_id=1, source_target_pairs={{1,2},{2,1},{3,4},{4,3},{5,6},{6,5},{7,8},{8,7},{9,10},{10,9},{11,... | collective-permute-start | bytes 307208 | tf_op jit(solution)/shard_map/ppermute | solution.py:502
  6.0 11.1 %copy-start = (bf16[4,256,1024]{2,1,0:T(8,128)(2,1)S(1)}, bf16[4,256,1024]{2,1,0:T(8,128)(2,1)}, u32[]{:S(2)}) copy-start(bf16[4,256,1024]{2,1,0:T(8,128)(2,1)} %constant.13.clone.shifts_ref.refs_10_) | copy-start | bytes 6291460
  6.0 11.0 %copy-start.1 = (bf16[4,384,128]{2,1,0:T(8,128)(2,1)S(1)}, bf16[4,384,128]{2,1,0:T(8,128)(2,1)}, u32[]{:S(2)}) copy-start(bf16[4,384,128]{2,1,0:T(8,128)(2,1)} %constant.12.clone.ends_ref.refs_9_) | copy-start | bytes 1179652
  6.0 11.0 %copy-start.2 = (bf16[256,512]{1,0:T(8,128)(2,1)S(1)}, bf16[256,512]{1,0:T(8,128)(2,1)}, u32[]{:S(2)}) copy-start(bf16[256,512]{1,0:T(8,128)(2,1)} %constant.11.clone.spread_ref.refs_8_) | copy-start | bytes 786436
  6.0 11.0 %copy-start.3 = (bf16[4,512,128]{2,1,0:T(8,128)(2,1)S(1)}, bf16[4,512,128]{2,1,0:T(8,128)(2,1)}, u32[]{:S(2)}) copy-start(bf16[4,512,128]{2,1,0:T(8,128)(2,1)} %constant.10.clone.strips_hbm.strips_ref) | copy-start | bytes 1572868
  6.0 11.0 %copy-start.4 = (bf16[6,64,512]{2,1,0:T(8,128)(2,1)S(1)}, bf16[6,64,512]{2,1,0:T(8,128)(2,1)}, u32[]{:S(2)}) copy-start(bf16[6,64,512]{2,1,0:T(8,128)(2,1)} %field_ref.1) | copy-start | bytes 1179652
  6.0 11.0 %copy-start.5 = (s32[6,6]{1,0:T(8,128)S(1)}, s32[6,6]{1,0:T(8,128)}, u32[]{:S(2)}) copy-start(s32[6,6]{1,0:T(8,128)} %refs_1_.5) | copy-start | bytes 436
  6.0 11.0 %copy-start.7 = (bf16[6,64,512]{2,1,0:T(8,128)(2,1)S(1)}, bf16[6,64,512]{2,1,0:T(8,128)(2,1)}, u32[]{:S(2)}) copy-start(bf16[6,64,512]{2,1,0:T(8,128)(2,1)} %upstream_ref.1) | copy-start | bytes 1179652
  6.0 11.0 %copy-start.9 = (s32[6,512]{1,0:T(8,128)S(1)}, s32[6,512]{1,0:T(8,128)}, u32[]{:S(2)}) copy-start(s32[6,512]{1,0:T(8,128)} %cortex_ref.1) | copy-start | bytes 36868
  6.0 11.0 %copy-start.10 = (f32[64]{0:T(128)S(1)}, f32[64]{0:T(128)}, u32[]{:S(2)}) copy-start(f32[64]{0:T(128)} %param.14) | copy-start | bytes 772
  6.1 11.0 %copy-start.11 = (f32[160,80]{1,0:T(8,128)S(1)}, f32[160,80]{1,0:T(8,128)}, u32[]{:S(2)}) copy-start(f32[160,80]{1,0:T(8,128)} %constant.20.fold_ref) | copy-start | bytes 153604
  6.6 10.4 %collective-permute-start.3 = (bf16[400,128]{1,0:T(8,128)(2,1)S(1)}, bf16[400,128]{1,0:T(8,128)(2,1)S(1)}, u32[]{:S(2)}, u32[]{:S(2)}) collective-permute-start(bf16[400,128]{1,0:T(8,128)(2,1)S(1)} %collective-permute-done.1.near_ref), channel_id=1, source_target_pairs={{0,1},{1,0},{2,3},{3,2},{4,5},{5,4},{6,7},{7,6},{8,9},{9,8},{10,11... | collective-permute-start | bytes 307208 | tf_op jit(solution)/shard_map/ppermute | solution.py:502
  15.8 1.2 %collective-permute-start.4 = (bf16[128,128]{1,0:T(8,128)(2,1)S(1)}, bf16[128,128]{1,0:T(8,128)(2,1)S(1)}, u32[]{:S(2)}, u32[]{:S(2)}) collective-permute-start(bf16[128,128]{1,0:T(8,128)(2,1)S(1)} %collective-permute-done.2.far_ref), channel_id=1, source_target_pairs={{0,1},{1,0},{2,3},{3,2},{4,5},{5,4},{6,7},{7,6},{8,9},{9,8},{10,11... | collective-permute-start | bytes 98312 | tf_op jit(solution)/shard_map/ppermute | solution.py:502
  24.0 1.6 %collective-permute-start.5 = (bf16[1040,128]{1,0:T(8,128)(2,1)S(1)}, bf16[1040,128]{1,0:T(8,128)(2,1)S(1)}, u32[]{:S(2)}, u32[]{:S(2)}) collective-permute-start(bf16[1040,128]{1,0:T(8,128)(2,1)S(1)} %get-tuple-element.43.own_ref.refs_3_), channel_id=1, source_target_pairs={{0,1},{1,0},{2,3},{3,2},{4,5},{5,4},{6,7},{7,6},{8,9},{9,8},{10,11... | collective-permute-start | bytes 798728 | tf_op jit(solution)/shard_map/ppermute | solution.py:502
  25.9 9.1 %collective-permute-start.8 = (bf16[400,128]{1,0:T(8,128)(2,1)S(1)}, bf16[400,128]{1,0:T(8,128)(2,1)S(1)}, u32[]{:S(2)}, u32[]{:S(2)}) collective-permute-start(bf16[400,128]{1,0:T(8,128)(2,1)S(1)} %get-tuple-element.46), channel_id=1, source_target_pairs={{1,2},{2,1},{3,4},{4,3},{5,6},{6,5},{7,8},{8,7},{9,10},{10,9},{11,... | collective-permute-start | bytes 307208 | tf_op jit(solution)/shard_map/ppermute | solution.py:502
  26.6 8.5 %collective-permute-start.6 = (f32[128,128]{1,0:T(8,128)S(1)}, f32[128,128]{1,0:T(8,128)S(1)}, u32[]{:S(2)}, u32[]{:S(2)}) collective-permute-start(f32[128,128]{1,0:T(8,128)S(1)} %get-tuple-element.47), channel_id=1, source_target_pairs={{0,2},{1,3},{2,0},{3,1},{4,6},{5,7},{6,4},{7,5},{8,10},{9,11},{10,... | collective-permute-start | bytes 196616 | tf_op jit(solution)/shard_map/ppermute | solution.py:502
  30.0 0.7 %collective-permute-start.7 = (bf16[128,128]{1,0:T(8,128)(2,1)S(1)}, bf16[128,128]{1,0:T(8,128)(2,1)S(1)}, u32[]{:S(2)}, u32[]{:S(2)}) collective-permute-start(bf16[128,128]{1,0:T(8,128)(2,1)S(1)} %get-tuple-element.45), channel_id=1, source_target_pairs={{1,4},{3,6},{4,1},{5,8},{6,3},{7,10},{8,5},{9,12},{10,7},{11,14},{... | collective-permute-start | bytes 98312 | tf_op jit(solution)/shard_map/ppermute | solution.py:502
  35.0 4.7 %collective-permute-start.10 = (bf16[528,128]{1,0:T(8,128)(2,1)S(1)}, bf16[528,128]{1,0:T(8,128)(2,1)S(1)}, u32[]{:S(2)}, u32[]{:S(2)}) collective-permute-start(bf16[528,128]{1,0:T(8,128)(2,1)S(1)} %shard_map.154.refs_5_), channel_id=1, source_target_pairs={{0,1},{1,0},{2,3},{3,2},{4,5},{5,4},{6,7},{7,6},{8,9},{9,8},{10,11... | collective-permute-start | bytes 405512 | tf_op jit(solution)/shard_map/ppermute | solution.py:502
  36.1 6.0 %collective-permute-start.9 = (f32[128,128]{1,0:T(8,128)S(1)}, f32[128,128]{1,0:T(8,128)S(1)}, u32[]{:S(2)}, u32[]{:S(2)}) collective-permute-start(f32[128,128]{1,0:T(8,128)S(1)} %add.9), channel_id=1, source_target_pairs={{0,4},{1,5},{2,6},{3,7},{4,0},{5,1},{6,2},{7,3},{8,12},{9,13},{10,... | collective-permute-start | bytes 196616 | tf_op jit(solution)/shard_map/ppermute | solution.py:502
  42.1 4.3 %collective-permute-start.11 = (f32[128,128]{1,0:T(8,128)S(1)}, f32[128,128]{1,0:T(8,128)S(1)}, u32[]{:S(2)}, u32[]{:S(2)}) collective-permute-start(f32[128,128]{1,0:T(8,128)S(1)} %add.10), channel_id=1, source_target_pairs={{0,8},{1,9},{2,10},{3,11},{4,12},{5,13},{6,14},{7,15},{8,0},{9,1},... | collective-permute-start | bytes 196616 | tf_op jit(solution)/shard_map/ppermute | solution.py:502
  46.4 5.3 %collective-permute-start.12 = (f32[128,128]{1,0:T(8,128)S(1)}, f32[128,128]{1,0:T(8,128)S(1)}, u32[]{:S(2)}, u32[]{:S(2)}) collective-permute-start(f32[128,128]{1,0:T(8,128)S(1)} %add.11.a_ref), channel_id=1, source_target_pairs={{0,16},{1,17},{2,18},{3,19},{4,20},{5,21},{6,22},{7,23},{8,24},{9,... | collective-permute-start | bytes 196616 | tf_op jit(solution)/shard_map/ppermute | solution.py:502
  (1 other events, 0.7 us)
